TPU v7x, 128 devices: a whole 4x4x4 slice. The times are simulated.
128 devices in a mesh: section: 2 (over y_lo), slab: 32 (over x, z, y_hi), rep: 2 (over core).
Axes of the slice: x: 4, y: 4 (y_hi: 2, y_lo: 2; y = y_hi * 2 + y_lo), z: 4, core: 2. Of those that a mesh axis runs over, the one named last changes fastest.
Arguments:
- latent: bfloat16 [4, 64, 64, 8, 128], P(('section', 'rep'), None, 'slab'), may hold values from -250 to 250, as said below
- g_weight: bfloat16 [4, 4, 4, 64, 32], replicated, may hold values from -0.25 to 0.25
- bn_gain: float32 [32], replicated, may hold values from 0.1 to 1.9
- bn_shift: float32 [32], replicated, may hold values from -3 to 3
- real_crops: bfloat16 [4, 32, 128, 16, 256], P(('section', 'rep'), None, 'slab'), may hold values from -6 to 6
- d_weight: bfloat16 [4, 4, 4, 32, 64], replicated, may hold values from -0.125 to 0.125
- cot_fake: bfloat16 [4, 64, 64, 8, 128], P(('section', 'rep'), None, 'slab'), may hold values from -6 to 6
- cot_real: bfloat16 [4, 64, 64, 8, 128], P(('section', 'rep'), None, 'slab'), may hold values from -6 to 6
Outputs:
- d_fake: bfloat16 [4, 64, 64, 8, 128], P(('section', 'rep'), None, 'slab')
- d_real: bfloat16 [4, 64, 64, 8, 128], P(('section', 'rep'), None, 'slab')
- fake_grad: bfloat16 [4, 32, 128, 16, 256], P(('section', 'rep'), None, 'slab')
- weight_grad: float32 [4, 4, 4, 32, 64], replicated
Inputs may be any that keep to these rules, and one draw needn't show every extreme that they name: `latent`: entries of order one up to some hundreds.
All inputs are finite; a program needn't handle non-finite values.
Results may differ from a plain program's by a relative error of at most 0.0058.
Values may be sent and summed in bfloat16 or wider, within the bound.
No kernel may reach another device: no remote copies, remote signals or barrier semaphores. Data moves between devices by JAX's collectives and lax.ppermute only.
A program may use at most 64 MiB of HBM per device.

v0:
```python
import jax
import jax.numpy as jnp
from jax import lax
from jax.sharding import PartitionSpec as P

phase_taps = (((1, 0), (3, -1)), ((0, 1), (2, 0)))
read_taps = ((1, -1), (0, 0), (1, 0), (0, 1))


def with_halo(cells, sides, width):
    for axis, dim in sides:
        count = lax.axis_size(axis)
        ends = count - 1
        head = lax.slice_in_dim(cells, 0, width, axis=dim)
        tail = lax.slice_in_dim(cells, cells.shape[dim] - width, cells.shape[dim], axis=dim)
        cells = jnp.concatenate(
            [
                lax.ppermute(tail, axis, [(i, (i + 1) % count) for i in range(ends)]),
                cells,
                lax.ppermute(head, axis, [((i + 1) % count, i) for i in range(ends)]),
            ],
            axis=dim,
        )
    return cells


def activate(before):
    squashed = jax.nn.sigmoid(4.0 * before)
    output = before * (0.2 + 0.8 * squashed)
    derivative = 0.2 + 0.8 * squashed + 3.2 * before * squashed * (1.0 - squashed)
    return (output, derivative)


def left_product(kernel, volume):
    return lax.dot_general(
        kernel, volume, (((0,), (0,)), ((), ())), preferred_element_type=jnp.float32
    )


def expand(padded, g_weight, start_row, row_count, height, breadth):
    phases = []
    for phase_z in range(2):
        for phase_y in range(2):
            for phase_x in range(2):
                total = None
                for kernel_z, offset_z in phase_taps[phase_z]:
                    for kernel_y, offset_y in phase_taps[phase_y]:
                        for kernel_x, offset_x in phase_taps[phase_x]:
                            begin_z = start_row + offset_z + 2
                            piece = padded[
                                :,
                                :,
                                begin_z : begin_z + row_count,
                                offset_y + 1 : offset_y + 1 + height,
                                offset_x + 1 : offset_x + 1 + breadth,
                            ]
                            term = left_product(g_weight[kernel_z, kernel_y, kernel_x], piece)
                            total = term if total is None else total + term
                phases.append(total)
    stacked = jnp.stack(phases)
    return stacked.reshape((2, 2, 2) + stacked.shape[1:])


def tap_piece(extended, kernel_z, kernel_y, kernel_x, depth_rows, height, breadth):
    phase_z, offset_z = read_taps[kernel_z]
    phase_y, offset_y = read_taps[kernel_y]
    phase_x, offset_x = read_taps[kernel_x]
    return extended[
        phase_z,
        phase_y,
        phase_x,
        :,
        :,
        1 + offset_z : 1 + offset_z + depth_rows,
        1 + offset_y : 1 + offset_y + height,
        1 + offset_x : 1 + offset_x + breadth,
    ]


def discriminate(extended, d_weight, depth_rows, height, breadth):
    total = None
    for kernel_z in range(4):
        for kernel_y in range(4):
            for kernel_x in range(4):
                piece = tap_piece(
                    extended, kernel_z, kernel_y, kernel_x, depth_rows, height, breadth
                )
                term = left_product(d_weight[kernel_z, kernel_y, kernel_x], piece)
                total = term if total is None else total + term
    return total


def kernel_terms(extended, grad_value, depth_rows, height, breadth):
    rows = []
    for kernel_z in range(4):
        for kernel_y in range(4):
            for kernel_x in range(4):
                piece = tap_piece(
                    extended, kernel_z, kernel_y, kernel_x, depth_rows, height, breadth
                )
                rows.append(
                    lax.dot_general(
                        piece,
                        grad_value,
                        (((1, 2, 3, 4), (1, 2, 3, 4)), ((), ())),
                        preferred_element_type=jnp.float32,
                    )
                )
    return jnp.stack(rows)


def back_project(grad_padded, d_weight, depth_rows, height, breadth):
    phases = []
    for phase_z in range(2):
        for phase_y in range(2):
            for phase_x in range(2):
                total = None
                for kernel_z, offset_z in phase_taps[phase_z]:
                    for kernel_y, offset_y in phase_taps[phase_y]:
                        for kernel_x, offset_x in phase_taps[phase_x]:
                            piece = grad_padded[
                                :,
                                :,
                                1 + offset_z : 1 + offset_z + depth_rows,
                                1 + offset_y : 1 + offset_y + height,
                                1 + offset_x : 1 + offset_x + breadth,
                            ]
                            weight_tap = d_weight[kernel_z, kernel_y, kernel_x]
                            term = lax.dot_general(
                                weight_tap,
                                piece,
                                (((1,), (0,)), ((), ())),
                                preferred_element_type=jnp.float32,
                            )
                            total = term if total is None else total + term
                phases.append(total)
    stacked = jnp.stack(phases)
    channels, batch_rows = (stacked.shape[1], stacked.shape[2])
    stacked = stacked.reshape(2, 2, 2, channels, batch_rows, depth_rows, height, breadth)
    stacked = stacked.transpose(4, 3, 5, 0, 6, 1, 7, 2)
    return stacked.reshape(batch_rows, channels, 2 * depth_rows, 2 * height, 2 * breadth)


def pad_plane(volume):
    widths = [(0, 0)] * (volume.ndim - 2) + [(1, 1), (1, 1)]
    return jnp.pad(volume, widths)


def local(latent, g_weight, bn_gain, bn_shift, real_crops, d_weight, cot_fake, cot_real):
    batch_rows, depth_rows, height, breadth = (
        latent.shape[0],
        latent.shape[2],
        latent.shape[3],
        latent.shape[4],
    )
    channels = g_weight.shape[4]
    latent_major = latent.transpose(1, 0, 2, 3, 4)
    rimmed = with_halo(latent_major, (("slab", 2),), 1)
    padded = jnp.pad(rimmed, ((0, 0), (0, 0), (1, 1), (1, 1), (1, 1)))
    before = expand(padded, g_weight, 0, depth_rows, height, breadth)
    total_count = float(
        8
        * batch_rows
        * depth_rows
        * height
        * breadth
        * lax.axis_size("section")
        * lax.axis_size("slab")
        * lax.axis_size("rep")
    )
    reduce_axes = (0, 1, 2, 4, 5, 6, 7)
    center = lax.psum(jnp.sum(before, axis=reduce_axes), ("section", "slab", "rep")) / total_count
    centered = before - center[:, None, None, None, None]
    variance = (
        lax.psum(jnp.sum(centered * centered, axis=reduce_axes), ("section", "slab", "rep"))
        / total_count
    )
    factor = bn_gain * lax.rsqrt(variance + 1e-05)
    shifted = (before - center[:, None, None, None, None]) * factor[
        :, None, None, None, None
    ] + bn_shift[:, None, None, None, None]
    fake_ext = with_halo(jnp.maximum(shifted, 0.0).astype(jnp.bfloat16), (("slab", 5),), 1)
    real_phased = real_crops.reshape(
        batch_rows, channels, depth_rows, 2, height, 2, breadth, 2
    ).transpose(3, 5, 7, 1, 0, 2, 4, 6)
    real_ext = with_halo(real_phased, (("slab", 5),), 1)
    fake_ext = pad_plane(fake_ext)
    real_ext = pad_plane(real_ext)
    before_fake = discriminate(fake_ext, d_weight, depth_rows, height, breadth)
    before_real = discriminate(real_ext, d_weight, depth_rows, height, breadth)
    out_fake, slope_fake = activate(before_fake)
    out_real, slope_real = activate(before_real)
    grad_fake = (cot_fake.transpose(1, 0, 2, 3, 4).astype(jnp.float32) * slope_fake).astype(
        jnp.bfloat16
    )
    grad_real = (cot_real.transpose(1, 0, 2, 3, 4).astype(jnp.float32) * slope_real).astype(
        jnp.bfloat16
    )
    local_grad = kernel_terms(fake_ext, grad_fake, depth_rows, height, breadth) + kernel_terms(
        real_ext, grad_real, depth_rows, height, breadth
    )
    summed_grad = lax.psum(
        local_grad.reshape(4, 4, 4, channels, d_weight.shape[4]), ("section", "slab", "rep")
    )
    grad_rimmed = with_halo(grad_fake, (("slab", 2),), 1)
    input_grad = back_project(pad_plane(grad_rimmed), d_weight, depth_rows, height, breadth)
    d_fake = out_fake.astype(jnp.bfloat16).transpose(1, 0, 2, 3, 4)
    d_real = out_real.astype(jnp.bfloat16).transpose(1, 0, 2, 3, 4)
    return (d_fake, d_real, input_grad.astype(jnp.bfloat16), summed_grad)


def solution(mesh):
    in_specs = (
        P(("section", "rep"), None, "slab", None, None),
        P(),
        P(),
        P(),
        P(("section", "rep"), None, "slab", None, None),
        P(),
        P(("section", "rep"), None, "slab", None, None),
        P(("section", "rep"), None, "slab", None, None),
    )
    out_specs = (
        P(("section", "rep"), None, "slab", None, None),
        P(("section", "rep"), None, "slab", None, None),
        P(("section", "rep"), None, "slab", None, None),
        P(),
    )
    return jax.shard_map(local, mesh=mesh, in_specs=in_specs, out_specs=out_specs, check_vma=False)
```

profile of v0, /device:TPU:1, one launch (start us, length us, event | category | flops | bytes accessed | tf_op | source)
XLA Modules:
  0.0 471.3 jit_solution(14725622830107944990)
XLA Ops:
  8.3 5.7 %collective-permute-start = (bf16[64,1,1,8,128]{4,0,3,2,1:T(8,128)(2,1)S(1)}, bf16[64,1,1,8,128]{4,0,3,2,1:T(8,128)(2,1)S(1)}, u32[]{:S(2)}, u32[]{:S(2)}) collective-permute-start(bf16[64,1,1,8,128]{4,0,3,2,1:T(8,128)(2,1)S(1)} %get-tuple-element.46), channel_id=1, source_target_pairs={{0,2},{2,4},{4,6},{6,8},{8,10},{10,12},{12,14},{14,16},{16,18},{18... | collective-permute-start | bytes 393224 | tf_op jit(solution)/shard_map/ppermute | solution.py:18
  13.9 1.3 collective-permute-start.1
  19.8 4.7 %copy.37 = bf16[1,32,4,16,256]{1,4,3,2,0:T(8,128)(2,1)} copy(bf16[1,32,4,16,256]{4,3,2,1,0:T(8,128)(2,1)} %param.12) | data formatting | bytes 2097152 | tf_op args[4]
  24.5 9.2 %copy.38 = bf16[1,32,2,2,8,2,128,2]{6,1,4,2,0,7,5,3:T(8,128)(2,1)S(1)} copy(bf16[1,32,2,2,8,2,128,2]{1,7,6,5,4,3,2,0:T(2,128)(2,1)} %bitcast.3717) | data formatting | bytes 2097152 | tf_op jit(solution)/shard_map/reshape | solution.py:183
  54.0 1.3 copy-done.1
  57.3 5.5 %collective-permute-start.4 = (bf16[2,2,2,32,1,1,8,128]{7,3,6,5,4,2,1,0:T(8,128)(2,1)}, bf16[2,2,2,32,1,1,8,128]{7,3,6,5,4,2,1,0:T(8,128)(2,1)S(1)}, u32[]{:S(2)}, u32[]{:S(2)}) collective-permute-start(bf16[2,2,2,32,1,1,8,128]{7,3,6,5,4,2,1,0:T(8,128)(2,1)} %get-tuple-element.32), channel_id=1, source_target_pairs={{0,2},{2,4},{4,6},{6,8},{8,10},{10,12},{12,14},{14,16},{16,18},{18... | collective-permute-start | bytes 1572872 | tf_op jit(solution)/shard_map/ppermute | solution.py:18
  62.8 71.9 %psum.21 = f32[32]{0:T(128)S(1)} all-reduce(f32[32]{0:T(128)S(1)} %add_add_fusion), channel_id=1, replica_groups=mesh['section'=2,'slab'=32,'rep'=2] {'section','slab','rep'}, use_global_device_ids=true, to_apply=%region_8.9 | all-reduce | flops 32 | bytes 256 | tf_op jit(solution)/shard_map/psum | solution.py:172
  134.7 2.0 multiply_reduce_fusion
  136.8 1.3 collective-permute-start.5
  138.0 72.4 %psum.22 = f32[32]{0:T(128)S(1)} all-reduce(f32[32]{0:T(128)S(1)} %multiply_reduce_fusion), channel_id=1, replica_groups=mesh['section'=2,'slab'=32,'rep'=2] {'section','slab','rep'}, use_global_device_ids=true, to_apply=%region_10.11 | all-reduce | flops 32 | bytes 256 | tf_op jit(solution)/shard_map/psum | solution.py:175
  210.5 2.1 maximum_convert_fusion
  212.6 3.4 collective-permute-start.2
  216.1 1.3 collective-permute-start.3
  217.4 3.9 select_maximum_fusion
  243.9 12.2 %fusion.301 = f32[64,32,64]{2,1,0:T(8,128)S(1)} fusion(f32[64,32,64]{2,1,0:T(8,128)S(1)} %fusion.302, bf16[32,2,8,128]{3,0,2,1:T(8,128)(2,1)S(1)} %get-tuple-element.30, bf16[64,2,8,128]{3,0,2,1:T(8,128)(2,1)S(1)} %get-tuple-element.40), kind=kOutput, calls=%fused_computation.525 | convolution fusion | flops 8388608 | bytes 409600 | tf_op jit(solution)/shard_map/dot_general | solution.py:102
  269.6 2.8 select_maximum_fusion.2
  310.4 1.2 add.1375
  311.7 1.3 collective-permute-start.7
  313.0 6.1 %collective-permute-start.6 = (bf16[64,1,1,8,128]{4,0,3,2,1:T(8,128)(2,1)S(1)}, bf16[64,1,1,8,128]{4,0,3,2,1:T(8,128)(2,1)S(1)}, u32[]{:S(2)}, u32[]{:S(2)}) collective-permute-start(bf16[64,1,1,8,128]{4,0,3,2,1:T(8,128)(2,1)S(1)} %get-tuple-element.44), channel_id=1, source_target_pairs={{0,2},{2,4},{4,6},{6,8},{8,10},{10,12},{12,14},{14,16},{16,18},{18... | collective-permute-start | bytes 393224 | tf_op jit(solution)/shard_map/ppermute | solution.py:18
  320.2 4.8 %collective-permute-done.6 = bf16[64,1,1,8,128]{4,0,3,2,1:T(8,128)(2,1)S(1)} collective-permute-done((bf16[64,1,1,8,128]{4,0,3,2,1:T(8,128)(2,1)S(1)}, bf16[64,1,1,8,128]{4,0,3,2,1:T(8,128)(2,1)S(1)}, u32[]{:S(2)}, u32[]{:S(2)}) %collective-permute-start.6) | collective-permute-done | bytes 131104 | tf_op jit(solution)/shard_map/ppermute | solution.py:18
  339.0 7.3 %copy.40 = bf16[2,2,2,32,1,2,8,128]{3,2,7,1,6,0,5,4:T(2,128)(2,1)} copy(bf16[2,2,2,32,1,2,8,128]{7,3,6,5,2,1,0,4:T(8,128)(2,1)S(1)} %bitcast.3720) | data formatting | bytes 2097152 | tf_op jit(solution)/shard_map/convert_element_type | solution.py:209
  346.2 4.8 %copy.44 = bf16[1,32,4,16,256]{4,3,2,1,0:T(8,128)(2,1)} copy(bf16[1,32,4,16,256]{1,4,3,2,0:T(8,128)(2,1)} %bitcast.3716) | data formatting | bytes 2097152
  351.1 110.7 %all-reduce.6.cloned.1.call-done = f32[4,4,4,32,64]{4,3,2,1,0:T(8,128)} async-done(((f32[4,4,4,32,64]{4,3,2,1,0:T(8,128)}), f32[4,4,4,32,64]{4,3,2,1,0:T(8,128)}) %all-reduce.6.cloned.1.call-update) | async-done | bytes 524304 | tf_op jit(solution)/shard_map/psum | solution.py:202
  461.8 2.3 copy.464
  (435 shorter events, 115.7 us)
Async XLA Ops:
  7.2 454.6 %all-reduce.6.cloned.1.call-start = ((), (), s32[]{:S(2)}) async-start(), calls=%async_computation | async-start | bytes 2097152 | tf_op jit(solution)/shard_map/psum | solution.py:202
  8.3 27.4 %collective-permute-start = (bf16[64,1,1,8,128]{4,0,3,2,1:T(8,128)(2,1)S(1)}, bf16[64,1,1,8,128]{4,0,3,2,1:T(8,128)(2,1)S(1)}, u32[]{:S(2)}, u32[]{:S(2)}) collective-permute-start(bf16[64,1,1,8,128]{4,0,3,2,1:T(8,128)(2,1)S(1)} %get-tuple-element.46), channel_id=1, source_target_pairs={{0,2},{2,4},{4,6},{6,8},{8,10},{10,12},{12,14},{14,16},{16,18},{18... | collective-permute-start | bytes 393224 | tf_op jit(solution)/shard_map/ppermute | solution.py:18
  13.9 21.7 %collective-permute-start.1 = (bf16[64,1,1,8,128]{4,0,3,2,1:T(8,128)(2,1)S(1)}, bf16[64,1,1,8,128]{4,0,3,2,1:T(8,128)(2,1)S(1)}, u32[]{:S(2)}, u32[]{:S(2)}) collective-permute-start(bf16[64,1,1,8,128]{4,0,3,2,1:T(8,128)(2,1)S(1)} %get-tuple-element.47), channel_id=1, source_target_pairs={{2,0},{4,2},{6,4},{8,6},{10,8},{12,10},{14,12},{16,14},{18,16},{20... | collective-permute-start | bytes 393224 | tf_op jit(solution)/shard_map/ppermute | solution.py:20
  19.8 15.0 %copy-start = (bf16[1,64,2,8,128]{4,3,2,1,0:T(8,128)(2,1)S(1)}, bf16[1,64,2,8,128]{4,3,2,1,0:T(8,128)(2,1)}, u32[]{:S(2)}) copy-start(bf16[1,64,2,8,128]{4,3,2,1,0:T(8,128)(2,1)} %param.8) | copy-start | bytes 786436
  33.7 6.9 %copy-start.6 = (bf16[4,4,4,64,32]{3,4,2,1,0:T(8,128)(2,1)S(1)}, bf16[4,4,4,64,32]{3,4,2,1,0:T(8,128)(2,1)}, u32[]{:S(2)}) copy-start(bf16[4,4,4,64,32]{3,4,2,1,0:T(8,128)(2,1)} %param.9) | copy-start | bytes 786436
  52.1 158.4 %copy-start.10 = (f32[32]{0:T(128)S(1)}, f32[32]{0:T(128)}, u32[]{:S(2)}) copy-start(f32[32]{0:T(128)} %param.10) | copy-start | bytes 388
  52.1 158.4 %copy-start.7 = (f32[32]{0:T(128)S(1)}, f32[32]{0:T(128)}, u32[]{:S(2)}) copy-start(f32[32]{0:T(128)} %param.11) | copy-start | bytes 388
  53.9 1.3 copy-start.1
  57.3 160.1 %collective-permute-start.4 = (bf16[2,2,2,32,1,1,8,128]{7,3,6,5,4,2,1,0:T(8,128)(2,1)}, bf16[2,2,2,32,1,1,8,128]{7,3,6,5,4,2,1,0:T(8,128)(2,1)S(1)}, u32[]{:S(2)}, u32[]{:S(2)}) collective-permute-start(bf16[2,2,2,32,1,1,8,128]{7,3,6,5,4,2,1,0:T(8,128)(2,1)} %get-tuple-element.32), channel_id=1, source_target_pairs={{0,2},{2,4},{4,6},{6,8},{8,10},{10,12},{12,14},{14,16},{16,18},{18... | collective-permute-start | bytes 1572872 | tf_op jit(solution)/shard_map/ppermute | solution.py:18
  136.8 80.6 %collective-permute-start.5 = (bf16[2,2,2,32,1,1,8,128]{7,3,6,5,4,2,1,0:T(8,128)(2,1)}, bf16[2,2,2,32,1,1,8,128]{7,3,6,5,4,2,1,0:T(8,128)(2,1)}, u32[]{:S(2)}, u32[]{:S(2)}) collective-permute-start(bf16[2,2,2,32,1,1,8,128]{7,3,6,5,4,2,1,0:T(8,128)(2,1)} %get-tuple-element.33), channel_id=1, source_target_pairs={{2,0},{4,2},{6,4},{8,6},{10,8},{12,10},{14,12},{16,14},{18,16},{20... | collective-permute-start | bytes 1572872 | tf_op jit(solution)/shard_map/ppermute | solution.py:20
  212.6 8.8 %copy-start.2 = (bf16[4,4,4,32,64]{4,3,2,1,0:T(8,128)(2,1)S(1)}, bf16[4,4,4,32,64]{4,3,2,1,0:T(8,128)(2,1)}, u32[]{:S(2)}) copy-start(bf16[4,4,4,32,64]{4,3,2,1,0:T(8,128)(2,1)} %param.13) | copy-start | bytes 786436
  212.6 56.9 %collective-permute-start.2 = (bf16[2,2,2,32,1,1,8,128]{7,3,6,5,4,2,1,0:T(8,128)(2,1)S(1)}, bf16[2,2,2,32,1,1,8,128]{7,3,6,5,4,2,1,0:T(8,128)(2,1)S(1)}, u32[]{:S(2)}, u32[]{:S(2)}) collective-permute-start(bf16[2,2,2,32,1,1,8,128]{7,3,6,5,4,2,1,0:T(8,128)(2,1)S(1)} %get-tuple-element.38), channel_id=1, source_target_pairs={{0,2},{2,4},{4,6},{6,8},{8,10},{10,12},{12,14},{14,16},{16,18},{18... | collective-permute-start | bytes 1572872 | tf_op jit(solution)/shard_map/ppermute | solution.py:18
  216.1 53.6 %collective-permute-start.3 = (bf16[2,2,2,32,1,1,8,128]{7,3,6,5,4,2,1,0:T(8,128)(2,1)S(1)}, bf16[2,2,2,32,1,1,8,128]{7,3,6,5,4,2,1,0:T(8,128)(2,1)S(1)}, u32[]{:S(2)}, u32[]{:S(2)}) collective-permute-start(bf16[2,2,2,32,1,1,8,128]{7,3,6,5,4,2,1,0:T(8,128)(2,1)S(1)} %get-tuple-element.39), channel_id=1, source_target_pairs={{2,0},{4,2},{6,4},{8,6},{10,8},{12,10},{14,12},{16,14},{18,16},{20... | collective-permute-start | bytes 1572872 | tf_op jit(solution)/shard_map/ppermute | solution.py:20
  238.4 2.6 copy-start.8
  288.8 2.7 copy-start.9
  311.7 8.5 %collective-permute-start.7 = (bf16[64,1,1,8,128]{4,0,3,2,1:T(8,128)(2,1)S(1)}, bf16[64,1,1,8,128]{4,0,3,2,1:T(8,128)(2,1)S(1)}, u32[]{:S(2)}, u32[]{:S(2)}) collective-permute-start(bf16[64,1,1,8,128]{4,0,3,2,1:T(8,128)(2,1)S(1)} %get-tuple-element.45), channel_id=1, source_target_pairs={{2,0},{4,2},{6,4},{8,6},{10,8},{12,10},{14,12},{16,14},{18,16},{20... | collective-permute-start | bytes 393224 | tf_op jit(solution)/shard_map/ppermute | solution.py:20
  313.0 11.9 %collective-permute-start.6 = (bf16[64,1,1,8,128]{4,0,3,2,1:T(8,128)(2,1)S(1)}, bf16[64,1,1,8,128]{4,0,3,2,1:T(8,128)(2,1)S(1)}, u32[]{:S(2)}, u32[]{:S(2)}) collective-permute-start(bf16[64,1,1,8,128]{4,0,3,2,1:T(8,128)(2,1)S(1)} %get-tuple-element.44), channel_id=1, source_target_pairs={{0,2},{2,4},{4,6},{6,8},{8,10},{10,12},{12,14},{14,16},{16,18},{18... | collective-permute-start | bytes 393224 | tf_op jit(solution)/shard_map/ppermute | solution.py:18
  328.9 5.3 %copy-start.3 = (f32[2,8,128,32]{2,3,1,0:T(8,128)S(1)}, f32[2,8,128,32]{2,3,1,0:T(8,128)}, u32[]{:S(2)}) copy-start(f32[2,8,128,32]{2,3,1,0:T(8,128)} %fusion.684) | copy-start | bytes 786436
  334.9 1.9 copy-start.4
  335.6 1.9 copy-start.5
Sparse Core Ops, SparseCore 0:
  311.8 149.9 all-reduce.5
where the time goes:
time: 480 us; the launch traced here: 471 us
  blocking collectives  144 us (30%)
  matrix products  119 us (25%)
  waiting for transfers between devices  116 us (24%)
  local copies, waits for them, and re-layouts  33.6 us (7%)
  starting transfers between devices  25.9 us (5%)
  other arithmetic  16.7 us (3%)
  between operations  16.1 us (3%)
    psum x1, waiting for transfers between devices, local(): lax.psum(local_grad.reshape(4, 4, 4, channels, d_weight.shape[4]), ('sect...  111 us
    psum x1, blocking collectives, local(): lax.psum(jnp.sum(centered * centered, axis=reduce_axes), ('section', 'sla...  72.4 us
    psum x1, blocking collectives, local(): lax.psum(jnp.sum(before, axis=reduce_axes), ('section', 'slab', 'rep'))  71.9 us
    dot_general x192, matrix products, left_product(): lax.dot_general(kernel, volume, (((0,), (0,)), ((), ())), preferred_eleme...  60.5 us
    dot_general x128, matrix products, kernel_terms(): lax.dot_general(piece, grad_value, (((1, 2, 3, 4), (1, 2, 3, 4)), ((), ()...  42.1 us
    ppermute x4, starting transfers between devices, with_halo(): lax.ppermute(tail, axis, [(i, (i + 1) % count) for i in range(ends)])  20.7 us
    dot_general x64, matrix products, back_project(): lax.dot_general(weight_tap, piece, (((1,), (0,)), ((), ())), preferred_el...  16.6 us
    unnamed x28, local copies, waits for them, and re-layouts  16 us
  transfers between devices with their start and end apart: 9, of which 2 were waited for; matrix products, arithmetic and copies ran while one was open for 22% of the time, Pallas kernels for 0%

commit v1 on v0

v1 whole, which is shorter than its diff:
```python
import jax
import jax.numpy as jnp
from jax import lax
from jax.experimental import pallas as pl
from jax.experimental.pallas import tpu as pltpu
from jax.sharding import PartitionSpec as P

AXES = ("section", "slab", "rep")
NDEV = 128
C = 64
G = 32
Y = 8
X = 128
CELLS = Y * X
F32 = jnp.float32
BF16 = jnp.bfloat16

phase_taps = (((1, 0), (3, -1)), ((0, 1), (2, 0)))


def dot(a, b, dims=(1, 0)):
    return lax.dot_general(a, b, (((dims[0],), (dims[1],)), ((), ())), preferred_element_type=F32)


def lanes(shape):
    return lax.broadcasted_iota(jnp.int32, shape, len(shape) - 1)


def from_left(tile, lane):
    return jnp.where(lane == 0, 0.0, pltpu.roll(tile, 1, 1))


def from_right(tile, lane):
    return jnp.where(lane == X - 1, 0.0, pltpu.roll(tile, X - 1, 1))


def spread_weights(taps_ref, wide_ref):
    wide_ref[...] = jnp.zeros_like(wide_ref)
    for pz in range(2):
        for py in range(2):
            for px in range(2):
                row = ((1 - pz) * 4 + py * 2 + px) * G
                for kz, oz in phase_taps[pz]:
                    tz = oz if pz == 1 else oz + 1
                    for ky, oy in phase_taps[py]:
                        for kx, ox in phase_taps[px]:
                            col = tz * 576 + (oy + 1) * 192 + (ox + 1) * 64
                            tap = (kz * 16 + ky * 4 + kx) * G
                            wide_ref[row : row + G, col : col + C] = taps_ref[tap : tap + G, :]


def spread_cells(tile, depth, y, lane, patch_ref):
    for xi, moved in ((0, from_left(tile, lane)), (1, tile), (2, from_right(tile, lane))):
        piece = moved.astype(BF16)
        for yi in range(3):
            to = y - (yi - 1)
            if 0 <= to < Y:
                row = depth * 576 + yi * 192 + xi * 64
                patch_ref[row : row + C, to * X : (to + 1) * X] = piece


def clear_rims(depth, patch_ref):
    edge = jnp.zeros((192, X), BF16)
    patch_ref[depth * 576 : depth * 576 + 192, 0:X] = edge
    patch_ref[depth * 576 + 384 : depth * 576 + 576, CELLS - X : CELLS] = edge


def as_row(column, shift):
    sub = lax.broadcasted_iota(jnp.int32, (G, 128), 0)
    return jnp.sum(jnp.where(lanes((G, 128)) == sub + shift, column, 0.0), axis=0, keepdims=True)


def as_column(row, shift):
    sub = lax.broadcasted_iota(jnp.int32, (G, 128), 0)
    return jnp.sum(jnp.where(lanes((G, 128)) == sub + shift, row, 0.0), axis=1, keepdims=True)


def generator_kernel(lat_ref, prev_ref, next_ref, taps_ref, before_ref, stats_ref, wide, patch, wide_lat):
    spread_weights(taps_ref, wide)
    wide_lat[0:1024, :] = lat_ref[...].astype(F32)
    wide_lat[1024:1536, :] = prev_ref[...].astype(F32)
    wide_lat[1536:2048, :] = next_ref[...].astype(F32)
    lane = lanes((C, X))
    for depth, (base, stride) in enumerate(((1024, 8), (0, 16), (8, 16), (1536, 8))):
        clear_rims(depth, patch)
        for y in range(Y):
            spread_cells(wide_lat[pl.ds(base + y, C, stride=stride), :], depth, y, lane, patch)
    for pair in range(3):
        before_ref[pair * 256 : (pair + 1) * 256, :] = dot(
            wide[...], patch[pair * 576 : pair * 576 + 1152, :]
        )
    count = 16.0 * CELLS
    total = jnp.zeros((G, CELLS), F32)
    for block in range(4, 20):
        total += before_ref[block * G : (block + 1) * G, :]
    mean = jnp.sum(total, axis=1, keepdims=True) * (1.0 / count)
    squares = jnp.zeros((G, CELLS), F32)
    for block in range(4, 20):
        off = before_ref[block * G : (block + 1) * G, :] - mean
        squares += off * off
    spread = jnp.sum(squares, axis=1, keepdims=True)
    stats_ref[...] = jnp.broadcast_to(as_row(mean, 0) + as_row(spread, G), (NDEV, 128))


def activate(before):
    squashed = jax.nn.sigmoid(4.0 * before)
    output = before * (0.2 + 0.8 * squashed)
    derivative = 0.2 + 0.8 * squashed + 3.2 * before * squashed * (1.0 - squashed)
    return (output, derivative)


def discriminate(patch, weight_ref, cot_ref, out_ref, wide_cot, wide_out, grad):
    wide_cot[...] = cot_ref[...].astype(F32)
    for m in range(2):
        pre = dot(weight_ref[...], patch[m * 1024 : m * 1024 + 2048, :])
        for y in range(Y):
            output, slope = activate(pre[:, y * X : (y + 1) * X])
            wide_out[pl.ds(m * Y + y, C, stride=16), :] = output
            cot = wide_cot[pl.ds(m * Y + y, C, stride=16), :]
            grad[m * C : (m + 1) * C, y * X : (y + 1) * X] = (cot * slope).astype(BF16)
    out_ref[...] = wide_out[...].astype(BF16)
    terms = None
    for m in range(2):
        part = dot(patch[m * 1024 : m * 1024 + 2048, :], grad[m * C : (m + 1) * C, :], (1, 1))
        terms = part if terms is None else terms + part
    return terms


def real_kernel(
    real_ref, prev_ref, next_ref, weight_ref, cot_ref, out_ref, terms_ref, patch, split, wide_cot, wide_out, grad
):
    source = lax.broadcasted_iota(jnp.int32, (2 * X, X), 0)
    for kx in range(4):
        pick = jnp.where(source == 2 * lanes((2 * X, X)) + kx - 1, 1.0, 0.0).astype(BF16)
        split[kx, 0:2048, :] = dot(real_ref[...], pick)
        split[kx, 2048:2560, :] = dot(prev_ref[...], pick)
        split[kx, 2560:3072, :] = dot(next_ref[...], pick)
    edge = jnp.zeros((128, X), BF16)
    places = ((2048, 16), (0, 64), (16, 64), (32, 64), (48, 64), (2560, 16))
    for depth, (base, stride) in enumerate(places):
        patch[depth * 512 : depth * 512 + 128, 0:X] = edge
        patch[depth * 512 + 384 : depth * 512 + 512, CELLS - X : CELLS] = edge
        for row in range(2 * Y):
            for kx in range(4):
                piece = split[kx, pl.ds(base + row, G, stride=stride), :].astype(BF16)
                for ky in range(4):
                    if (row + 1 - ky) % 2 == 0 and 0 <= (row + 1 - ky) // 2 < Y:
                        y = (row + 1 - ky) // 2
                        at = depth * 512 + ky * 128 + kx * G
                        patch[at : at + G, y * X : (y + 1) * X] = piece
    terms_ref[...] = discriminate(patch, weight_ref, cot_ref, out_ref, wide_cot, wide_out, grad)


def fake_kernel(
    inside_ref,
    before_ref,
    stats_ref,
    gain_ref,
    shift_ref,
    weight_ref,
    cot_ref,
    real_terms_ref,
    out_ref,
    low_ref,
    high_ref,
    terms_ref,
    patch,
    wide_cot,
    wide_out,
    grad,
):
    stats = stats_ref[...]
    count = 16.0 * CELLS
    sums = jnp.sum(stats, axis=0, keepdims=True)
    mean_row = sums * (1.0 / NDEV)
    off = stats - mean_row
    between = as_column(jnp.sum(off * off, axis=0, keepdims=True), 0)
    center = as_column(mean_row, 0)
    variance = (as_column(sums, G) + count * between) * (1.0 / (count * NDEV))
    factor = as_column(gain_ref[...], 0) * lax.rsqrt(variance + 1e-05)
    shift = as_column(shift_ref[...], 0)
    lane = lanes((G, X))
    edge = jnp.zeros((128, X), BF16)
    for depth in range(6):
        patch[depth * 512 : depth * 512 + 128, 0:X] = edge
        patch[depth * 512 + 384 : depth * 512 + 512, CELLS - X : CELLS] = edge
        for py in range(2):
            for px in range(2):
                block = (depth * 4 + py * 2 + px) * G
                for y in range(Y):
                    cells = before_ref[block : block + G, y * X : (y + 1) * X]
                    fake = jnp.maximum((cells - center) * factor + shift, 0.0)
                    if depth == 0:
                        fake = jnp.where(inside_ref[0] > 0, fake, 0.0)
                    if depth == 5:
                        fake = jnp.where(inside_ref[1] > 0, fake, 0.0)
                    if px == 1:
                        pieces = ((2, fake), (0, from_left(fake, lane)))
                    else:
                        pieces = ((1, fake), (3, from_right(fake, lane)))
                    for kx, piece in pieces:
                        piece = piece.astype(BF16)
                        for ky, to in ((2, y), (0, y + 1)) if py == 1 else ((1, y), (3, y - 1)):
                            if 0 <= to < Y:
                                at = depth * 512 + ky * 128 + kx * G
                                patch[at : at + G, to * X : (to + 1) * X] = piece
    terms = discriminate(patch, weight_ref, cot_ref, out_ref, wide_cot, wide_out, grad)
    low_ref[...] = grad[0:C, :]
    high_ref[...] = grad[C : 2 * C, :]
    terms = (terms + real_terms_ref[...]).reshape(NDEV, 16, C)
    terms_ref[...] = jnp.concatenate([terms[:, 0:8, :], terms[:, 8:16, :]], axis=2)


def pullback_kernel(prev_ref, low_ref, high_ref, next_ref, taps_ref, out_ref, wide, patch, wide_out):
    spread_weights(taps_ref, wide)
    lane = lanes((C, X))
    for depth, ref in enumerate((prev_ref, low_ref, high_ref, next_ref)):
        clear_rims(depth, patch)
        for y in range(Y):
            spread_cells(ref[:, y * X : (y + 1) * X].astype(F32), depth, y, lane, patch)
    column = lax.broadcasted_iota(jnp.int32, (2 * X, 2 * X), 1)
    source = lax.broadcasted_iota(jnp.int32, (2 * X, 2 * X), 0)
    weave = jnp.where(source == (column % 2) * X + column // 2, 1.0, 0.0).astype(BF16)
    for pair, first, depths in ((0, 128, (0,)), (1, 0, (1, 2)), (2, 0, (3,))):
        rows = 128 * len(depths)
        result = dot(wide[first : first + rows, :], patch[pair * 576 : pair * 576 + 1152, :])
        result = result.astype(BF16)
        for at, depth in enumerate(depths):
            for py in range(2):
                even = result[at * 128 + py * 64 : at * 128 + py * 64 + G, :]
                odd = result[at * 128 + py * 64 + G : at * 128 + py * 64 + 2 * G, :]
                both = jnp.concatenate(
                    [
                        jnp.concatenate([even[:, y * X : (y + 1) * X], odd[:, y * X : (y + 1) * X]], axis=1)
                        for y in range(Y)
                    ],
                    axis=0,
                )
                woven = dot(both, weave)
                for y in range(Y):
                    place = pl.ds(depth * 16 + 2 * y + py, G, stride=64)
                    wide_out[0, place, :] = woven[y * G : (y + 1) * G, 0:X]
                    wide_out[1, place, :] = woven[y * G : (y + 1) * G, X : 2 * X]
    out_ref[:, 0:X] = wide_out[0].astype(BF16)
    out_ref[:, X : 2 * X] = wide_out[1].astype(BF16)


def call(body, name, args, outs, scratch, flops, smem=0):
    moved = sum(a.size * a.dtype.itemsize for a in args) + sum(o.size * o.dtype.itemsize for o in outs)
    return pl.pallas_call(
        body,
        name=name,
        out_shape=outs,
        in_specs=[pl.BlockSpec(memory_space=pltpu.SMEM)] * smem
        + [pl.BlockSpec(memory_space=pltpu.VMEM)] * (len(args) - smem),
        out_specs=[pl.BlockSpec(memory_space=pltpu.VMEM)] * len(outs),
        scratch_shapes=scratch,
        compiler_params=pltpu.CompilerParams(vmem_limit_bytes=48 * 1024 * 1024),
        cost_estimate=pl.CostEstimate(flops=flops, bytes_accessed=moved, transcendentals=0),
    )(*args)


def exchange(low, high):
    ends = lax.axis_size("slab") - 1
    before = lax.ppermute(high, "slab", [(i, i + 1) for i in range(ends)])
    after = lax.ppermute(low, "slab", [(i + 1, i) for i in range(ends)])
    return before, after


def local(latent, g_weight, bn_gain, bn_shift, real_crops, d_weight, cot_fake, cot_real):
    shape = jax.ShapeDtypeStruct
    taps_g = g_weight.transpose(0, 1, 2, 4, 3).reshape(64 * G, C)
    taps_d = d_weight.reshape(64 * G, C)
    weight = taps_d.T
    lat = latent[0]
    lat_prev, lat_next = exchange(lat[:, 0].reshape(C * Y, X), lat[:, 1].reshape(C * Y, X))
    real = real_crops[0]
    real_prev, real_next = exchange(
        real[:, 0].reshape(G * 2 * Y, 2 * X), real[:, 3].reshape(G * 2 * Y, 2 * X)
    )
    before, stats = call(
        generator_kernel,
        "generator",
        (lat.reshape(C * 2 * Y, X), lat_prev, lat_next, taps_g),
        [shape((768, CELLS), F32), shape((NDEV, 128), F32)],
        [
            pltpu.VMEM((256, 1152), BF16),
            pltpu.VMEM((4 * 576, CELLS), BF16),
            pltpu.VMEM((2048, X), F32),
        ],
        2 * 768 * 1152 * CELLS,
    )
    stats = lax.all_to_all(stats, AXES, 0, 0, tiled=True)
    working = [
        pltpu.VMEM((C * 2 * Y, X), F32),
        pltpu.VMEM((C * 2 * Y, X), F32),
        pltpu.VMEM((2 * C, CELLS), BF16),
    ]
    d_real, real_terms = call(
        real_kernel,
        "real_branch",
        (real.reshape(G * 64, 2 * X), real_prev, real_next, weight, cot_real.reshape(C * 2 * Y, X)),
        [shape((C * 2 * Y, X), BF16), shape((2048, C), F32)],
        [pltpu.VMEM((6 * 512, CELLS), BF16), pltpu.VMEM((4, 3072, X), F32)] + working,
        8 * 2048 * C * CELLS * 2,
    )
    at = lax.axis_index("slab")
    inside = jnp.stack([at > 0, at < lax.axis_size("slab") - 1]).astype(jnp.int32)
    d_fake, low, high, terms = call(
        fake_kernel,
        "fake_branch",
        (
            inside,
            before,
            stats,
            jnp.pad(bn_gain, (0, 128 - G)).reshape(1, 128),
            jnp.pad(bn_shift, (0, 128 - G)).reshape(1, 128),
            weight,
            cot_fake.reshape(C * 2 * Y, X),
            real_terms,
        ),
        [
            shape((C * 2 * Y, X), BF16),
            shape((C, CELLS), BF16),
            shape((C, CELLS), BF16),
            shape((NDEV, 8, 128), F32),
        ],
        [pltpu.VMEM((6 * 512, CELLS), BF16)] + working,
        8 * 2048 * C * CELLS * 2,
        smem=1,
    )
    grad_prev, grad_next = exchange(low, high)
    parts = lax.all_to_all(terms, AXES, 0, 0, tiled=True)
    (fake_grad,) = call(
        pullback_kernel,
        "pullback",
        (grad_prev, low, high, grad_next, taps_d),
        [shape((G * 64, 2 * X), BF16)],
        [
            pltpu.VMEM((256, 1152), BF16),
            pltpu.VMEM((4 * 576, CELLS), BF16),
            pltpu.VMEM((2, G * 64, X), F32),
        ],
        2 * 512 * 1152 * CELLS,
    )
    summed = jnp.broadcast_to(jnp.sum(parts, axis=0, keepdims=True), (NDEV, 8, 128))
    whole = lax.all_to_all(summed, AXES, 0, 0, tiled=True)
    weight_grad = whole.reshape(NDEV, 8, 2, C).transpose(0, 2, 1, 3).reshape(4, 4, 4, G, C)
    return (
        d_fake.reshape(1, C, 2, Y, X),
        d_real.reshape(1, C, 2, Y, X),
        fake_grad.reshape(1, G, 4, 2 * Y, 2 * X),
        weight_grad,
    )


def solution(mesh):
    split = P(("section", "rep"), None, "slab", None, None)
    in_specs = (split, P(), P(), P(), split, P(), split, split)
    out_specs = (split, split, split, P())
    return jax.shard_map(local, mesh=mesh, in_specs=in_specs, out_specs=out_specs, check_vma=False)
```

time: 480 us -> 112 us (0.23); the launches traced: 471 us -> 111 us
  blocking collectives: 144 us -> 23.2 us
  matrix products: 119 us -> 0 us
  waiting for transfers between devices: 116 us -> 9.52 us
  Pallas kernels: 0 us -> 25.3 us
  local copies, waits for them, and re-layouts: 33.6 us -> 11.9 us
  other arithmetic: 16.7 us -> 0.22 us
  between operations: 16.1 us -> 0.8 us
  starting transfers between devices: 25.9 us -> 40.1 us
    psum x2 -> x0, blocking collectives: 144 us -> none  [the longest x1 72.4 us: local(): lax.psum(jnp.sum(centered * centered, axis=reduce_axes), ('section', 'sla...]
    dot_general x384 -> x0, matrix products: 119 us -> none  [the longest x192 60.5 us: left_product(): lax.dot_general(kernel, volume, (((0,), (0,)), ((), ())), preferred_eleme...]
    psum x1 -> x0, waiting for transfers between devices: 111 us -> none  [local(): lax.psum(local_grad.reshape(4, 4, 4, channels, d_weight.shape[4]), ('sect...]
    pallas_call x0 -> x4, Pallas kernels: none -> 25.3 us  [call(): pl.pallas_call(body, name=name, out_shape=outs, in_specs=[pl.BlockSpec(me...]
    all_to_all x0 -> x1, blocking collectives: none -> 23.2 us  [local(): parts = lax.all_to_all(terms, AXES, 0, 0, tiled=True)]
    all_to_all x0 -> x2, starting transfers between devices: none -> 19.4 us  [the longest x1 14.7 us: local(): stats = lax.all_to_all(stats, AXES, 0, 0, tiled=True)]
    unnamed x28 -> x16, local copies, waits for them, and re-layouts: 16 us -> 5.54 us
    reshape x1, local copies, waits for them, and re-layouts: 9.15 us -> 0.68 us  [local(): jnp.pad(bn_shift, (0, 128 - G)).reshape(1, 128)]
  transfers between devices with their start and end apart: 9 -> 8, of which waited for: 2 -> 2; matrix products, arithmetic and copies ran while one was open for 22% -> 3% of each run, Pallas kernels for 0% -> 18%
where the time goes in v1:
time: 112 us; the launch traced here: 111 us
  starting transfers between devices  40.1 us (36%)
  Pallas kernels  25.3 us (23%)
  blocking collectives  23.2 us (21%)
  local copies, waits for them, and re-layouts  11.9 us (11%)
  waiting for transfers between devices  9.52 us (8%)
    pallas_call x4, Pallas kernels, call(): pl.pallas_call(body, name=name, out_shape=outs, in_specs=[pl.BlockSpec(me...  25.3 us
    all_to_all x1, blocking collectives, local(): parts = lax.all_to_all(terms, AXES, 0, 0, tiled=True)  23.2 us
    ppermute x3, starting transfers between devices, exchange(): before = lax.ppermute(high, 'slab', [(i, i + 1) for i in range(ends)])  16.9 us
    all_to_all x1, starting transfers between devices, local(): stats = lax.all_to_all(stats, AXES, 0, 0, tiled=True)  14.7 us
    ppermute x3, waiting for transfers between devices, exchange(): after = lax.ppermute(low, 'slab', [(i + 1, i) for i in range(ends)])  6.1 us
    unnamed x16, local copies, waits for them, and re-layouts  5.54 us
    all_to_all x1, starting transfers between devices, local(): whole = lax.all_to_all(summed, AXES, 0, 0, tiled=True)  4.62 us
    ppermute x3, starting transfers between devices, exchange(): after = lax.ppermute(low, 'slab', [(i + 1, i) for i in range(ends)])  3.88 us
  transfers between devices with their start and end apart: 8, of which 2 were waited for; matrix products, arithmetic and copies ran while one was open for 3% of the time, Pallas kernels for 18%

profile of v1, /device:TPU:1, one launch (start us, length us, event | category | flops | bytes accessed | tf_op | source)
XLA Modules:
  0.0 111.1 jit_solution(2666480633074575814)
XLA Ops:
  0.6 1.0 slice_bitcast_fusion
  1.6 1.3 %collective-permute-start.1 = (bf16[512,128]{1,0:T(8,128)(2,1)S(1)}, bf16[512,128]{1,0:T(8,128)(2,1)S(1)}, u32[]{:S(2)}, u32[]{:S(2)}) collective-permute-start(bf16[512,128]{1,0:T(8,128)(2,1)S(1)} %get-tuple-element.22), channel_id=1, source_target_pairs={{2,0},{4,2},{6,4},{8,6},{10,8},{12,10},{14,12},{16,14},{18,16},{20... | collective-permute-start | bytes 393224 | tf_op jit(solution)/shard_map/ppermute | solution.py:266
  2.9 6.3 %collective-permute-start = (bf16[512,128]{1,0:T(8,128)(2,1)S(1)}, bf16[512,128]{1,0:T(8,128)(2,1)S(1)}, u32[]{:S(2)}, u32[]{:S(2)}) collective-permute-start(bf16[512,128]{1,0:T(8,128)(2,1)S(1)} %get-tuple-element.23), channel_id=1, source_target_pairs={{0,2},{2,4},{4,6},{6,8},{8,10},{10,12},{12,14},{14,16},{16,18},{18... | collective-permute-start | bytes 393224 | tf_op jit(solution)/shard_map/ppermute | solution.py:265
  9.2 1.1 fusion
  10.3 5.8 %collective-permute-start.2 = (bf16[512,256]{1,0:T(8,128)(2,1)S(1)}, bf16[512,256]{1,0:T(8,128)(2,1)S(1)}, u32[]{:S(2)}, u32[]{:S(2)}) collective-permute-start(bf16[512,256]{1,0:T(8,128)(2,1)S(1)} %bitcast.48), channel_id=1, source_target_pairs={{0,2},{2,4},{4,6},{6,8},{8,10},{10,12},{12,14},{14,16},{16,18},{18... | collective-permute-start | bytes 786440 | tf_op jit(solution)/shard_map/ppermute | solution.py:265
  16.1 1.3 %collective-permute-start.3 = (bf16[512,256]{1,0:T(8,128)(2,1)S(1)}, bf16[512,256]{1,0:T(8,128)(2,1)S(1)}, u32[]{:S(2)}, u32[]{:S(2)}) collective-permute-start(bf16[512,256]{1,0:T(8,128)(2,1)S(1)} %bitcast.47), channel_id=1, source_target_pairs={{2,0},{4,2},{6,4},{8,6},{10,8},{12,10},{14,12},{16,14},{18,16},{20... | collective-permute-start | bytes 786440 | tf_op jit(solution)/shard_map/ppermute | solution.py:266
  18.1 1.2 %copy.21.weight_ref = bf16[64,2048]{1,0:T(8,128)(2,1)S(1)} copy(bf16[64,2048]{0,1:T(8,128)(2,1)} %bitcast.35) | data formatting | bytes 524288 | tf_op jit(solution)/shard_map/transpose | solution.py:274
  19.4 0.9 copy-done.2
  20.3 1.0 copy-done.3
  21.4 3.7 %generator.1 = (f32[768,1024]{1,0:T(8,128)S(1)}, f32[128,128]{1,0:T(8,128)}) custom-call(bf16[1024,128]{1,0:T(8,128)(2,1)S(1)} %bitcast.40, bf16[512,128]{1,0:T(8,128)(2,1)S(1)} %collective-permute-done.prev_ref, bf16[512,128]{1,0:T(8,128)(2,1)S(1)} %collective-permute-done.1.next_ref, bf16[2048,64]{1,0:T(8,128)(2,1)S(1)} %bitcast.42), custom_call_target="tpu_custom_call" | custom-call | flops 1811939328 | bytes 3997696 | tf_op jit(solution)/shard_map/generator/pallas_call | solution.py:250
  25.1 1.6 %copy-done.6 = f32[768,1024]{1,0:T(8,128)} copy-done((f32[768,1024]{1,0:T(8,128)}, f32[768,1024]{1,0:T(8,128)S(1)}, u32[]{:S(2)}) %copy-start.6) | copy-done | bytes 3145752
  26.7 14.7 %all-to-all-start = ((f32[128,1,128]{2,1,0:T(1,128)}), f32[128,1,128]{2,1,0:T(1,128)S(1)}, u32[]{:S(2)}, u32[]{:S(2)}) async-start(f32[128,1,128]{2,1,0:T(1,128)} %bitcast.9), calls=%async_computation | async-start | bytes 131072 | tf_op jit(solution)/shard_map/all_to_all | solution.py:293
  41.5 10.9 %real_branch.1 = (bf16[1024,128]{1,0:T(8,128)(2,1)}, f32[2048,64]{1,0:T(8,128)S(1)}) custom-call(bf16[2048,256]{1,0:T(8,128)(2,1)S(1)} %bitcast.38, bf16[512,256]{1,0:T(8,128)(2,1)S(1)} %collective-permute-done.2.prev_ref, bf16[512,256]{1,0:T(8,128)(2,1)S(1)} %collective-permute-done.3.next_ref, bf16[64,2048]{1,0:T(8,128)(2,1)S(1)} %copy.21.weight_ref, ...), custom_call_target="tpu_custom_call" | custom-call | flops 2147483648 | bytes 2883584 | tf_op jit(solution)/shard_map/real_branch/pallas_call | solution.py:250
  52.5 1.9 %copy-done.7 = f32[768,1024]{1,0:T(8,128)S(1)} copy-done((f32[768,1024]{1,0:T(8,128)S(1)}, f32[768,1024]{1,0:T(8,128)}, u32[]{:S(2)}) %copy-start.7) | copy-done | bytes 3145752
  54.3 5.8 %fake_branch.1 = (bf16[1024,128]{1,0:T(8,128)(2,1)}, bf16[64,1024]{1,0:T(8,128)(2,1)S(1)}, bf16[64,1024]{1,0:T(8,128)(2,1)S(1)}, f32[128,8,128]{2,1,0:T(8,128)S(1)}) custom-call(s32[2]{0:T(128)S(1)} %add_convert_fusion.inside_ref, f32[768,1024]{1,0:T(8,128)S(1)} %copy-done.7, f32[128,128]{1,0:T(8,128)S(1)} %bitcast.41, ...), custom_call_target="tpu_custom_call" | custom-call | flops 2147483648 | bytes 5309448 | tf_op jit(solution)/shard_map/fake_branch/pallas_call | solution.py:250
  60.1 23.2 %all_to_all.21 = f32[128,8,128]{2,1,0:T(8,128)S(1)} all-to-all(f32[128,8,128]{2,1,0:T(8,128)S(1)} %get-tuple-element.19), channel_id=1, replica_groups=mesh['section'=2,'slab'=32,'rep'=2] {'section','slab','rep'}, dimensions={0} | all-to-all | bytes 1048576 | tf_op jit(solution)/shard_map/all_to_all | solution.py:333
  83.5 0.8 broadcast_in_dim.2
  84.3 4.6 %all-to-all-start.2 = ((f32[128,8,128]{2,1,0:T(8,128)}), f32[128,8,128]{2,1,0:T(8,128)S(1)}, u32[]{:S(2)}, u32[]{:S(2)}) async-start(f32[128,8,128]{2,1,0:T(8,128)} %broadcast_in_dim.2), calls=%async_computation.2 | async-start | bytes 1048576 | tf_op jit(solution)/shard_map/all_to_all | solution.py:347
  89.0 4.8 %collective-permute-start.4 = (bf16[64,1024]{1,0:T(8,128)(2,1)S(1)}, bf16[64,1024]{1,0:T(8,128)(2,1)S(1)}, u32[]{:S(2)}, u32[]{:S(2)}) collective-permute-start(bf16[64,1024]{1,0:T(8,128)(2,1)S(1)} %get-tuple-element.17.high_ref), channel_id=1, source_target_pairs={{0,2},{2,4},{4,6},{6,8},{8,10},{10,12},{12,14},{14,16},{16,18},{18... | collective-permute-start | bytes 393224 | tf_op jit(solution)/shard_map/ppermute | solution.py:265
  93.8 1.3 %collective-permute-start.5 = (bf16[64,1024]{1,0:T(8,128)(2,1)S(1)}, bf16[64,1024]{1,0:T(8,128)(2,1)S(1)}, u32[]{:S(2)}, u32[]{:S(2)}) collective-permute-start(bf16[64,1024]{1,0:T(8,128)(2,1)S(1)} %get-tuple-element.18.low_ref), channel_id=1, source_target_pairs={{2,0},{4,2},{6,4},{8,6},{10,8},{12,10},{14,12},{16,14},{18,16},{20... | collective-permute-start | bytes 393224 | tf_op jit(solution)/shard_map/ppermute | solution.py:266
  95.1 3.4 %collective-permute-done.4.prev_ref = bf16[64,1024]{1,0:T(8,128)(2,1)S(1)} collective-permute-done((bf16[64,1024]{1,0:T(8,128)(2,1)S(1)}, bf16[64,1024]{1,0:T(8,128)(2,1)S(1)}, u32[]{:S(2)}, u32[]{:S(2)}) %collective-permute-start.4) | collective-permute-done | bytes 131104 | tf_op jit(solution)/shard_map/ppermute | solution.py:265
  98.5 6.1 %collective-permute-done.5.next_ref = bf16[64,1024]{1,0:T(8,128)(2,1)S(1)} collective-permute-done((bf16[64,1024]{1,0:T(8,128)(2,1)S(1)}, bf16[64,1024]{1,0:T(8,128)(2,1)S(1)}, u32[]{:S(2)}, u32[]{:S(2)}) %collective-permute-start.5) | collective-permute-done | bytes 131104 | tf_op jit(solution)/shard_map/ppermute | solution.py:266
  104.6 4.9 %pullback.1 = bf16[2048,256]{1,0:T(8,128)(2,1)} custom-call(bf16[64,1024]{1,0:T(8,128)(2,1)S(1)} %collective-permute-done.4.prev_ref, bf16[64,1024]{1,0:T(8,128)(2,1)S(1)} %get-tuple-element.18.low_ref, bf16[64,1024]{1,0:T(8,128)(2,1)S(1)} %get-tuple-element.17.high_ref, bf16[64,1024]{1,0:T(8,128)(2,1)S(1)} %collective-permute-done.5.next_ref, ...), custom_call_target="tpu_custom_call" | custom-call | flops 1207959552 | bytes 1835008 | tf_op jit(solution)/shard_map/pullback/pallas_call | solution.py:250
  109.8 1.4 %copy.23 = f32[128,2,8,64]{3,2,1,0:T(8,128)} copy(f32[128,2,8,64]{0,3,1,2:T(8,128)S(1)} %bitcast.45) | data formatting | bytes 1048576 | tf_op jit(solution)/shard_map/transpose | solution.py:348
  (22 shorter events, 1.2 us)
Async XLA Ops:
  1.6 17.7 %collective-permute-start.1 = (bf16[512,128]{1,0:T(8,128)(2,1)S(1)}, bf16[512,128]{1,0:T(8,128)(2,1)S(1)}, u32[]{:S(2)}, u32[]{:S(2)}) collective-permute-start(bf16[512,128]{1,0:T(8,128)(2,1)S(1)} %get-tuple-element.22), channel_id=1, source_target_pairs={{2,0},{4,2},{6,4},{8,6},{10,8},{12,10},{14,12},{16,14},{18,16},{20... | collective-permute-start | bytes 393224 | tf_op jit(solution)/shard_map/ppermute | solution.py:266
  2.9 16.5 %collective-permute-start = (bf16[512,128]{1,0:T(8,128)(2,1)S(1)}, bf16[512,128]{1,0:T(8,128)(2,1)S(1)}, u32[]{:S(2)}, u32[]{:S(2)}) collective-permute-start(bf16[512,128]{1,0:T(8,128)(2,1)S(1)} %get-tuple-element.23), channel_id=1, source_target_pairs={{0,2},{2,4},{4,6},{6,8},{8,10},{10,12},{12,14},{14,16},{16,18},{18... | collective-permute-start | bytes 393224 | tf_op jit(solution)/shard_map/ppermute | solution.py:265
  10.3 31.2 %collective-permute-start.2 = (bf16[512,256]{1,0:T(8,128)(2,1)S(1)}, bf16[512,256]{1,0:T(8,128)(2,1)S(1)}, u32[]{:S(2)}, u32[]{:S(2)}) collective-permute-start(bf16[512,256]{1,0:T(8,128)(2,1)S(1)} %bitcast.48), channel_id=1, source_target_pairs={{0,2},{2,4},{4,6},{6,8},{8,10},{10,12},{12,14},{14,16},{16,18},{18... | collective-permute-start | bytes 786440 | tf_op jit(solution)/shard_map/ppermute | solution.py:265
  16.1 25.4 %collective-permute-start.3 = (bf16[512,256]{1,0:T(8,128)(2,1)S(1)}, bf16[512,256]{1,0:T(8,128)(2,1)S(1)}, u32[]{:S(2)}, u32[]{:S(2)}) collective-permute-start(bf16[512,256]{1,0:T(8,128)(2,1)S(1)} %bitcast.47), channel_id=1, source_target_pairs={{2,0},{4,2},{6,4},{8,6},{10,8},{12,10},{14,12},{16,14},{18,16},{20... | collective-permute-start | bytes 786440 | tf_op jit(solution)/shard_map/ppermute | solution.py:266
  19.4 1.0 copy-start.2
  20.3 1.0 copy-start.3
  21.4 20.1 %copy-start.1 = (bf16[1,32,4,16,256]{4,3,2,1,0:T(8,128)(2,1)S(1)}, bf16[1,32,4,16,256]{4,3,2,1,0:T(8,128)(2,1)}, u32[]{:S(2)}) copy-start(bf16[1,32,4,16,256]{4,3,2,1,0:T(8,128)(2,1)} %param.12) | copy-start | bytes 3145732
  21.4 20.1 %copy-start.4 = (bf16[1,64,2,8,128]{4,3,2,1,0:T(8,128)(2,1)S(1)}, bf16[1,64,2,8,128]{4,3,2,1,0:T(8,128)(2,1)}, u32[]{:S(2)}) copy-start(bf16[1,64,2,8,128]{4,3,2,1,0:T(8,128)(2,1)} %param.15) | copy-start | bytes 786436
  25.0 1.6 %copy-start.6 = (f32[768,1024]{1,0:T(8,128)}, f32[768,1024]{1,0:T(8,128)S(1)}, u32[]{:S(2)}) copy-start(f32[768,1024]{1,0:T(8,128)S(1)} %get-tuple-element.12.before_ref) | copy-start | bytes 9437188
  26.7 25.7 %all-to-all-start = ((f32[128,1,128]{2,1,0:T(1,128)}), f32[128,1,128]{2,1,0:T(1,128)S(1)}, u32[]{:S(2)}, u32[]{:S(2)}) async-start(f32[128,1,128]{2,1,0:T(1,128)} %bitcast.9), calls=%async_computation | async-start | bytes 131072 | tf_op jit(solution)/shard_map/all_to_all | solution.py:293
  41.5 10.9 %copy-start.5 = (bf16[1,64,2,8,128]{4,3,2,1,0:T(8,128)(2,1)S(1)}, bf16[1,64,2,8,128]{4,3,2,1,0:T(8,128)(2,1)}, u32[]{:S(2)}) copy-start(bf16[1,64,2,8,128]{4,3,2,1,0:T(8,128)(2,1)} %param.14) | copy-start | bytes 786436
  52.4 1.9 %copy-start.7 = (f32[768,1024]{1,0:T(8,128)S(1)}, f32[768,1024]{1,0:T(8,128)}, u32[]{:S(2)}) copy-start(f32[768,1024]{1,0:T(8,128)} %copy-done.6) | copy-start | bytes 9437188
  60.1 44.5 %copy-start = (bf16[4,4,4,32,64]{4,3,2,1,0:T(8,128)(2,1)S(1)}, bf16[4,4,4,32,64]{4,3,2,1,0:T(8,128)(2,1)}, u32[]{:S(2)}) copy-start(bf16[4,4,4,32,64]{4,3,2,1,0:T(8,128)(2,1)} %param.13) | copy-start | bytes 786436
  84.3 25.2 %all-to-all-start.2 = ((f32[128,8,128]{2,1,0:T(8,128)}), f32[128,8,128]{2,1,0:T(8,128)S(1)}, u32[]{:S(2)}, u32[]{:S(2)}) async-start(f32[128,8,128]{2,1,0:T(8,128)} %broadcast_in_dim.2), calls=%async_computation.2 | async-start | bytes 1048576 | tf_op jit(solution)/shard_map/all_to_all | solution.py:347
  89.0 9.5 %collective-permute-start.4 = (bf16[64,1024]{1,0:T(8,128)(2,1)S(1)}, bf16[64,1024]{1,0:T(8,128)(2,1)S(1)}, u32[]{:S(2)}, u32[]{:S(2)}) collective-permute-start(bf16[64,1024]{1,0:T(8,128)(2,1)S(1)} %get-tuple-element.17.high_ref), channel_id=1, source_target_pairs={{0,2},{2,4},{4,6},{6,8},{8,10},{10,12},{12,14},{14,16},{16,18},{18... | collective-permute-start | bytes 393224 | tf_op jit(solution)/shard_map/ppermute | solution.py:265
  93.8 10.8 %collective-permute-start.5 = (bf16[64,1024]{1,0:T(8,128)(2,1)S(1)}, bf16[64,1024]{1,0:T(8,128)(2,1)S(1)}, u32[]{:S(2)}, u32[]{:S(2)}) collective-permute-start(bf16[64,1024]{1,0:T(8,128)(2,1)S(1)} %get-tuple-element.18.low_ref), channel_id=1, source_target_pairs={{2,0},{4,2},{6,4},{8,6},{10,8},{12,10},{14,12},{16,14},{18,16},{20... | collective-permute-start | bytes 393224 | tf_op jit(solution)/shard_map/ppermute | solution.py:266

commit v2 on v1

--- a/solution.py
+++ b/solution.py
@@ -75,28 +75,39 @@
     return jnp.sum(jnp.where(lanes((G, 128)) == sub + shift, row, 0.0), axis=1, keepdims=True)
 
 
-def generator_kernel(lat_ref, prev_ref, next_ref, taps_ref, before_ref, stats_ref, wide, patch, wide_lat):
-    spread_weights(taps_ref, wide)
-    wide_lat[0:1024, :] = lat_ref[...].astype(F32)
-    wide_lat[1024:1536, :] = prev_ref[...].astype(F32)
-    wide_lat[1536:2048, :] = next_ref[...].astype(F32)
+def own_kernel(lat_ref, taps_ref, wide_ref, own_ref, first_ref, middle_ref, last_ref, wide_lat):
+    spread_weights(taps_ref, wide_ref)
+    wide_lat[...] = lat_ref[...].astype(F32)
     lane = lanes((C, X))
-    for depth, (base, stride) in enumerate(((1024, 8), (0, 16), (8, 16), (1536, 8))):
-        clear_rims(depth, patch)
+    for depth in range(2):
+        clear_rims(depth, own_ref)
         for y in range(Y):
-            spread_cells(wide_lat[pl.ds(base + y, C, stride=stride), :], depth, y, lane, patch)
-    for pair in range(3):
-        before_ref[pair * 256 : (pair + 1) * 256, :] = dot(
-            wide[...], patch[pair * 576 : pair * 576 + 1152, :]
-        )
+            spread_cells(wide_lat[pl.ds(depth * Y + y, C, stride=16), :], depth, y, lane, own_ref)
+    first_ref[...] = dot(wide_ref[:, 576:1152], own_ref[0:576, :])
+    middle_ref[...] = dot(wide_ref[...], own_ref[...])
+    last_ref[...] = dot(wide_ref[:, 0:576], own_ref[576:1152, :])
+
+
+def rim_kernel(prev_ref, next_ref, wide_ref, first_in, middle_ref, last_in, first_ref, last_ref, stats_ref, patch, wide_lat):
+    wide_lat[0:512, :] = prev_ref[...].astype(F32)
+    wide_lat[512:1024, :] = next_ref[...].astype(F32)
+    lane = lanes((C, X))
+    for side in range(2):
+        clear_rims(side, patch)
+        for y in range(Y):
+            spread_cells(wide_lat[pl.ds(side * 512 + y, C, stride=8), :], side, y, lane, patch)
+    first_ref[...] = first_in[...] + dot(wide_ref[:, 0:576], patch[0:576, :])
+    last_ref[...] = last_in[...] + dot(wide_ref[:, 576:1152], patch[576:1152, :])
     count = 16.0 * CELLS
+    blocks = [(first_ref, r) for r in range(4, 8)] + [(middle_ref, r) for r in range(8)]
+    blocks += [(last_ref, r) for r in range(4)]
     total = jnp.zeros((G, CELLS), F32)
-    for block in range(4, 20):
-        total += before_ref[block * G : (block + 1) * G, :]
+    for ref, block in blocks:
+        total += ref[block * G : (block + 1) * G, :]
     mean = jnp.sum(total, axis=1, keepdims=True) * (1.0 / count)
     squares = jnp.zeros((G, CELLS), F32)
-    for block in range(4, 20):
-        off = before_ref[block * G : (block + 1) * G, :] - mean
+    for ref, block in blocks:
+        off = ref[block * G : (block + 1) * G, :] - mean
         squares += off * off
     spread = jnp.sum(squares, axis=1, keepdims=True)
     stats_ref[...] = jnp.broadcast_to(as_row(mean, 0) + as_row(spread, G), (NDEV, 128))
@@ -111,38 +122,51 @@
 
 def discriminate(patch, weight_ref, cot_ref, out_ref, wide_cot, wide_out, grad):
     wide_cot[...] = cot_ref[...].astype(F32)
+    early = weight_ref[:, 0:1024]
+    late = weight_ref[:, 1024:2048]
+    shared = dot(jnp.concatenate([late, early], axis=0), patch[1024:2048, :])
+    pre = (
+        dot(early, patch[0:1024, :]) + shared[0:C, :],
+        shared[C : 2 * C, :] + dot(late, patch[2048:3072, :]),
+    )
+    nothing = jnp.zeros((C, CELLS), BF16)
+    grad[0:C, :] = nothing
+    grad[3 * C : 4 * C, :] = nothing
     for m in range(2):
-        pre = dot(weight_ref[...], patch[m * 1024 : m * 1024 + 2048, :])
         for y in range(Y):
-            output, slope = activate(pre[:, y * X : (y + 1) * X])
+            output, slope = activate(pre[m][:, y * X : (y + 1) * X])
             wide_out[pl.ds(m * Y + y, C, stride=16), :] = output
             cot = wide_cot[pl.ds(m * Y + y, C, stride=16), :]
-            grad[m * C : (m + 1) * C, y * X : (y + 1) * X] = (cot * slope).astype(BF16)
+            grad[(2 - m) * C : (3 - m) * C, y * X : (y + 1) * X] = (cot * slope).astype(BF16)
     out_ref[...] = wide_out[...].astype(BF16)
-    terms = None
-    for m in range(2):
-        part = dot(patch[m * 1024 : m * 1024 + 2048, :], grad[m * C : (m + 1) * C, :], (1, 1))
-        terms = part if terms is None else terms + part
-    return terms
+    terms = dot(patch[0:1024, :], grad[128:256, :], (1, 1))
+    terms += dot(patch[1024:2048, :], grad[64:192, :], (1, 1))
+    return terms + dot(patch[2048:3072, :], grad[0:128, :], (1, 1))
 
 
 def real_kernel(
-    real_ref, prev_ref, next_ref, weight_ref, cot_ref, out_ref, terms_ref, patch, split, wide_cot, wide_out, grad
+    real_ref, prev_ref, next_ref, weight_ref, cot_ref, out_ref, terms_ref, patch, halves, rows, wide_cot, wide_out, grad
 ):
-    source = lax.broadcasted_iota(jnp.int32, (2 * X, X), 0)
-    for kx in range(4):
-        pick = jnp.where(source == 2 * lanes((2 * X, X)) + kx - 1, 1.0, 0.0).astype(BF16)
-        split[kx, 0:2048, :] = dot(real_ref[...], pick)
-        split[kx, 2048:2560, :] = dot(prev_ref[...], pick)
-        split[kx, 2560:3072, :] = dot(next_ref[...], pick)
+    for half in range(2):
+        halves[half, 0:2048, :] = real_ref[:, half * X : (half + 1) * X].astype(F32)
+        halves[half, 2048:2560, :] = prev_ref[:, half * X : (half + 1) * X].astype(F32)
+        halves[half, 2560:3072, :] = next_ref[:, half * X : (half + 1) * X].astype(F32)
+    column = lanes((2 * X, 4 * X))
+    source = lax.broadcasted_iota(jnp.int32, (2 * X, 4 * X), 0)
+    pick = jnp.where(source == 2 * (column % X) + column // X - 1, 1.0, 0.0).astype(BF16)
     edge = jnp.zeros((128, X), BF16)
     places = ((2048, 16), (0, 64), (16, 64), (32, 64), (48, 64), (2560, 16))
     for depth, (base, stride) in enumerate(places):
         patch[depth * 512 : depth * 512 + 128, 0:X] = edge
         patch[depth * 512 + 384 : depth * 512 + 512, CELLS - X : CELLS] = edge
         for row in range(2 * Y):
+            for half in range(2):
+                cells = halves[half, pl.ds(base + row, G, stride=stride), :].astype(BF16)
+                rows[depth * 512 + row * G : depth * 512 + (row + 1) * G, half * X : (half + 1) * X] = cells
+        split = dot(rows[depth * 512 : (depth + 1) * 512, :], pick).astype(BF16)
+        for row in range(2 * Y):
             for kx in range(4):
-                piece = split[kx, pl.ds(base + row, G, stride=stride), :].astype(BF16)
+                piece = split[row * G : (row + 1) * G, kx * X : (kx + 1) * X]
                 for ky in range(4):
                     if (row + 1 - ky) % 2 == 0 and 0 <= (row + 1 - ky) // 2 < Y:
                         y = (row + 1 - ky) // 2
@@ -153,7 +177,9 @@
 
 def fake_kernel(
     inside_ref,
-    before_ref,
+    first_ref,
+    middle_ref,
+    last_ref,
     stats_ref,
     gain_ref,
     shift_ref,
@@ -182,11 +208,12 @@
     lane = lanes((G, X))
     edge = jnp.zeros((128, X), BF16)
     for depth in range(6):
+        before_ref = (first_ref, middle_ref, last_ref)[depth // 2]
         patch[depth * 512 : depth * 512 + 128, 0:X] = edge
         patch[depth * 512 + 384 : depth * 512 + 512, CELLS - X : CELLS] = edge
         for py in range(2):
             for px in range(2):
-                block = (depth * 4 + py * 2 + px) * G
+                block = (depth % 2 * 4 + py * 2 + px) * G
                 for y in range(Y):
                     cells = before_ref[block : block + G, y * X : (y + 1) * X]
                     fake = jnp.maximum((cells - center) * factor + shift, 0.0)
@@ -205,13 +232,25 @@
                                 at = depth * 512 + ky * 128 + kx * G
                                 patch[at : at + G, to * X : (to + 1) * X] = piece
     terms = discriminate(patch, weight_ref, cot_ref, out_ref, wide_cot, wide_out, grad)
-    low_ref[...] = grad[0:C, :]
+    low_ref[...] = grad[2 * C : 3 * C, :]
     high_ref[...] = grad[C : 2 * C, :]
-    terms = (terms + real_terms_ref[...]).reshape(NDEV, 16, C)
-    terms_ref[...] = jnp.concatenate([terms[:, 0:8, :], terms[:, 8:16, :]], axis=2)
-
-
-def pullback_kernel(prev_ref, low_ref, high_ref, next_ref, taps_ref, out_ref, wide, patch, wide_out):
+    terms_ref[...] = terms + real_terms_ref[...]
+
+
+def sum_kernel(parts_ref, prev_ref, next_ref, sums_ref):
+    del prev_ref, next_ref
+    total = jnp.sum(parts_ref[...].reshape(NDEV, 8, 128), axis=0, keepdims=True)
+    sums_ref[...] = jnp.broadcast_to(total, (NDEV, 8, 128)).reshape(NDEV * 8, 128).astype(BF16)
+
+
+def unpack_kernel(sums_ref, out_ref):
+    sums = sums_ref[...].astype(F32)
+    out_ref[0:1024, :] = sums[:, 0:C]
+    out_ref[1024:2048, :] = sums[:, C : 2 * C]
+
+
+def pullback_kernel(prev_ref, low_ref, high_ref, next_ref, taps_ref, sums_ref, out_ref, wide, patch, wide_out):
+    del sums_ref
     spread_weights(taps_ref, wide)
     lane = lanes((C, X))
     for depth, ref in enumerate((prev_ref, low_ref, high_ref, next_ref)):
@@ -245,17 +284,19 @@
     out_ref[:, X : 2 * X] = wide_out[1].astype(BF16)
 
 
-def call(body, name, args, outs, scratch, flops, smem=0):
+def call(body, name, args, outs, scratch, flops, mebibytes, smem=(), unread=()):
     moved = sum(a.size * a.dtype.itemsize for a in args) + sum(o.size * o.dtype.itemsize for o in outs)
+    spaces = [
+        pltpu.SMEM if i in smem else pl.ANY if i in unread else pltpu.VMEM for i in range(len(args))
+    ]
     return pl.pallas_call(
         body,
         name=name,
         out_shape=outs,
-        in_specs=[pl.BlockSpec(memory_space=pltpu.SMEM)] * smem
-        + [pl.BlockSpec(memory_space=pltpu.VMEM)] * (len(args) - smem),
+        in_specs=[pl.BlockSpec(memory_space=space) for space in spaces],
         out_specs=[pl.BlockSpec(memory_space=pltpu.VMEM)] * len(outs),
         scratch_shapes=scratch,
-        compiler_params=pltpu.CompilerParams(vmem_limit_bytes=48 * 1024 * 1024),
+        compiler_params=pltpu.CompilerParams(vmem_limit_bytes=mebibytes * 1024 * 1024),
         cost_estimate=pl.CostEstimate(flops=flops, bytes_accessed=moved, transcendentals=0),
     )(*args)
 
@@ -278,31 +319,43 @@
     real_prev, real_next = exchange(
         real[:, 0].reshape(G * 2 * Y, 2 * X), real[:, 3].reshape(G * 2 * Y, 2 * X)
     )
-    before, stats = call(
-        generator_kernel,
-        "generator",
-        (lat.reshape(C * 2 * Y, X), lat_prev, lat_next, taps_g),
-        [shape((768, CELLS), F32), shape((NDEV, 128), F32)],
-        [
-            pltpu.VMEM((256, 1152), BF16),
-            pltpu.VMEM((4 * 576, CELLS), BF16),
-            pltpu.VMEM((2048, X), F32),
-        ],
-        2 * 768 * 1152 * CELLS,
+    wide, own, first, middle, last = call(
+        own_kernel,
+        "own_cells",
+        (lat.reshape(C * 2 * Y, X), taps_g),
+        [shape((256, 1152), BF16), shape((1152, CELLS), BF16)] + [shape((256, CELLS), F32)] * 3,
+        [pltpu.VMEM((1024, X), F32)],
+        4 * 256 * 1152 * CELLS,
+        16,
+    )
+    first, last, stats = call(
+        rim_kernel,
+        "rim_cells",
+        (lat_prev, lat_next, wide, first, middle, last),
+        [shape((256, CELLS), F32), shape((256, CELLS), F32), shape((NDEV, 128), F32)],
+        [pltpu.VMEM((1152, CELLS), BF16), pltpu.VMEM((1024, X), F32)],
+        2 * 256 * 1152 * CELLS,
+        20,
     )
     stats = lax.all_to_all(stats, AXES, 0, 0, tiled=True)
     working = [
         pltpu.VMEM((C * 2 * Y, X), F32),
         pltpu.VMEM((C * 2 * Y, X), F32),
-        pltpu.VMEM((2 * C, CELLS), BF16),
+        pltpu.VMEM((4 * C, CELLS), BF16),
     ]
     d_real, real_terms = call(
         real_kernel,
         "real_branch",
         (real.reshape(G * 64, 2 * X), real_prev, real_next, weight, cot_real.reshape(C * 2 * Y, X)),
-        [shape((C * 2 * Y, X), BF16), shape((2048, C), F32)],
-        [pltpu.VMEM((6 * 512, CELLS), BF16), pltpu.VMEM((4, 3072, X), F32)] + working,
+        [shape((C * 2 * Y, X), BF16), shape((1024, 2 * C), F32)],
+        [
+            pltpu.VMEM((6 * 512, CELLS), BF16),
+            pltpu.VMEM((2, 3072, X), F32),
+            pltpu.VMEM((3072, 2 * X), BF16),
+        ]
+        + working,
         8 * 2048 * C * CELLS * 2,
+        28,
     )
     at = lax.axis_index("slab")
     inside = jnp.stack([at > 0, at < lax.axis_size("slab") - 1]).astype(jnp.int32)
@@ -311,7 +364,9 @@
         "fake_branch",
         (
             inside,
-            before,
+            first,
+            middle,
+            last,
             stats,
             jnp.pad(bn_gain, (0, 128 - G)).reshape(1, 128),
             jnp.pad(bn_shift, (0, 128 - G)).reshape(1, 128),
@@ -323,18 +378,30 @@
             shape((C * 2 * Y, X), BF16),
             shape((C, CELLS), BF16),
             shape((C, CELLS), BF16),
-            shape((NDEV, 8, 128), F32),
+            shape((NDEV * 8, 128), F32),
         ],
         [pltpu.VMEM((6 * 512, CELLS), BF16)] + working,
         8 * 2048 * C * CELLS * 2,
-        smem=1,
-    )
+        28,
+        smem=(0,),
+    )
+    parts = lax.all_to_all(terms.reshape(NDEV, 8, 128), AXES, 0, 0, tiled=True)
     grad_prev, grad_next = exchange(low, high)
-    parts = lax.all_to_all(terms, AXES, 0, 0, tiled=True)
+    (sums,) = call(
+        sum_kernel,
+        "sum_terms",
+        (parts.reshape(NDEV * 8, 128), grad_prev, grad_next),
+        [shape((NDEV * 8, 128), BF16)],
+        [],
+        NDEV * 1024,
+        8,
+        unread=(1, 2),
+    )
+    whole = lax.all_to_all(sums.reshape(NDEV, 8, 128), AXES, 0, 0, tiled=True)
     (fake_grad,) = call(
         pullback_kernel,
         "pullback",
-        (grad_prev, low, high, grad_next, taps_d),
+        (grad_prev, low, high, grad_next, taps_d, sums),
         [shape((G * 64, 2 * X), BF16)],
         [
             pltpu.VMEM((256, 1152), BF16),
@@ -342,15 +409,23 @@
             pltpu.VMEM((2, G * 64, X), F32),
         ],
         2 * 512 * 1152 * CELLS,
-    )
-    summed = jnp.broadcast_to(jnp.sum(parts, axis=0, keepdims=True), (NDEV, 8, 128))
-    whole = lax.all_to_all(summed, AXES, 0, 0, tiled=True)
-    weight_grad = whole.reshape(NDEV, 8, 2, C).transpose(0, 2, 1, 3).reshape(4, 4, 4, G, C)
+        24,
+        unread=(5,),
+    )
+    (weight_grad,) = call(
+        unpack_kernel,
+        "unpack",
+        (whole.reshape(NDEV * 8, 128),),
+        [shape((2048, C), F32)],
+        [],
+        0,
+        8,
+    )
     return (
         d_fake.reshape(1, C, 2, Y, X),
         d_real.reshape(1, C, 2, Y, X),
         fake_grad.reshape(1, G, 4, 2 * Y, 2 * X),
-        weight_grad,
+        weight_grad.reshape(4, 4, 4, G, C),
     )
 
 

time: 112 us -> 106 us (0.946)
  blocking collectives: 23.2 us -> 0 us
  starting transfers between devices: 40.1 us -> 50.8 us
  waiting for transfers between devices: 9.52 us -> 16.5 us
  local copies, waits for them, and re-layouts: 11.9 us -> 13.4 us
  Pallas kernels: 25.3 us -> 23.9 us
    all_to_all x1 -> x0, blocking collectives: 23.2 us -> none  [local(): parts = lax.all_to_all(terms, AXES, 0, 0, tiled=True)]
    all_to_all x1 -> x2, starting transfers between devices: 4.62 us -> 17.6 us  [the longest x1 8.95 us: local(): parts = lax.all_to_all(terms.reshape(NDEV, 8, 128), AXES, 0, 0, tiled=True)]
    all_to_all x1 -> x2, waiting for transfers between devices: 0.01 us -> 6.13 us  [the longest x1 6.13 us: local(): whole = lax.all_to_all(sums.reshape(NDEV, 8, 128), AXES, 0, 0, tiled=True)]
    unnamed x16 -> x28, local copies, waits for them, and re-layouts: 5.54 us -> 7.9 us
    pallas_call x4 -> x7, Pallas kernels: 25.3 us -> 23.9 us  [call(): pl.pallas_call(body, name=name, out_shape=outs, in_specs=[pl.BlockSpec(me...]
    transpose x1 -> x0, local copies, waits for them, and re-layouts: 1.38 us -> none  [local(): whole.reshape(NDEV, 8, 2, C).transpose(0, 2, 1, 3).reshape(4, 4, 4, G, C)]
    all_to_all x1, starting transfers between devices: 14.7 us -> 13.4 us  [local(): stats = lax.all_to_all(stats, AXES, 0, 0, tiled=True)]
  transfers between devices with their start and end apart: 8 -> 9, of which waited for: 2 -> 4; matrix products, arithmetic and copies ran while one was open for 3% -> 4% of each run, Pallas kernels for 18% -> 16%
where the time goes in v2:
time: 106 us; the launch traced here: 105 us
  starting transfers between devices  50.8 us (48%)
  Pallas kernels  23.9 us (23%)
  waiting for transfers between devices  16.5 us (16%)
  local copies, waits for them, and re-layouts  13.4 us (13%)
    pallas_call x7, Pallas kernels, call(): pl.pallas_call(body, name=name, out_shape=outs, in_specs=[pl.BlockSpec(me...  23.9 us
    ppermute x3, starting transfers between devices, exchange(): before = lax.ppermute(high, 'slab', [(i, i + 1) for i in range(ends)])  15.9 us
    all_to_all x1, starting transfers between devices, local(): stats = lax.all_to_all(stats, AXES, 0, 0, tiled=True)  13.4 us
    all_to_all x1, starting transfers between devices, local(): parts = lax.all_to_all(terms.reshape(NDEV, 8, 128), AXES, 0, 0, tiled=True)  8.95 us
    all_to_all x1, starting transfers between devices, local(): whole = lax.all_to_all(sums.reshape(NDEV, 8, 128), AXES, 0, 0, tiled=True)  8.67 us
    unnamed x28, local copies, waits for them, and re-layouts  7.9 us
    all_to_all x1, waiting for transfers between devices, local(): whole = lax.all_to_all(sums.reshape(NDEV, 8, 128), AXES, 0, 0, tiled=True)  6.13 us
    ppermute x3, waiting for transfers between devices, exchange(): after = lax.ppermute(low, 'slab', [(i + 1, i) for i in range(ends)])  6.1 us
  transfers between devices with their start and end apart: 9, of which 4 were waited for; matrix products, arithmetic and copies ran while one was open for 4% of the time, Pallas kernels for 16%

profile of v2, /device:TPU:1, one launch (start us, length us, event | category | flops | bytes accessed | tf_op | source)
XLA Modules:
  0.0 105.4 jit_solution(17254138032472373192)
XLA Ops:
  0.7 1.7 %slice_bitcast_fusion = (bf16[512,128]{1,0:T(8,128)(2,1)S(1)}, bf16[512,128]{1,0:T(8,128)(2,1)}) fusion(bf16[64,2,8,128]{3,2,1,0:T(8,128)(2,1)} %bitcast.42), kind=kLoop, calls=%fused_computation | loop fusion | bytes 524288 | tf_op jit(solution)/shard_map/reshape;squeeze | solution.py:317
  2.4 5.6 %collective-permute-start = (bf16[512,128]{1,0:T(8,128)(2,1)}, bf16[512,128]{1,0:T(8,128)(2,1)S(1)}, u32[]{:S(2)}, u32[]{:S(2)}) collective-permute-start(bf16[512,128]{1,0:T(8,128)(2,1)} %get-tuple-element.33), channel_id=1, source_target_pairs={{0,2},{2,4},{4,6},{6,8},{8,10},{10,12},{12,14},{14,16},{16,18},{18... | collective-permute-start | bytes 393224 | tf_op jit(solution)/shard_map/ppermute | solution.py:306
  8.0 1.3 %collective-permute-start.1 = (bf16[512,128]{1,0:T(8,128)(2,1)S(1)}, bf16[512,128]{1,0:T(8,128)(2,1)S(1)}, u32[]{:S(2)}, u32[]{:S(2)}) collective-permute-start(bf16[512,128]{1,0:T(8,128)(2,1)S(1)} %get-tuple-element.32), channel_id=1, source_target_pairs={{2,0},{4,2},{6,4},{8,6},{10,8},{12,10},{14,12},{16,14},{18,16},{20... | collective-permute-start | bytes 393224 | tf_op jit(solution)/shard_map/ppermute | solution.py:307
  9.3 1.9 %fusion = (bf16[32,1,16,256]{3,2,1,0:T(8,128)(2,1)}, bf16[32,1,16,256]{3,2,1,0:T(8,128)(2,1)}) fusion(bf16[32,4,16,256]{3,2,1,0:T(8,128)(2,1)} %bitcast.40), kind=kLoop, calls=%fused_computation.5 | loop fusion | bytes 1048576 | tf_op jit(solution)/shard_map/slice | solution.py:320
  11.2 5.5 %collective-permute-start.2 = (bf16[512,256]{1,0:T(8,128)(2,1)}, bf16[512,256]{1,0:T(8,128)(2,1)S(1)}, u32[]{:S(2)}, u32[]{:S(2)}) collective-permute-start(bf16[512,256]{1,0:T(8,128)(2,1)} %bitcast.18), channel_id=1, source_target_pairs={{0,2},{2,4},{4,6},{6,8},{8,10},{10,12},{12,14},{14,16},{16,18},{18... | collective-permute-start | bytes 786440 | tf_op jit(solution)/shard_map/ppermute | solution.py:306
  16.7 1.3 %collective-permute-start.3 = (bf16[512,256]{1,0:T(8,128)(2,1)}, bf16[512,256]{1,0:T(8,128)(2,1)S(1)}, u32[]{:S(2)}, u32[]{:S(2)}) collective-permute-start(bf16[512,256]{1,0:T(8,128)(2,1)} %bitcast.19), channel_id=1, source_target_pairs={{2,0},{4,2},{6,4},{8,6},{10,8},{12,10},{14,12},{16,14},{18,16},{20... | collective-permute-start | bytes 786440 | tf_op jit(solution)/shard_map/ppermute | solution.py:307
  18.7 1.2 %copy.16.weight_ref = bf16[64,2048]{1,0:T(8,128)(2,1)S(1)} copy(bf16[64,2048]{0,1:T(8,128)(2,1)} %bitcast.38) | data formatting | bytes 524288 | tf_op jit(solution)/shard_map/transpose | solution.py:315
  20.0 3.1 %own_cells.1 = (bf16[256,1152]{1,0:T(8,128)(2,1)S(1)}, bf16[1152,1024]{1,0:T(8,128)(2,1)}, f32[256,1024]{1,0:T(8,128)S(1)}, f32[256,1024]{1,0:T(8,128)S(1)}, f32[256,1024]{1,0:T(8,128)S(1)}) custom-call(bf16[1024,128]{1,0:T(8,128)(2,1)S(1)} %bitcast.43, bf16[2048,64]{1,0:T(8,128)(2,1)S(1)} %bitcast.45), custom_call_target="tpu_custom_call" | custom-call | flops 1207959552 | bytes 6619136 | tf_op jit(solution)/shard_map/own_cells/pallas_call | solution.py:292
  23.1 2.3 %rim_cells.1 = (f32[256,1024]{1,0:T(8,128)S(1)}, f32[256,1024]{1,0:T(8,128)S(1)}, f32[128,128]{1,0:T(8,128)}) custom-call(bf16[512,128]{1,0:T(8,128)(2,1)S(1)} %collective-permute-done.prev_ref, bf16[512,128]{1,0:T(8,128)(2,1)S(1)} %collective-permute-done.1.next_ref, bf16[256,1152]{1,0:T(8,128)(2,1)S(1)} %get-tuple-element.17.wide_ref, ...), custom_call_target="tpu_custom_call" | custom-call | flops 603979776 | bytes 6160384 | tf_op jit(solution)/shard_map/rim_cells/pallas_call | solution.py:292
  27.3 13.4 %all-to-all-start = ((f32[128,1,128]{2,1,0:T(1,128)}), f32[128,1,128]{2,1,0:T(1,128)S(1)}, u32[]{:S(2)}, u32[]{:S(2)}) async-start(f32[128,1,128]{2,1,0:T(1,128)} %bitcast.9), calls=%async_computation | async-start | bytes 131072 | tf_op jit(solution)/shard_map/all_to_all | solution.py:340
  42.4 6.2 %real_branch.1 = (bf16[1024,128]{1,0:T(8,128)(2,1)}, f32[1024,128]{1,0:T(8,128)S(1)}) custom-call(bf16[2048,256]{1,0:T(8,128)(2,1)S(1)} %bitcast.41, bf16[512,256]{1,0:T(8,128)(2,1)S(1)} %collective-permute-done.2.prev_ref, bf16[512,256]{1,0:T(8,128)(2,1)S(1)} %copy-done.11, bf16[64,2048]{1,0:T(8,128)(2,1)S(1)} %copy.16.weight_ref, ...), custom_call_target="tpu_custom_call" | custom-call | flops 2147483648 | bytes 2883584 | tf_op jit(solution)/shard_map/real_branch/pallas_call | solution.py:292
  50.3 1.2 %copy-done.4 = f32[256,1024]{1,0:T(8,128)S(1)} copy-done((f32[256,1024]{1,0:T(8,128)S(1)}, f32[256,1024]{1,0:T(8,128)}, u32[]{:S(2)}) %copy-start.4) | copy-done | bytes 1048600
  51.5 1.2 %copy-done.6 = f32[256,1024]{1,0:T(8,128)S(1)} copy-done((f32[256,1024]{1,0:T(8,128)S(1)}, f32[256,1024]{1,0:T(8,128)}, u32[]{:S(2)}) %copy-start.6) | copy-done | bytes 1048600
  52.7 1.0 copy-done.13
  53.8 5.4 %fake_branch.1 = (bf16[1024,128]{1,0:T(8,128)(2,1)}, bf16[64,1024]{1,0:T(8,128)(2,1)S(1)}, bf16[64,1024]{1,0:T(8,128)(2,1)S(1)}, f32[1024,128]{1,0:T(8,128)}) custom-call(s32[2]{0:T(128)S(1)} %add_convert_fusion.inside_ref, f32[256,1024]{1,0:T(8,128)S(1)} %copy-done.4, f32[256,1024]{1,0:T(8,128)S(1)} %get-tuple-element.19.middle_ref, ...), custom_call_target="tpu_custom_call" | custom-call | flops 2147483648 | bytes 5309448 | tf_op jit(solution)/shard_map/fake_branch/pallas_call | solution.py:292
  59.1 9.0 %all-to-all-start.1 = ((f32[128,8,128]{2,1,0:T(8,128)}), f32[128,8,128]{2,1,0:T(8,128)S(1)}, u32[]{:S(2)}, u32[]{:S(2)}) async-start(f32[128,8,128]{2,1,0:T(8,128)} %bitcast.23), calls=%async_computation.1 | async-start | bytes 1048576 | tf_op jit(solution)/shard_map/all_to_all | solution.py:388
  68.1 4.8 %collective-permute-start.4 = (bf16[64,1024]{1,0:T(8,128)(2,1)S(1)}, bf16[64,1024]{1,0:T(8,128)(2,1)S(1)}, u32[]{:S(2)}, u32[]{:S(2)}) collective-permute-start(bf16[64,1024]{1,0:T(8,128)(2,1)S(1)} %get-tuple-element.27.high_ref), channel_id=1, source_target_pairs={{0,2},{2,4},{4,6},{6,8},{8,10},{10,12},{12,14},{14,16},{16,18},{18... | collective-permute-start | bytes 393224 | tf_op jit(solution)/shard_map/ppermute | solution.py:306
  72.9 1.3 %collective-permute-start.5 = (bf16[64,1024]{1,0:T(8,128)(2,1)S(1)}, bf16[64,1024]{1,0:T(8,128)(2,1)S(1)}, u32[]{:S(2)}, u32[]{:S(2)}) collective-permute-start(bf16[64,1024]{1,0:T(8,128)(2,1)S(1)} %get-tuple-element.28.low_ref), channel_id=1, source_target_pairs={{2,0},{4,2},{6,4},{8,6},{10,8},{12,10},{14,12},{16,14},{18,16},{20... | collective-permute-start | bytes 393224 | tf_op jit(solution)/shard_map/ppermute | solution.py:307
  74.2 3.4 %collective-permute-done.4.prev_ref = bf16[64,1024]{1,0:T(8,128)(2,1)S(1)} collective-permute-done((bf16[64,1024]{1,0:T(8,128)(2,1)S(1)}, bf16[64,1024]{1,0:T(8,128)(2,1)S(1)}, u32[]{:S(2)}, u32[]{:S(2)}) %collective-permute-start.4) | collective-permute-done | bytes 131104 | tf_op jit(solution)/shard_map/ppermute | solution.py:306
  77.6 6.1 %collective-permute-done.5.next_ref = bf16[64,1024]{1,0:T(8,128)(2,1)S(1)} collective-permute-done((bf16[64,1024]{1,0:T(8,128)(2,1)S(1)}, bf16[64,1024]{1,0:T(8,128)(2,1)S(1)}, u32[]{:S(2)}, u32[]{:S(2)}) %collective-permute-start.5) | collective-permute-done | bytes 131104 | tf_op jit(solution)/shard_map/ppermute | solution.py:307
  84.6 8.7 %all-to-all-start.2 = ((bf16[128,8,128]{2,1,0:T(8,128)(2,1)}), bf16[128,8,128]{2,1,0:T(8,128)(2,1)S(1)}, u32[]{:S(2)}, u32[]{:S(2)}) async-start(bf16[128,8,128]{2,1,0:T(8,128)(2,1)} %bitcast.26), calls=%async_computation.2 | async-start | bytes 524288 | tf_op jit(solution)/shard_map/all_to_all | solution.py:400
  93.2 4.9 %pullback.1 = bf16[2048,256]{1,0:T(8,128)(2,1)} custom-call(bf16[64,1024]{1,0:T(8,128)(2,1)S(1)} %collective-permute-done.4.prev_ref, bf16[64,1024]{1,0:T(8,128)(2,1)S(1)} %get-tuple-element.28.low_ref, bf16[64,1024]{1,0:T(8,128)(2,1)S(1)} %get-tuple-element.27.high_ref, bf16[64,1024]{1,0:T(8,128)(2,1)S(1)} %collective-permute-done.5.next_ref, ...), custom_call_target="tpu_custom_call" | custom-call | flops 1207959552 | bytes 2097152 | tf_op jit(solution)/shard_map/pullback/pallas_call | solution.py:292
  98.2 6.1 %all-to-all-done.2 = bf16[128,8,128]{2,1,0:T(8,128)(2,1)S(1)} async-done(((bf16[128,8,128]{2,1,0:T(8,128)(2,1)}), bf16[128,8,128]{2,1,0:T(8,128)(2,1)S(1)}, u32[]{:S(2)}, u32[]{:S(2)}) %all-to-all-start.2) | async-done | bytes 262176 | tf_op jit(solution)/shard_map/all_to_all | solution.py:400
  104.3 1.1 %unpack.1 = f32[2048,64]{1,0:T(8,128)} custom-call(bf16[1024,128]{1,0:T(8,128)(2,1)S(1)} %bitcast.37), custom_call_target="tpu_custom_call" | custom-call | bytes 786432 | tf_op jit(solution)/shard_map/unpack/pallas_call | solution.py:292
  (34 shorter events, 6.9 us)
Async XLA Ops:
  0.6 19.3 %copy-start.2 = (bf16[1,64,2,8,128]{4,3,2,1,0:T(8,128)(2,1)S(1)}, bf16[1,64,2,8,128]{4,3,2,1,0:T(8,128)(2,1)}, u32[]{:S(2)}) copy-start(bf16[1,64,2,8,128]{4,3,2,1,0:T(8,128)(2,1)} %param.8) | copy-start | bytes 786436
  0.6 19.3 %copy-start.7 = (bf16[4,4,4,64,32]{3,4,2,1,0:T(8,128)(2,1)S(1)}, bf16[4,4,4,64,32]{3,4,2,1,0:T(8,128)(2,1)}, u32[]{:S(2)}) copy-start(bf16[4,4,4,64,32]{3,4,2,1,0:T(8,128)(2,1)} %param.9) | copy-start | bytes 786436
  2.4 20.8 %collective-permute-start = (bf16[512,128]{1,0:T(8,128)(2,1)}, bf16[512,128]{1,0:T(8,128)(2,1)S(1)}, u32[]{:S(2)}, u32[]{:S(2)}) collective-permute-start(bf16[512,128]{1,0:T(8,128)(2,1)} %get-tuple-element.33), channel_id=1, source_target_pairs={{0,2},{2,4},{4,6},{6,8},{8,10},{10,12},{12,14},{14,16},{16,18},{18... | collective-permute-start | bytes 393224 | tf_op jit(solution)/shard_map/ppermute | solution.py:306
  8.0 15.1 %collective-permute-start.1 = (bf16[512,128]{1,0:T(8,128)(2,1)S(1)}, bf16[512,128]{1,0:T(8,128)(2,1)S(1)}, u32[]{:S(2)}, u32[]{:S(2)}) collective-permute-start(bf16[512,128]{1,0:T(8,128)(2,1)S(1)} %get-tuple-element.32), channel_id=1, source_target_pairs={{2,0},{4,2},{6,4},{8,6},{10,8},{12,10},{14,12},{16,14},{18,16},{20... | collective-permute-start | bytes 393224 | tf_op jit(solution)/shard_map/ppermute | solution.py:307
  11.2 29.5 %collective-permute-start.2 = (bf16[512,256]{1,0:T(8,128)(2,1)}, bf16[512,256]{1,0:T(8,128)(2,1)S(1)}, u32[]{:S(2)}, u32[]{:S(2)}) collective-permute-start(bf16[512,256]{1,0:T(8,128)(2,1)} %bitcast.18), channel_id=1, source_target_pairs={{0,2},{2,4},{4,6},{6,8},{8,10},{10,12},{12,14},{14,16},{16,18},{18... | collective-permute-start | bytes 786440 | tf_op jit(solution)/shard_map/ppermute | solution.py:306
  16.7 24.0 %collective-permute-start.3 = (bf16[512,256]{1,0:T(8,128)(2,1)}, bf16[512,256]{1,0:T(8,128)(2,1)S(1)}, u32[]{:S(2)}, u32[]{:S(2)}) collective-permute-start(bf16[512,256]{1,0:T(8,128)(2,1)} %bitcast.19), channel_id=1, source_target_pairs={{2,0},{4,2},{6,4},{8,6},{10,8},{12,10},{14,12},{16,14},{18,16},{20... | collective-permute-start | bytes 786440 | tf_op jit(solution)/shard_map/ppermute | solution.py:307
  23.1 18.3 %copy-start.1 = (bf16[1,32,4,16,256]{4,3,2,1,0:T(8,128)(2,1)S(1)}, bf16[1,32,4,16,256]{4,3,2,1,0:T(8,128)(2,1)}, u32[]{:S(2)}) copy-start(bf16[1,32,4,16,256]{4,3,2,1,0:T(8,128)(2,1)} %param.12) | copy-start | bytes 3145732
  23.1 18.3 %copy-start.8 = (bf16[1,64,2,8,128]{4,3,2,1,0:T(8,128)(2,1)S(1)}, bf16[1,64,2,8,128]{4,3,2,1,0:T(8,128)(2,1)}, u32[]{:S(2)}) copy-start(bf16[1,64,2,8,128]{4,3,2,1,0:T(8,128)(2,1)} %param.15) | copy-start | bytes 786436
  25.4 1.0 copy-start.3
  26.4 1.0 copy-start.5
  27.3 22.9 %all-to-all-start = ((f32[128,1,128]{2,1,0:T(1,128)}), f32[128,1,128]{2,1,0:T(1,128)S(1)}, u32[]{:S(2)}, u32[]{:S(2)}) async-start(f32[128,1,128]{2,1,0:T(1,128)} %bitcast.9), calls=%async_computation | async-start | bytes 131072 | tf_op jit(solution)/shard_map/all_to_all | solution.py:340
  40.7 0.7 copy-start.10
  41.4 1.0 copy-start.11
  42.4 7.9 %copy-start.9 = (bf16[1,64,2,8,128]{4,3,2,1,0:T(8,128)(2,1)S(1)}, bf16[1,64,2,8,128]{4,3,2,1,0:T(8,128)(2,1)}, u32[]{:S(2)}) copy-start(bf16[1,64,2,8,128]{4,3,2,1,0:T(8,128)(2,1)} %param.14) | copy-start | bytes 786436
  48.6 0.8 copy-start.12
  50.3 1.2 %copy-start.4 = (f32[256,1024]{1,0:T(8,128)S(1)}, f32[256,1024]{1,0:T(8,128)}, u32[]{:S(2)}) copy-start(f32[256,1024]{1,0:T(8,128)} %copy-done.3) | copy-start | bytes 3145732
  51.5 1.2 %copy-start.6 = (f32[256,1024]{1,0:T(8,128)S(1)}, f32[256,1024]{1,0:T(8,128)}, u32[]{:S(2)}) copy-start(f32[256,1024]{1,0:T(8,128)} %copy-done.5) | copy-start | bytes 3145732
  52.7 1.0 copy-start.13
  59.1 34.1 %copy-start = (bf16[4,4,4,32,64]{4,3,2,1,0:T(8,128)(2,1)S(1)}, bf16[4,4,4,32,64]{4,3,2,1,0:T(8,128)(2,1)}, u32[]{:S(2)}) copy-start(bf16[4,4,4,32,64]{4,3,2,1,0:T(8,128)(2,1)} %param.13) | copy-start | bytes 786436
  59.1 24.6 %all-to-all-start.1 = ((f32[128,8,128]{2,1,0:T(8,128)}), f32[128,8,128]{2,1,0:T(8,128)S(1)}, u32[]{:S(2)}, u32[]{:S(2)}) async-start(f32[128,8,128]{2,1,0:T(8,128)} %bitcast.23), calls=%async_computation.1 | async-start | bytes 1048576 | tf_op jit(solution)/shard_map/all_to_all | solution.py:388
  68.1 9.5 %collective-permute-start.4 = (bf16[64,1024]{1,0:T(8,128)(2,1)S(1)}, bf16[64,1024]{1,0:T(8,128)(2,1)S(1)}, u32[]{:S(2)}, u32[]{:S(2)}) collective-permute-start(bf16[64,1024]{1,0:T(8,128)(2,1)S(1)} %get-tuple-element.27.high_ref), channel_id=1, source_target_pairs={{0,2},{2,4},{4,6},{6,8},{8,10},{10,12},{12,14},{14,16},{16,18},{18... | collective-permute-start | bytes 393224 | tf_op jit(solution)/shard_map/ppermute | solution.py:306
  72.9 10.8 %collective-permute-start.5 = (bf16[64,1024]{1,0:T(8,128)(2,1)S(1)}, bf16[64,1024]{1,0:T(8,128)(2,1)S(1)}, u32[]{:S(2)}, u32[]{:S(2)}) collective-permute-start(bf16[64,1024]{1,0:T(8,128)(2,1)S(1)} %get-tuple-element.28.low_ref), channel_id=1, source_target_pairs={{2,0},{4,2},{6,4},{8,6},{10,8},{12,10},{14,12},{16,14},{18,16},{20... | collective-permute-start | bytes 393224 | tf_op jit(solution)/shard_map/ppermute | solution.py:307
  84.6 19.8 %all-to-all-start.2 = ((bf16[128,8,128]{2,1,0:T(8,128)(2,1)}), bf16[128,8,128]{2,1,0:T(8,128)(2,1)S(1)}, u32[]{:S(2)}, u32[]{:S(2)}) async-start(bf16[128,8,128]{2,1,0:T(8,128)(2,1)} %bitcast.26), calls=%async_computation.2 | async-start | bytes 524288 | tf_op jit(solution)/shard_map/all_to_all | solution.py:400

commit v3 on v2

--- a/solution.py
+++ b/solution.py
@@ -65,30 +65,64 @@
     patch_ref[depth * 576 + 384 : depth * 576 + 576, CELLS - X : CELLS] = edge
 
 
+def fetch(source, target, sem):
+    copy = pltpu.make_async_copy(source, target, sem)
+    copy.start()
+    return copy
+
+
 def as_row(column, shift):
     sub = lax.broadcasted_iota(jnp.int32, (G, 128), 0)
     return jnp.sum(jnp.where(lanes((G, 128)) == sub + shift, column, 0.0), axis=0, keepdims=True)
 
 
 def as_column(row, shift):
-    sub = lax.broadcasted_iota(jnp.int32, (G, 128), 0)
-    return jnp.sum(jnp.where(lanes((G, 128)) == sub + shift, row, 0.0), axis=1, keepdims=True)
-
-
-def own_kernel(lat_ref, taps_ref, wide_ref, own_ref, first_ref, middle_ref, last_ref, wide_lat):
+    shape = (G, row.shape[1])
+    sub = lax.broadcasted_iota(jnp.int32, shape, 0)
+    return jnp.sum(jnp.where(lanes(shape) == sub + shift, row, 0.0), axis=1, keepdims=True)
+
+
+def own_kernel(lat_ref, taps_ref, taps_d_ref, wide_ref, first_ref, middle_ref, last_ref, weight_ref, patch, wide_lat):
     spread_weights(taps_ref, wide_ref)
     wide_lat[...] = lat_ref[...].astype(F32)
     lane = lanes((C, X))
     for depth in range(2):
-        clear_rims(depth, own_ref)
+        clear_rims(depth, patch)
         for y in range(Y):
-            spread_cells(wide_lat[pl.ds(depth * Y + y, C, stride=16), :], depth, y, lane, own_ref)
-    first_ref[...] = dot(wide_ref[:, 576:1152], own_ref[0:576, :])
-    middle_ref[...] = dot(wide_ref[...], own_ref[...])
-    last_ref[...] = dot(wide_ref[:, 0:576], own_ref[576:1152, :])
-
-
-def rim_kernel(prev_ref, next_ref, wide_ref, first_in, middle_ref, last_in, first_ref, last_ref, stats_ref, patch, wide_lat):
+            spread_cells(wide_lat[pl.ds(depth * Y + y, C, stride=16), :], depth, y, lane, patch)
+    first_ref[...] = dot(wide_ref[:, 576:1152], patch[0:576, :])
+    middle_ref[...] = dot(wide_ref[...], patch[...])
+    last_ref[...] = dot(wide_ref[:, 0:576], patch[576:1152, :])
+    same = lax.broadcasted_iota(jnp.int32, (C, C), 0) == lanes((C, C))
+    unit = jnp.where(same, 1.0, 0.0).astype(BF16)
+    weight_ref[...] = dot(unit, taps_d_ref[...], (1, 1)).astype(BF16)
+
+
+def rim_kernel(
+    prev_ref,
+    next_ref,
+    wide_ref,
+    first_in,
+    middle_in,
+    last_in,
+    real_ref,
+    first_out,
+    middle_out,
+    last_out,
+    stats_ref,
+    low_out,
+    high_out,
+    patch,
+    wide_lat,
+    first,
+    last,
+    sems,
+):
+    copies = [
+        fetch(real_ref.at[:, 0], low_out, sems.at[0]),
+        fetch(real_ref.at[:, 3], high_out, sems.at[1]),
+        fetch(middle_in, middle_out, sems.at[2]),
+    ]
     wide_lat[0:512, :] = prev_ref[...].astype(F32)
     wide_lat[512:1024, :] = next_ref[...].astype(F32)
     lane = lanes((C, X))
@@ -96,11 +130,13 @@
         clear_rims(side, patch)
         for y in range(Y):
             spread_cells(wide_lat[pl.ds(side * 512 + y, C, stride=8), :], side, y, lane, patch)
-    first_ref[...] = first_in[...] + dot(wide_ref[:, 0:576], patch[0:576, :])
-    last_ref[...] = last_in[...] + dot(wide_ref[:, 576:1152], patch[576:1152, :])
+    first[...] = first_in[...] + dot(wide_ref[:, 0:576], patch[0:576, :])
+    copies.append(fetch(first, first_out, sems.at[3]))
+    last[...] = last_in[...] + dot(wide_ref[:, 576:1152], patch[576:1152, :])
+    copies.append(fetch(last, last_out, sems.at[4]))
     count = 16.0 * CELLS
-    blocks = [(first_ref, r) for r in range(4, 8)] + [(middle_ref, r) for r in range(8)]
-    blocks += [(last_ref, r) for r in range(4)]
+    blocks = [(first, r) for r in range(4, 8)] + [(middle_in, r) for r in range(8)]
+    blocks += [(last, r) for r in range(4)]
     total = jnp.zeros((G, CELLS), F32)
     for ref, block in blocks:
         total += ref[block * G : (block + 1) * G, :]
@@ -111,6 +147,8 @@
         squares += off * off
     spread = jnp.sum(squares, axis=1, keepdims=True)
     stats_ref[...] = jnp.broadcast_to(as_row(mean, 0) + as_row(spread, G), (NDEV, 128))
+    for copy in copies:
+        copy.wait()
 
 
 def activate(before):
@@ -120,15 +158,8 @@
     return (output, derivative)
 
 
-def discriminate(patch, weight_ref, cot_ref, out_ref, wide_cot, wide_out, grad):
+def finish(pre, cot_ref, out_ref, wide_cot, wide_out, grad):
     wide_cot[...] = cot_ref[...].astype(F32)
-    early = weight_ref[:, 0:1024]
-    late = weight_ref[:, 1024:2048]
-    shared = dot(jnp.concatenate([late, early], axis=0), patch[1024:2048, :])
-    pre = (
-        dot(early, patch[0:1024, :]) + shared[0:C, :],
-        shared[C : 2 * C, :] + dot(late, patch[2048:3072, :]),
-    )
     nothing = jnp.zeros((C, CELLS), BF16)
     grad[0:C, :] = nothing
     grad[3 * C : 4 * C, :] = nothing
@@ -139,62 +170,114 @@
             cot = wide_cot[pl.ds(m * Y + y, C, stride=16), :]
             grad[(2 - m) * C : (3 - m) * C, y * X : (y + 1) * X] = (cot * slope).astype(BF16)
     out_ref[...] = wide_out[...].astype(BF16)
-    terms = dot(patch[0:1024, :], grad[128:256, :], (1, 1))
-    terms += dot(patch[1024:2048, :], grad[64:192, :], (1, 1))
-    return terms + dot(patch[2048:3072, :], grad[0:128, :], (1, 1))
-
-
-def real_kernel(
-    real_ref, prev_ref, next_ref, weight_ref, cot_ref, out_ref, terms_ref, patch, halves, rows, wide_cot, wide_out, grad
-):
+
+
+def kernel_terms(planes, grad):
+    halves = []
     for half in range(2):
-        halves[half, 0:2048, :] = real_ref[:, half * X : (half + 1) * X].astype(F32)
-        halves[half, 2048:2560, :] = prev_ref[:, half * X : (half + 1) * X].astype(F32)
-        halves[half, 2560:3072, :] = next_ref[:, half * X : (half + 1) * X].astype(F32)
+        terms = dot(planes[half], grad[128:256, :], (1, 1))
+        terms += dot(planes[half + 2], grad[64:192, :], (1, 1))
+        halves.append(terms + dot(planes[half + 4], grad[0:128, :], (1, 1)))
+    return halves
+
+
+def split_depth(at, places, halves, rows, patch):
+    base, stride = places
     column = lanes((2 * X, 4 * X))
     source = lax.broadcasted_iota(jnp.int32, (2 * X, 4 * X), 0)
     pick = jnp.where(source == 2 * (column % X) + column // X - 1, 1.0, 0.0).astype(BF16)
     edge = jnp.zeros((128, X), BF16)
-    places = ((2048, 16), (0, 64), (16, 64), (32, 64), (48, 64), (2560, 16))
-    for depth, (base, stride) in enumerate(places):
-        patch[depth * 512 : depth * 512 + 128, 0:X] = edge
-        patch[depth * 512 + 384 : depth * 512 + 512, CELLS - X : CELLS] = edge
-        for row in range(2 * Y):
-            for half in range(2):
-                cells = halves[half, pl.ds(base + row, G, stride=stride), :].astype(BF16)
-                rows[depth * 512 + row * G : depth * 512 + (row + 1) * G, half * X : (half + 1) * X] = cells
-        split = dot(rows[depth * 512 : (depth + 1) * 512, :], pick).astype(BF16)
-        for row in range(2 * Y):
-            for kx in range(4):
-                piece = split[row * G : (row + 1) * G, kx * X : (kx + 1) * X]
-                for ky in range(4):
-                    if (row + 1 - ky) % 2 == 0 and 0 <= (row + 1 - ky) // 2 < Y:
-                        y = (row + 1 - ky) // 2
-                        at = depth * 512 + ky * 128 + kx * G
-                        patch[at : at + G, y * X : (y + 1) * X] = piece
-    terms_ref[...] = discriminate(patch, weight_ref, cot_ref, out_ref, wide_cot, wide_out, grad)
+    patch[at : at + 128, 0:X] = edge
+    patch[at + 384 : at + 512, CELLS - X : CELLS] = edge
+    for row in range(2 * Y):
+        for half in range(2):
+            cells = halves[half, pl.ds(base + row, G, stride=stride), :].astype(BF16)
+            rows[at + row * G : at + (row + 1) * G, half * X : (half + 1) * X] = cells
+    split = dot(rows[at : at + 512, :], pick).astype(BF16)
+    for row in range(2 * Y):
+        for kx in range(4):
+            piece = split[row * G : (row + 1) * G, kx * X : (kx + 1) * X]
+            for ky in range(4):
+                if (row + 1 - ky) % 2 == 0 and 0 <= (row + 1 - ky) // 2 < Y:
+                    y = (row + 1 - ky) // 2
+                    place = at + ky * 128 + kx * G
+                    patch[place : place + G, y * X : (y + 1) * X] = piece
+
+
+def real_own_kernel(real_ref, weight_ref, low_ref, patch_ref, pre_ref, halves, rows):
+    del low_ref
+    for half in range(2):
+        halves[half] = real_ref[:, half * X : (half + 1) * X].astype(F32)
+    for depth in range(4):
+        split_depth(depth * 512, (depth * 16, 64), halves, rows, patch_ref)
+    late_early = jnp.concatenate([weight_ref[:, 1024:2048], weight_ref[:, 0:1024]], axis=0)
+    both = dot(late_early, patch_ref[512:1536, :])
+    pre_ref[0:C, :] = both[0:C, :] + dot(weight_ref[:, 512:1024], patch_ref[0:512, :])
+    pre_ref[C : 2 * C, :] = both[C : 2 * C, :] + dot(weight_ref[:, 1024:1536], patch_ref[1536:2048, :])
+
+
+def real_kernel(
+    prev_ref,
+    next_ref,
+    own_ref,
+    pre_ref,
+    weight_ref,
+    cot_ref,
+    out_ref,
+    terms_out,
+    terms_ref,
+    sem,
+    patch,
+    halves,
+    rows,
+    wide_cot,
+    wide_out,
+    grad,
+):
+    for half in range(2):
+        halves[half, 0:512, :] = prev_ref[:, half * X : (half + 1) * X].astype(F32)
+        halves[half, 512:1024, :] = next_ref[:, half * X : (half + 1) * X].astype(F32)
+    for side in range(2):
+        split_depth(side * 512, (side * 512, 16), halves, rows, patch)
+    pre = (
+        pre_ref[0:C, :] + dot(weight_ref[:, 0:512], patch[0:512, :]),
+        pre_ref[C : 2 * C, :] + dot(weight_ref[:, 1536:2048], patch[512:1024, :]),
+    )
+    finish(pre, cot_ref, out_ref, wide_cot, wide_out, grad)
+    own = [own_ref[depth * 512 : (depth + 1) * 512, :] for depth in range(4)]
+    planes = [patch[0:512, :]] + own + [patch[512:1024, :]]
+    for half, terms in enumerate(kernel_terms(planes, grad)):
+        terms_ref[half * 512 : (half + 1) * 512, :] = terms
+    fetch(terms_ref, terms_out, sem).wait()
 
 
 def fake_kernel(
     inside_ref,
-    first_ref,
-    middle_ref,
-    last_ref,
+    first_in,
+    middle_in,
+    last_in,
     stats_ref,
     gain_ref,
     shift_ref,
     weight_ref,
     cot_ref,
-    real_terms_ref,
+    real_terms_in,
     out_ref,
     low_ref,
     high_ref,
     terms_ref,
+    before,
+    real_terms,
+    sems,
     patch,
     wide_cot,
     wide_out,
     grad,
 ):
+    befores = [
+        fetch(ref, before.at[i], sems.at[i]) for i, ref in enumerate((first_in, middle_in, last_in))
+    ]
+    real_copy = fetch(real_terms_in, real_terms, sems.at[3])
     stats = stats_ref[...]
     count = 16.0 * CELLS
     sums = jnp.sum(stats, axis=0, keepdims=True)
@@ -208,14 +291,15 @@
     lane = lanes((G, X))
     edge = jnp.zeros((128, X), BF16)
     for depth in range(6):
-        before_ref = (first_ref, middle_ref, last_ref)[depth // 2]
+        if depth % 2 == 0:
+            befores[depth // 2].wait()
         patch[depth * 512 : depth * 512 + 128, 0:X] = edge
         patch[depth * 512 + 384 : depth * 512 + 512, CELLS - X : CELLS] = edge
         for py in range(2):
             for px in range(2):
                 block = (depth % 2 * 4 + py * 2 + px) * G
                 for y in range(Y):
-                    cells = before_ref[block : block + G, y * X : (y + 1) * X]
+                    cells = before[depth // 2, block : block + G, y * X : (y + 1) * X]
                     fake = jnp.maximum((cells - center) * factor + shift, 0.0)
                     if depth == 0:
                         fake = jnp.where(inside_ref[0] > 0, fake, 0.0)
@@ -231,14 +315,25 @@
                             if 0 <= to < Y:
                                 at = depth * 512 + ky * 128 + kx * G
                                 patch[at : at + G, to * X : (to + 1) * X] = piece
-    terms = discriminate(patch, weight_ref, cot_ref, out_ref, wide_cot, wide_out, grad)
+    early = weight_ref[:, 0:1024]
+    late = weight_ref[:, 1024:2048]
+    shared = dot(jnp.concatenate([late, early], axis=0), patch[1024:2048, :])
+    pre = (
+        dot(early, patch[0:1024, :]) + shared[0:C, :],
+        shared[C : 2 * C, :] + dot(late, patch[2048:3072, :]),
+    )
+    finish(pre, cot_ref, out_ref, wide_cot, wide_out, grad)
     low_ref[...] = grad[2 * C : 3 * C, :]
     high_ref[...] = grad[C : 2 * C, :]
-    terms_ref[...] = terms + real_terms_ref[...]
-
-
-def sum_kernel(parts_ref, prev_ref, next_ref, sums_ref):
-    del prev_ref, next_ref
+    planes = [patch[depth * 512 : (depth + 1) * 512, :] for depth in range(6)]
+    real_copy.wait()
+    for half, terms in enumerate(kernel_terms(planes, grad)):
+        rows = slice(half * 512, (half + 1) * 512)
+        terms_ref[rows, :] = terms + real_terms[rows, :]
+
+
+def sum_kernel(parts_ref, edge_ref, sums_ref):
+    del edge_ref
     total = jnp.sum(parts_ref[...].reshape(NDEV, 8, 128), axis=0, keepdims=True)
     sums_ref[...] = jnp.broadcast_to(total, (NDEV, 8, 128)).reshape(NDEV * 8, 128).astype(BF16)
 
@@ -284,17 +379,22 @@
     out_ref[:, X : 2 * X] = wide_out[1].astype(BF16)
 
 
-def call(body, name, args, outs, scratch, flops, mebibytes, smem=(), unread=()):
+def call(body, name, args, outs, scratch, flops, mebibytes, smem=(), far=(), far_outs=()):
     moved = sum(a.size * a.dtype.itemsize for a in args) + sum(o.size * o.dtype.itemsize for o in outs)
     spaces = [
-        pltpu.SMEM if i in smem else pl.ANY if i in unread else pltpu.VMEM for i in range(len(args))
+        pltpu.SMEM if i in smem else pl.ANY if i in far else pltpu.VMEM for i in range(len(args))
+    ]
+    out_spaces = [pltpu.HBM if i in far_outs else pltpu.VMEM for i in range(len(outs))]
+    outs = [pltpu.HBM(o.shape, o.dtype) if i in far_outs else o for i, o in enumerate(outs)]
+    args = [
+        pltpu.with_memory_space_constraint(a, pltpu.HBM) if i in far else a for i, a in enumerate(args)
     ]
     return pl.pallas_call(
         body,
         name=name,
         out_shape=outs,
         in_specs=[pl.BlockSpec(memory_space=space) for space in spaces],
-        out_specs=[pl.BlockSpec(memory_space=pltpu.VMEM)] * len(outs),
+        out_specs=[pl.BlockSpec(memory_space=space) for space in out_spaces],
         scratch_shapes=scratch,
         compiler_params=pltpu.CompilerParams(vmem_limit_bytes=mebibytes * 1024 * 1024),
         cost_estimate=pl.CostEstimate(flops=flops, bytes_accessed=moved, transcendentals=0),
@@ -312,32 +412,49 @@
     shape = jax.ShapeDtypeStruct
     taps_g = g_weight.transpose(0, 1, 2, 4, 3).reshape(64 * G, C)
     taps_d = d_weight.reshape(64 * G, C)
-    weight = taps_d.T
     lat = latent[0]
     lat_prev, lat_next = exchange(lat[:, 0].reshape(C * Y, X), lat[:, 1].reshape(C * Y, X))
     real = real_crops[0]
-    real_prev, real_next = exchange(
-        real[:, 0].reshape(G * 2 * Y, 2 * X), real[:, 3].reshape(G * 2 * Y, 2 * X)
-    )
-    wide, own, first, middle, last = call(
+    wide, first, middle, last, weight = call(
         own_kernel,
         "own_cells",
-        (lat.reshape(C * 2 * Y, X), taps_g),
-        [shape((256, 1152), BF16), shape((1152, CELLS), BF16)] + [shape((256, CELLS), F32)] * 3,
-        [pltpu.VMEM((1024, X), F32)],
+        (lat.reshape(C * 2 * Y, X), taps_g, taps_d),
+        [shape((256, 1152), BF16)] + [shape((256, CELLS), F32)] * 3 + [shape((C, 2048), BF16)],
+        [pltpu.VMEM((1152, CELLS), BF16), pltpu.VMEM((1024, X), F32)],
         4 * 256 * 1152 * CELLS,
         16,
     )
-    first, last, stats = call(
+    first, middle, last, stats, real_low, real_high = call(
         rim_kernel,
         "rim_cells",
-        (lat_prev, lat_next, wide, first, middle, last),
-        [shape((256, CELLS), F32), shape((256, CELLS), F32), shape((NDEV, 128), F32)],
-        [pltpu.VMEM((1152, CELLS), BF16), pltpu.VMEM((1024, X), F32)],
+        (lat_prev, lat_next, wide, first, middle, last, real),
+        [shape((256, CELLS), F32)] * 3
+        + [shape((NDEV, 128), F32)]
+        + [shape((G, 2 * Y, 2 * X), BF16)] * 2,
+        [
+            pltpu.VMEM((1152, CELLS), BF16),
+            pltpu.VMEM((1024, X), F32),
+            pltpu.VMEM((256, CELLS), F32),
+            pltpu.VMEM((256, CELLS), F32),
+            pltpu.SemaphoreType.DMA((5,)),
+        ],
         2 * 256 * 1152 * CELLS,
         20,
+        far=(6,),
+        far_outs=(0, 1, 2, 4, 5),
     )
     stats = lax.all_to_all(stats, AXES, 0, 0, tiled=True)
+    real_prev, real_next = exchange(real_low, real_high)
+    real_patch, real_pre = call(
+        real_own_kernel,
+        "real_own",
+        (real.reshape(G * 64, 2 * X), weight, real_low),
+        [shape((2048, CELLS), BF16), shape((2 * C, CELLS), F32)],
+        [pltpu.VMEM((2, 2048, X), F32), pltpu.VMEM((2048, 2 * X), BF16)],
+        4 * 2048 * C * CELLS,
+        16,
+        far=(2,),
+    )
     working = [
         pltpu.VMEM((C * 2 * Y, X), F32),
         pltpu.VMEM((C * 2 * Y, X), F32),
@@ -346,16 +463,26 @@
     d_real, real_terms = call(
         real_kernel,
         "real_branch",
-        (real.reshape(G * 64, 2 * X), real_prev, real_next, weight, cot_real.reshape(C * 2 * Y, X)),
+        (
+            real_prev.reshape(G * 16, 2 * X),
+            real_next.reshape(G * 16, 2 * X),
+            real_patch,
+            real_pre,
+            weight,
+            cot_real.reshape(C * 2 * Y, X),
+        ),
         [shape((C * 2 * Y, X), BF16), shape((1024, 2 * C), F32)],
         [
-            pltpu.VMEM((6 * 512, CELLS), BF16),
-            pltpu.VMEM((2, 3072, X), F32),
-            pltpu.VMEM((3072, 2 * X), BF16),
+            pltpu.VMEM((1024, 2 * C), F32),
+            pltpu.SemaphoreType.DMA,
+            pltpu.VMEM((1024, CELLS), BF16),
+            pltpu.VMEM((2, 1024, X), F32),
+            pltpu.VMEM((1024, 2 * X), BF16),
         ]
         + working,
-        8 * 2048 * C * CELLS * 2,
-        28,
+        8 * 2048 * C * CELLS,
+        20,
+        far_outs=(1,),
     )
     at = lax.axis_index("slab")
     inside = jnp.stack([at > 0, at < lax.axis_size("slab") - 1]).astype(jnp.int32)
@@ -368,8 +495,8 @@
             middle,
             last,
             stats,
-            jnp.pad(bn_gain, (0, 128 - G)).reshape(1, 128),
-            jnp.pad(bn_shift, (0, 128 - G)).reshape(1, 128),
+            bn_gain.reshape(1, G),
+            bn_shift.reshape(1, G),
             weight,
             cot_fake.reshape(C * 2 * Y, X),
             real_terms,
@@ -380,22 +507,29 @@
             shape((C, CELLS), BF16),
             shape((NDEV * 8, 128), F32),
         ],
-        [pltpu.VMEM((6 * 512, CELLS), BF16)] + working,
+        [
+            pltpu.VMEM((3, 256, CELLS), F32),
+            pltpu.VMEM((NDEV * 8, 128), F32),
+            pltpu.SemaphoreType.DMA((4,)),
+            pltpu.VMEM((6 * 512, CELLS), BF16),
+        ]
+        + working,
         8 * 2048 * C * CELLS * 2,
         28,
         smem=(0,),
+        far=(1, 2, 3, 9),
     )
     parts = lax.all_to_all(terms.reshape(NDEV, 8, 128), AXES, 0, 0, tiled=True)
     grad_prev, grad_next = exchange(low, high)
     (sums,) = call(
         sum_kernel,
         "sum_terms",
-        (parts.reshape(NDEV * 8, 128), grad_prev, grad_next),
+        (parts.reshape(NDEV * 8, 128), grad_prev),
         [shape((NDEV * 8, 128), BF16)],
         [],
         NDEV * 1024,
         8,
-        unread=(1, 2),
+        far=(1,),
     )
     whole = lax.all_to_all(sums.reshape(NDEV, 8, 128), AXES, 0, 0, tiled=True)
     (fake_grad,) = call(
@@ -410,7 +544,7 @@
         ],
         2 * 512 * 1152 * CELLS,
         24,
-        unread=(5,),
+        far=(5,),
     )
     (weight_grad,) = call(
         unpack_kernel,

time: 106 us -> 119 us (1.12)
  Pallas kernels: 23.9 us -> 42 us
  local copies, waits for them, and re-layouts: 13.4 us -> 4.96 us
  waiting for transfers between devices: 16.5 us -> 19.3 us
    pallas_call x7 -> x8, Pallas kernels: 23.9 us -> 42 us  [call(): pl.pallas_call(body, name=name, out_shape=outs, in_specs=[pl.BlockSpec(me...]
    all_to_all x1, waiting for transfers between devices: 6.13 us -> 0.01 us  [local(): whole = lax.all_to_all(sums.reshape(NDEV, 8, 128), AXES, 0, 0, tiled=True)]
    all_to_all x1, waiting for transfers between devices: 0.01 us -> 4.14 us  [local(): parts = lax.all_to_all(terms.reshape(NDEV, 8, 128), AXES, 0, 0, tiled=True)]
    unnamed x28 -> x22, local copies, waits for them, and re-layouts: 7.9 us -> 3.97 us
    ppermute x3, waiting for transfers between devices: 6.1 us -> 8.94 us  [exchange(): after = lax.ppermute(low, 'slab', [(i + 1, i) for i in range(ends)])]
    all_to_all x1, starting transfers between devices: 13.4 us -> 15.8 us  [local(): stats = lax.all_to_all(stats, AXES, 0, 0, tiled=True)]
    all_to_all x1, starting transfers between devices: 8.67 us -> 6.61 us  [local(): whole = lax.all_to_all(sums.reshape(NDEV, 8, 128), AXES, 0, 0, tiled=True)]
    slice x1 -> x0, local copies, waits for them, and re-layouts: 1.86 us -> none  [local(): real[:, 0].reshape(G * 2 * Y, 2 * X)]
  transfers between devices with their start and end apart: 9 -> 9, of which waited for: 4 -> 5; matrix products, arithmetic and copies ran while one was open for 4% -> 0% of each run, Pallas kernels for 16% -> 13%
where the time goes in v3:
time: 119 us; the launch traced here: 118 us
  starting transfers between devices  50.9 us (43%)
  Pallas kernels  42 us (35%)
  waiting for transfers between devices  19.3 us (16%)
  local copies, waits for them, and re-layouts  4.96 us (4%)
    pallas_call x8, Pallas kernels, call(): pl.pallas_call(body, name=name, out_shape=outs, in_specs=[pl.BlockSpec(me...  42 us
    ppermute x3, starting transfers between devices, exchange(): before = lax.ppermute(high, 'slab', [(i, i + 1) for i in range(ends)])  16 us
    all_to_all x1, starting transfers between devices, local(): stats = lax.all_to_all(stats, AXES, 0, 0, tiled=True)  15.8 us
    ppermute x3, waiting for transfers between devices, exchange(): after = lax.ppermute(low, 'slab', [(i + 1, i) for i in range(ends)])  8.94 us
    all_to_all x1, starting transfers between devices, local(): parts = lax.all_to_all(terms.reshape(NDEV, 8, 128), AXES, 0, 0, tiled=True)  8.3 us
    all_to_all x1, starting transfers between devices, local(): whole = lax.all_to_all(sums.reshape(NDEV, 8, 128), AXES, 0, 0, tiled=True)  6.61 us
    ppermute x3, waiting for transfers between devices, exchange(): before = lax.ppermute(high, 'slab', [(i, i + 1) for i in range(ends)])  4.71 us
    ppermute x3, starting transfers between devices, exchange(): after = lax.ppermute(low, 'slab', [(i + 1, i) for i in range(ends)])  4.23 us
  transfers between devices with their start and end apart: 9, of which 5 were waited for; matrix products, arithmetic and copies ran while one was open for 0% of the time, Pallas kernels for 13%

profile of v3, /device:TPU:1, one launch (start us, length us, event | category | flops | bytes accessed | tf_op | source)
XLA Modules:
  0.0 118.1 jit_solution(1075097295097073477)
XLA Ops:
  0.6 1.0 slice_bitcast_fusion
  1.6 5.7 %collective-permute-start = (bf16[512,128]{1,0:T(8,128)(2,1)S(1)}, bf16[512,128]{1,0:T(8,128)(2,1)S(1)}, u32[]{:S(2)}, u32[]{:S(2)}) collective-permute-start(bf16[512,128]{1,0:T(8,128)(2,1)S(1)} %get-tuple-element.43), channel_id=1, source_target_pairs={{0,2},{2,4},{4,6},{6,8},{8,10},{10,12},{12,14},{14,16},{16,18},{18... | collective-permute-start | bytes 393224 | tf_op jit(solution)/shard_map/ppermute | solution.py:406
  7.3 1.3 %collective-permute-start.1 = (bf16[512,128]{1,0:T(8,128)(2,1)S(1)}, bf16[512,128]{1,0:T(8,128)(2,1)S(1)}, u32[]{:S(2)}, u32[]{:S(2)}) collective-permute-start(bf16[512,128]{1,0:T(8,128)(2,1)S(1)} %get-tuple-element.42), channel_id=1, source_target_pairs={{2,0},{4,2},{6,4},{8,6},{10,8},{12,10},{14,12},{16,14},{18,16},{20... | collective-permute-start | bytes 393224 | tf_op jit(solution)/shard_map/ppermute | solution.py:407
  8.6 0.9 copy-done.2
  9.5 1.0 copy-done.5
  10.6 1.0 copy-done.6
  11.6 2.2 %own_cells.1 = (bf16[256,1152]{1,0:T(8,128)(2,1)S(1)}, f32[256,1024]{1,0:T(8,128)S(1)}, f32[256,1024]{1,0:T(8,128)S(1)}, f32[256,1024]{1,0:T(8,128)S(1)}, bf16[64,2048]{1,0:T(8,128)(2,1)S(1)}) custom-call(bf16[1024,128]{1,0:T(8,128)(2,1)S(1)} %bitcast.40, bf16[2048,64]{1,0:T(8,128)(2,1)S(1)} %bitcast.42, bf16[2048,64]{1,0:T(8,128)(2,1)S(1)} %bitcast.43), custom_call_target="tpu_custom_call" | custom-call | flops 1207959552 | bytes 4784128 | tf_op jit(solution)/shard_map/own_cells/pallas_call | solution.py:392
  14.5 17.6 %rim_cells.1 = (f32[256,1024]{1,0:T(8,128)}, f32[256,1024]{1,0:T(8,128)}, f32[256,1024]{1,0:T(8,128)}, f32[128,128]{1,0:T(8,128)}, bf16[32,16,256]{2,1,0:T(8,128)(2,1)}, /*index=5*/bf16[32,16,256]{2,1,0:T(8,128)(2,1)}) custom-call(bf16[512,128]{1,0:T(8,128)(2,1)S(1)} %collective-permute-done.prev_ref, bf16[512,128]{1,0:T(8,128)(2,1)S(1)} %collective-permute-done.1.next_ref, ...), custom_call_target="tpu_custom_call" | custom-call | flops 603979776 | bytes 8781824 | tf_op jit(solution)/shard_map/rim_cells/pallas_call | solution.py:392
  32.2 1.4 %collective-permute-start.3 = (bf16[32,16,256]{2,1,0:T(8,128)(2,1)}, bf16[32,16,256]{2,1,0:T(8,128)(2,1)S(1)}, u32[]{:S(2)}, u32[]{:S(2)}) collective-permute-start(bf16[32,16,256]{2,1,0:T(8,128)(2,1)} %get-tuple-element.33.low_ref), channel_id=1, source_target_pairs={{2,0},{4,2},{6,4},{8,6},{10,8},{12,10},{14,12},{16,14},{18,16},{20... | collective-permute-start | bytes 786440 | tf_op jit(solution)/shard_map/ppermute | solution.py:407
  33.6 5.5 %collective-permute-start.2 = (bf16[32,16,256]{2,1,0:T(8,128)(2,1)}, bf16[32,16,256]{2,1,0:T(8,128)(2,1)S(1)}, u32[]{:S(2)}, u32[]{:S(2)}) collective-permute-start(bf16[32,16,256]{2,1,0:T(8,128)(2,1)} %get-tuple-element.32), channel_id=1, source_target_pairs={{0,2},{2,4},{4,6},{6,8},{8,10},{10,12},{12,14},{14,16},{16,18},{18... | collective-permute-start | bytes 786440 | tf_op jit(solution)/shard_map/ppermute | solution.py:406
  39.2 15.8 %all-to-all-start = ((f32[128,1,128]{2,1,0:T(1,128)}), f32[128,1,128]{2,1,0:T(1,128)S(1)}, u32[]{:S(2)}, u32[]{:S(2)}) async-start(f32[128,1,128]{2,1,0:T(1,128)} %bitcast.11), calls=%async_computation | async-start | bytes 131072 | tf_op jit(solution)/shard_map/all_to_all | solution.py:446
  55.0 3.3 %real_own.1 = (bf16[2048,1024]{1,0:T(8,128)(2,1)S(1)}, f32[128,1024]{1,0:T(8,128)S(1)}) custom-call(bf16[2048,256]{1,0:T(8,128)(2,1)S(1)} %bitcast.34, bf16[64,2048]{1,0:T(8,128)(2,1)S(1)} %get-tuple-element.31.weight_ref, bf16[32,16,256]{2,1,0:T(8,128)(2,1)} %get-tuple-element.33.low_ref), custom_call_target="tpu_custom_call" | custom-call | flops 536870912 | bytes 6291456 | tf_op jit(solution)/shard_map/real_own/pallas_call | solution.py:392
  58.3 4.7 %real_branch.1 = (bf16[1024,128]{1,0:T(8,128)(2,1)}, f32[1024,128]{1,0:T(8,128)}) custom-call(bf16[512,256]{1,0:T(8,128)(2,1)S(1)} %bitcast.38, bf16[512,256]{1,0:T(8,128)(2,1)S(1)} %bitcast.37, bf16[2048,1024]{1,0:T(8,128)(2,1)S(1)} %get-tuple-element.34.own_ref, f32[128,1024]{1,0:T(8,128)S(1)} %get-tuple-element.35.pre_ref, ...), custom_call_target="tpu_custom_call" | custom-call | flops 1073741824 | bytes 6553600 | tf_op jit(solution)/shard_map/real_branch/pallas_call | solution.py:392
  63.1 1.5 %all-to-all-done = f32[128,1,128]{2,1,0:T(1,128)S(1)} async-done(((f32[128,1,128]{2,1,0:T(1,128)}), f32[128,1,128]{2,1,0:T(1,128)S(1)}, u32[]{:S(2)}, u32[]{:S(2)}) %all-to-all-start) | async-done | bytes 65568 | tf_op jit(solution)/shard_map/all_to_all | solution.py:446
  64.6 7.3 %fake_branch.1 = (bf16[1024,128]{1,0:T(8,128)(2,1)}, bf16[64,1024]{1,0:T(8,128)(2,1)S(1)}, bf16[64,1024]{1,0:T(8,128)(2,1)S(1)}, f32[1024,128]{1,0:T(8,128)}) custom-call(s32[2]{0:T(128)S(1)} %add_convert_fusion.inside_ref, f32[256,1024]{1,0:T(8,128)} %get-tuple-element.27.first_in, f32[256,1024]{1,0:T(8,128)} %get-tuple-element.28.middle_in, ...), custom_call_target="tpu_custom_call" | custom-call | flops 2147483648 | bytes 5308680 | tf_op jit(solution)/shard_map/fake_branch/pallas_call | solution.py:392
  71.9 8.3 %all-to-all-start.1 = ((f32[128,8,128]{2,1,0:T(8,128)}), f32[128,8,128]{2,1,0:T(8,128)S(1)}, u32[]{:S(2)}, u32[]{:S(2)}) async-start(f32[128,8,128]{2,1,0:T(8,128)} %bitcast.22), calls=%async_computation.1 | async-start | bytes 1048576 | tf_op jit(solution)/shard_map/all_to_all | solution.py:522
  80.2 4.8 %collective-permute-start.4 = (bf16[64,1024]{1,0:T(8,128)(2,1)S(1)}, bf16[64,1024]{1,0:T(8,128)(2,1)S(1)}, u32[]{:S(2)}, u32[]{:S(2)}) collective-permute-start(bf16[64,1024]{1,0:T(8,128)(2,1)S(1)} %get-tuple-element.39.high_ref), channel_id=1, source_target_pairs={{0,2},{2,4},{4,6},{6,8},{8,10},{10,12},{12,14},{14,16},{16,18},{18... | collective-permute-start | bytes 393224 | tf_op jit(solution)/shard_map/ppermute | solution.py:406
  85.0 4.7 %collective-permute-done.4.edge_ref.prev_ref = bf16[64,1024]{1,0:T(8,128)(2,1)S(1)} collective-permute-done((bf16[64,1024]{1,0:T(8,128)(2,1)S(1)}, bf16[64,1024]{1,0:T(8,128)(2,1)S(1)}, u32[]{:S(2)}, u32[]{:S(2)}) %collective-permute-start.4) | collective-permute-done | bytes 131104 | tf_op jit(solution)/shard_map/ppermute | solution.py:406
  89.7 4.1 %all-to-all-done.1 = f32[128,8,128]{2,1,0:T(8,128)S(1)} async-done(((f32[128,8,128]{2,1,0:T(8,128)}), f32[128,8,128]{2,1,0:T(8,128)S(1)}, u32[]{:S(2)}, u32[]{:S(2)}) %all-to-all-start.1) | async-done | bytes 524320 | tf_op jit(solution)/shard_map/all_to_all | solution.py:522
  94.7 6.6 %all-to-all-start.2 = ((bf16[128,8,128]{2,1,0:T(8,128)(2,1)}), bf16[128,8,128]{2,1,0:T(8,128)(2,1)S(1)}, u32[]{:S(2)}, u32[]{:S(2)}) async-start(bf16[128,8,128]{2,1,0:T(8,128)(2,1)} %bitcast.25), calls=%async_computation.2 | async-start | bytes 524288 | tf_op jit(solution)/shard_map/all_to_all | solution.py:534
  101.3 1.5 %collective-permute-start.5 = (bf16[64,1024]{1,0:T(8,128)(2,1)S(1)}, bf16[64,1024]{1,0:T(8,128)(2,1)S(1)}, u32[]{:S(2)}, u32[]{:S(2)}) collective-permute-start(bf16[64,1024]{1,0:T(8,128)(2,1)S(1)} %get-tuple-element.40.low_ref), channel_id=1, source_target_pairs={{2,0},{4,2},{6,4},{8,6},{10,8},{12,10},{14,12},{16,14},{18,16},{20... | collective-permute-start | bytes 393224 | tf_op jit(solution)/shard_map/ppermute | solution.py:407
  102.8 8.3 %collective-permute-done.5.next_ref = bf16[64,1024]{1,0:T(8,128)(2,1)S(1)} collective-permute-done((bf16[64,1024]{1,0:T(8,128)(2,1)S(1)}, bf16[64,1024]{1,0:T(8,128)(2,1)S(1)}, u32[]{:S(2)}, u32[]{:S(2)}) %collective-permute-start.5) | collective-permute-done | bytes 131104 | tf_op jit(solution)/shard_map/ppermute | solution.py:407
  112.1 4.9 %pullback.1 = bf16[2048,256]{1,0:T(8,128)(2,1)} custom-call(bf16[64,1024]{1,0:T(8,128)(2,1)S(1)} %copy-done.4, bf16[64,1024]{1,0:T(8,128)(2,1)S(1)} %get-tuple-element.40.low_ref, bf16[64,1024]{1,0:T(8,128)(2,1)S(1)} %get-tuple-element.39.high_ref, bf16[64,1024]{1,0:T(8,128)(2,1)S(1)} %collective-permute-done.5.next_ref, bf16[2048,64]{1,0:T(8,128)(2,1)S(1)} %bitcast.44, ...), custom_call_target="tpu_custom_call" | custom-call | flops 1207959552 | bytes 2097152 | tf_op jit(solution)/shard_map/pullback/pallas_call | solution.py:392
  117.0 1.1 unpack.1
  (26 shorter events, 2.5 us)
Async XLA Ops:
  1.6 12.2 %collective-permute-start = (bf16[512,128]{1,0:T(8,128)(2,1)S(1)}, bf16[512,128]{1,0:T(8,128)(2,1)S(1)}, u32[]{:S(2)}, u32[]{:S(2)}) collective-permute-start(bf16[512,128]{1,0:T(8,128)(2,1)S(1)} %get-tuple-element.43), channel_id=1, source_target_pairs={{0,2},{2,4},{4,6},{6,8},{8,10},{10,12},{12,14},{14,16},{16,18},{18... | collective-permute-start | bytes 393224 | tf_op jit(solution)/shard_map/ppermute | solution.py:406
  7.3 7.2 %collective-permute-start.1 = (bf16[512,128]{1,0:T(8,128)(2,1)S(1)}, bf16[512,128]{1,0:T(8,128)(2,1)S(1)}, u32[]{:S(2)}, u32[]{:S(2)}) collective-permute-start(bf16[512,128]{1,0:T(8,128)(2,1)S(1)} %get-tuple-element.42), channel_id=1, source_target_pairs={{2,0},{4,2},{6,4},{8,6},{10,8},{12,10},{14,12},{16,14},{18,16},{20... | collective-permute-start | bytes 393224 | tf_op jit(solution)/shard_map/ppermute | solution.py:407
  8.6 1.0 copy-start.2
  9.5 1.0 copy-start.5
  10.6 1.0 copy-start.6
  11.6 43.4 %copy-start = (bf16[1,32,4,16,256]{4,3,2,1,0:T(8,128)(2,1)S(1)}, bf16[1,32,4,16,256]{4,3,2,1,0:T(8,128)(2,1)}, u32[]{:S(2)}) copy-start(bf16[1,32,4,16,256]{4,3,2,1,0:T(8,128)(2,1)} %param.12) | copy-start | bytes 3145732
  13.9 44.5 %copy-start.1 = (bf16[1,64,2,8,128]{4,3,2,1,0:T(8,128)(2,1)S(1)}, bf16[1,64,2,8,128]{4,3,2,1,0:T(8,128)(2,1)}, u32[]{:S(2)}) copy-start(bf16[1,64,2,8,128]{4,3,2,1,0:T(8,128)(2,1)} %param.15) | copy-start | bytes 786436
  32.2 32.4 %copy-start.8 = (bf16[1,64,2,8,128]{4,3,2,1,0:T(8,128)(2,1)S(1)}, bf16[1,64,2,8,128]{4,3,2,1,0:T(8,128)(2,1)}, u32[]{:S(2)}) copy-start(bf16[1,64,2,8,128]{4,3,2,1,0:T(8,128)(2,1)} %param.14) | copy-start | bytes 786436
  32.2 32.4 %copy-start.9 = (f32[32]{0:T(128)S(1)}, f32[32]{0:T(128)}, u32[]{:S(2)}) copy-start(f32[32]{0:T(128)} %param.10) | copy-start | bytes 388
  32.2 32.4 %copy-start.10 = (f32[32]{0:T(128)S(1)}, f32[32]{0:T(128)}, u32[]{:S(2)}) copy-start(f32[32]{0:T(128)} %param.11) | copy-start | bytes 388
  32.2 26.1 %collective-permute-start.3 = (bf16[32,16,256]{2,1,0:T(8,128)(2,1)}, bf16[32,16,256]{2,1,0:T(8,128)(2,1)S(1)}, u32[]{:S(2)}, u32[]{:S(2)}) collective-permute-start(bf16[32,16,256]{2,1,0:T(8,128)(2,1)} %get-tuple-element.33.low_ref), channel_id=1, source_target_pairs={{2,0},{4,2},{6,4},{8,6},{10,8},{12,10},{14,12},{16,14},{18,16},{20... | collective-permute-start | bytes 786440 | tf_op jit(solution)/shard_map/ppermute | solution.py:407
  33.6 24.7 %collective-permute-start.2 = (bf16[32,16,256]{2,1,0:T(8,128)(2,1)}, bf16[32,16,256]{2,1,0:T(8,128)(2,1)S(1)}, u32[]{:S(2)}, u32[]{:S(2)}) collective-permute-start(bf16[32,16,256]{2,1,0:T(8,128)(2,1)} %get-tuple-element.32), channel_id=1, source_target_pairs={{0,2},{2,4},{4,6},{6,8},{8,10},{10,12},{12,14},{14,16},{16,18},{18... | collective-permute-start | bytes 786440 | tf_op jit(solution)/shard_map/ppermute | solution.py:406
  39.2 25.3 %all-to-all-start = ((f32[128,1,128]{2,1,0:T(1,128)}), f32[128,1,128]{2,1,0:T(1,128)S(1)}, u32[]{:S(2)}, u32[]{:S(2)}) async-start(f32[128,1,128]{2,1,0:T(1,128)} %bitcast.11), calls=%async_computation | async-start | bytes 131072 | tf_op jit(solution)/shard_map/all_to_all | solution.py:446
  64.6 46.6 %copy-start.7 = (bf16[4,4,4,32,64]{4,3,2,1,0:T(8,128)(2,1)S(1)}, bf16[4,4,4,32,64]{4,3,2,1,0:T(8,128)(2,1)}, u32[]{:S(2)}) copy-start(bf16[4,4,4,32,64]{4,3,2,1,0:T(8,128)(2,1)} %param.13) | copy-start | bytes 786436
  71.9 22.0 %all-to-all-start.1 = ((f32[128,8,128]{2,1,0:T(8,128)}), f32[128,8,128]{2,1,0:T(8,128)S(1)}, u32[]{:S(2)}, u32[]{:S(2)}) async-start(f32[128,8,128]{2,1,0:T(8,128)} %bitcast.22), calls=%async_computation.1 | async-start | bytes 1048576 | tf_op jit(solution)/shard_map/all_to_all | solution.py:522
  80.2 9.5 %collective-permute-start.4 = (bf16[64,1024]{1,0:T(8,128)(2,1)S(1)}, bf16[64,1024]{1,0:T(8,128)(2,1)S(1)}, u32[]{:S(2)}, u32[]{:S(2)}) collective-permute-start(bf16[64,1024]{1,0:T(8,128)(2,1)S(1)} %get-tuple-element.39.high_ref), channel_id=1, source_target_pairs={{0,2},{2,4},{4,6},{6,8},{8,10},{10,12},{12,14},{14,16},{16,18},{18... | collective-permute-start | bytes 393224 | tf_op jit(solution)/shard_map/ppermute | solution.py:406
  89.7 4.1 %copy-start.3 = (bf16[64,1024]{1,0:T(8,128)(2,1)}, bf16[64,1024]{1,0:T(8,128)(2,1)S(1)}, u32[]{:S(2)}) copy-start(bf16[64,1024]{1,0:T(8,128)(2,1)S(1)} %collective-permute-done.4.edge_ref.prev_ref) | copy-start | bytes 393220
  94.7 22.3 %all-to-all-start.2 = ((bf16[128,8,128]{2,1,0:T(8,128)(2,1)}), bf16[128,8,128]{2,1,0:T(8,128)(2,1)S(1)}, u32[]{:S(2)}, u32[]{:S(2)}) async-start(bf16[128,8,128]{2,1,0:T(8,128)(2,1)} %bitcast.25), calls=%async_computation.2 | async-start | bytes 524288 | tf_op jit(solution)/shard_map/all_to_all | solution.py:534
  101.3 9.8 %collective-permute-start.5 = (bf16[64,1024]{1,0:T(8,128)(2,1)S(1)}, bf16[64,1024]{1,0:T(8,128)(2,1)S(1)}, u32[]{:S(2)}, u32[]{:S(2)}) collective-permute-start(bf16[64,1024]{1,0:T(8,128)(2,1)S(1)} %get-tuple-element.40.low_ref), channel_id=1, source_target_pairs={{2,0},{4,2},{6,4},{8,6},{10,8},{12,10},{14,12},{16,14},{18,16},{20... | collective-permute-start | bytes 393224 | tf_op jit(solution)/shard_map/ppermute | solution.py:407
  111.2 0.9 copy-start.4

commit v4 on v3

--- a/solution.py
+++ b/solution.py
@@ -82,20 +82,60 @@
     return jnp.sum(jnp.where(lanes(shape) == sub + shift, row, 0.0), axis=1, keepdims=True)
 
 
-def own_kernel(lat_ref, taps_ref, taps_d_ref, wide_ref, first_ref, middle_ref, last_ref, weight_ref, patch, wide_lat):
-    spread_weights(taps_ref, wide_ref)
-    wide_lat[...] = lat_ref[...].astype(F32)
+def edge_kernel(lat_ref, real_ref, low_ref, high_ref, lat_edge, real_edge, sems):
+    copies = []
+    for side in range(2):
+        copies.append(fetch(lat_ref.at[:, side], lat_edge.at[side], sems.at[2 * side]))
+        copies.append(fetch(real_ref.at[:, 3 * side], real_edge.at[side], sems.at[2 * side + 1]))
+    for side, ref in enumerate((low_ref, high_ref)):
+        copies[2 * side].wait()
+        ref[0:512, :] = lat_edge[side].reshape(512, X)
+        copies[2 * side + 1].wait()
+        edge = real_edge[side].reshape(512, 2 * X)
+        ref[512:1024, :] = edge[:, 0:X]
+        ref[1024:1536, :] = edge[:, X : 2 * X]
+
+
+def own_kernel(
+    lat_in,
+    taps_in,
+    taps_d_in,
+    wide_ref,
+    first_ref,
+    middle_ref,
+    last_ref,
+    weight_out,
+    lat,
+    taps,
+    taps_d,
+    weight,
+    sems,
+    patch,
+    wide_lat,
+):
+    copies = [
+        fetch(lat_in, lat, sems.at[0]),
+        fetch(taps_in, taps, sems.at[1]),
+        fetch(taps_d_in, taps_d, sems.at[2]),
+    ]
+    copies[0].wait()
+    wide_lat[...] = lat[...].astype(F32)
     lane = lanes((C, X))
     for depth in range(2):
         clear_rims(depth, patch)
         for y in range(Y):
             spread_cells(wide_lat[pl.ds(depth * Y + y, C, stride=16), :], depth, y, lane, patch)
+    copies[2].wait()
+    same = lax.broadcasted_iota(jnp.int32, (C, C), 0) == lanes((C, C))
+    unit = jnp.where(same, 1.0, 0.0).astype(BF16)
+    weight[...] = dot(unit, taps_d[...], (1, 1)).astype(BF16)
+    weight_copy = fetch(weight, weight_out, sems.at[3])
+    copies[1].wait()
+    spread_weights(taps, wide_ref)
     first_ref[...] = dot(wide_ref[:, 576:1152], patch[0:576, :])
     middle_ref[...] = dot(wide_ref[...], patch[...])
     last_ref[...] = dot(wide_ref[:, 0:576], patch[576:1152, :])
-    same = lax.broadcasted_iota(jnp.int32, (C, C), 0) == lanes((C, C))
-    unit = jnp.where(same, 1.0, 0.0).astype(BF16)
-    weight_ref[...] = dot(unit, taps_d_ref[...], (1, 1)).astype(BF16)
+    weight_copy.wait()
 
 
 def rim_kernel(
@@ -105,26 +145,27 @@
     first_in,
     middle_in,
     last_in,
-    real_ref,
+    pre_ref,
     first_out,
     middle_out,
     last_out,
     stats_ref,
-    low_out,
-    high_out,
+    real_prev_out,
+    real_next_out,
     patch,
     wide_lat,
     first,
     last,
     sems,
 ):
+    del pre_ref
     copies = [
-        fetch(real_ref.at[:, 0], low_out, sems.at[0]),
-        fetch(real_ref.at[:, 3], high_out, sems.at[1]),
+        fetch(prev_ref.at[512:1536], real_prev_out, sems.at[0]),
+        fetch(next_ref.at[512:1536], real_next_out, sems.at[1]),
         fetch(middle_in, middle_out, sems.at[2]),
     ]
-    wide_lat[0:512, :] = prev_ref[...].astype(F32)
-    wide_lat[512:1024, :] = next_ref[...].astype(F32)
+    wide_lat[0:512, :] = prev_ref[0:512, :].astype(F32)
+    wide_lat[512:1024, :] = next_ref[0:512, :].astype(F32)
     lane = lanes((C, X))
     for side in range(2):
         clear_rims(side, patch)
@@ -204,29 +245,47 @@
                     patch[place : place + G, y * X : (y + 1) * X] = piece
 
 
-def real_own_kernel(real_ref, weight_ref, low_ref, patch_ref, pre_ref, halves, rows):
-    del low_ref
-    for half in range(2):
-        halves[half] = real_ref[:, half * X : (half + 1) * X].astype(F32)
+def real_own_kernel(real_in, weight_in, patch_out, pre_out, real, weight, patch, pre, sems, halves, rows):
+    real_copies = []
+    for part in range(4):
+        piece = pl.ds(part * 512, 512)
+        real_copies.append(fetch(real_in.at[piece], real.at[piece], sems.at[part]))
+    weight_copy = fetch(weight_in, weight, sems.at[4])
+    for part in range(4):
+        real_copies[part].wait()
+        for half in range(2):
+            piece = slice(part * 512, (part + 1) * 512)
+            halves[half, piece, :] = real[piece, half * X : (half + 1) * X].astype(F32)
+    copies = []
     for depth in range(4):
-        split_depth(depth * 512, (depth * 16, 64), halves, rows, patch_ref)
-    late_early = jnp.concatenate([weight_ref[:, 1024:2048], weight_ref[:, 0:1024]], axis=0)
-    both = dot(late_early, patch_ref[512:1536, :])
-    pre_ref[0:C, :] = both[0:C, :] + dot(weight_ref[:, 512:1024], patch_ref[0:512, :])
-    pre_ref[C : 2 * C, :] = both[C : 2 * C, :] + dot(weight_ref[:, 1024:1536], patch_ref[1536:2048, :])
+        split_depth(depth * 512, (depth * 16, 64), halves, rows, patch)
+        piece = pl.ds(depth * 512, 512)
+        copies.append(fetch(patch.at[piece], patch_out.at[piece], sems.at[5 + depth]))
+    weight_copy.wait()
+    late_early = jnp.concatenate([weight[:, 1024:2048], weight[:, 0:1024]], axis=0)
+    both = dot(late_early, patch[512:1536, :])
+    pre[0:C, :] = both[0:C, :] + dot(weight[:, 512:1024], patch[0:512, :])
+    pre[C : 2 * C, :] = both[C : 2 * C, :] + dot(weight[:, 1024:1536], patch[1536:2048, :])
+    copies.append(fetch(pre, pre_out, sems.at[9]))
+    for copy in copies:
+        copy.wait()
 
 
 def real_kernel(
-    prev_ref,
-    next_ref,
-    own_ref,
-    pre_ref,
-    weight_ref,
+    prev_in,
+    next_in,
+    own_in,
+    pre_in,
+    weight_in,
     cot_ref,
     out_ref,
     terms_out,
     terms_ref,
-    sem,
+    sems,
+    edges,
+    own,
+    pre_own,
+    weight,
     patch,
     halves,
     rows,
@@ -234,21 +293,34 @@
     wide_out,
     grad,
 ):
-    for half in range(2):
-        halves[half, 0:512, :] = prev_ref[:, half * X : (half + 1) * X].astype(F32)
-        halves[half, 512:1024, :] = next_ref[:, half * X : (half + 1) * X].astype(F32)
+    edge_copies = [
+        fetch(prev_in, edges.at[0], sems.at[0]),
+        fetch(next_in, edges.at[1], sems.at[1]),
+    ]
+    copies = [
+        fetch(weight_in, weight, sems.at[2]),
+        fetch(pre_in, pre_own, sems.at[3]),
+    ]
+    own_copy = fetch(own_in, own, sems.at[4])
     for side in range(2):
+        edge_copies[side].wait()
+        for half in range(2):
+            cells = edges[side, half * 512 : (half + 1) * 512, :]
+            halves[half, side * 512 : (side + 1) * 512, :] = cells.astype(F32)
         split_depth(side * 512, (side * 512, 16), halves, rows, patch)
+    for copy in copies:
+        copy.wait()
     pre = (
-        pre_ref[0:C, :] + dot(weight_ref[:, 0:512], patch[0:512, :]),
-        pre_ref[C : 2 * C, :] + dot(weight_ref[:, 1536:2048], patch[512:1024, :]),
+        pre_own[0:C, :] + dot(weight[:, 0:512], patch[0:512, :]),
+        pre_own[C : 2 * C, :] + dot(weight[:, 1536:2048], patch[512:1024, :]),
     )
     finish(pre, cot_ref, out_ref, wide_cot, wide_out, grad)
-    own = [own_ref[depth * 512 : (depth + 1) * 512, :] for depth in range(4)]
-    planes = [patch[0:512, :]] + own + [patch[512:1024, :]]
+    own_copy.wait()
+    own_planes = [own[depth * 512 : (depth + 1) * 512, :] for depth in range(4)]
+    planes = [patch[0:512, :]] + own_planes + [patch[512:1024, :]]
     for half, terms in enumerate(kernel_terms(planes, grad)):
         terms_ref[half * 512 : (half + 1) * 512, :] = terms
-    fetch(terms_ref, terms_out, sem).wait()
+    fetch(terms_ref, terms_out, sems.at[5]).wait()
 
 
 def fake_kernel(
@@ -259,25 +331,29 @@
     stats_ref,
     gain_ref,
     shift_ref,
-    weight_ref,
+    weight_in,
     cot_ref,
     real_terms_in,
     out_ref,
-    low_ref,
-    high_ref,
+    low_out,
+    high_out,
     terms_ref,
     before,
     real_terms,
+    weight_ref,
     sems,
     patch,
     wide_cot,
     wide_out,
     grad,
 ):
-    befores = [
-        fetch(ref, before.at[i], sems.at[i]) for i, ref in enumerate((first_in, middle_in, last_in))
-    ]
-    real_copy = fetch(real_terms_in, real_terms, sems.at[3])
+    befores = []
+    for depth in range(6):
+        ref = (first_in, middle_in, last_in)[depth // 2]
+        half = pl.ds(depth % 2 * 128, 128)
+        befores.append(fetch(ref.at[half], before.at[depth], sems.at[depth]))
+    weight_copy = fetch(weight_in, weight_ref, sems.at[6])
+    real_copy = fetch(real_terms_in, real_terms, sems.at[7])
     stats = stats_ref[...]
     count = 16.0 * CELLS
     sums = jnp.sum(stats, axis=0, keepdims=True)
@@ -291,15 +367,14 @@
     lane = lanes((G, X))
     edge = jnp.zeros((128, X), BF16)
     for depth in range(6):
-        if depth % 2 == 0:
-            befores[depth // 2].wait()
+        befores[depth].wait()
         patch[depth * 512 : depth * 512 + 128, 0:X] = edge
         patch[depth * 512 + 384 : depth * 512 + 512, CELLS - X : CELLS] = edge
         for py in range(2):
             for px in range(2):
-                block = (depth % 2 * 4 + py * 2 + px) * G
+                block = (py * 2 + px) * G
                 for y in range(Y):
-                    cells = before[depth // 2, block : block + G, y * X : (y + 1) * X]
+                    cells = before[depth, block : block + G, y * X : (y + 1) * X]
                     fake = jnp.maximum((cells - center) * factor + shift, 0.0)
                     if depth == 0:
                         fake = jnp.where(inside_ref[0] > 0, fake, 0.0)
@@ -315,6 +390,7 @@
                             if 0 <= to < Y:
                                 at = depth * 512 + ky * 128 + kx * G
                                 patch[at : at + G, to * X : (to + 1) * X] = piece
+    weight_copy.wait()
     early = weight_ref[:, 0:1024]
     late = weight_ref[:, 1024:2048]
     shared = dot(jnp.concatenate([late, early], axis=0), patch[1024:2048, :])
@@ -323,17 +399,21 @@
         shared[C : 2 * C, :] + dot(late, patch[2048:3072, :]),
     )
     finish(pre, cot_ref, out_ref, wide_cot, wide_out, grad)
-    low_ref[...] = grad[2 * C : 3 * C, :]
-    high_ref[...] = grad[C : 2 * C, :]
+    edge_copies = [
+        fetch(grad.at[2 * C : 3 * C], low_out, sems.at[8]),
+        fetch(grad.at[C : 2 * C], high_out, sems.at[9]),
+    ]
     planes = [patch[depth * 512 : (depth + 1) * 512, :] for depth in range(6)]
     real_copy.wait()
     for half, terms in enumerate(kernel_terms(planes, grad)):
         rows = slice(half * 512, (half + 1) * 512)
         terms_ref[rows, :] = terms + real_terms[rows, :]
-
-
-def sum_kernel(parts_ref, edge_ref, sums_ref):
-    del edge_ref
+    for copy in edge_copies:
+        copy.wait()
+
+
+def sum_kernel(parts_ref, prev_ref, next_ref, middle_ref, sums_ref):
+    del prev_ref, next_ref, middle_ref
     total = jnp.sum(parts_ref[...].reshape(NDEV, 8, 128), axis=0, keepdims=True)
     sums_ref[...] = jnp.broadcast_to(total, (NDEV, 8, 128)).reshape(NDEV * 8, 128).astype(BF16)
 
@@ -344,37 +424,104 @@
     out_ref[1024:2048, :] = sums[:, C : 2 * C]
 
 
-def pullback_kernel(prev_ref, low_ref, high_ref, next_ref, taps_ref, sums_ref, out_ref, wide, patch, wide_out):
-    del sums_ref
-    spread_weights(taps_ref, wide)
+def pull_own_kernel(
+    low_in,
+    high_in,
+    taps_in,
+    wide_out,
+    first_out,
+    middle_out,
+    last_out,
+    cells,
+    taps,
+    wide,
+    first,
+    middle,
+    last,
+    patch,
+    sems,
+):
+    edges = [fetch(ref, cells.at[i], sems.at[i]) for i, ref in enumerate((low_in, high_in))]
+    taps_copy = fetch(taps_in, taps, sems.at[2])
     lane = lanes((C, X))
-    for depth, ref in enumerate((prev_ref, low_ref, high_ref, next_ref)):
+    for depth in range(2):
+        edges[depth].wait()
         clear_rims(depth, patch)
         for y in range(Y):
-            spread_cells(ref[:, y * X : (y + 1) * X].astype(F32), depth, y, lane, patch)
-    column = lax.broadcasted_iota(jnp.int32, (2 * X, 2 * X), 1)
+            spread_cells(cells[depth, :, y * X : (y + 1) * X].astype(F32), depth, y, lane, patch)
+    taps_copy.wait()
+    spread_weights(taps, wide)
+    copies = [fetch(wide, wide_out, sems.at[3])]
+    first[...] = dot(wide[128:256, 576:1152], patch[0:576, :])
+    copies.append(fetch(first, first_out, sems.at[4]))
+    middle[...] = dot(wide[...], patch[...]).astype(BF16)
+    copies.append(fetch(middle, middle_out, sems.at[5]))
+    last[...] = dot(wide[0:128, 0:576], patch[576:1152, :])
+    copies.append(fetch(last, last_out, sems.at[6]))
+    for copy in copies:
+        copy.wait()
+
+
+def pullback_kernel(
+    prev_in,
+    next_in,
+    wide_in,
+    first_in,
+    middle_in,
+    last_in,
+    sums_ref,
+    out_ref,
+    cells,
+    wide,
+    first,
+    middle,
+    last,
+    patch,
+    wide_out,
+    sems,
+):
+    del sums_ref
+    middle_copy = fetch(middle_in, middle, sems.at[2])
+    edges = [fetch(ref, cells.at[i], sems.at[i]) for i, ref in enumerate((prev_in, next_in))]
+    copies = [
+        fetch(wide_in, wide, sems.at[3]),
+        fetch(first_in, first, sems.at[4]),
+        fetch(last_in, last, sems.at[5]),
+    ]
+    column = lanes((2 * X, 2 * X))
     source = lax.broadcasted_iota(jnp.int32, (2 * X, 2 * X), 0)
     weave = jnp.where(source == (column % 2) * X + column // 2, 1.0, 0.0).astype(BF16)
-    for pair, first, depths in ((0, 128, (0,)), (1, 0, (1, 2)), (2, 0, (3,))):
-        rows = 128 * len(depths)
-        result = dot(wide[first : first + rows, :], patch[pair * 576 : pair * 576 + 1152, :])
-        result = result.astype(BF16)
-        for at, depth in enumerate(depths):
-            for py in range(2):
-                even = result[at * 128 + py * 64 : at * 128 + py * 64 + G, :]
-                odd = result[at * 128 + py * 64 + G : at * 128 + py * 64 + 2 * G, :]
-                both = jnp.concatenate(
-                    [
-                        jnp.concatenate([even[:, y * X : (y + 1) * X], odd[:, y * X : (y + 1) * X]], axis=1)
-                        for y in range(Y)
-                    ],
-                    axis=0,
-                )
-                woven = dot(both, weave)
-                for y in range(Y):
-                    place = pl.ds(depth * 16 + 2 * y + py, G, stride=64)
-                    wide_out[0, place, :] = woven[y * G : (y + 1) * G, 0:X]
-                    wide_out[1, place, :] = woven[y * G : (y + 1) * G, X : 2 * X]
+
+    def place(result, depth):
+        for py in range(2):
+            even = result[py * 64 : py * 64 + G, :]
+            odd = result[py * 64 + G : py * 64 + 2 * G, :]
+            both = jnp.concatenate(
+                [
+                    jnp.concatenate([even[:, y * X : (y + 1) * X], odd[:, y * X : (y + 1) * X]], axis=1)
+                    for y in range(Y)
+                ],
+                axis=0,
+            )
+            woven = dot(both, weave)
+            for y in range(Y):
+                rows = pl.ds(depth * 16 + 2 * y + py, G, stride=64)
+                wide_out[0, rows, :] = woven[y * G : (y + 1) * G, 0:X]
+                wide_out[1, rows, :] = woven[y * G : (y + 1) * G, X : 2 * X]
+
+    middle_copy.wait()
+    place(middle[0:128, :], 1)
+    place(middle[128:256, :], 2)
+    lane = lanes((C, X))
+    for side in range(2):
+        edges[side].wait()
+        clear_rims(side, patch)
+        for y in range(Y):
+            spread_cells(cells[side, :, y * X : (y + 1) * X].astype(F32), side, y, lane, patch)
+    for copy in copies:
+        copy.wait()
+    place((first[...] + dot(wide[128:256, 0:576], patch[0:576, :])).astype(BF16), 0)
+    place((last[...] + dot(wide[0:128, 576:1152], patch[576:1152, :])).astype(BF16), 3)
     out_ref[:, 0:X] = wide_out[0].astype(BF16)
     out_ref[:, X : 2 * X] = wide_out[1].astype(BF16)
 
@@ -413,24 +560,65 @@
     taps_g = g_weight.transpose(0, 1, 2, 4, 3).reshape(64 * G, C)
     taps_d = d_weight.reshape(64 * G, C)
     lat = latent[0]
-    lat_prev, lat_next = exchange(lat[:, 0].reshape(C * Y, X), lat[:, 1].reshape(C * Y, X))
     real = real_crops[0]
+    low, high = call(
+        edge_kernel,
+        "edges",
+        (lat, real),
+        [shape((1536, X), BF16)] * 2,
+        [
+            pltpu.VMEM((2, C, Y, X), BF16),
+            pltpu.VMEM((2, G, 2 * Y, 2 * X), BF16),
+            pltpu.SemaphoreType.DMA((4,)),
+        ],
+        0,
+        8,
+        far=(0, 1),
+    )
+    prev, next_ = exchange(low, high)
     wide, first, middle, last, weight = call(
         own_kernel,
         "own_cells",
         (lat.reshape(C * 2 * Y, X), taps_g, taps_d),
         [shape((256, 1152), BF16)] + [shape((256, CELLS), F32)] * 3 + [shape((C, 2048), BF16)],
-        [pltpu.VMEM((1152, CELLS), BF16), pltpu.VMEM((1024, X), F32)],
+        [
+            pltpu.VMEM((1024, X), BF16),
+            pltpu.VMEM((2048, C), BF16),
+            pltpu.VMEM((2048, C), BF16),
+            pltpu.VMEM((C, 2048), BF16),
+            pltpu.SemaphoreType.DMA((4,)),
+            pltpu.VMEM((1152, CELLS), BF16),
+            pltpu.VMEM((1024, X), F32),
+        ],
         4 * 256 * 1152 * CELLS,
         16,
-    )
-    first, middle, last, stats, real_low, real_high = call(
+        far=(0, 1, 2),
+        far_outs=(4,),
+    )
+    real_patch, real_pre = call(
+        real_own_kernel,
+        "real_own",
+        (real.reshape(G * 64, 2 * X), weight),
+        [shape((2048, CELLS), BF16), shape((2 * C, CELLS), F32)],
+        [
+            pltpu.VMEM((2048, 2 * X), BF16),
+            pltpu.VMEM((C, 2048), BF16),
+            pltpu.VMEM((2048, CELLS), BF16),
+            pltpu.VMEM((2 * C, CELLS), F32),
+            pltpu.SemaphoreType.DMA((10,)),
+            pltpu.VMEM((2, 2048, X), F32),
+            pltpu.VMEM((2048, 2 * X), BF16),
+        ],
+        4 * 2048 * C * CELLS,
+        20,
+        far=(0, 1),
+        far_outs=(0, 1),
+    )
+    first, middle, last, stats, real_prev, real_next = call(
         rim_kernel,
         "rim_cells",
-        (lat_prev, lat_next, wide, first, middle, last, real),
-        [shape((256, CELLS), F32)] * 3
-        + [shape((NDEV, 128), F32)]
-        + [shape((G, 2 * Y, 2 * X), BF16)] * 2,
+        (prev, next_, wide, first, middle, last, real_pre),
+        [shape((256, CELLS), F32)] * 3 + [shape((NDEV, 128), F32)] + [shape((1024, X), BF16)] * 2,
         [
             pltpu.VMEM((1152, CELLS), BF16),
             pltpu.VMEM((1024, X), F32),
@@ -444,17 +632,6 @@
         far_outs=(0, 1, 2, 4, 5),
     )
     stats = lax.all_to_all(stats, AXES, 0, 0, tiled=True)
-    real_prev, real_next = exchange(real_low, real_high)
-    real_patch, real_pre = call(
-        real_own_kernel,
-        "real_own",
-        (real.reshape(G * 64, 2 * X), weight, real_low),
-        [shape((2048, CELLS), BF16), shape((2 * C, CELLS), F32)],
-        [pltpu.VMEM((2, 2048, X), F32), pltpu.VMEM((2048, 2 * X), BF16)],
-        4 * 2048 * C * CELLS,
-        16,
-        far=(2,),
-    )
     working = [
         pltpu.VMEM((C * 2 * Y, X), F32),
         pltpu.VMEM((C * 2 * Y, X), F32),
@@ -463,25 +640,23 @@
     d_real, real_terms = call(
         real_kernel,
         "real_branch",
-        (
-            real_prev.reshape(G * 16, 2 * X),
-            real_next.reshape(G * 16, 2 * X),
-            real_patch,
-            real_pre,
-            weight,
-            cot_real.reshape(C * 2 * Y, X),
-        ),
+        (real_prev, real_next, real_patch, real_pre, weight, cot_real.reshape(C * 2 * Y, X)),
         [shape((C * 2 * Y, X), BF16), shape((1024, 2 * C), F32)],
         [
             pltpu.VMEM((1024, 2 * C), F32),
-            pltpu.SemaphoreType.DMA,
+            pltpu.SemaphoreType.DMA((6,)),
+            pltpu.VMEM((2, 1024, X), BF16),
+            pltpu.VMEM((2048, CELLS), BF16),
+            pltpu.VMEM((2 * C, CELLS), F32),
+            pltpu.VMEM((C, 2048), BF16),
             pltpu.VMEM((1024, CELLS), BF16),
             pltpu.VMEM((2, 1024, X), F32),
             pltpu.VMEM((1024, 2 * X), BF16),
         ]
         + working,
         8 * 2048 * C * CELLS,
-        20,
+        24,
+        far=(0, 1, 2, 3, 4),
         far_outs=(1,),
     )
     at = lax.axis_index("slab")
@@ -508,43 +683,75 @@
             shape((NDEV * 8, 128), F32),
         ],
         [
-            pltpu.VMEM((3, 256, CELLS), F32),
+            pltpu.VMEM((6, 128, CELLS), F32),
             pltpu.VMEM((NDEV * 8, 128), F32),
-            pltpu.SemaphoreType.DMA((4,)),
+            pltpu.VMEM((C, 2048), BF16),
+            pltpu.SemaphoreType.DMA((10,)),
             pltpu.VMEM((6 * 512, CELLS), BF16),
         ]
         + working,
         8 * 2048 * C * CELLS * 2,
         28,
         smem=(0,),
-        far=(1, 2, 3, 9),
+        far=(1, 2, 3, 7, 9),
+        far_outs=(1, 2),
     )
     parts = lax.all_to_all(terms.reshape(NDEV, 8, 128), AXES, 0, 0, tiled=True)
     grad_prev, grad_next = exchange(low, high)
+    pull_wide, pull_first, pull_middle, pull_last = call(
+        pull_own_kernel,
+        "pull_own",
+        (low, high, taps_d),
+        [
+            shape((256, 1152), BF16),
+            shape((128, CELLS), F32),
+            shape((256, CELLS), BF16),
+            shape((128, CELLS), F32),
+        ],
+        [
+            pltpu.VMEM((2, C, CELLS), BF16),
+            pltpu.VMEM((2048, C), BF16),
+            pltpu.VMEM((256, 1152), BF16),
+            pltpu.VMEM((128, CELLS), F32),
+            pltpu.VMEM((256, CELLS), BF16),
+            pltpu.VMEM((128, CELLS), F32),
+            pltpu.VMEM((1152, CELLS), BF16),
+            pltpu.SemaphoreType.DMA((7,)),
+        ],
+        2 * 384 * 1152 * CELLS,
+        16,
+        far=(0, 1, 2),
+        far_outs=(0, 1, 2, 3),
+    )
     (sums,) = call(
         sum_kernel,
         "sum_terms",
-        (parts.reshape(NDEV * 8, 128), grad_prev),
+        (parts.reshape(NDEV * 8, 128), grad_prev, grad_next, pull_middle),
         [shape((NDEV * 8, 128), BF16)],
         [],
         NDEV * 1024,
         8,
-        far=(1,),
+        far=(1, 2, 3),
     )
     whole = lax.all_to_all(sums.reshape(NDEV, 8, 128), AXES, 0, 0, tiled=True)
     (fake_grad,) = call(
         pullback_kernel,
         "pullback",
-        (grad_prev, low, high, grad_next, taps_d, sums),
+        (grad_prev, grad_next, pull_wide, pull_first, pull_middle, pull_last, sums),
         [shape((G * 64, 2 * X), BF16)],
         [
+            pltpu.VMEM((2, C, CELLS), BF16),
             pltpu.VMEM((256, 1152), BF16),
-            pltpu.VMEM((4 * 576, CELLS), BF16),
+            pltpu.VMEM((128, CELLS), F32),
+            pltpu.VMEM((256, CELLS), BF16),
+            pltpu.VMEM((128, CELLS), F32),
+            pltpu.VMEM((1152, CELLS), BF16),
             pltpu.VMEM((2, G * 64, X), F32),
+            pltpu.SemaphoreType.DMA((6,)),
         ],
-        2 * 512 * 1152 * CELLS,
-        24,
-        far=(5,),
+        2 * 128 * 1152 * CELLS,
+        16,
+        far=(0, 1, 2, 3, 4, 5, 6),
     )
     (weight_grad,) = call(
         unpack_kernel,

time: 119 us -> 102 us (0.86)
  starting transfers between devices: 50.9 us -> 39.2 us
  Pallas kernels: 42 us -> 37.5 us
  local copies, waits for them, and re-layouts: 4.96 us -> 0.67 us
  waiting for transfers between devices: 19.3 us -> 23.2 us
    all_to_all x1, waiting for transfers between devices: 0.01 us -> 5.94 us  [local(): whole = lax.all_to_all(sums.reshape(NDEV, 8, 128), AXES, 0, 0, tiled=True)]
    ppermute x3 -> x2, starting transfers between devices: 16 us -> 10.5 us  [exchange(): before = lax.ppermute(high, 'slab', [(i, i + 1) for i in range(ends)])]
    all_to_all x1, starting transfers between devices: 15.8 us -> 11.1 us  [local(): stats = lax.all_to_all(stats, AXES, 0, 0, tiled=True)]
    pallas_call x8 -> x10, Pallas kernels: 42 us -> 37.5 us  [call(): pl.pallas_call(body, name=name, out_shape=outs, in_specs=[pl.BlockSpec(me...]
    all_to_all x1, waiting for transfers between devices: 4.14 us -> 0.01 us  [local(): parts = lax.all_to_all(terms.reshape(NDEV, 8, 128), AXES, 0, 0, tiled=True)]
    unnamed x22 -> x12, local copies, waits for them, and re-layouts: 3.97 us -> 0.67 us
    all_to_all x1, starting transfers between devices: 6.61 us -> 8.88 us  [local(): whole = lax.all_to_all(sums.reshape(NDEV, 8, 128), AXES, 0, 0, tiled=True)]
    all_to_all x1, waiting for transfers between devices: 1.5 us -> 3.62 us  [local(): stats = lax.all_to_all(stats, AXES, 0, 0, tiled=True)]
  transfers between devices with their start and end apart: 9 -> 7, of which waited for: 5 -> 6; matrix products, arithmetic and copies ran while one was open for 0% -> 0% of each run, Pallas kernels for 13% -> 23%
where the time goes in v4:
time: 102 us; the launch traced here: 101 us
  starting transfers between devices  39.2 us (38%)
  Pallas kernels  37.5 us (37%)
  waiting for transfers between devices  23.2 us (23%)
    pallas_call x10, Pallas kernels, call(): pl.pallas_call(body, name=name, out_shape=outs, in_specs=[pl.BlockSpec(me...  37.5 us
    all_to_all x1, starting transfers between devices, local(): stats = lax.all_to_all(stats, AXES, 0, 0, tiled=True)  11.1 us
    ppermute x2, starting transfers between devices, exchange(): before = lax.ppermute(high, 'slab', [(i, i + 1) for i in range(ends)])  10.5 us
    all_to_all x1, starting transfers between devices, local(): whole = lax.all_to_all(sums.reshape(NDEV, 8, 128), AXES, 0, 0, tiled=True)  8.88 us
    ppermute x2, waiting for transfers between devices, exchange(): after = lax.ppermute(low, 'slab', [(i + 1, i) for i in range(ends)])  7.91 us
    all_to_all x1, starting transfers between devices, local(): parts = lax.all_to_all(terms.reshape(NDEV, 8, 128), AXES, 0, 0, tiled=True)  6.19 us
    all_to_all x1, waiting for transfers between devices, local(): whole = lax.all_to_all(sums.reshape(NDEV, 8, 128), AXES, 0, 0, tiled=True)  5.94 us
    ppermute x2, waiting for transfers between devices, exchange(): before = lax.ppermute(high, 'slab', [(i, i + 1) for i in range(ends)])  5.72 us
  transfers between devices with their start and end apart: 7, of which 6 were waited for; matrix products, arithmetic and copies ran while one was open for 0% of the time, Pallas kernels for 23%

profile of v4, /device:TPU:1, one launch (start us, length us, event | category | flops | bytes accessed | tf_op | source)
XLA Modules:
  0.0 101.5 jit_solution(1528766557629401109)
XLA Ops:
  0.6 1.2 %edges.1 = (bf16[1536,128]{1,0:T(8,128)(2,1)S(1)}, bf16[1536,128]{1,0:T(8,128)(2,1)S(1)}) custom-call(bf16[64,2,8,128]{3,2,1,0:T(8,128)(2,1)} %bitcast.37, bf16[32,4,16,256]{3,2,1,0:T(8,128)(2,1)} %bitcast.34), custom_call_target="tpu_custom_call" | custom-call | bytes 2097152 | tf_op jit(solution)/shard_map/edges/pallas_call | solution.py:539
  1.9 5.7 %collective-permute-start = (bf16[1536,128]{1,0:T(8,128)(2,1)S(1)}, bf16[1536,128]{1,0:T(8,128)(2,1)S(1)}, u32[]{:S(2)}, u32[]{:S(2)}) collective-permute-start(bf16[1536,128]{1,0:T(8,128)(2,1)S(1)} %get-tuple-element.29), channel_id=1, source_target_pairs={{0,2},{2,4},{4,6},{6,8},{8,10},{10,12},{12,14},{14,16},{16,18},{18... | collective-permute-start | bytes 1179656 | tf_op jit(solution)/shard_map/ppermute | solution.py:553
  7.6 1.3 %collective-permute-start.1 = (bf16[1536,128]{1,0:T(8,128)(2,1)S(1)}, bf16[1536,128]{1,0:T(8,128)(2,1)S(1)}, u32[]{:S(2)}, u32[]{:S(2)}) collective-permute-start(bf16[1536,128]{1,0:T(8,128)(2,1)S(1)} %get-tuple-element.30), channel_id=1, source_target_pairs={{2,0},{4,2},{6,4},{8,6},{10,8},{12,10},{14,12},{16,14},{18,16},{20... | collective-permute-start | bytes 1179656 | tf_op jit(solution)/shard_map/ppermute | solution.py:554
  8.9 3.7 %own_cells.1 = (bf16[256,1152]{1,0:T(8,128)(2,1)S(1)}, f32[256,1024]{1,0:T(8,128)S(1)}, f32[256,1024]{1,0:T(8,128)S(1)}, f32[256,1024]{1,0:T(8,128)S(1)}, bf16[64,2048]{1,0:T(8,128)(2,1)}) custom-call(bf16[1024,128]{1,0:T(8,128)(2,1)} %bitcast.38, bf16[2048,64]{1,0:T(8,128)(2,1)} %bitcast.39, bf16[2048,64]{1,0:T(8,128)(2,1)} %bitcast.40), custom_call_target="tpu_custom_call" | custom-call | flops 1207959552 | bytes 4784128 | tf_op jit(solution)/shard_map/own_cells/pallas_call | solution.py:539
  12.6 5.5 %real_own.1 = (bf16[2048,1024]{1,0:T(8,128)(2,1)}, f32[128,1024]{1,0:T(8,128)}) custom-call(bf16[2048,256]{1,0:T(8,128)(2,1)} %bitcast.35, bf16[64,2048]{1,0:T(8,128)(2,1)} %get-tuple-element.35.weight_in), custom_call_target="tpu_custom_call" | custom-call | flops 536870912 | bytes 6029312 | tf_op jit(solution)/shard_map/real_own/pallas_call | solution.py:539
  18.1 5.6 %collective-permute-done.prev_ref = bf16[1536,128]{1,0:T(8,128)(2,1)S(1)} collective-permute-done((bf16[1536,128]{1,0:T(8,128)(2,1)S(1)}, bf16[1536,128]{1,0:T(8,128)(2,1)S(1)}, u32[]{:S(2)}, u32[]{:S(2)}) %collective-permute-start) | collective-permute-done | bytes 393248 | tf_op jit(solution)/shard_map/ppermute | solution.py:553
  23.7 2.1 %collective-permute-done.1.next_ref = bf16[1536,128]{1,0:T(8,128)(2,1)S(1)} collective-permute-done((bf16[1536,128]{1,0:T(8,128)(2,1)S(1)}, bf16[1536,128]{1,0:T(8,128)(2,1)S(1)}, u32[]{:S(2)}, u32[]{:S(2)}) %collective-permute-start.1) | collective-permute-done | bytes 393248 | tf_op jit(solution)/shard_map/ppermute | solution.py:554
  25.9 3.2 %rim_cells.1 = (f32[256,1024]{1,0:T(8,128)}, f32[256,1024]{1,0:T(8,128)}, f32[256,1024]{1,0:T(8,128)}, f32[128,128]{1,0:T(8,128)}, bf16[1024,128]{1,0:T(8,128)(2,1)}, /*index=5*/bf16[1024,128]{1,0:T(8,128)(2,1)}) custom-call(bf16[1536,128]{1,0:T(8,128)(2,1)S(1)} %collective-permute-done.prev_ref, bf16[1536,128]{1,0:T(8,128)(2,1)S(1)} %collective-permute-done.1.next_ref, ...), custom_call_target="tpu_custom_call" | custom-call | flops 603979776 | bytes 8781824 | tf_op jit(solution)/shard_map/rim_cells/pallas_call | solution.py:539
  29.1 11.1 %all-to-all-start = ((f32[128,1,128]{2,1,0:T(1,128)}), f32[128,1,128]{2,1,0:T(1,128)S(1)}, u32[]{:S(2)}, u32[]{:S(2)}) async-start(f32[128,1,128]{2,1,0:T(1,128)} %bitcast.10), calls=%async_computation | async-start | bytes 131072 | tf_op jit(solution)/shard_map/all_to_all | solution.py:634
  40.2 5.9 %real_branch.1 = (bf16[1024,128]{1,0:T(8,128)(2,1)}, f32[1024,128]{1,0:T(8,128)}) custom-call(bf16[1024,128]{1,0:T(8,128)(2,1)} %get-tuple-element.41.prev_in, bf16[1024,128]{1,0:T(8,128)(2,1)} %get-tuple-element.42.next_in, bf16[2048,1024]{1,0:T(8,128)(2,1)} %get-tuple-element.43.own_in, f32[128,1024]{1,0:T(8,128)} %get-tuple-element.36.pre_ref.pre_in, ...), custom_call_target="tpu_custom_call" | custom-call | flops 1073741824 | bytes 6553600 | tf_op jit(solution)/shard_map/real_branch/pallas_call | solution.py:539
  46.2 3.6 %all-to-all-done = f32[128,1,128]{2,1,0:T(1,128)S(1)} async-done(((f32[128,1,128]{2,1,0:T(1,128)}), f32[128,1,128]{2,1,0:T(1,128)S(1)}, u32[]{:S(2)}, u32[]{:S(2)}) %all-to-all-start) | async-done | bytes 65568 | tf_op jit(solution)/shard_map/all_to_all | solution.py:634
  49.8 7.3 %fake_branch.1 = (bf16[1024,128]{1,0:T(8,128)(2,1)}, bf16[64,1024]{1,0:T(8,128)(2,1)}, bf16[64,1024]{1,0:T(8,128)(2,1)}, f32[1024,128]{1,0:T(8,128)}) custom-call(s32[2]{0:T(128)S(1)} %add_convert_fusion.inside_ref, f32[256,1024]{1,0:T(8,128)} %get-tuple-element.37.first_in, f32[256,1024]{1,0:T(8,128)} %get-tuple-element.38.middle_in, ...), custom_call_target="tpu_custom_call" | custom-call | flops 2147483648 | bytes 5308680 | tf_op jit(solution)/shard_map/fake_branch/pallas_call | solution.py:539
  57.1 6.2 %all-to-all-start.1 = ((f32[128,8,128]{2,1,0:T(8,128)}), f32[128,8,128]{2,1,0:T(8,128)S(1)}, u32[]{:S(2)}, u32[]{:S(2)}) async-start(f32[128,8,128]{2,1,0:T(8,128)} %bitcast.18), calls=%async_computation.1 | async-start | bytes 1048576 | tf_op jit(solution)/shard_map/all_to_all | solution.py:699
  63.3 4.8 %collective-permute-start.2 = (bf16[64,1024]{1,0:T(8,128)(2,1)}, bf16[64,1024]{1,0:T(8,128)(2,1)S(1)}, u32[]{:S(2)}, u32[]{:S(2)}) collective-permute-start(bf16[64,1024]{1,0:T(8,128)(2,1)} %get-tuple-element.47.high_in), channel_id=1, source_target_pairs={{0,2},{2,4},{4,6},{6,8},{8,10},{10,12},{12,14},{14,16},{16,18},{18... | collective-permute-start | bytes 393224 | tf_op jit(solution)/shard_map/ppermute | solution.py:553
  68.1 1.3 %collective-permute-start.3 = (bf16[64,1024]{1,0:T(8,128)(2,1)}, bf16[64,1024]{1,0:T(8,128)(2,1)S(1)}, u32[]{:S(2)}, u32[]{:S(2)}) collective-permute-start(bf16[64,1024]{1,0:T(8,128)(2,1)} %get-tuple-element.48.low_in), channel_id=1, source_target_pairs={{2,0},{4,2},{6,4},{8,6},{10,8},{12,10},{14,12},{16,14},{18,16},{20... | collective-permute-start | bytes 393224 | tf_op jit(solution)/shard_map/ppermute | solution.py:554
  69.4 3.6 %pull_own.1 = (bf16[256,1152]{1,0:T(8,128)(2,1)}, f32[128,1024]{1,0:T(8,128)}, bf16[256,1024]{1,0:T(8,128)(2,1)}, f32[128,1024]{1,0:T(8,128)}) custom-call(bf16[64,1024]{1,0:T(8,128)(2,1)} %get-tuple-element.48.low_in, bf16[64,1024]{1,0:T(8,128)(2,1)} %get-tuple-element.47.high_in, bf16[2048,64]{1,0:T(8,128)(2,1)} %bitcast.41), custom_call_target="tpu_custom_call" | custom-call | flops 905969664 | bytes 2686976 | tf_op jit(solution)/shard_map/pull_own/pallas_call | solution.py:539
  73.0 0.1 collective-permute-done.2.prev_ref.prev_in
  73.2 5.8 %collective-permute-done.3.next_ref.next_in = bf16[64,1024]{1,0:T(8,128)(2,1)S(1)} collective-permute-done((bf16[64,1024]{1,0:T(8,128)(2,1)}, bf16[64,1024]{1,0:T(8,128)(2,1)S(1)}, u32[]{:S(2)}, u32[]{:S(2)}) %collective-permute-start.3) | collective-permute-done | bytes 131104 | tf_op jit(solution)/shard_map/ppermute | solution.py:554
  78.9 0.6 copy-done.5
  79.6 0.8 sum_terms.1.sums_ref
  80.4 8.9 %all-to-all-start.2 = ((bf16[128,8,128]{2,1,0:T(8,128)(2,1)}), bf16[128,8,128]{2,1,0:T(8,128)(2,1)S(1)}, u32[]{:S(2)}, u32[]{:S(2)}) async-start(bf16[128,8,128]{2,1,0:T(8,128)(2,1)} %bitcast.21), calls=%async_computation.2 | async-start | bytes 524288 | tf_op jit(solution)/shard_map/all_to_all | solution.py:736
  89.3 5.1 %pullback.1 = bf16[2048,256]{1,0:T(8,128)(2,1)} custom-call(bf16[64,1024]{1,0:T(8,128)(2,1)} %copy-done.4, bf16[64,1024]{1,0:T(8,128)(2,1)} %copy-done.5, bf16[256,1152]{1,0:T(8,128)(2,1)} %get-tuple-element.49.wide_in, f32[128,1024]{1,0:T(8,128)} %get-tuple-element.50.first_in, bf16[256,1024]{1,0:T(8,128)(2,1)} %get-tuple-element.51.middle_ref.middle_in, ...), custom_call_target="tpu_custom_call" | custom-call | flops 301989888 | bytes 3735552 | tf_op jit(solution)/shard_map/pullback/pallas_call | solution.py:539
  94.4 5.9 %all-to-all-done.2 = bf16[128,8,128]{2,1,0:T(8,128)(2,1)S(1)} async-done(((bf16[128,8,128]{2,1,0:T(8,128)(2,1)}), bf16[128,8,128]{2,1,0:T(8,128)(2,1)S(1)}, u32[]{:S(2)}, u32[]{:S(2)}) %all-to-all-start.2) | async-done | bytes 262176 | tf_op jit(solution)/shard_map/all_to_all | solution.py:736
  100.4 1.1 %unpack.1 = f32[2048,64]{1,0:T(8,128)} custom-call(bf16[1024,128]{1,0:T(8,128)(2,1)S(1)} %bitcast.27), custom_call_target="tpu_custom_call" | custom-call | bytes 786432 | tf_op jit(solution)/shard_map/unpack/pallas_call | solution.py:539
  (13 shorter events, 0.1 us)
Async XLA Ops:
  1.9 21.8 %collective-permute-start = (bf16[1536,128]{1,0:T(8,128)(2,1)S(1)}, bf16[1536,128]{1,0:T(8,128)(2,1)S(1)}, u32[]{:S(2)}, u32[]{:S(2)}) collective-permute-start(bf16[1536,128]{1,0:T(8,128)(2,1)S(1)} %get-tuple-element.29), channel_id=1, source_target_pairs={{0,2},{2,4},{4,6},{6,8},{8,10},{10,12},{12,14},{14,16},{16,18},{18... | collective-permute-start | bytes 1179656 | tf_op jit(solution)/shard_map/ppermute | solution.py:553
  7.6 18.3 %collective-permute-start.1 = (bf16[1536,128]{1,0:T(8,128)(2,1)S(1)}, bf16[1536,128]{1,0:T(8,128)(2,1)S(1)}, u32[]{:S(2)}, u32[]{:S(2)}) collective-permute-start(bf16[1536,128]{1,0:T(8,128)(2,1)S(1)} %get-tuple-element.30), channel_id=1, source_target_pairs={{2,0},{4,2},{6,4},{8,6},{10,8},{12,10},{14,12},{16,14},{18,16},{20... | collective-permute-start | bytes 1179656 | tf_op jit(solution)/shard_map/ppermute | solution.py:554
  12.5 27.7 %copy-start = (bf16[1,64,2,8,128]{4,3,2,1,0:T(8,128)(2,1)S(1)}, bf16[1,64,2,8,128]{4,3,2,1,0:T(8,128)(2,1)}, u32[]{:S(2)}) copy-start(bf16[1,64,2,8,128]{4,3,2,1,0:T(8,128)(2,1)} %param.15) | copy-start | bytes 786436
  29.1 20.7 %copy-start.1 = (bf16[1,64,2,8,128]{4,3,2,1,0:T(8,128)(2,1)S(1)}, bf16[1,64,2,8,128]{4,3,2,1,0:T(8,128)(2,1)}, u32[]{:S(2)}) copy-start(bf16[1,64,2,8,128]{4,3,2,1,0:T(8,128)(2,1)} %param.14) | copy-start | bytes 786436
  29.1 20.7 %copy-start.2 = (f32[32]{0:T(128)S(1)}, f32[32]{0:T(128)}, u32[]{:S(2)}) copy-start(f32[32]{0:T(128)} %param.10) | copy-start | bytes 388
  29.1 20.7 %copy-start.3 = (f32[32]{0:T(128)S(1)}, f32[32]{0:T(128)}, u32[]{:S(2)}) copy-start(f32[32]{0:T(128)} %param.11) | copy-start | bytes 388
  29.1 20.7 %all-to-all-start = ((f32[128,1,128]{2,1,0:T(1,128)}), f32[128,1,128]{2,1,0:T(1,128)S(1)}, u32[]{:S(2)}, u32[]{:S(2)}) async-start(f32[128,1,128]{2,1,0:T(1,128)} %bitcast.10), calls=%async_computation | async-start | bytes 131072 | tf_op jit(solution)/shard_map/all_to_all | solution.py:634
  57.1 21.8 %all-to-all-start.1 = ((f32[128,8,128]{2,1,0:T(8,128)}), f32[128,8,128]{2,1,0:T(8,128)S(1)}, u32[]{:S(2)}, u32[]{:S(2)}) async-start(f32[128,8,128]{2,1,0:T(8,128)} %bitcast.18), calls=%async_computation.1 | async-start | bytes 1048576 | tf_op jit(solution)/shard_map/all_to_all | solution.py:699
  63.3 9.8 %collective-permute-start.2 = (bf16[64,1024]{1,0:T(8,128)(2,1)}, bf16[64,1024]{1,0:T(8,128)(2,1)S(1)}, u32[]{:S(2)}, u32[]{:S(2)}) collective-permute-start(bf16[64,1024]{1,0:T(8,128)(2,1)} %get-tuple-element.47.high_in), channel_id=1, source_target_pairs={{0,2},{2,4},{4,6},{6,8},{8,10},{10,12},{12,14},{14,16},{16,18},{18... | collective-permute-start | bytes 393224 | tf_op jit(solution)/shard_map/ppermute | solution.py:553
  68.1 10.8 %collective-permute-start.3 = (bf16[64,1024]{1,0:T(8,128)(2,1)}, bf16[64,1024]{1,0:T(8,128)(2,1)S(1)}, u32[]{:S(2)}, u32[]{:S(2)}) collective-permute-start(bf16[64,1024]{1,0:T(8,128)(2,1)} %get-tuple-element.48.low_in), channel_id=1, source_target_pairs={{2,0},{4,2},{6,4},{8,6},{10,8},{12,10},{14,12},{16,14},{18,16},{20... | collective-permute-start | bytes 393224 | tf_op jit(solution)/shard_map/ppermute | solution.py:554
  73.2 5.8 %copy-start.4 = (bf16[64,1024]{1,0:T(8,128)(2,1)}, bf16[64,1024]{1,0:T(8,128)(2,1)S(1)}, u32[]{:S(2)}) copy-start(bf16[64,1024]{1,0:T(8,128)(2,1)S(1)} %collective-permute-done.2.prev_ref.prev_in) | copy-start | bytes 393220
  78.9 0.6 copy-start.5
  80.4 20.0 %all-to-all-start.2 = ((bf16[128,8,128]{2,1,0:T(8,128)(2,1)}), bf16[128,8,128]{2,1,0:T(8,128)(2,1)S(1)}, u32[]{:S(2)}, u32[]{:S(2)}) async-start(bf16[128,8,128]{2,1,0:T(8,128)(2,1)} %bitcast.21), calls=%async_computation.2 | async-start | bytes 524288 | tf_op jit(solution)/shard_map/all_to_all | solution.py:736

commit v5 on v4

v5 whole, which is shorter than its diff:
```python
import jax
import jax.numpy as jnp
from jax import lax
from jax.experimental import pallas as pl
from jax.experimental.pallas import tpu as pltpu
from jax.sharding import PartitionSpec as P

AXES = ("section", "slab", "rep")
NDEV = 128
C = 64
G = 32
Y = 8
X = 128
CELLS = Y * X
F32 = jnp.float32
BF16 = jnp.bfloat16

phase_taps = (((1, 0), (3, -1)), ((0, 1), (2, 0)))


def dot(a, b, dims=(1, 0)):
    return lax.dot_general(a, b, (((dims[0],), (dims[1],)), ((), ())), preferred_element_type=F32)


def lanes(shape):
    return lax.broadcasted_iota(jnp.int32, shape, len(shape) - 1)


def from_left(tile, lane):
    return jnp.where(lane == 0, 0.0, pltpu.roll(tile, 1, 1))


def from_right(tile, lane):
    return jnp.where(lane == X - 1, 0.0, pltpu.roll(tile, X - 1, 1))


def spread_weights(taps_ref, wide_ref):
    wide_ref[...] = jnp.zeros_like(wide_ref)
    for pz in range(2):
        for py in range(2):
            for px in range(2):
                row = ((1 - pz) * 4 + py * 2 + px) * G
                for kz, oz in phase_taps[pz]:
                    tz = oz if pz == 1 else oz + 1
                    for ky, oy in phase_taps[py]:
                        for kx, ox in phase_taps[px]:
                            col = tz * 576 + (oy + 1) * 192 + (ox + 1) * 64
                            tap = (kz * 16 + ky * 4 + kx) * G
                            wide_ref[row : row + G, col : col + C] = taps_ref[tap : tap + G, :]


def spread_cells(tile, depth, y, lane, patch_ref):
    for xi, moved in ((0, from_left(tile, lane)), (1, tile), (2, from_right(tile, lane))):
        piece = moved.astype(BF16)
        for yi in range(3):
            to = y - (yi - 1)
            if 0 <= to < Y:
                row = depth * 576 + yi * 192 + xi * 64
                patch_ref[row : row + C, to * X : (to + 1) * X] = piece


def clear_rims(depth, patch_ref):
    edge = jnp.zeros((192, X), BF16)
    patch_ref[depth * 576 : depth * 576 + 192, 0:X] = edge
    patch_ref[depth * 576 + 384 : depth * 576 + 576, CELLS - X : CELLS] = edge


def fetch(source, target, sem):
    copy = pltpu.make_async_copy(source, target, sem)
    copy.start()
    return copy


def as_row(column, shift):
    sub = lax.broadcasted_iota(jnp.int32, (G, 128), 0)
    return jnp.sum(jnp.where(lanes((G, 128)) == sub + shift, column, 0.0), axis=0, keepdims=True)


def as_column(row, shift):
    shape = (G, row.shape[1])
    sub = lax.broadcasted_iota(jnp.int32, shape, 0)
    return jnp.sum(jnp.where(lanes(shape) == sub + shift, row, 0.0), axis=1, keepdims=True)


def edge_kernel(lat_in, real_in, edge_ref, lat_edge, real_edge, sems):
    copies = [
        fetch(lat_in.at[:, 0], lat_edge, sems.at[0]),
        fetch(real_in.at[:, 0], real_edge, sems.at[1]),
    ]
    join_edge(copies, lat_edge, real_edge, edge_ref)


def join_edge(copies, lat_edge, real_edge, edge_ref):
    copies[0].wait()
    edge_ref[0:512, :] = lat_edge[...].reshape(512, X)
    copies[1].wait()
    edge = real_edge[...].reshape(512, 2 * X)
    edge_ref[512:1024, :] = edge[:, 0:X]
    edge_ref[1024:1536, :] = edge[:, X : 2 * X]


def cell_stats(ref, first, count):
    blocks = range(first, first + count)
    total = jnp.zeros((G, CELLS), F32)
    for block in blocks:
        total += ref[block * G : (block + 1) * G, :]
    mean = jnp.sum(total, axis=1, keepdims=True) * (1.0 / (count * CELLS))
    squares = jnp.zeros((G, CELLS), F32)
    for block in blocks:
        off = ref[block * G : (block + 1) * G, :] - mean
        squares += off * off
    return mean, jnp.sum(squares, axis=1, keepdims=True)


def own_kernel(
    lat_in,
    real_in,
    taps_in,
    taps_d_in,
    wide_out,
    first_out,
    middle_out,
    last_out,
    sums_ref,
    edge_ref,
    weight_out,
    lat_edge,
    real_edge,
    lat,
    taps,
    taps_d,
    weight,
    wide,
    first,
    middle,
    last,
    sems,
    patch,
    wide_lat,
):
    edge_copies = [
        fetch(lat_in.at[:, 1], lat_edge, sems.at[0]),
        fetch(real_in.at[:, 3], real_edge, sems.at[1]),
    ]
    lat_copy = fetch(lat_in, lat, sems.at[2])
    taps_copy = fetch(taps_in, taps, sems.at[3])
    taps_d_copy = fetch(taps_d_in, taps_d, sems.at[4])
    lat_copy.wait()
    wide_lat[...] = lat[...].reshape(1024, X).astype(F32)
    lane = lanes((C, X))
    for depth in range(2):
        clear_rims(depth, patch)
        for y in range(Y):
            spread_cells(wide_lat[pl.ds(depth * Y + y, C, stride=16), :], depth, y, lane, patch)
    taps_copy.wait()
    spread_weights(taps, wide)
    copies = [fetch(wide, wide_out, sems.at[5])]
    last[...] = dot(wide[:, 0:576], patch[576:1152, :])
    copies.append(fetch(last, last_out, sems.at[6]))
    middle[...] = dot(wide[...], patch[...])
    copies.append(fetch(middle, middle_out, sems.at[7]))
    first[...] = dot(wide[:, 576:1152], patch[0:576, :])
    copies.append(fetch(first, first_out, sems.at[8]))
    taps_d_copy.wait()
    same = lax.broadcasted_iota(jnp.int32, (C, C), 0) == lanes((C, C))
    unit = jnp.where(same, 1.0, 0.0).astype(BF16)
    weight[...] = dot(unit, taps_d[...], (1, 1)).astype(BF16)
    copies.append(fetch(weight, weight_out, sems.at[9]))
    join_edge(edge_copies, lat_edge, real_edge, edge_ref)
    place = lanes((G, 128))
    sums = jnp.zeros((G, 128), F32)
    for at, column in enumerate(cell_stats(middle, 0, 8) + cell_stats(first, 4, 4)):
        sums = jnp.where(place == at, column, sums)
    sums_ref[...] = sums
    for copy in copies:
        copy.wait()


def rim_kernel(
    inside_ref,
    next_ref,
    sums_ref,
    wide_in,
    last_in,
    last_out,
    stats_out,
    real_next_out,
    patch,
    wide_lat,
    wide,
    last,
    stats,
    sems,
):
    wide_copy = fetch(wide_in, wide, sems.at[0])
    last_copy = fetch(last_in, last, sems.at[1])
    copies = [fetch(next_ref.at[512:1536], real_next_out, sems.at[2])]
    wide_lat[...] = next_ref[0:512, :].astype(F32)
    lane = lanes((C, X))
    clear_rims(0, patch)
    for y in range(Y):
        spread_cells(wide_lat[pl.ds(y, C, stride=8), :], 0, y, lane, patch)
    wide_copy.wait()
    last_copy.wait()
    last[...] += dot(wide[:, 576:1152], patch[...])
    copies.append(fetch(last, last_out, sems.at[3]))
    groups = [(2.0, sums_ref[:, 0:1], sums_ref[:, 1:2])]
    groups.append((jnp.where(inside_ref[0] > 0, 0.0, 1.0), sums_ref[:, 2:3], sums_ref[:, 3:4]))
    groups.append((1.0,) + cell_stats(last, 0, 4))
    groups.append((jnp.where(inside_ref[1] > 0, 1.0, 0.0),) + cell_stats(last, 4, 4))
    depths = jnp.zeros((G, 1), F32)
    mean = jnp.zeros((G, 1), F32)
    for weight, one, _ in groups:
        depths += weight
        mean += weight * one
    mean /= depths
    spread = jnp.zeros((G, 1), F32)
    for weight, one, squares in groups:
        own = squares if isinstance(weight, float) else weight * squares
        spread += own + weight * (4.0 * CELLS) * (one - mean) * (one - mean)
    stats[...] = jnp.broadcast_to(as_row(mean, 0) + as_row(spread, G), (NDEV, 128))
    copies.append(fetch(stats, stats_out, sems.at[4]))
    for copy in copies:
        copy.wait()


def activate(before):
    squashed = jax.nn.sigmoid(4.0 * before)
    output = before * (0.2 + 0.8 * squashed)
    derivative = 0.2 + 0.8 * squashed + 3.2 * before * squashed * (1.0 - squashed)
    return (output, derivative)


def convolve(weight_ref, patch):
    early = weight_ref[:, 0:1024]
    late = weight_ref[:, 1024:2048]
    shared = dot(jnp.concatenate([late, early], axis=0), patch[1024:2048, :])
    return (
        dot(early, patch[0:1024, :]) + shared[0:C, :],
        shared[C : 2 * C, :] + dot(late, patch[2048:3072, :]),
    )


def finish(pre, cot_ref, out_ref, wide_cot, wide_out, grad):
    wide_cot[...] = cot_ref[...].astype(F32)
    nothing = jnp.zeros((C, CELLS), BF16)
    grad[0:C, :] = nothing
    grad[3 * C : 4 * C, :] = nothing
    for m in range(2):
        for y in range(Y):
            output, slope = activate(pre[m][:, y * X : (y + 1) * X])
            wide_out[pl.ds(m * Y + y, C, stride=16), :] = output
            cot = wide_cot[pl.ds(m * Y + y, C, stride=16), :]
            grad[(2 - m) * C : (3 - m) * C, y * X : (y + 1) * X] = (cot * slope).astype(BF16)
    out_ref[...] = wide_out[...].astype(BF16)


def kernel_terms(planes, grad):
    halves = []
    for half in range(2):
        terms = dot(planes[half], grad[128:256, :], (1, 1))
        terms += dot(planes[half + 2], grad[64:192, :], (1, 1))
        halves.append(terms + dot(planes[half + 4], grad[0:128, :], (1, 1)))
    return halves


def split_depth(at, places, halves, rows, patch):
    base, stride = places
    column = lanes((2 * X, 4 * X))
    source = lax.broadcasted_iota(jnp.int32, (2 * X, 4 * X), 0)
    pick = jnp.where(source == 2 * (column % X) + column // X - 1, 1.0, 0.0).astype(BF16)
    edge = jnp.zeros((128, X), BF16)
    patch[at : at + 128, 0:X] = edge
    patch[at + 384 : at + 512, CELLS - X : CELLS] = edge
    for row in range(2 * Y):
        for half in range(2):
            cells = halves[half, pl.ds(base + row, G, stride=stride), :].astype(BF16)
            rows[at + row * G : at + (row + 1) * G, half * X : (half + 1) * X] = cells
    split = dot(rows[at : at + 512, :], pick).astype(BF16)
    for row in range(2 * Y):
        for kx in range(4):
            piece = split[row * G : (row + 1) * G, kx * X : (kx + 1) * X]
            for ky in range(4):
                if (row + 1 - ky) % 2 == 0 and 0 <= (row + 1 - ky) // 2 < Y:
                    y = (row + 1 - ky) // 2
                    place = at + ky * 128 + kx * G
                    patch[place : place + G, y * X : (y + 1) * X] = piece


def real_kernel(
    real_ref,
    prev_ref,
    next_in,
    weight_in,
    cot_ref,
    wide_in,
    first_in,
    out_ref,
    terms_out,
    first_out,
    edge,
    weight,
    wide,
    first,
    terms_ref,
    sems,
    patch,
    lat_patch,
    halves,
    rows,
    wide_cot,
    wide_out,
    grad,
):
    copies = [
        fetch(wide_in, wide, sems.at[0]),
        fetch(first_in, first, sems.at[1]),
        fetch(next_in, edge, sems.at[2]),
        fetch(weight_in, weight, sems.at[3]),
    ]
    halves[0, 0:512, :] = prev_ref[0:512, :].astype(F32)
    lane = lanes((C, X))
    clear_rims(0, lat_patch)
    for y in range(Y):
        spread_cells(halves[0, pl.ds(y, C, stride=8), :], 0, y, lane, lat_patch)
    copies[0].wait()
    copies[1].wait()
    first[...] += dot(wide[:, 0:576], lat_patch[...])
    first_copy = fetch(first, first_out, sems.at[4])
    copies[2].wait()
    for half in range(2):
        part = slice(512 + half * 512, 1024 + half * 512)
        halves[half, 0:2048, :] = real_ref[:, half * X : (half + 1) * X].astype(F32)
        halves[half, 2048:2560, :] = prev_ref[part, :].astype(F32)
        halves[half, 2560:3072, :] = edge[half * 512 : (half + 1) * 512, :].astype(F32)
    places = ((2048, 16), (0, 64), (16, 64), (32, 64), (48, 64), (2560, 16))
    for depth in range(6):
        split_depth(depth * 512, places[depth], halves, rows, patch)
    copies[3].wait()
    finish(convolve(weight, patch), cot_ref, out_ref, wide_cot, wide_out, grad)
    planes = [patch[depth * 512 : (depth + 1) * 512, :] for depth in range(6)]
    for half, terms in enumerate(kernel_terms(planes, grad)):
        terms_ref[half * 512 : (half + 1) * 512, :] = terms
    fetch(terms_ref, terms_out, sems.at[5]).wait()
    first_copy.wait()


def fake_kernel(
    inside_ref,
    first_in,
    middle_in,
    last_in,
    stats_ref,
    gain_ref,
    shift_ref,
    weight_in,
    cot_ref,
    real_terms_in,
    out_ref,
    low_out,
    high_out,
    terms_ref,
    before,
    real_terms,
    weight_ref,
    sems,
    patch,
    wide_cot,
    wide_out,
    grad,
):
    befores = []
    for depth in range(6):
        ref = (first_in, middle_in, last_in)[depth // 2]
        half = pl.ds(depth % 2 * 128, 128)
        befores.append(fetch(ref.at[half], before.at[depth], sems.at[depth]))
    weight_copy = fetch(weight_in, weight_ref, sems.at[6])
    real_copy = fetch(real_terms_in, real_terms, sems.at[7])
    stats = stats_ref[...]
    slab = lax.broadcasted_iota(jnp.int32, (NDEV, 128), 0) // 2 % 32
    depths = jnp.where(slab == 0, 5.0, jnp.where(slab == 31, 3.0, 4.0))
    mean_row = jnp.sum(stats * depths, axis=0, keepdims=True) * (1.0 / (4.0 * NDEV))
    off = stats - mean_row
    between = as_column(jnp.sum(off * off * depths, axis=0, keepdims=True), 0)
    center = as_column(mean_row, 0)
    within = as_column(jnp.sum(stats, axis=0, keepdims=True), G)
    variance = (within + 4.0 * CELLS * between) * (1.0 / (16.0 * CELLS * NDEV))
    factor = as_column(gain_ref[...], 0) * lax.rsqrt(variance + 1e-05)
    shift = as_column(shift_ref[...], 0)
    lane = lanes((G, X))
    edge = jnp.zeros((128, X), BF16)
    for depth in range(6):
        befores[depth].wait()
        patch[depth * 512 : depth * 512 + 128, 0:X] = edge
        patch[depth * 512 + 384 : depth * 512 + 512, CELLS - X : CELLS] = edge
        for py in range(2):
            for px in range(2):
                block = (py * 2 + px) * G
                for y in range(Y):
                    cells = before[depth, block : block + G, y * X : (y + 1) * X]
                    fake = jnp.maximum((cells - center) * factor + shift, 0.0)
                    if depth == 0:
                        fake = jnp.where(inside_ref[0] > 0, fake, 0.0)
                    if depth == 5:
                        fake = jnp.where(inside_ref[1] > 0, fake, 0.0)
                    if px == 1:
                        pieces = ((2, fake), (0, from_left(fake, lane)))
                    else:
                        pieces = ((1, fake), (3, from_right(fake, lane)))
                    for kx, piece in pieces:
                        piece = piece.astype(BF16)
                        for ky, to in ((2, y), (0, y + 1)) if py == 1 else ((1, y), (3, y - 1)):
                            if 0 <= to < Y:
                                at = depth * 512 + ky * 128 + kx * G
                                patch[at : at + G, to * X : (to + 1) * X] = piece
    weight_copy.wait()
    pre = convolve(weight_ref, patch)
    finish(pre, cot_ref, out_ref, wide_cot, wide_out, grad)
    edge_copies = [
        fetch(grad.at[2 * C : 3 * C], low_out, sems.at[8]),
        fetch(grad.at[C : 2 * C], high_out, sems.at[9]),
    ]
    planes = [patch[depth * 512 : (depth + 1) * 512, :] for depth in range(6)]
    real_copy.wait()
    for half, terms in enumerate(kernel_terms(planes, grad)):
        rows = slice(half * 512, (half + 1) * 512)
        terms_ref[rows, :] = terms + real_terms[rows, :]
    for copy in edge_copies:
        copy.wait()


def sum_kernel(parts_ref, prev_ref, middle_ref, sums_ref):
    del prev_ref, middle_ref
    total = jnp.sum(parts_ref[...].reshape(NDEV, 8, 128), axis=0, keepdims=True)
    sums_ref[...] = jnp.broadcast_to(total, (NDEV, 8, 128)).reshape(NDEV * 8, 128).astype(BF16)


def unpack_kernel(sums_ref, out_ref):
    sums = sums_ref[...].astype(F32)
    out_ref[0:1024, :] = sums[:, 0:C]
    out_ref[1024:2048, :] = sums[:, C : 2 * C]


def pull_own_kernel(
    low_in,
    high_in,
    taps_in,
    wide_out,
    first_out,
    middle_out,
    last_out,
    cells,
    taps,
    wide,
    first,
    middle,
    last,
    patch,
    sems,
):
    edges = [fetch(ref, cells.at[i], sems.at[i]) for i, ref in enumerate((low_in, high_in))]
    taps_copy = fetch(taps_in, taps, sems.at[2])
    lane = lanes((C, X))
    for depth in range(2):
        edges[depth].wait()
        clear_rims(depth, patch)
        for y in range(Y):
            spread_cells(cells[depth, :, y * X : (y + 1) * X].astype(F32), depth, y, lane, patch)
    taps_copy.wait()
    spread_weights(taps, wide)
    copies = [fetch(wide, wide_out, sems.at[3])]
    first[...] = dot(wide[128:256, 576:1152], patch[0:576, :])
    copies.append(fetch(first, first_out, sems.at[4]))
    middle[...] = dot(wide[...], patch[...]).astype(BF16)
    copies.append(fetch(middle, middle_out, sems.at[5]))
    last[...] = dot(wide[0:128, 0:576], patch[576:1152, :])
    copies.append(fetch(last, last_out, sems.at[6]))
    for copy in copies:
        copy.wait()


def weave_into(result, depth, wide_out):
    column = lanes((2 * X, 2 * X))
    source = lax.broadcasted_iota(jnp.int32, (2 * X, 2 * X), 0)
    weave = jnp.where(source == (column % 2) * X + column // 2, 1.0, 0.0).astype(BF16)
    for py in range(2):
        even = result[py * 64 : py * 64 + G, :]
        odd = result[py * 64 + G : py * 64 + 2 * G, :]
        both = jnp.concatenate(
            [
                jnp.concatenate([even[:, y * X : (y + 1) * X], odd[:, y * X : (y + 1) * X]], axis=1)
                for y in range(Y)
            ],
            axis=0,
        )
        woven = dot(both, weave)
        for y in range(Y):
            rows = pl.ds(depth * 16 + 2 * y + py, G, stride=64)
            wide_out[0, rows, :] = woven[y * G : (y + 1) * G, 0:X]
            wide_out[1, rows, :] = woven[y * G : (y + 1) * G, X : 2 * X]


def spread_edge(cells, patch):
    lane = lanes((C, X))
    clear_rims(0, patch)
    for y in range(Y):
        spread_cells(cells[:, y * X : (y + 1) * X].astype(F32), 0, y, lane, patch)


def pull_prev_kernel(
    prev_in, wide_in, first_in, middle_in, sums_ref, rows_ref, cells, wide, first, middle, patch, sems
):
    del sums_ref
    copies = [
        fetch(middle_in, middle, sems.at[0]),
        fetch(prev_in, cells, sems.at[1]),
        fetch(wide_in, wide, sems.at[2]),
        fetch(first_in, first, sems.at[3]),
    ]
    rows_ref[...] = jnp.zeros_like(rows_ref)
    copies[0].wait()
    weave_into(middle[0:128, :], 1, rows_ref)
    weave_into(middle[128:256, :], 2, rows_ref)
    copies[1].wait()
    spread_edge(cells, patch)
    copies[2].wait()
    copies[3].wait()
    weave_into((first[...] + dot(wide[128:256, 0:576], patch[...])).astype(BF16), 0, rows_ref)


def pull_next_kernel(next_ref, wide_in, last_in, rows_ref, out_ref, wide, last, patch, wide_out, sems):
    copies = [fetch(wide_in, wide, sems.at[0]), fetch(last_in, last, sems.at[1])]
    spread_edge(next_ref, patch)
    wide_out[...] = rows_ref[...]
    copies[0].wait()
    copies[1].wait()
    weave_into((last[...] + dot(wide[0:128, 576:1152], patch[...])).astype(BF16), 3, wide_out)
    out_ref[:, 0:X] = wide_out[0].astype(BF16)
    out_ref[:, X : 2 * X] = wide_out[1].astype(BF16)


def call(body, name, args, outs, scratch, flops, mebibytes, smem=(), far=(), far_outs=()):
    moved = sum(a.size * a.dtype.itemsize for a in args) + sum(o.size * o.dtype.itemsize for o in outs)
    spaces = [
        pltpu.SMEM if i in smem else pl.ANY if i in far else pltpu.VMEM for i in range(len(args))
    ]
    out_spaces = [pltpu.HBM if i in far_outs else pltpu.VMEM for i in range(len(outs))]
    outs = [pltpu.HBM(o.shape, o.dtype) if i in far_outs else o for i, o in enumerate(outs)]
    args = [
        pltpu.with_memory_space_constraint(a, pltpu.HBM) if i in far else a for i, a in enumerate(args)
    ]
    return pl.pallas_call(
        body,
        name=name,
        out_shape=outs,
        in_specs=[pl.BlockSpec(memory_space=space) for space in spaces],
        out_specs=[pl.BlockSpec(memory_space=space) for space in out_spaces],
        scratch_shapes=scratch,
        compiler_params=pltpu.CompilerParams(vmem_limit_bytes=mebibytes * 1024 * 1024),
        cost_estimate=pl.CostEstimate(flops=flops, bytes_accessed=moved, transcendentals=0),
    )(*args)


def to_next(edge):
    ends = lax.axis_size("slab") - 1
    return lax.ppermute(edge, "slab", [(i, i + 1) for i in range(ends)])


def to_prev(edge):
    ends = lax.axis_size("slab") - 1
    return lax.ppermute(edge, "slab", [(i + 1, i) for i in range(ends)])


def local(latent, g_weight, bn_gain, bn_shift, real_crops, d_weight, cot_fake, cot_real):
    shape = jax.ShapeDtypeStruct
    taps_g = g_weight.transpose(0, 1, 2, 4, 3).reshape(64 * G, C)
    taps_d = d_weight.reshape(64 * G, C)
    lat = latent[0]
    real = real_crops[0]
    at = lax.axis_index("slab")
    inside = jnp.stack([at > 0, at < lax.axis_size("slab") - 1]).astype(jnp.int32)
    (low,) = call(
        edge_kernel,
        "edges",
        (lat, real),
        [shape((1536, X), BF16)],
        [
            pltpu.VMEM((C, Y, X), BF16),
            pltpu.VMEM((G, 2 * Y, 2 * X), BF16),
            pltpu.SemaphoreType.DMA((2,)),
        ],
        0,
        4,
        far=(0, 1),
    )
    next_ = to_prev(low)
    wide, first, middle, last, sums, high, weight = call(
        own_kernel,
        "own_cells",
        (lat, real, taps_g, taps_d),
        [shape((256, 1152), BF16)]
        + [shape((256, CELLS), F32)] * 3
        + [shape((G, 128), F32), shape((1536, X), BF16), shape((C, 2048), BF16)],
        [
            pltpu.VMEM((C, Y, X), BF16),
            pltpu.VMEM((G, 2 * Y, 2 * X), BF16),
            pltpu.VMEM((C, 2, Y, X), BF16),
            pltpu.VMEM((2048, C), BF16),
            pltpu.VMEM((2048, C), BF16),
            pltpu.VMEM((C, 2048), BF16),
            pltpu.VMEM((256, 1152), BF16),
            pltpu.VMEM((256, CELLS), F32),
            pltpu.VMEM((256, CELLS), F32),
            pltpu.VMEM((256, CELLS), F32),
            pltpu.SemaphoreType.DMA((10,)),
            pltpu.VMEM((1152, CELLS), BF16),
            pltpu.VMEM((1024, X), F32),
        ],
        4 * 256 * 1152 * CELLS,
        16,
        far=(0, 1, 2, 3),
        far_outs=(0, 1, 2, 3, 6),
    )
    prev = to_next(high)
    last, stats, real_next = call(
        rim_kernel,
        "rim_cells",
        (inside, next_, sums, wide, last),
        [shape((256, CELLS), F32), shape((NDEV, 128), F32), shape((1024, X), BF16)],
        [
            pltpu.VMEM((576, CELLS), BF16),
            pltpu.VMEM((512, X), F32),
            pltpu.VMEM((256, 1152), BF16),
            pltpu.VMEM((256, CELLS), F32),
            pltpu.VMEM((NDEV, 128), F32),
            pltpu.SemaphoreType.DMA((5,)),
        ],
        256 * 1152 * CELLS,
        12,
        smem=(0,),
        far=(3, 4),
        far_outs=(0, 1, 2),
    )
    stats = lax.all_to_all(stats, AXES, 0, 0, tiled=True)
    working = [
        pltpu.VMEM((C * 2 * Y, X), F32),
        pltpu.VMEM((C * 2 * Y, X), F32),
        pltpu.VMEM((4 * C, CELLS), BF16),
    ]
    d_real, real_terms, first = call(
        real_kernel,
        "real_branch",
        (
            real.reshape(G * 64, 2 * X),
            prev,
            real_next,
            weight,
            cot_real.reshape(C * 2 * Y, X),
            wide,
            first,
        ),
        [shape((C * 2 * Y, X), BF16), shape((1024, 2 * C), F32), shape((256, CELLS), F32)],
        [
            pltpu.VMEM((1024, X), BF16),
            pltpu.VMEM((C, 2048), BF16),
            pltpu.VMEM((256, 1152), BF16),
            pltpu.VMEM((256, CELLS), F32),
            pltpu.VMEM((1024, 2 * C), F32),
            pltpu.SemaphoreType.DMA((6,)),
            pltpu.VMEM((6 * 512, CELLS), BF16),
            pltpu.VMEM((576, CELLS), BF16),
            pltpu.VMEM((2, 3072, X), F32),
            pltpu.VMEM((3072, 2 * X), BF16),
        ]
        + working,
        16 * 2048 * C * CELLS,
        26,
        far=(2, 3, 5, 6),
        far_outs=(1, 2),
    )
    d_fake, low, high, terms = call(
        fake_kernel,
        "fake_branch",
        (
            inside,
            first,
            middle,
            last,
            stats,
            bn_gain.reshape(1, G),
            bn_shift.reshape(1, G),
            weight,
            cot_fake.reshape(C * 2 * Y, X),
            real_terms,
        ),
        [
            shape((C * 2 * Y, X), BF16),
            shape((C, CELLS), BF16),
            shape((C, CELLS), BF16),
            shape((NDEV * 8, 128), F32),
        ],
        [
            pltpu.VMEM((6, 128, CELLS), F32),
            pltpu.VMEM((NDEV * 8, 128), F32),
            pltpu.VMEM((C, 2048), BF16),
            pltpu.SemaphoreType.DMA((10,)),
            pltpu.VMEM((6 * 512, CELLS), BF16),
        ]
        + working,
        8 * 2048 * C * CELLS * 2,
        26,
        smem=(0,),
        far=(1, 2, 3, 7, 9),
        far_outs=(1, 2),
    )
    parts = lax.all_to_all(terms.reshape(NDEV, 8, 128), AXES, 0, 0, tiled=True)
    grad_prev = to_next(high)
    grad_next = to_prev(low)
    pull_wide, pull_first, pull_middle, pull_last = call(
        pull_own_kernel,
        "pull_own",
        (low, high, taps_d),
        [
            shape((256, 1152), BF16),
            shape((128, CELLS), F32),
            shape((256, CELLS), BF16),
            shape((128, CELLS), F32),
        ],
        [
            pltpu.VMEM((2, C, CELLS), BF16),
            pltpu.VMEM((2048, C), BF16),
            pltpu.VMEM((256, 1152), BF16),
            pltpu.VMEM((128, CELLS), F32),
            pltpu.VMEM((256, CELLS), BF16),
            pltpu.VMEM((128, CELLS), F32),
            pltpu.VMEM((1152, CELLS), BF16),
            pltpu.SemaphoreType.DMA((7,)),
        ],
        2 * 384 * 1152 * CELLS,
        8,
        far=(0, 1, 2),
        far_outs=(0, 1, 2, 3),
    )
    (sums,) = call(
        sum_kernel,
        "sum_terms",
        (parts.reshape(NDEV * 8, 128), grad_prev, pull_middle),
        [shape((NDEV * 8, 128), BF16)],
        [],
        NDEV * 1024,
        4,
        far=(1, 2),
    )
    whole = lax.all_to_all(sums.reshape(NDEV, 8, 128), AXES, 0, 0, tiled=True)
    (pull_rows,) = call(
        pull_prev_kernel,
        "pull_prev",
        (grad_prev, pull_wide, pull_first, pull_middle, sums),
        [shape((2, G * 64, X), F32)],
        [
            pltpu.VMEM((C, CELLS), BF16),
            pltpu.VMEM((256, 1152), BF16),
            pltpu.VMEM((128, CELLS), F32),
            pltpu.VMEM((256, CELLS), BF16),
            pltpu.VMEM((576, CELLS), BF16),
            pltpu.SemaphoreType.DMA((4,)),
        ],
        2 * 128 * 1152 * CELLS,
        8,
        far=(0, 1, 2, 3, 4),
    )
    (fake_grad,) = call(
        pull_next_kernel,
        "pull_next",
        (grad_next, pull_wide, pull_last, pull_rows),
        [shape((G * 64, 2 * X), BF16)],
        [
            pltpu.VMEM((256, 1152), BF16),
            pltpu.VMEM((128, CELLS), F32),
            pltpu.VMEM((576, CELLS), BF16),
            pltpu.VMEM((2, G * 64, X), F32),
            pltpu.SemaphoreType.DMA((2,)),
        ],
        2 * 128 * 576 * CELLS,
        8,
        far=(1, 2),
    )
    (weight_grad,) = call(
        unpack_kernel,
        "unpack",
        (whole.reshape(NDEV * 8, 128),),
        [shape((2048, C), F32)],
        [],
        0,
        4,
    )
    return (
        d_fake.reshape(1, C, 2, Y, X),
        d_real.reshape(1, C, 2, Y, X),
        fake_grad.reshape(1, G, 4, 2 * Y, 2 * X),
        weight_grad.reshape(4, 4, 4, G, C),
    )


def solution(mesh):
    split = P(("section", "rep"), None, "slab", None, None)
    in_specs = (split, P(), P(), P(), split, P(), split, split)
    out_specs = (split, split, split, P())
    return jax.shard_map(local, mesh=mesh, in_specs=in_specs, out_specs=out_specs, check_vma=False)
```

time: 102 us -> 97.9 us (0.960)
  waiting for transfers between devices: 23.2 us -> 12.4 us
  starting transfers between devices: 39.2 us -> 45.1 us
  Pallas kernels: 37.5 us -> 38.6 us
    all_to_all x1, waiting for transfers between devices: 5.94 us -> 0.01 us  [local(): whole = lax.all_to_all(sums.reshape(NDEV, 8, 128), AXES, 0, 0, tiled=True)]
    ppermute x4, waiting for transfers between devices: 13.6 us -> 8.54 us  [the longest x2 7.39 us: to_prev(): return lax.ppermute(edge, 'slab', [(i + 1, i) for i in range(ends)])]
    all_to_all x1, waiting for transfers between devices: 0.01 us -> 3.81 us  [local(): parts = lax.all_to_all(terms.reshape(NDEV, 8, 128), AXES, 0, 0, tiled=True)]
    all_to_all x1, waiting for transfers between devices: 3.62 us -> 0.01 us  [local(): stats = lax.all_to_all(stats, AXES, 0, 0, tiled=True)]
    all_to_all x1, starting transfers between devices: 6.19 us -> 9.76 us  [local(): parts = lax.all_to_all(terms.reshape(NDEV, 8, 128), AXES, 0, 0, tiled=True)]
    all_to_all x1, starting transfers between devices: 11.1 us -> 14.7 us  [local(): stats = lax.all_to_all(stats, AXES, 0, 0, tiled=True)]
    all_to_all x1, starting transfers between devices: 8.88 us -> 6.61 us  [local(): whole = lax.all_to_all(sums.reshape(NDEV, 8, 128), AXES, 0, 0, tiled=True)]
    pallas_call x10, Pallas kernels: 37.5 us -> 38.6 us  [call(): pl.pallas_call(body, name=name, out_shape=outs, in_specs=[pl.BlockSpec(me...]
  transfers between devices with their start and end apart: 7 -> 7, of which waited for: 6 -> 4; matrix products, arithmetic and copies ran while one was open for 0% -> 0% of each run, Pallas kernels for 23% -> 29%
where the time goes in v5:
time: 97.9 us; the launch traced here: 97 us
  starting transfers between devices  45.1 us (46%)
  Pallas kernels  38.6 us (39%)
  waiting for transfers between devices  12.4 us (13%)
    pallas_call x10, Pallas kernels, call(): pl.pallas_call(body, name=name, out_shape=outs, in_specs=[pl.BlockSpec(me...  38.6 us
    all_to_all x1, starting transfers between devices, local(): stats = lax.all_to_all(stats, AXES, 0, 0, tiled=True)  14.7 us
    ppermute x2, starting transfers between devices, to_next(): return lax.ppermute(edge, 'slab', [(i, i + 1) for i in range(ends)])  11.5 us
    all_to_all x1, starting transfers between devices, local(): parts = lax.all_to_all(terms.reshape(NDEV, 8, 128), AXES, 0, 0, tiled=True)  9.76 us
    ppermute x2, waiting for transfers between devices, to_prev(): return lax.ppermute(edge, 'slab', [(i + 1, i) for i in range(ends)])  7.39 us
    all_to_all x1, starting transfers between devices, local(): whole = lax.all_to_all(sums.reshape(NDEV, 8, 128), AXES, 0, 0, tiled=True)  6.61 us
    all_to_all x1, waiting for transfers between devices, local(): parts = lax.all_to_all(terms.reshape(NDEV, 8, 128), AXES, 0, 0, tiled=True)  3.81 us
    ppermute x2, starting transfers between devices, to_prev(): return lax.ppermute(edge, 'slab', [(i + 1, i) for i in range(ends)])  2.58 us
  transfers between devices with their start and end apart: 7, of which 4 were waited for; matrix products, arithmetic and copies ran while one was open for 0% of the time, Pallas kernels for 29%

profile of v5, /device:TPU:1, one launch (start us, length us, event | category | flops | bytes accessed | tf_op | source)
XLA Modules:
  0.0 97.0 jit_solution(6052304470330312252)
XLA Ops:
  0.6 1.1 %edges.1 = bf16[1536,128]{1,0:T(8,128)(2,1)S(1)} custom-call(bf16[64,2,8,128]{3,2,1,0:T(8,128)(2,1)} %bitcast.37, bf16[32,4,16,256]{3,2,1,0:T(8,128)(2,1)} %bitcast.27), custom_call_target="tpu_custom_call" | custom-call | bytes 1703936 | tf_op jit(solution)/shard_map/edges/pallas_call | solution.py:552
  1.7 1.3 %collective-permute-start.1 = (bf16[1536,128]{1,0:T(8,128)(2,1)S(1)}, bf16[1536,128]{1,0:T(8,128)(2,1)S(1)}, u32[]{:S(2)}, u32[]{:S(2)}) collective-permute-start(bf16[1536,128]{1,0:T(8,128)(2,1)S(1)} %edges.1), channel_id=1, source_target_pairs={{2,0},{4,2},{6,4},{8,6},{10,8},{12,10},{14,12},{16,14},{18,16},{20... | collective-permute-start | bytes 1179656 | tf_op jit(solution)/shard_map/ppermute | solution.py:571
  3.0 4.5 %own_cells.1 = (bf16[256,1152]{1,0:T(8,128)(2,1)}, f32[256,1024]{1,0:T(8,128)}, f32[256,1024]{1,0:T(8,128)}, f32[256,1024]{1,0:T(8,128)}, f32[32,128]{1,0:T(8,12...) custom-call(bf16[64,2,8,128]{3,2,1,0:T(8,128)(2,1)} %bitcast.38, bf16[32,4,16,256]{3,2,1,0:T(8,128)(2,1)} %bitcast.28, ...), custom_call_target="tpu_custom_call" | custom-call | flops 1207959552 | bytes 6242304 | tf_op jit(solution)/shard_map/own_cells/pallas_call | solution.py:552
  7.5 0.0 copy-start
  7.5 6.4 %collective-permute-start = (bf16[1536,128]{1,0:T(8,128)(2,1)S(1)}, bf16[1536,128]{1,0:T(8,128)(2,1)S(1)}, u32[]{:S(2)}, u32[]{:S(2)}) collective-permute-start(bf16[1536,128]{1,0:T(8,128)(2,1)S(1)} %get-tuple-element.25), channel_id=1, source_target_pairs={{0,2},{2,4},{4,6},{6,8},{8,10},{10,12},{12,14},{14,16},{16,18},{18... | collective-permute-start | bytes 1179656 | tf_op jit(solution)/shard_map/ppermute | solution.py:566
  14.0 0.1 add_convert_fusion.inside_ref
  14.0 1.9 %collective-permute-done.1.next_ref = bf16[1536,128]{1,0:T(8,128)(2,1)S(1)} collective-permute-done((bf16[1536,128]{1,0:T(8,128)(2,1)S(1)}, bf16[1536,128]{1,0:T(8,128)(2,1)S(1)}, u32[]{:S(2)}, u32[]{:S(2)}) %collective-permute-start.1) | collective-permute-done | bytes 393248 | tf_op jit(solution)/shard_map/ppermute | solution.py:571
  15.9 3.8 %rim_cells.1 = (f32[256,1024]{1,0:T(8,128)}, f32[128,128]{1,0:T(8,128)}, bf16[1024,128]{1,0:T(8,128)(2,1)}) custom-call(s32[2]{0:T(128)S(1)} %add_convert_fusion.inside_ref, bf16[1536,128]{1,0:T(8,128)(2,1)S(1)} %collective-permute-done.1.next_ref, f32[32,128]{1,0:T(8,128)S(1)} %get-tuple-element.26.sums_ref, bf16[256,1152]{1,0:T(8,128)(2,1)} %get-tuple-element.27.wide_in, ...), custom_call_target="tpu_custom_call" | custom-call | flops 301989888 | bytes 3424264 | tf_op jit(solution)/shard_map/rim_cells/pallas_call | solution.py:552
  19.7 14.7 %all-to-all-start = ((f32[128,1,128]{2,1,0:T(1,128)}), f32[128,1,128]{2,1,0:T(1,128)S(1)}, u32[]{:S(2)}, u32[]{:S(2)}) async-start(f32[128,1,128]{2,1,0:T(1,128)} %bitcast.39), calls=%async_computation | async-start | bytes 131072 | tf_op jit(solution)/shard_map/all_to_all | solution.py:644
  34.4 0.0 copy-start.2
  34.4 10.0 %real_branch.1 = (bf16[1024,128]{1,0:T(8,128)(2,1)}, f32[1024,128]{1,0:T(8,128)}, f32[256,1024]{1,0:T(8,128)}) custom-call(bf16[2048,256]{1,0:T(8,128)(2,1)S(1)} %bitcast.29, bf16[1536,128]{1,0:T(8,128)(2,1)S(1)} %collective-permute-done.prev_ref, bf16[1024,128]{1,0:T(8,128)(2,1)} %get-tuple-element.29.next_in, ...), custom_call_target="tpu_custom_call" | custom-call | flops 2147483648 | bytes 5701632 | tf_op jit(solution)/shard_map/real_branch/pallas_call | solution.py:552
  44.5 7.3 %fake_branch.1 = (bf16[1024,128]{1,0:T(8,128)(2,1)}, bf16[64,1024]{1,0:T(8,128)(2,1)}, bf16[64,1024]{1,0:T(8,128)(2,1)}, f32[1024,128]{1,0:T(8,128)}) custom-call(s32[2]{0:T(128)S(1)} %add_convert_fusion.inside_ref, f32[256,1024]{1,0:T(8,128)} %get-tuple-element.32.first_in, f32[256,1024]{1,0:T(8,128)} %get-tuple-element.33.middle_in, ...), custom_call_target="tpu_custom_call" | custom-call | flops 2147483648 | bytes 5308680 | tf_op jit(solution)/shard_map/fake_branch/pallas_call | solution.py:552
  51.8 9.8 %all-to-all-start.1 = ((f32[128,8,128]{2,1,0:T(8,128)}), f32[128,8,128]{2,1,0:T(8,128)S(1)}, u32[]{:S(2)}, u32[]{:S(2)}) async-start(f32[128,8,128]{2,1,0:T(8,128)} %bitcast.17), calls=%async_computation.1 | async-start | bytes 1048576 | tf_op jit(solution)/shard_map/all_to_all | solution.py:716
  61.6 5.0 %collective-permute-start.3 = (bf16[64,1024]{1,0:T(8,128)(2,1)}, bf16[64,1024]{1,0:T(8,128)(2,1)S(1)}, u32[]{:S(2)}, u32[]{:S(2)}) collective-permute-start(bf16[64,1024]{1,0:T(8,128)(2,1)} %get-tuple-element.40.high_in), channel_id=1, source_target_pairs={{0,2},{2,4},{4,6},{6,8},{8,10},{10,12},{12,14},{14,16},{16,18},{18... | collective-permute-start | bytes 393224 | tf_op jit(solution)/shard_map/ppermute | solution.py:566
  66.7 3.7 %pull_own.1 = (bf16[256,1152]{1,0:T(8,128)(2,1)}, f32[128,1024]{1,0:T(8,128)}, bf16[256,1024]{1,0:T(8,128)(2,1)}, f32[128,1024]{1,0:T(8,128)}) custom-call(bf16[64,1024]{1,0:T(8,128)(2,1)} %get-tuple-element.39.low_in, bf16[64,1024]{1,0:T(8,128)(2,1)} %get-tuple-element.40.high_in, bf16[2048,64]{1,0:T(8,128)(2,1)} %bitcast.42), custom_call_target="tpu_custom_call" | custom-call | flops 905969664 | bytes 2686976 | tf_op jit(solution)/shard_map/pull_own/pallas_call | solution.py:552
  70.3 1.1 %collective-permute-done.3.prev_ref.prev_in = bf16[64,1024]{1,0:T(8,128)(2,1)S(1)} collective-permute-done((bf16[64,1024]{1,0:T(8,128)(2,1)}, bf16[64,1024]{1,0:T(8,128)(2,1)S(1)}, u32[]{:S(2)}, u32[]{:S(2)}) %collective-permute-start.3) | collective-permute-done | bytes 131104 | tf_op jit(solution)/shard_map/ppermute | solution.py:566
  71.5 3.8 %all-to-all-done.1 = f32[128,8,128]{2,1,0:T(8,128)S(1)} async-done(((f32[128,8,128]{2,1,0:T(8,128)}), f32[128,8,128]{2,1,0:T(8,128)S(1)}, u32[]{:S(2)}, u32[]{:S(2)}) %all-to-all-start.1) | async-done | bytes 524320 | tf_op jit(solution)/shard_map/all_to_all | solution.py:716
  75.3 0.9 sum_terms.1.sums_ref
  76.1 6.6 %all-to-all-start.2 = ((bf16[128,8,128]{2,1,0:T(8,128)(2,1)}), bf16[128,8,128]{2,1,0:T(8,128)(2,1)S(1)}, u32[]{:S(2)}, u32[]{:S(2)}) async-start(bf16[128,8,128]{2,1,0:T(8,128)(2,1)} %bitcast.20), calls=%async_computation.2 | async-start | bytes 524288 | tf_op jit(solution)/shard_map/all_to_all | solution.py:754
  82.8 1.3 %collective-permute-start.2 = (bf16[64,1024]{1,0:T(8,128)(2,1)S(1)}, bf16[64,1024]{1,0:T(8,128)(2,1)S(1)}, u32[]{:S(2)}, u32[]{:S(2)}) collective-permute-start(bf16[64,1024]{1,0:T(8,128)(2,1)S(1)} %copy-done.6), channel_id=1, source_target_pairs={{2,0},{4,2},{6,4},{8,6},{10,8},{12,10},{14,12},{16,14},{18,16},{20... | collective-permute-start | bytes 393224 | tf_op jit(solution)/shard_map/ppermute | solution.py:571
  84.1 3.0 %pull_prev.1.rows_ref = f32[2,2048,128]{2,1,0:T(8,128)S(1)} custom-call(bf16[64,1024]{1,0:T(8,128)(2,1)} %copy-done.5, bf16[256,1152]{1,0:T(8,128)(2,1)} %get-tuple-element.41.wide_in, f32[128,1024]{1,0:T(8,128)} %get-tuple-element.43.first_in, bf16[256,1024]{1,0:T(8,128)(2,1)} %get-tuple-element.44.middle_ref.middle_in, bf16[1024,128]{1,0:T(8,128)(2,1)} %sum_terms.1.sums_ref), custom_call_target="tpu_custom_call" | custom-call | flops 301989888 | bytes 4128768 | tf_op jit(solution)/shard_map/pull_prev/pallas_call | solution.py:552
  87.1 5.5 %collective-permute-done.2.next_ref = bf16[64,1024]{1,0:T(8,128)(2,1)S(1)} collective-permute-done((bf16[64,1024]{1,0:T(8,128)(2,1)S(1)}, bf16[64,1024]{1,0:T(8,128)(2,1)S(1)}, u32[]{:S(2)}, u32[]{:S(2)}) %collective-permute-start.2) | collective-permute-done | bytes 131104 | tf_op jit(solution)/shard_map/ppermute | solution.py:571
  92.6 3.3 %pull_next.1 = bf16[2048,256]{1,0:T(8,128)(2,1)} custom-call(bf16[64,1024]{1,0:T(8,128)(2,1)S(1)} %collective-permute-done.2.next_ref, bf16[256,1152]{1,0:T(8,128)(2,1)} %get-tuple-element.41.wide_in, f32[128,1024]{1,0:T(8,128)} %get-tuple-element.42.last_in, f32[2,2048,128]{2,1,0:T(8,128)S(1)} %pull_prev.1.rows_ref), custom_call_target="tpu_custom_call" | custom-call | flops 150994944 | bytes 4390912 | tf_op jit(solution)/shard_map/pull_next/pallas_call | solution.py:552
  95.9 1.1 %unpack.1 = f32[2048,64]{1,0:T(8,128)} custom-call(bf16[1024,128]{1,0:T(8,128)(2,1)S(1)} %bitcast.26), custom_call_target="tpu_custom_call" | custom-call | bytes 786432 | tf_op jit(solution)/shard_map/unpack/pallas_call | solution.py:552
  (15 shorter events, 0.0 us)
Async XLA Ops:
  1.7 14.2 %collective-permute-start.1 = (bf16[1536,128]{1,0:T(8,128)(2,1)S(1)}, bf16[1536,128]{1,0:T(8,128)(2,1)S(1)}, u32[]{:S(2)}, u32[]{:S(2)}) collective-permute-start(bf16[1536,128]{1,0:T(8,128)(2,1)S(1)} %edges.1), channel_id=1, source_target_pairs={{2,0},{4,2},{6,4},{8,6},{10,8},{12,10},{14,12},{16,14},{18,16},{20... | collective-permute-start | bytes 1179656 | tf_op jit(solution)/shard_map/ppermute | solution.py:571
  7.5 26.9 %copy-start = (bf16[1,32,4,16,256]{4,3,2,1,0:T(8,128)(2,1)S(1)}, bf16[1,32,4,16,256]{4,3,2,1,0:T(8,128)(2,1)}, u32[]{:S(2)}) copy-start(bf16[1,32,4,16,256]{4,3,2,1,0:T(8,128)(2,1)} %param.12) | copy-start | bytes 3145732
  7.5 26.9 %copy-start.1 = (bf16[1,64,2,8,128]{4,3,2,1,0:T(8,128)(2,1)S(1)}, bf16[1,64,2,8,128]{4,3,2,1,0:T(8,128)(2,1)}, u32[]{:S(2)}) copy-start(bf16[1,64,2,8,128]{4,3,2,1,0:T(8,128)(2,1)} %param.15) | copy-start | bytes 786436
  7.5 26.9 %collective-permute-start = (bf16[1536,128]{1,0:T(8,128)(2,1)S(1)}, bf16[1536,128]{1,0:T(8,128)(2,1)S(1)}, u32[]{:S(2)}, u32[]{:S(2)}) collective-permute-start(bf16[1536,128]{1,0:T(8,128)(2,1)S(1)} %get-tuple-element.25), channel_id=1, source_target_pairs={{0,2},{2,4},{4,6},{6,8},{8,10},{10,12},{12,14},{14,16},{16,18},{18... | collective-permute-start | bytes 1179656 | tf_op jit(solution)/shard_map/ppermute | solution.py:566
  19.7 24.8 %all-to-all-start = ((f32[128,1,128]{2,1,0:T(1,128)}), f32[128,1,128]{2,1,0:T(1,128)S(1)}, u32[]{:S(2)}, u32[]{:S(2)}) async-start(f32[128,1,128]{2,1,0:T(1,128)} %bitcast.39), calls=%async_computation | async-start | bytes 131072 | tf_op jit(solution)/shard_map/all_to_all | solution.py:644
  34.4 10.1 %copy-start.2 = (bf16[1,64,2,8,128]{4,3,2,1,0:T(8,128)(2,1)S(1)}, bf16[1,64,2,8,128]{4,3,2,1,0:T(8,128)(2,1)}, u32[]{:S(2)}) copy-start(bf16[1,64,2,8,128]{4,3,2,1,0:T(8,128)(2,1)} %param.14) | copy-start | bytes 786436
  34.4 10.1 %copy-start.3 = (f32[32]{0:T(128)S(1)}, f32[32]{0:T(128)}, u32[]{:S(2)}) copy-start(f32[32]{0:T(128)} %param.10) | copy-start | bytes 388
  34.4 10.1 %copy-start.4 = (f32[32]{0:T(128)S(1)}, f32[32]{0:T(128)}, u32[]{:S(2)}) copy-start(f32[32]{0:T(128)} %param.11) | copy-start | bytes 388
  51.8 23.4 %all-to-all-start.1 = ((f32[128,8,128]{2,1,0:T(8,128)}), f32[128,8,128]{2,1,0:T(8,128)S(1)}, u32[]{:S(2)}, u32[]{:S(2)}) async-start(f32[128,8,128]{2,1,0:T(8,128)} %bitcast.17), calls=%async_computation.1 | async-start | bytes 1048576 | tf_op jit(solution)/shard_map/all_to_all | solution.py:716
  61.6 9.8 %collective-permute-start.3 = (bf16[64,1024]{1,0:T(8,128)(2,1)}, bf16[64,1024]{1,0:T(8,128)(2,1)S(1)}, u32[]{:S(2)}, u32[]{:S(2)}) collective-permute-start(bf16[64,1024]{1,0:T(8,128)(2,1)} %get-tuple-element.40.high_in), channel_id=1, source_target_pairs={{0,2},{2,4},{4,6},{6,8},{8,10},{10,12},{12,14},{14,16},{16,18},{18... | collective-permute-start | bytes 393224 | tf_op jit(solution)/shard_map/ppermute | solution.py:566
  66.6 16.1 %copy-start.6 = (bf16[64,1024]{1,0:T(8,128)(2,1)S(1)}, bf16[64,1024]{1,0:T(8,128)(2,1)}, u32[]{:S(2)}) copy-start(bf16[64,1024]{1,0:T(8,128)(2,1)} %get-tuple-element.39.low_in) | copy-start | bytes 393220
  71.5 3.8 %copy-start.5 = (bf16[64,1024]{1,0:T(8,128)(2,1)}, bf16[64,1024]{1,0:T(8,128)(2,1)S(1)}, u32[]{:S(2)}) copy-start(bf16[64,1024]{1,0:T(8,128)(2,1)S(1)} %collective-permute-done.3.prev_ref.prev_in) | copy-start | bytes 393220
  76.1 19.8 %all-to-all-start.2 = ((bf16[128,8,128]{2,1,0:T(8,128)(2,1)}), bf16[128,8,128]{2,1,0:T(8,128)(2,1)S(1)}, u32[]{:S(2)}, u32[]{:S(2)}) async-start(bf16[128,8,128]{2,1,0:T(8,128)(2,1)} %bitcast.20), calls=%async_computation.2 | async-start | bytes 524288 | tf_op jit(solution)/shard_map/all_to_all | solution.py:754
  82.8 9.8 %collective-permute-start.2 = (bf16[64,1024]{1,0:T(8,128)(2,1)S(1)}, bf16[64,1024]{1,0:T(8,128)(2,1)S(1)}, u32[]{:S(2)}, u32[]{:S(2)}) collective-permute-start(bf16[64,1024]{1,0:T(8,128)(2,1)S(1)} %copy-done.6), channel_id=1, source_target_pairs={{2,0},{4,2},{6,4},{8,6},{10,8},{12,10},{14,12},{16,14},{18,16},{20... | collective-permute-start | bytes 393224 | tf_op jit(solution)/shard_map/ppermute | solution.py:571

commit v6 on v5

--- a/solution.py
+++ b/solution.py
@@ -44,9 +44,9 @@
                     tz = oz if pz == 1 else oz + 1
                     for ky, oy in phase_taps[py]:
                         for kx, ox in phase_taps[px]:
-                            col = tz * 576 + (oy + 1) * 192 + (ox + 1) * 64
+                            col = (oy + 1) * 192 + (ox + 1) * 64
                             tap = (kz * 16 + ky * 4 + kx) * G
-                            wide_ref[row : row + G, col : col + C] = taps_ref[tap : tap + G, :]
+                            wide_ref[tz, row : row + G, col : col + C] = taps_ref[tap : tap + G, :]
 
 
 def spread_cells(tile, depth, y, lane, patch_ref):
@@ -155,11 +155,11 @@
     taps_copy.wait()
     spread_weights(taps, wide)
     copies = [fetch(wide, wide_out, sems.at[5])]
-    last[...] = dot(wide[:, 0:576], patch[576:1152, :])
+    last[...] = dot(wide[0], patch[576:1152, :])
     copies.append(fetch(last, last_out, sems.at[6]))
-    middle[...] = dot(wide[...], patch[...])
+    middle[...] = dot(wide[0], patch[0:576, :]) + dot(wide[1], patch[576:1152, :])
     copies.append(fetch(middle, middle_out, sems.at[7]))
-    first[...] = dot(wide[:, 576:1152], patch[0:576, :])
+    first[...] = dot(wide[1], patch[0:576, :])
     copies.append(fetch(first, first_out, sems.at[8]))
     taps_d_copy.wait()
     same = lax.broadcasted_iota(jnp.int32, (C, C), 0) == lanes((C, C))
@@ -180,6 +180,8 @@
     inside_ref,
     next_ref,
     sums_ref,
+    gain_ref,
+    shift_ref,
     wide_in,
     last_in,
     last_out,
@@ -192,7 +194,7 @@
     stats,
     sems,
 ):
-    wide_copy = fetch(wide_in, wide, sems.at[0])
+    wide_copy = fetch(wide_in.at[1], wide, sems.at[0])
     last_copy = fetch(last_in, last, sems.at[1])
     copies = [fetch(next_ref.at[512:1536], real_next_out, sems.at[2])]
     wide_lat[...] = next_ref[0:512, :].astype(F32)
@@ -201,8 +203,9 @@
     for y in range(Y):
         spread_cells(wide_lat[pl.ds(y, C, stride=8), :], 0, y, lane, patch)
     wide_copy.wait()
+    added = dot(wide[...], patch[...])
     last_copy.wait()
-    last[...] += dot(wide[:, 576:1152], patch[...])
+    last[...] += added
     copies.append(fetch(last, last_out, sems.at[3]))
     groups = [(2.0, sums_ref[:, 0:1], sums_ref[:, 1:2])]
     groups.append((jnp.where(inside_ref[0] > 0, 0.0, 1.0), sums_ref[:, 2:3], sums_ref[:, 3:4]))
@@ -218,7 +221,9 @@
     for weight, one, squares in groups:
         own = squares if isinstance(weight, float) else weight * squares
         spread += own + weight * (4.0 * CELLS) * (one - mean) * (one - mean)
-    stats[...] = jnp.broadcast_to(as_row(mean, 0) + as_row(spread, G), (NDEV, 128))
+    row = as_row(mean, 0) + as_row(spread, G)
+    row += as_row(as_column(gain_ref[...], 0), 2 * G) + as_row(as_column(shift_ref[...], 0), 3 * G)
+    stats[...] = jnp.broadcast_to(row, (NDEV, 128))
     copies.append(fetch(stats, stats_out, sems.at[4]))
     for copy in copies:
         copy.wait()
@@ -312,31 +317,33 @@
     wide_out,
     grad,
 ):
+    edge_copy = fetch(next_in, edge, sems.at[0])
+    for half in range(2):
+        part = slice(512 + half * 512, 1024 + half * 512)
+        halves[half, 0:2048, :] = real_ref[:, half * X : (half + 1) * X].astype(F32)
+        halves[half, 2048:2560, :] = prev_ref[part, :].astype(F32)
+    places = ((2048, 16), (0, 64), (16, 64), (32, 64), (48, 64), (2560, 16))
+    for depth in range(2):
+        split_depth(depth * 512, places[depth], halves, rows, patch)
+    edge_copy.wait()
     copies = [
-        fetch(wide_in, wide, sems.at[0]),
-        fetch(first_in, first, sems.at[1]),
-        fetch(next_in, edge, sems.at[2]),
-        fetch(weight_in, weight, sems.at[3]),
+        fetch(weight_in, weight, sems.at[1]),
+        fetch(wide_in.at[0], wide, sems.at[2]),
+        fetch(first_in, first, sems.at[3]),
     ]
+    for half in range(2):
+        halves[half, 2560:3072, :] = edge[half * 512 : (half + 1) * 512, :].astype(F32)
+    for depth in range(2, 6):
+        split_depth(depth * 512, places[depth], halves, rows, patch)
     halves[0, 0:512, :] = prev_ref[0:512, :].astype(F32)
     lane = lanes((C, X))
     clear_rims(0, lat_patch)
     for y in range(Y):
         spread_cells(halves[0, pl.ds(y, C, stride=8), :], 0, y, lane, lat_patch)
-    copies[0].wait()
-    copies[1].wait()
-    first[...] += dot(wide[:, 0:576], lat_patch[...])
+    for copy in copies:
+        copy.wait()
+    first[...] += dot(wide[...], lat_patch[...])
     first_copy = fetch(first, first_out, sems.at[4])
-    copies[2].wait()
-    for half in range(2):
-        part = slice(512 + half * 512, 1024 + half * 512)
-        halves[half, 0:2048, :] = real_ref[:, half * X : (half + 1) * X].astype(F32)
-        halves[half, 2048:2560, :] = prev_ref[part, :].astype(F32)
-        halves[half, 2560:3072, :] = edge[half * 512 : (half + 1) * 512, :].astype(F32)
-    places = ((2048, 16), (0, 64), (16, 64), (32, 64), (48, 64), (2560, 16))
-    for depth in range(6):
-        split_depth(depth * 512, places[depth], halves, rows, patch)
-    copies[3].wait()
     finish(convolve(weight, patch), cot_ref, out_ref, wide_cot, wide_out, grad)
     planes = [patch[depth * 512 : (depth + 1) * 512, :] for depth in range(6)]
     for half, terms in enumerate(kernel_terms(planes, grad)):
@@ -351,8 +358,6 @@
     middle_in,
     last_in,
     stats_ref,
-    gain_ref,
-    shift_ref,
     weight_in,
     cot_ref,
     real_terms_in,
@@ -369,13 +374,12 @@
     wide_out,
     grad,
 ):
-    befores = []
-    for depth in range(6):
+    def fetch_before(depth):
         ref = (first_in, middle_in, last_in)[depth // 2]
         half = pl.ds(depth % 2 * 128, 128)
-        befores.append(fetch(ref.at[half], before.at[depth], sems.at[depth]))
-    weight_copy = fetch(weight_in, weight_ref, sems.at[6])
-    real_copy = fetch(real_terms_in, real_terms, sems.at[7])
+        return fetch(ref.at[half], before.at[depth], sems.at[depth])
+
+    befores = [fetch_before(depth) for depth in range(3)]
     stats = stats_ref[...]
     slab = lax.broadcasted_iota(jnp.int32, (NDEV, 128), 0) // 2 % 32
     depths = jnp.where(slab == 0, 5.0, jnp.where(slab == 31, 3.0, 4.0))
@@ -385,12 +389,18 @@
     center = as_column(mean_row, 0)
     within = as_column(jnp.sum(stats, axis=0, keepdims=True), G)
     variance = (within + 4.0 * CELLS * between) * (1.0 / (16.0 * CELLS * NDEV))
-    factor = as_column(gain_ref[...], 0) * lax.rsqrt(variance + 1e-05)
-    shift = as_column(shift_ref[...], 0)
+    factor = as_column(stats[0:1, :], 2 * G) * lax.rsqrt(variance + 1e-05)
+    shift = as_column(stats[0:1, :], 3 * G)
     lane = lanes((G, X))
     edge = jnp.zeros((128, X), BF16)
     for depth in range(6):
         befores[depth].wait()
+        if depth < 3:
+            befores.append(fetch_before(depth + 3))
+        elif depth == 3:
+            weight_copy = fetch(weight_in, weight_ref, sems.at[6])
+        elif depth == 4:
+            real_copy = fetch(real_terms_in, real_terms, sems.at[7])
         patch[depth * 512 : depth * 512 + 128, 0:X] = edge
         patch[depth * 512 + 384 : depth * 512 + 512, CELLS - X : CELLS] = edge
         for py in range(2):
@@ -429,57 +439,27 @@
         copy.wait()
 
 
-def sum_kernel(parts_ref, prev_ref, middle_ref, sums_ref):
-    del prev_ref, middle_ref
+def sum_kernel(parts_ref, prev_ref, next_ref, first_ref, sums_ref):
+    del prev_ref, next_ref, first_ref
     total = jnp.sum(parts_ref[...].reshape(NDEV, 8, 128), axis=0, keepdims=True)
     sums_ref[...] = jnp.broadcast_to(total, (NDEV, 8, 128)).reshape(NDEV * 8, 128).astype(BF16)
 
 
-def unpack_kernel(sums_ref, out_ref):
-    sums = sums_ref[...].astype(F32)
-    out_ref[0:1024, :] = sums[:, 0:C]
-    out_ref[1024:2048, :] = sums[:, C : 2 * C]
-
-
-def pull_own_kernel(
-    low_in,
-    high_in,
-    taps_in,
-    wide_out,
-    first_out,
-    middle_out,
-    last_out,
-    cells,
-    taps,
-    wide,
-    first,
-    middle,
-    last,
-    patch,
-    sems,
-):
-    edges = [fetch(ref, cells.at[i], sems.at[i]) for i, ref in enumerate((low_in, high_in))]
-    taps_copy = fetch(taps_in, taps, sems.at[2])
-    lane = lanes((C, X))
-    for depth in range(2):
-        edges[depth].wait()
-        clear_rims(depth, patch)
-        for y in range(Y):
-            spread_cells(cells[depth, :, y * X : (y + 1) * X].astype(F32), depth, y, lane, patch)
-    taps_copy.wait()
-    spread_weights(taps, wide)
-    copies = [fetch(wide, wide_out, sems.at[3])]
-    first[...] = dot(wide[128:256, 576:1152], patch[0:576, :])
-    copies.append(fetch(first, first_out, sems.at[4]))
-    middle[...] = dot(wide[...], patch[...]).astype(BF16)
-    copies.append(fetch(middle, middle_out, sems.at[5]))
-    last[...] = dot(wide[0:128, 0:576], patch[576:1152, :])
-    copies.append(fetch(last, last_out, sems.at[6]))
+def unpack_kernel(sums_ref, out, whole, sems):
+    copies = []
+    for part in range(4):
+        rows = slice(part * 256, (part + 1) * 256)
+        sums = sums_ref[rows, :].astype(F32)
+        whole[0, rows, :] = sums[:, 0:C]
+        whole[1, rows, :] = sums[:, C : 2 * C]
+        for half in range(2):
+            piece = pl.ds(part * 256, 256)
+            copies.append(fetch(whole.at[half, piece], out.at[half, piece], sems.at[2 * part + half]))
     for copy in copies:
         copy.wait()
 
 
-def weave_into(result, depth, wide_out):
+def weave_into(result, first_row, stride, wide_out):
     column = lanes((2 * X, 2 * X))
     source = lax.broadcasted_iota(jnp.int32, (2 * X, 2 * X), 0)
     weave = jnp.where(source == (column % 2) * X + column // 2, 1.0, 0.0).astype(BF16)
@@ -495,51 +475,103 @@
         )
         woven = dot(both, weave)
         for y in range(Y):
-            rows = pl.ds(depth * 16 + 2 * y + py, G, stride=64)
+            rows = pl.ds(first_row + 2 * y + py, G, stride=stride)
             wide_out[0, rows, :] = woven[y * G : (y + 1) * G, 0:X]
             wide_out[1, rows, :] = woven[y * G : (y + 1) * G, X : 2 * X]
 
 
-def spread_edge(cells, patch):
+def spread_edge(cells, depth, patch):
     lane = lanes((C, X))
-    clear_rims(0, patch)
+    clear_rims(depth, patch)
     for y in range(Y):
-        spread_cells(cells[:, y * X : (y + 1) * X].astype(F32), 0, y, lane, patch)
-
-
-def pull_prev_kernel(
-    prev_in, wide_in, first_in, middle_in, sums_ref, rows_ref, cells, wide, first, middle, patch, sems
+        spread_cells(cells[:, y * X : (y + 1) * X].astype(F32), depth, y, lane, patch)
+
+
+def pull_own_kernel(
+    low_in,
+    high_in,
+    taps_in,
+    wide_out,
+    first_out,
+    last_out,
+    image_out,
+    cells,
+    taps,
+    wide,
+    first,
+    last,
+    patch,
+    wide_rows,
+    image,
+    sems,
 ):
-    del sums_ref
+    edges = [fetch(ref, cells.at[i], sems.at[i]) for i, ref in enumerate((low_in, high_in))]
+    taps_copy = fetch(taps_in, taps, sems.at[2])
+    for depth in range(2):
+        edges[depth].wait()
+        spread_edge(cells[depth], depth, patch)
+    taps_copy.wait()
+    spread_weights(taps, wide)
+    copies = [fetch(wide, wide_out, sems.at[3])]
+    first[...] = dot(wide[1, 128:256, :], patch[0:576, :])
+    copies.append(fetch(first, first_out, sems.at[4]))
+    last[...] = dot(wide[0, 0:128, :], patch[576:1152, :])
+    copies.append(fetch(last, last_out, sems.at[5]))
+    middle = dot(wide[0], patch[0:576, :]) + dot(wide[1], patch[576:1152, :])
+    middle = middle.astype(BF16)
+    weave_into(middle[0:128, :], 0, 32, wide_rows)
+    weave_into(middle[128:256, :], 16, 32, wide_rows)
+    for half in range(2):
+        image[:, :, half * X : (half + 1) * X] = wide_rows[half].reshape(G, 32, X).astype(BF16)
+    copies.append(fetch(image, image_out.at[:, 16:48], sems.at[6]))
+    for copy in copies:
+        copy.wait()
+
+
+def pullback_kernel(
+    prev_in,
+    next_in,
+    wide_in,
+    first_in,
+    last_in,
+    sums_ref,
+    image_in,
+    image_out,
+    cells,
+    wide,
+    outer,
+    patch,
+    wide_rows,
+    image,
+    sems,
+):
+    del sums_ref, image_in
+    edges = [fetch(ref, cells.at[i], sems.at[i]) for i, ref in enumerate((prev_in, next_in))]
     copies = [
-        fetch(middle_in, middle, sems.at[0]),
-        fetch(prev_in, cells, sems.at[1]),
         fetch(wide_in, wide, sems.at[2]),
-        fetch(first_in, first, sems.at[3]),
+        fetch(first_in, outer.at[0], sems.at[3]),
+        fetch(last_in, outer.at[1], sems.at[4]),
     ]
-    rows_ref[...] = jnp.zeros_like(rows_ref)
-    copies[0].wait()
-    weave_into(middle[0:128, :], 1, rows_ref)
-    weave_into(middle[128:256, :], 2, rows_ref)
-    copies[1].wait()
-    spread_edge(cells, patch)
-    copies[2].wait()
-    copies[3].wait()
-    weave_into((first[...] + dot(wide[128:256, 0:576], patch[...])).astype(BF16), 0, rows_ref)
-
-
-def pull_next_kernel(next_ref, wide_in, last_in, rows_ref, out_ref, wide, last, patch, wide_out, sems):
-    copies = [fetch(wide_in, wide, sems.at[0]), fetch(last_in, last, sems.at[1])]
-    spread_edge(next_ref, patch)
-    wide_out[...] = rows_ref[...]
-    copies[0].wait()
-    copies[1].wait()
-    weave_into((last[...] + dot(wide[0:128, 576:1152], patch[...])).astype(BF16), 3, wide_out)
-    out_ref[:, 0:X] = wide_out[0].astype(BF16)
-    out_ref[:, X : 2 * X] = wide_out[1].astype(BF16)
-
-
-def call(body, name, args, outs, scratch, flops, mebibytes, smem=(), far=(), far_outs=()):
+    for side in range(2):
+        edges[side].wait()
+        spread_edge(cells[side], side, patch)
+    for copy in copies:
+        copy.wait()
+    stores = []
+    for side in range(2):
+        rows = slice(128 - side * 128, 256 - side * 128)
+        added = dot(wide[side, rows, :], patch[side * 576 : (side + 1) * 576, :])
+        weave_into((outer[side] + added).astype(BF16), 0, 16, wide_rows.at[side])
+        for half in range(2):
+            columns = slice(half * X, (half + 1) * X)
+            image[side, :, :, columns] = wide_rows[side, half].reshape(G, 16, X).astype(BF16)
+        place = pl.ds(side * 48, 16)
+        stores.append(fetch(image.at[side], image_out.at[:, place], sems.at[5 + side]))
+    for copy in stores:
+        copy.wait()
+
+
+def call(body, name, args, outs, scratch, flops, mebibytes, smem=(), far=(), far_outs=(), aliases=()):
     moved = sum(a.size * a.dtype.itemsize for a in args) + sum(o.size * o.dtype.itemsize for o in outs)
     spaces = [
         pltpu.SMEM if i in smem else pl.ANY if i in far else pltpu.VMEM for i in range(len(args))
@@ -556,6 +588,7 @@
         in_specs=[pl.BlockSpec(memory_space=space) for space in spaces],
         out_specs=[pl.BlockSpec(memory_space=space) for space in out_spaces],
         scratch_shapes=scratch,
+        input_output_aliases=dict(aliases),
         compiler_params=pltpu.CompilerParams(vmem_limit_bytes=mebibytes * 1024 * 1024),
         cost_estimate=pl.CostEstimate(flops=flops, bytes_accessed=moved, transcendentals=0),
     )(*args)
@@ -598,7 +631,7 @@
         own_kernel,
         "own_cells",
         (lat, real, taps_g, taps_d),
-        [shape((256, 1152), BF16)]
+        [shape((2, 256, 576), BF16)]
         + [shape((256, CELLS), F32)] * 3
         + [shape((G, 128), F32), shape((1536, X), BF16), shape((C, 2048), BF16)],
         [
@@ -608,7 +641,7 @@
             pltpu.VMEM((2048, C), BF16),
             pltpu.VMEM((2048, C), BF16),
             pltpu.VMEM((C, 2048), BF16),
-            pltpu.VMEM((256, 1152), BF16),
+            pltpu.VMEM((2, 256, 576), BF16),
             pltpu.VMEM((256, CELLS), F32),
             pltpu.VMEM((256, CELLS), F32),
             pltpu.VMEM((256, CELLS), F32),
@@ -625,12 +658,12 @@
     last, stats, real_next = call(
         rim_kernel,
         "rim_cells",
-        (inside, next_, sums, wide, last),
+        (inside, next_, sums, bn_gain.reshape(1, G), bn_shift.reshape(1, G), wide, last),
         [shape((256, CELLS), F32), shape((NDEV, 128), F32), shape((1024, X), BF16)],
         [
             pltpu.VMEM((576, CELLS), BF16),
             pltpu.VMEM((512, X), F32),
-            pltpu.VMEM((256, 1152), BF16),
+            pltpu.VMEM((256, 576), BF16),
             pltpu.VMEM((256, CELLS), F32),
             pltpu.VMEM((NDEV, 128), F32),
             pltpu.SemaphoreType.DMA((5,)),
@@ -638,7 +671,7 @@
         256 * 1152 * CELLS,
         12,
         smem=(0,),
-        far=(3, 4),
+        far=(5, 6),
         far_outs=(0, 1, 2),
     )
     stats = lax.all_to_all(stats, AXES, 0, 0, tiled=True)
@@ -663,7 +696,7 @@
         [
             pltpu.VMEM((1024, X), BF16),
             pltpu.VMEM((C, 2048), BF16),
-            pltpu.VMEM((256, 1152), BF16),
+            pltpu.VMEM((256, 576), BF16),
             pltpu.VMEM((256, CELLS), F32),
             pltpu.VMEM((1024, 2 * C), F32),
             pltpu.SemaphoreType.DMA((6,)),
@@ -687,8 +720,6 @@
             middle,
             last,
             stats,
-            bn_gain.reshape(1, G),
-            bn_shift.reshape(1, G),
             weight,
             cot_fake.reshape(C * 2 * Y, X),
             real_terms,
@@ -710,89 +741,78 @@
         8 * 2048 * C * CELLS * 2,
         26,
         smem=(0,),
-        far=(1, 2, 3, 7, 9),
+        far=(1, 2, 3, 5, 7),
         far_outs=(1, 2),
     )
     parts = lax.all_to_all(terms.reshape(NDEV, 8, 128), AXES, 0, 0, tiled=True)
     grad_prev = to_next(high)
     grad_next = to_prev(low)
-    pull_wide, pull_first, pull_middle, pull_last = call(
+    pull_wide, pull_first, pull_last, image = call(
         pull_own_kernel,
         "pull_own",
         (low, high, taps_d),
         [
-            shape((256, 1152), BF16),
+            shape((2, 256, 576), BF16),
             shape((128, CELLS), F32),
-            shape((256, CELLS), BF16),
             shape((128, CELLS), F32),
+            shape((G, 64, 2 * X), BF16),
         ],
         [
             pltpu.VMEM((2, C, CELLS), BF16),
             pltpu.VMEM((2048, C), BF16),
-            pltpu.VMEM((256, 1152), BF16),
+            pltpu.VMEM((2, 256, 576), BF16),
             pltpu.VMEM((128, CELLS), F32),
-            pltpu.VMEM((256, CELLS), BF16),
             pltpu.VMEM((128, CELLS), F32),
             pltpu.VMEM((1152, CELLS), BF16),
+            pltpu.VMEM((2, G * 32, X), F32),
+            pltpu.VMEM((G, 32, 2 * X), BF16),
             pltpu.SemaphoreType.DMA((7,)),
         ],
         2 * 384 * 1152 * CELLS,
-        8,
+        16,
         far=(0, 1, 2),
         far_outs=(0, 1, 2, 3),
     )
     (sums,) = call(
         sum_kernel,
         "sum_terms",
-        (parts.reshape(NDEV * 8, 128), grad_prev, pull_middle),
+        (parts.reshape(NDEV * 8, 128), grad_prev, grad_next, pull_first),
         [shape((NDEV * 8, 128), BF16)],
         [],
         NDEV * 1024,
-        4,
-        far=(1, 2),
+        6,
+        far=(1, 2, 3),
     )
     whole = lax.all_to_all(sums.reshape(NDEV, 8, 128), AXES, 0, 0, tiled=True)
-    (pull_rows,) = call(
-        pull_prev_kernel,
-        "pull_prev",
-        (grad_prev, pull_wide, pull_first, pull_middle, sums),
-        [shape((2, G * 64, X), F32)],
+    (fake_grad,) = call(
+        pullback_kernel,
+        "pullback",
+        (grad_prev, grad_next, pull_wide, pull_first, pull_last, sums, image),
+        [shape((G, 64, 2 * X), BF16)],
         [
-            pltpu.VMEM((C, CELLS), BF16),
-            pltpu.VMEM((256, 1152), BF16),
-            pltpu.VMEM((128, CELLS), F32),
-            pltpu.VMEM((256, CELLS), BF16),
-            pltpu.VMEM((576, CELLS), BF16),
-            pltpu.SemaphoreType.DMA((4,)),
+            pltpu.VMEM((2, C, CELLS), BF16),
+            pltpu.VMEM((2, 256, 576), BF16),
+            pltpu.VMEM((2, 128, CELLS), F32),
+            pltpu.VMEM((1152, CELLS), BF16),
+            pltpu.VMEM((2, 2, G * 16, X), F32),
+            pltpu.VMEM((2, G, 16, 2 * X), BF16),
+            pltpu.SemaphoreType.DMA((7,)),
         ],
         2 * 128 * 1152 * CELLS,
-        8,
-        far=(0, 1, 2, 3, 4),
-    )
-    (fake_grad,) = call(
-        pull_next_kernel,
-        "pull_next",
-        (grad_next, pull_wide, pull_last, pull_rows),
-        [shape((G * 64, 2 * X), BF16)],
-        [
-            pltpu.VMEM((256, 1152), BF16),
-            pltpu.VMEM((128, CELLS), F32),
-            pltpu.VMEM((576, CELLS), BF16),
-            pltpu.VMEM((2, G * 64, X), F32),
-            pltpu.SemaphoreType.DMA((2,)),
-        ],
-        2 * 128 * 576 * CELLS,
-        8,
-        far=(1, 2),
+        16,
+        far=(0, 1, 2, 3, 4, 5, 6),
+        far_outs=(0,),
+        aliases=((6, 0),),
     )
     (weight_grad,) = call(
         unpack_kernel,
         "unpack",
         (whole.reshape(NDEV * 8, 128),),
-        [shape((2048, C), F32)],
-        [],
+        [shape((2, 1024, C), F32)],
+        [pltpu.VMEM((2, 1024, C), F32), pltpu.SemaphoreType.DMA((8,))],
         0,
-        4,
+        6,
+        far_outs=(0,),
     )
     return (
         d_fake.reshape(1, C, 2, Y, X),

time: 97.9 us -> 101 us (1.032)
  Pallas kernels: 38.6 us -> 36.4 us
  waiting for transfers between devices: 12.4 us -> 14.6 us
  starting transfers between devices: 45.1 us -> 46.8 us
  local copies, waits for them, and re-layouts: 0.04 us -> 1.33 us
    all_to_all x1, waiting for transfers between devices: 0.01 us -> 7.64 us  [local(): whole = lax.all_to_all(sums.reshape(NDEV, 8, 128), AXES, 0, 0, tiled=True)]
    all_to_all x1, waiting for transfers between devices: 3.81 us -> 0.01 us  [local(): parts = lax.all_to_all(terms.reshape(NDEV, 8, 128), AXES, 0, 0, tiled=True)]
    pallas_call x10 -> x9, Pallas kernels: 38.6 us -> 36.4 us  [call(): pl.pallas_call(body, name=name, out_shape=outs, in_specs=[pl.BlockSpec(me...]
    all_to_all x1, starting transfers between devices: 6.61 us -> 8.68 us  [local(): whole = lax.all_to_all(sums.reshape(NDEV, 8, 128), AXES, 0, 0, tiled=True)]
    unnamed x14 -> x18, local copies, waits for them, and re-layouts: 0.04 us -> 1.33 us
    ppermute x2, waiting for transfers between devices: 1.15 us -> 0.01 us  [to_next(): return lax.ppermute(edge, 'slab', [(i, i + 1) for i in range(ends)])]
  transfers between devices with their start and end apart: 7 -> 7, of which waited for: 4 -> 4; matrix products, arithmetic and copies ran while one was open for 0% -> 0% of each run, Pallas kernels for 29% -> 25%
where the time goes in v6:
time: 101 us; the launch traced here: 100 us
  starting transfers between devices  46.8 us (46%)
  Pallas kernels  36.4 us (36%)
  waiting for transfers between devices  14.6 us (14%)
  local copies, waits for them, and re-layouts  1.33 us (1%)
  between operations  1.02 us (1%)
    pallas_call x9, Pallas kernels, call(): pl.pallas_call(body, name=name, out_shape=outs, in_specs=[pl.BlockSpec(me...  36.4 us
    all_to_all x1, starting transfers between devices, local(): stats = lax.all_to_all(stats, AXES, 0, 0, tiled=True)  14.7 us
    ppermute x2, starting transfers between devices, to_next(): return lax.ppermute(edge, 'slab', [(i, i + 1) for i in range(ends)])  11.1 us
    all_to_all x1, starting transfers between devices, local(): parts = lax.all_to_all(terms.reshape(NDEV, 8, 128), AXES, 0, 0, tiled=True)  9.53 us
    all_to_all x1, starting transfers between devices, local(): whole = lax.all_to_all(sums.reshape(NDEV, 8, 128), AXES, 0, 0, tiled=True)  8.68 us
    all_to_all x1, waiting for transfers between devices, local(): whole = lax.all_to_all(sums.reshape(NDEV, 8, 128), AXES, 0, 0, tiled=True)  7.64 us
    ppermute x2, waiting for transfers between devices, to_prev(): return lax.ppermute(edge, 'slab', [(i + 1, i) for i in range(ends)])  6.69 us
    ppermute x2, starting transfers between devices, to_prev(): return lax.ppermute(edge, 'slab', [(i + 1, i) for i in range(ends)])  2.8 us
  transfers between devices with their start and end apart: 7, of which 4 were waited for; matrix products, arithmetic and copies ran while one was open for 0% of the time, Pallas kernels for 25%

profile of v6, /device:TPU:1, one launch (start us, length us, event | category | flops | bytes accessed | tf_op | source)
XLA Modules:
  0.0 100.2 jit_solution(15630407537942494894)
XLA Ops:
  0.6 1.1 %edges.1 = bf16[1536,128]{1,0:T(8,128)(2,1)S(1)} custom-call(bf16[64,2,8,128]{3,2,1,0:T(8,128)(2,1)} %bitcast.37, bf16[32,4,16,256]{3,2,1,0:T(8,128)(2,1)} %bitcast.27), custom_call_target="tpu_custom_call" | custom-call | bytes 1703936 | tf_op jit(solution)/shard_map/edges/pallas_call | solution.py:584
  1.7 1.3 %collective-permute-start.1 = (bf16[1536,128]{1,0:T(8,128)(2,1)S(1)}, bf16[1536,128]{1,0:T(8,128)(2,1)S(1)}, u32[]{:S(2)}, u32[]{:S(2)}) collective-permute-start(bf16[1536,128]{1,0:T(8,128)(2,1)S(1)} %edges.1), channel_id=1, source_target_pairs={{2,0},{4,2},{6,4},{8,6},{10,8},{12,10},{14,12},{16,14},{18,16},{20... | collective-permute-start | bytes 1179656 | tf_op jit(solution)/shard_map/ppermute | solution.py:604
  3.0 4.6 %own_cells.1 = (bf16[2,256,576]{2,1,0:T(8,128)(2,1)}, f32[256,1024]{1,0:T(8,128)}, f32[256,1024]{1,0:T(8,128)}, f32[256,1024]{1,0:T(8,128)}, f32[32,128]{1,0:T(8...) custom-call(bf16[64,2,8,128]{3,2,1,0:T(8,128)(2,1)} %bitcast.38, bf16[32,4,16,256]{3,2,1,0:T(8,128)(2,1)} %bitcast.28, ...), custom_call_target="tpu_custom_call" | custom-call | flops 1207959552 | bytes 6242304 | tf_op jit(solution)/shard_map/own_cells/pallas_call | solution.py:584
  7.6 6.3 %collective-permute-start = (bf16[1536,128]{1,0:T(8,128)(2,1)S(1)}, bf16[1536,128]{1,0:T(8,128)(2,1)S(1)}, u32[]{:S(2)}, u32[]{:S(2)}) collective-permute-start(bf16[1536,128]{1,0:T(8,128)(2,1)S(1)} %get-tuple-element.25), channel_id=1, source_target_pairs={{0,2},{2,4},{4,6},{6,8},{8,10},{10,12},{12,14},{14,16},{16,18},{18... | collective-permute-start | bytes 1179656 | tf_op jit(solution)/shard_map/ppermute | solution.py:599
  13.9 0.1 add_convert_fusion.inside_ref
  14.0 1.9 %collective-permute-done.1.next_ref = bf16[1536,128]{1,0:T(8,128)(2,1)S(1)} collective-permute-done((bf16[1536,128]{1,0:T(8,128)(2,1)S(1)}, bf16[1536,128]{1,0:T(8,128)(2,1)S(1)}, u32[]{:S(2)}, u32[]{:S(2)}) %collective-permute-start.1) | collective-permute-done | bytes 393248 | tf_op jit(solution)/shard_map/ppermute | solution.py:604
  15.9 0.7 copy-done.1
  16.6 0.0 copy-done.2
  16.6 3.4 %rim_cells.1 = (f32[256,1024]{1,0:T(8,128)}, f32[128,128]{1,0:T(8,128)}, bf16[1024,128]{1,0:T(8,128)(2,1)}) custom-call(s32[2]{0:T(128)S(1)} %add_convert_fusion.inside_ref, bf16[1536,128]{1,0:T(8,128)(2,1)S(1)} %collective-permute-done.1.next_ref, f32[32,128]{1,0:T(8,128)S(1)} %get-tuple-element.26.sums_ref, f32[1,32]{1,0:T(1,128)S(1)} %bitcast.31, ...), custom_call_target="tpu_custom_call" | custom-call | flops 301989888 | bytes 3424520 | tf_op jit(solution)/shard_map/rim_cells/pallas_call | solution.py:584
  20.0 14.7 %all-to-all-start = ((f32[128,1,128]{2,1,0:T(1,128)}), f32[128,1,128]{2,1,0:T(1,128)S(1)}, u32[]{:S(2)}, u32[]{:S(2)}) async-start(f32[128,1,128]{2,1,0:T(1,128)} %bitcast.39), calls=%async_computation | async-start | bytes 131072 | tf_op jit(solution)/shard_map/all_to_all | solution.py:677
  34.7 9.2 %real_branch.1 = (bf16[1024,128]{1,0:T(8,128)(2,1)}, f32[1024,128]{1,0:T(8,128)}, f32[256,1024]{1,0:T(8,128)}) custom-call(bf16[2048,256]{1,0:T(8,128)(2,1)S(1)} %bitcast.29, bf16[1536,128]{1,0:T(8,128)(2,1)S(1)} %collective-permute-done.prev_ref, bf16[1024,128]{1,0:T(8,128)(2,1)} %get-tuple-element.29.next_in, ...), custom_call_target="tpu_custom_call" | custom-call | flops 2147483648 | bytes 5701632 | tf_op jit(solution)/shard_map/real_branch/pallas_call | solution.py:584
  43.9 0.3 all-to-all-done
  44.2 8.3 %fake_branch.1 = (bf16[1024,128]{1,0:T(8,128)(2,1)}, bf16[64,1024]{1,0:T(8,128)(2,1)}, bf16[64,1024]{1,0:T(8,128)(2,1)}, f32[1024,128]{1,0:T(8,128)}) custom-call(s32[2]{0:T(128)S(1)} %add_convert_fusion.inside_ref, f32[256,1024]{1,0:T(8,128)} %get-tuple-element.32.first_in, f32[256,1024]{1,0:T(8,128)} %get-tuple-element.33.middle_in, ...), custom_call_target="tpu_custom_call" | custom-call | flops 2147483648 | bytes 5308424 | tf_op jit(solution)/shard_map/fake_branch/pallas_call | solution.py:584
  52.5 9.5 %all-to-all-start.1 = ((f32[128,8,128]{2,1,0:T(8,128)}), f32[128,8,128]{2,1,0:T(8,128)S(1)}, u32[]{:S(2)}, u32[]{:S(2)}) async-start(f32[128,8,128]{2,1,0:T(8,128)} %bitcast.17), calls=%async_computation.1 | async-start | bytes 1048576 | tf_op jit(solution)/shard_map/all_to_all | solution.py:747
  62.1 4.8 %collective-permute-start.2 = (bf16[64,1024]{1,0:T(8,128)(2,1)S(1)}, bf16[64,1024]{1,0:T(8,128)(2,1)S(1)}, u32[]{:S(2)}, u32[]{:S(2)}) collective-permute-start(bf16[64,1024]{1,0:T(8,128)(2,1)S(1)} %copy-done.8), channel_id=1, source_target_pairs={{0,2},{2,4},{4,6},{6,8},{8,10},{10,12},{12,14},{14,16},{16,18},{18... | collective-permute-start | bytes 393224 | tf_op jit(solution)/shard_map/ppermute | solution.py:599
  66.9 1.5 %collective-permute-start.3 = (bf16[64,1024]{1,0:T(8,128)(2,1)S(1)}, bf16[64,1024]{1,0:T(8,128)(2,1)S(1)}, u32[]{:S(2)}, u32[]{:S(2)}) collective-permute-start(bf16[64,1024]{1,0:T(8,128)(2,1)S(1)} %copy-done.7), channel_id=1, source_target_pairs={{2,0},{4,2},{6,4},{8,6},{10,8},{12,10},{14,12},{16,14},{18,16},{20... | collective-permute-start | bytes 393224 | tf_op jit(solution)/shard_map/ppermute | solution.py:604
  68.4 4.5 %pull_own.1 = (bf16[2,256,576]{2,1,0:T(8,128)(2,1)}, f32[128,1024]{1,0:T(8,128)}, f32[128,1024]{1,0:T(8,128)}, bf16[32,64,256]{2,1,0:T(8,128)(2,1)}) custom-call(bf16[64,1024]{1,0:T(8,128)(2,1)} %get-tuple-element.40.low_in, bf16[64,1024]{1,0:T(8,128)(2,1)} %get-tuple-element.39.high_in, bf16[2048,64]{1,0:T(8,128)(2,1)} %bitcast.42), custom_call_target="tpu_custom_call" | custom-call | flops 905969664 | bytes 3211264 | tf_op jit(solution)/shard_map/pull_own/pallas_call | solution.py:584
  72.9 4.8 %collective-permute-done.3.next_ref.next_in = bf16[64,1024]{1,0:T(8,128)(2,1)S(1)} collective-permute-done((bf16[64,1024]{1,0:T(8,128)(2,1)S(1)}, bf16[64,1024]{1,0:T(8,128)(2,1)S(1)}, u32[]{:S(2)}, u32[]{:S(2)}) %collective-permute-start.3) | collective-permute-done | bytes 131104 | tf_op jit(solution)/shard_map/ppermute | solution.py:604
  77.7 0.6 copy-done.6
  78.3 0.8 sum_terms.1.sums_ref
  79.2 8.7 %all-to-all-start.2 = ((bf16[128,8,128]{2,1,0:T(8,128)(2,1)}), bf16[128,8,128]{2,1,0:T(8,128)(2,1)S(1)}, u32[]{:S(2)}, u32[]{:S(2)}) async-start(bf16[128,8,128]{2,1,0:T(8,128)(2,1)} %bitcast.20), calls=%async_computation.2 | async-start | bytes 524288 | tf_op jit(solution)/shard_map/all_to_all | solution.py:786
  87.9 3.4 %pullback.1 = bf16[32,64,256]{2,1,0:T(8,128)(2,1)} custom-call(bf16[64,1024]{1,0:T(8,128)(2,1)} %copy-done.5, bf16[64,1024]{1,0:T(8,128)(2,1)} %copy-done.6, bf16[2,256,576]{2,1,0:T(8,128)(2,1)} %get-tuple-element.41.wide_in, f32[128,1024]{1,0:T(8,128)} %get-tuple-element.42.first_ref.first_in, ...), custom_call_target="tpu_custom_call", output_to_operand_aliasing={{}: (6, {})} | custom-call | flops 301989888 | bytes 4259840 | tf_op jit(solution)/shard_map/pullback/pallas_call | solution.py:584
  91.3 7.6 %all-to-all-done.2 = bf16[128,8,128]{2,1,0:T(8,128)(2,1)S(1)} async-done(((bf16[128,8,128]{2,1,0:T(8,128)(2,1)}), bf16[128,8,128]{2,1,0:T(8,128)(2,1)S(1)}, u32[]{:S(2)}, u32[]{:S(2)}) %all-to-all-start.2) | async-done | bytes 262176 | tf_op jit(solution)/shard_map/all_to_all | solution.py:786
  98.9 1.1 %unpack.1 = f32[2,1024,64]{2,1,0:T(8,128)} custom-call(bf16[1024,128]{1,0:T(8,128)(2,1)S(1)} %bitcast.26), custom_call_target="tpu_custom_call" | custom-call | bytes 786432 | tf_op jit(solution)/shard_map/unpack/pallas_call | solution.py:584
  (18 shorter events, 0.0 us)
Async XLA Ops:
  1.7 14.2 %collective-permute-start.1 = (bf16[1536,128]{1,0:T(8,128)(2,1)S(1)}, bf16[1536,128]{1,0:T(8,128)(2,1)S(1)}, u32[]{:S(2)}, u32[]{:S(2)}) collective-permute-start(bf16[1536,128]{1,0:T(8,128)(2,1)S(1)} %edges.1), channel_id=1, source_target_pairs={{2,0},{4,2},{6,4},{8,6},{10,8},{12,10},{14,12},{16,14},{18,16},{20... | collective-permute-start | bytes 1179656 | tf_op jit(solution)/shard_map/ppermute | solution.py:604
  7.6 27.0 %collective-permute-start = (bf16[1536,128]{1,0:T(8,128)(2,1)S(1)}, bf16[1536,128]{1,0:T(8,128)(2,1)S(1)}, u32[]{:S(2)}, u32[]{:S(2)}) collective-permute-start(bf16[1536,128]{1,0:T(8,128)(2,1)S(1)} %get-tuple-element.25), channel_id=1, source_target_pairs={{0,2},{2,4},{4,6},{6,8},{8,10},{10,12},{12,14},{14,16},{16,18},{18... | collective-permute-start | bytes 1179656 | tf_op jit(solution)/shard_map/ppermute | solution.py:599
  15.9 0.7 copy-start.1
  15.9 0.7 copy-start.2
  16.6 18.1 %copy-start = (bf16[1,32,4,16,256]{4,3,2,1,0:T(8,128)(2,1)S(1)}, bf16[1,32,4,16,256]{4,3,2,1,0:T(8,128)(2,1)}, u32[]{:S(2)}) copy-start(bf16[1,32,4,16,256]{4,3,2,1,0:T(8,128)(2,1)} %param.12) | copy-start | bytes 3145732
  16.6 18.1 %copy-start.3 = (bf16[1,64,2,8,128]{4,3,2,1,0:T(8,128)(2,1)S(1)}, bf16[1,64,2,8,128]{4,3,2,1,0:T(8,128)(2,1)}, u32[]{:S(2)}) copy-start(bf16[1,64,2,8,128]{4,3,2,1,0:T(8,128)(2,1)} %param.15) | copy-start | bytes 786436
  20.0 24.2 %all-to-all-start = ((f32[128,1,128]{2,1,0:T(1,128)}), f32[128,1,128]{2,1,0:T(1,128)S(1)}, u32[]{:S(2)}, u32[]{:S(2)}) async-start(f32[128,1,128]{2,1,0:T(1,128)} %bitcast.39), calls=%async_computation | async-start | bytes 131072 | tf_op jit(solution)/shard_map/all_to_all | solution.py:677
  34.7 9.5 %copy-start.4 = (bf16[1,64,2,8,128]{4,3,2,1,0:T(8,128)(2,1)S(1)}, bf16[1,64,2,8,128]{4,3,2,1,0:T(8,128)(2,1)}, u32[]{:S(2)}) copy-start(bf16[1,64,2,8,128]{4,3,2,1,0:T(8,128)(2,1)} %param.14) | copy-start | bytes 786436
  52.5 9.6 %copy-start.8 = (bf16[64,1024]{1,0:T(8,128)(2,1)S(1)}, bf16[64,1024]{1,0:T(8,128)(2,1)}, u32[]{:S(2)}) copy-start(bf16[64,1024]{1,0:T(8,128)(2,1)} %get-tuple-element.39.high_in) | copy-start | bytes 393220
  52.5 14.4 %copy-start.7 = (bf16[64,1024]{1,0:T(8,128)(2,1)S(1)}, bf16[64,1024]{1,0:T(8,128)(2,1)}, u32[]{:S(2)}) copy-start(bf16[64,1024]{1,0:T(8,128)(2,1)} %get-tuple-element.40.low_in) | copy-start | bytes 393220
  52.5 25.2 %all-to-all-start.1 = ((f32[128,8,128]{2,1,0:T(8,128)}), f32[128,8,128]{2,1,0:T(8,128)S(1)}, u32[]{:S(2)}, u32[]{:S(2)}) async-start(f32[128,8,128]{2,1,0:T(8,128)} %bitcast.17), calls=%async_computation.1 | async-start | bytes 1048576 | tf_op jit(solution)/shard_map/all_to_all | solution.py:747
  62.1 10.8 %collective-permute-start.2 = (bf16[64,1024]{1,0:T(8,128)(2,1)S(1)}, bf16[64,1024]{1,0:T(8,128)(2,1)S(1)}, u32[]{:S(2)}, u32[]{:S(2)}) collective-permute-start(bf16[64,1024]{1,0:T(8,128)(2,1)S(1)} %copy-done.8), channel_id=1, source_target_pairs={{0,2},{2,4},{4,6},{6,8},{8,10},{10,12},{12,14},{14,16},{16,18},{18... | collective-permute-start | bytes 393224 | tf_op jit(solution)/shard_map/ppermute | solution.py:599
  66.9 10.8 %collective-permute-start.3 = (bf16[64,1024]{1,0:T(8,128)(2,1)S(1)}, bf16[64,1024]{1,0:T(8,128)(2,1)S(1)}, u32[]{:S(2)}, u32[]{:S(2)}) collective-permute-start(bf16[64,1024]{1,0:T(8,128)(2,1)S(1)} %copy-done.7), channel_id=1, source_target_pairs={{2,0},{4,2},{6,4},{8,6},{10,8},{12,10},{14,12},{16,14},{18,16},{20... | collective-permute-start | bytes 393224 | tf_op jit(solution)/shard_map/ppermute | solution.py:604
  72.9 4.8 %copy-start.5 = (bf16[64,1024]{1,0:T(8,128)(2,1)}, bf16[64,1024]{1,0:T(8,128)(2,1)S(1)}, u32[]{:S(2)}) copy-start(bf16[64,1024]{1,0:T(8,128)(2,1)S(1)} %collective-permute-done.2.prev_ref.prev_in) | copy-start | bytes 393220
  77.7 0.6 copy-start.6
  79.2 19.8 %all-to-all-start.2 = ((bf16[128,8,128]{2,1,0:T(8,128)(2,1)}), bf16[128,8,128]{2,1,0:T(8,128)(2,1)S(1)}, u32[]{:S(2)}, u32[]{:S(2)}) async-start(bf16[128,8,128]{2,1,0:T(8,128)(2,1)} %bitcast.20), calls=%async_computation.2 | async-start | bytes 524288 | tf_op jit(solution)/shard_map/all_to_all | solution.py:786

commit v7 on v6

--- a/solution.py
+++ b/solution.py
@@ -1,3 +1,5 @@
+import functools
+
 import jax
 import jax.numpy as jnp
 from jax import lax
@@ -180,8 +182,8 @@
     inside_ref,
     next_ref,
     sums_ref,
-    gain_ref,
-    shift_ref,
+    gain_in,
+    shift_in,
     wide_in,
     last_in,
     last_out,
@@ -192,10 +194,13 @@
     wide,
     last,
     stats,
+    gain,
+    shift,
     sems,
 ):
     wide_copy = fetch(wide_in.at[1], wide, sems.at[0])
     last_copy = fetch(last_in, last, sems.at[1])
+    affine_copies = [fetch(gain_in, gain, sems.at[5]), fetch(shift_in, shift, sems.at[6])]
     copies = [fetch(next_ref.at[512:1536], real_next_out, sems.at[2])]
     wide_lat[...] = next_ref[0:512, :].astype(F32)
     lane = lanes((C, X))
@@ -222,7 +227,9 @@
         own = squares if isinstance(weight, float) else weight * squares
         spread += own + weight * (4.0 * CELLS) * (one - mean) * (one - mean)
     row = as_row(mean, 0) + as_row(spread, G)
-    row += as_row(as_column(gain_ref[...], 0), 2 * G) + as_row(as_column(shift_ref[...], 0), 3 * G)
+    for copy in affine_copies:
+        copy.wait()
+    row += as_row(as_column(gain[...], 0), 2 * G) + as_row(as_column(shift[...], 0), 3 * G)
     stats[...] = jnp.broadcast_to(row, (NDEV, 128))
     copies.append(fetch(stats, stats_out, sems.at[4]))
     for copy in copies:
@@ -356,7 +363,7 @@
     inside_ref,
     first_in,
     middle_in,
-    last_in,
+    last_ref,
     stats_ref,
     weight_in,
     cot_ref,
@@ -365,7 +372,8 @@
     low_out,
     high_out,
     terms_ref,
-    before,
+    first_ref,
+    middle_ref,
     real_terms,
     weight_ref,
     sems,
@@ -374,12 +382,10 @@
     wide_out,
     grad,
 ):
-    def fetch_before(depth):
-        ref = (first_in, middle_in, last_in)[depth // 2]
-        half = pl.ds(depth % 2 * 128, 128)
-        return fetch(ref.at[half], before.at[depth], sems.at[depth])
-
-    befores = [fetch_before(depth) for depth in range(3)]
+    middle_copy = fetch(middle_in, middle_ref, sems.at[4])
+    first_copy = fetch(first_in, first_ref, sems.at[0])
+    weight_copy = fetch(weight_in, weight_ref, sems.at[5])
+    real_copy = fetch(real_terms_in, real_terms, sems.at[1])
     stats = stats_ref[...]
     slab = lax.broadcasted_iota(jnp.int32, (NDEV, 128), 0) // 2 % 32
     depths = jnp.where(slab == 0, 5.0, jnp.where(slab == 31, 3.0, 4.0))
@@ -393,21 +399,19 @@
     shift = as_column(stats[0:1, :], 3 * G)
     lane = lanes((G, X))
     edge = jnp.zeros((128, X), BF16)
-    for depth in range(6):
-        befores[depth].wait()
-        if depth < 3:
-            befores.append(fetch_before(depth + 3))
-        elif depth == 3:
-            weight_copy = fetch(weight_in, weight_ref, sems.at[6])
-        elif depth == 4:
-            real_copy = fetch(real_terms_in, real_terms, sems.at[7])
+    for depth in (4, 5, 2, 3, 0, 1):
+        if depth == 2:
+            middle_copy.wait()
+        elif depth == 0:
+            first_copy.wait()
+        before_ref = (first_ref, middle_ref, last_ref)[depth // 2]
         patch[depth * 512 : depth * 512 + 128, 0:X] = edge
         patch[depth * 512 + 384 : depth * 512 + 512, CELLS - X : CELLS] = edge
         for py in range(2):
             for px in range(2):
-                block = (py * 2 + px) * G
+                block = (depth % 2 * 4 + py * 2 + px) * G
                 for y in range(Y):
-                    cells = before[depth, block : block + G, y * X : (y + 1) * X]
+                    cells = before_ref[block : block + G, y * X : (y + 1) * X]
                     fake = jnp.maximum((cells - center) * factor + shift, 0.0)
                     if depth == 0:
                         fake = jnp.where(inside_ref[0] > 0, fake, 0.0)
@@ -427,8 +431,8 @@
     pre = convolve(weight_ref, patch)
     finish(pre, cot_ref, out_ref, wide_cot, wide_out, grad)
     edge_copies = [
-        fetch(grad.at[2 * C : 3 * C], low_out, sems.at[8]),
-        fetch(grad.at[C : 2 * C], high_out, sems.at[9]),
+        fetch(grad.at[2 * C : 3 * C], low_out, sems.at[2]),
+        fetch(grad.at[C : 2 * C], high_out, sems.at[3]),
     ]
     planes = [patch[depth * 512 : (depth + 1) * 512, :] for depth in range(6)]
     real_copy.wait()
@@ -439,8 +443,8 @@
         copy.wait()
 
 
-def sum_kernel(parts_ref, prev_ref, next_ref, first_ref, sums_ref):
-    del prev_ref, next_ref, first_ref
+def sum_kernel(parts_ref, prev_ref, first_ref, sums_ref):
+    del prev_ref, first_ref
     total = jnp.sum(parts_ref[...].reshape(NDEV, 8, 128), axis=0, keepdims=True)
     sums_ref[...] = jnp.broadcast_to(total, (NDEV, 8, 128)).reshape(NDEV * 8, 128).astype(BF16)
 
@@ -528,47 +532,24 @@
         copy.wait()
 
 
-def pullback_kernel(
-    prev_in,
-    next_in,
-    wide_in,
-    first_in,
-    last_in,
-    sums_ref,
-    image_in,
-    image_out,
-    cells,
-    wide,
-    outer,
-    patch,
-    wide_rows,
-    image,
-    sems,
+def pull_outer_kernel(
+    side, edge_in, wide_in, share_in, after_ref, image_in, image_out, cells, wide, share, patch, wide_rows, image, sems
 ):
-    del sums_ref, image_in
-    edges = [fetch(ref, cells.at[i], sems.at[i]) for i, ref in enumerate((prev_in, next_in))]
+    del after_ref, image_in
+    edge_copy = fetch(edge_in, cells, sems.at[0])
     copies = [
-        fetch(wide_in, wide, sems.at[2]),
-        fetch(first_in, outer.at[0], sems.at[3]),
-        fetch(last_in, outer.at[1], sems.at[4]),
+        fetch(wide_in.at[side], wide, sems.at[1]),
+        fetch(share_in, share, sems.at[2]),
     ]
-    for side in range(2):
-        edges[side].wait()
-        spread_edge(cells[side], side, patch)
+    edge_copy.wait()
+    spread_edge(cells, 0, patch)
     for copy in copies:
         copy.wait()
-    stores = []
-    for side in range(2):
-        rows = slice(128 - side * 128, 256 - side * 128)
-        added = dot(wide[side, rows, :], patch[side * 576 : (side + 1) * 576, :])
-        weave_into((outer[side] + added).astype(BF16), 0, 16, wide_rows.at[side])
-        for half in range(2):
-            columns = slice(half * X, (half + 1) * X)
-            image[side, :, :, columns] = wide_rows[side, half].reshape(G, 16, X).astype(BF16)
-        place = pl.ds(side * 48, 16)
-        stores.append(fetch(image.at[side], image_out.at[:, place], sems.at[5 + side]))
-    for copy in stores:
-        copy.wait()
+    rows = slice(128 - side * 128, 256 - side * 128)
+    weave_into((share[...] + dot(wide[rows, :], patch[...])).astype(BF16), 0, 16, wide_rows)
+    for half in range(2):
+        image[:, :, half * X : (half + 1) * X] = wide_rows[half].reshape(G, 16, X).astype(BF16)
+    fetch(image, image_out.at[:, pl.ds(side * 48, 16)], sems.at[3]).wait()
 
 
 def call(body, name, args, outs, scratch, flops, mebibytes, smem=(), far=(), far_outs=(), aliases=()):
@@ -666,12 +647,14 @@
             pltpu.VMEM((256, 576), BF16),
             pltpu.VMEM((256, CELLS), F32),
             pltpu.VMEM((NDEV, 128), F32),
-            pltpu.SemaphoreType.DMA((5,)),
+            pltpu.VMEM((1, G), F32),
+            pltpu.VMEM((1, G), F32),
+            pltpu.SemaphoreType.DMA((7,)),
         ],
         256 * 1152 * CELLS,
         12,
         smem=(0,),
-        far=(5, 6),
+        far=(3, 4, 5, 6),
         far_outs=(0, 1, 2),
     )
     stats = lax.all_to_all(stats, AXES, 0, 0, tiled=True)
@@ -731,17 +714,18 @@
             shape((NDEV * 8, 128), F32),
         ],
         [
-            pltpu.VMEM((6, 128, CELLS), F32),
+            pltpu.VMEM((256, CELLS), F32),
+            pltpu.VMEM((256, CELLS), F32),
             pltpu.VMEM((NDEV * 8, 128), F32),
             pltpu.VMEM((C, 2048), BF16),
-            pltpu.SemaphoreType.DMA((10,)),
+            pltpu.SemaphoreType.DMA((6,)),
             pltpu.VMEM((6 * 512, CELLS), BF16),
         ]
         + working,
         8 * 2048 * C * CELLS * 2,
         26,
         smem=(0,),
-        far=(1, 2, 3, 5, 7),
+        far=(1, 2, 5, 7),
         far_outs=(1, 2),
     )
     parts = lax.all_to_all(terms.reshape(NDEV, 8, 128), AXES, 0, 0, tiled=True)
@@ -776,34 +760,35 @@
     (sums,) = call(
         sum_kernel,
         "sum_terms",
-        (parts.reshape(NDEV * 8, 128), grad_prev, grad_next, pull_first),
+        (parts.reshape(NDEV * 8, 128), grad_prev, pull_first),
         [shape((NDEV * 8, 128), BF16)],
         [],
         NDEV * 1024,
         6,
-        far=(1, 2, 3),
+        far=(1, 2),
     )
     whole = lax.all_to_all(sums.reshape(NDEV, 8, 128), AXES, 0, 0, tiled=True)
-    (fake_grad,) = call(
-        pullback_kernel,
-        "pullback",
-        (grad_prev, grad_next, pull_wide, pull_first, pull_last, sums, image),
-        [shape((G, 64, 2 * X), BF16)],
-        [
-            pltpu.VMEM((2, C, CELLS), BF16),
-            pltpu.VMEM((2, 256, 576), BF16),
-            pltpu.VMEM((2, 128, CELLS), F32),
-            pltpu.VMEM((1152, CELLS), BF16),
-            pltpu.VMEM((2, 2, G * 16, X), F32),
-            pltpu.VMEM((2, G, 16, 2 * X), BF16),
-            pltpu.SemaphoreType.DMA((7,)),
-        ],
-        2 * 128 * 1152 * CELLS,
-        16,
-        far=(0, 1, 2, 3, 4, 5, 6),
-        far_outs=(0,),
-        aliases=((6, 0),),
-    )
+    for side, edge, share in ((0, grad_prev, pull_first), (1, grad_next, pull_last)):
+        (image,) = call(
+            functools.partial(pull_outer_kernel, side),
+            "pull_prev" if side == 0 else "pull_next",
+            (edge, pull_wide, share, sums, image),
+            [shape((G, 64, 2 * X), BF16)],
+            [
+                pltpu.VMEM((C, CELLS), BF16),
+                pltpu.VMEM((256, 576), BF16),
+                pltpu.VMEM((128, CELLS), F32),
+                pltpu.VMEM((576, CELLS), BF16),
+                pltpu.VMEM((2, G * 16, X), F32),
+                pltpu.VMEM((G, 16, 2 * X), BF16),
+                pltpu.SemaphoreType.DMA((4,)),
+            ],
+            128 * 1152 * CELLS,
+            12,
+            far=(0, 1, 2, 3, 4) if side == 0 else (1, 2, 3, 4),
+            far_outs=(0,),
+            aliases=((4, 0),),
+        )
     (weight_grad,) = call(
         unpack_kernel,
         "unpack",
@@ -817,7 +802,7 @@
     return (
         d_fake.reshape(1, C, 2, Y, X),
         d_real.reshape(1, C, 2, Y, X),
-        fake_grad.reshape(1, G, 4, 2 * Y, 2 * X),
+        image.reshape(1, G, 4, 2 * Y, 2 * X),
         weight_grad.reshape(4, 4, 4, G, C),
     )
 

time: 101 us -> 96.4 us (0.954)
  waiting for transfers between devices: 14.6 us -> 12.3 us
  starting transfers between devices: 46.8 us -> 44.7 us
  local copies, waits for them, and re-layouts: 1.33 us -> 0.03 us
    all_to_all x1, waiting for transfers between devices: 7.64 us -> 0.01 us  [local(): whole = lax.all_to_all(sums.reshape(NDEV, 8, 128), AXES, 0, 0, tiled=True)]
    all_to_all x1, waiting for transfers between devices: 0.01 us -> 4.12 us  [local(): parts = lax.all_to_all(terms.reshape(NDEV, 8, 128), AXES, 0, 0, tiled=True)]
    all_to_all x1, starting transfers between devices: 8.68 us -> 6.61 us  [local(): whole = lax.all_to_all(sums.reshape(NDEV, 8, 128), AXES, 0, 0, tiled=True)]
    unnamed x18 -> x14, local copies, waits for them, and re-layouts: 1.33 us -> 0.03 us
    ppermute x2, waiting for transfers between devices: 6.69 us -> 7.85 us  [to_prev(): return lax.ppermute(edge, 'slab', [(i + 1, i) for i in range(ends)])]
    pallas_call x9 -> x10, Pallas kernels: 36.4 us -> 37.4 us  [call(): pl.pallas_call(body, name=name, out_shape=outs, in_specs=[pl.BlockSpec(me...]
  transfers between devices with their start and end apart: 7 -> 7, of which waited for: 4 -> 4; matrix products, arithmetic and copies ran while one was open for 0% -> 0% of each run, Pallas kernels for 25% -> 28%
where the time goes in v7:
time: 96.4 us; the launch traced here: 95.5 us
  starting transfers between devices  44.7 us (46%)
  Pallas kernels  37.4 us (39%)
  waiting for transfers between devices  12.3 us (13%)
  between operations  1.02 us (1%)
    pallas_call x10, Pallas kernels, call(): pl.pallas_call(body, name=name, out_shape=outs, in_specs=[pl.BlockSpec(me...  37.4 us
    all_to_all x1, starting transfers between devices, local(): stats = lax.all_to_all(stats, AXES, 0, 0, tiled=True)  14.7 us
    ppermute x2, starting transfers between devices, to_next(): return lax.ppermute(edge, 'slab', [(i, i + 1) for i in range(ends)])  11.3 us
    all_to_all x1, starting transfers between devices, local(): parts = lax.all_to_all(terms.reshape(NDEV, 8, 128), AXES, 0, 0, tiled=True)  9.53 us
    ppermute x2, waiting for transfers between devices, to_prev(): return lax.ppermute(edge, 'slab', [(i + 1, i) for i in range(ends)])  7.85 us
    all_to_all x1, starting transfers between devices, local(): whole = lax.all_to_all(sums.reshape(NDEV, 8, 128), AXES, 0, 0, tiled=True)  6.61 us
    all_to_all x1, waiting for transfers between devices, local(): parts = lax.all_to_all(terms.reshape(NDEV, 8, 128), AXES, 0, 0, tiled=True)  4.12 us
    ppermute x2, starting transfers between devices, to_prev(): return lax.ppermute(edge, 'slab', [(i + 1, i) for i in range(ends)])  2.58 us
  transfers between devices with their start and end apart: 7, of which 4 were waited for; matrix products, arithmetic and copies ran while one was open for 0% of the time, Pallas kernels for 28%

profile of v7, /device:TPU:1, one launch (start us, length us, event | category | flops | bytes accessed | tf_op | source)
XLA Modules:
  0.0 95.5 jit_solution(5356929172463539746)
XLA Ops:
  0.6 1.1 %edges.1 = bf16[1536,128]{1,0:T(8,128)(2,1)S(1)} custom-call(bf16[64,2,8,128]{3,2,1,0:T(8,128)(2,1)} %bitcast.35, bf16[32,4,16,256]{3,2,1,0:T(8,128)(2,1)} %bitcast.27), custom_call_target="tpu_custom_call" | custom-call | bytes 1703936 | tf_op jit(solution)/shard_map/edges/pallas_call | solution.py:565
  1.7 1.3 %collective-permute-start.1 = (bf16[1536,128]{1,0:T(8,128)(2,1)S(1)}, bf16[1536,128]{1,0:T(8,128)(2,1)S(1)}, u32[]{:S(2)}, u32[]{:S(2)}) collective-permute-start(bf16[1536,128]{1,0:T(8,128)(2,1)S(1)} %edges.1), channel_id=1, source_target_pairs={{2,0},{4,2},{6,4},{8,6},{10,8},{12,10},{14,12},{16,14},{18,16},{20... | collective-permute-start | bytes 1179656 | tf_op jit(solution)/shard_map/ppermute | solution.py:585
  3.0 4.6 %own_cells.1 = (bf16[2,256,576]{2,1,0:T(8,128)(2,1)}, f32[256,1024]{1,0:T(8,128)}, f32[256,1024]{1,0:T(8,128)}, f32[256,1024]{1,0:T(8,128)}, f32[32,128]{1,0:T(8...) custom-call(bf16[64,2,8,128]{3,2,1,0:T(8,128)(2,1)} %bitcast.36, bf16[32,4,16,256]{3,2,1,0:T(8,128)(2,1)} %bitcast.28, ...), custom_call_target="tpu_custom_call" | custom-call | flops 1207959552 | bytes 6242304 | tf_op jit(solution)/shard_map/own_cells/pallas_call | solution.py:565
  7.6 6.3 %collective-permute-start = (bf16[1536,128]{1,0:T(8,128)(2,1)S(1)}, bf16[1536,128]{1,0:T(8,128)(2,1)S(1)}, u32[]{:S(2)}, u32[]{:S(2)}) collective-permute-start(bf16[1536,128]{1,0:T(8,128)(2,1)S(1)} %get-tuple-element.25), channel_id=1, source_target_pairs={{0,2},{2,4},{4,6},{6,8},{8,10},{10,12},{12,14},{14,16},{16,18},{18... | collective-permute-start | bytes 1179656 | tf_op jit(solution)/shard_map/ppermute | solution.py:580
  13.9 0.1 add_convert_fusion.inside_ref
  14.0 1.9 %collective-permute-done.1.next_ref = bf16[1536,128]{1,0:T(8,128)(2,1)S(1)} collective-permute-done((bf16[1536,128]{1,0:T(8,128)(2,1)S(1)}, bf16[1536,128]{1,0:T(8,128)(2,1)S(1)}, u32[]{:S(2)}, u32[]{:S(2)}) %collective-permute-start.1) | collective-permute-done | bytes 393248 | tf_op jit(solution)/shard_map/ppermute | solution.py:585
  15.9 3.5 %rim_cells.1 = (f32[256,1024]{1,0:T(8,128)}, f32[128,128]{1,0:T(8,128)}, bf16[1024,128]{1,0:T(8,128)(2,1)}) custom-call(s32[2]{0:T(128)S(1)} %add_convert_fusion.inside_ref, bf16[1536,128]{1,0:T(8,128)(2,1)S(1)} %collective-permute-done.1.next_ref, f32[32,128]{1,0:T(8,128)S(1)} %get-tuple-element.26.sums_ref, f32[1,32]{1,0:T(1,128)} %bitcast.38, ...), custom_call_target="tpu_custom_call" | custom-call | flops 301989888 | bytes 3424520 | tf_op jit(solution)/shard_map/rim_cells/pallas_call | solution.py:565
  19.4 14.7 %all-to-all-start = ((f32[128,1,128]{2,1,0:T(1,128)}), f32[128,1,128]{2,1,0:T(1,128)S(1)}, u32[]{:S(2)}, u32[]{:S(2)}) async-start(f32[128,1,128]{2,1,0:T(1,128)} %bitcast.37), calls=%async_computation | async-start | bytes 131072 | tf_op jit(solution)/shard_map/all_to_all | solution.py:660
  34.1 0.0 copy-start.3
  34.1 9.2 %real_branch.1 = (bf16[1024,128]{1,0:T(8,128)(2,1)}, f32[1024,128]{1,0:T(8,128)}, f32[256,1024]{1,0:T(8,128)}) custom-call(bf16[2048,256]{1,0:T(8,128)(2,1)S(1)} %bitcast.29, bf16[1536,128]{1,0:T(8,128)(2,1)S(1)} %collective-permute-done.prev_ref, bf16[1024,128]{1,0:T(8,128)(2,1)} %get-tuple-element.29.next_in, ...), custom_call_target="tpu_custom_call" | custom-call | flops 2147483648 | bytes 5701632 | tf_op jit(solution)/shard_map/real_branch/pallas_call | solution.py:565
  43.4 0.3 all-to-all-done
  43.6 7.4 %fake_branch.1 = (bf16[1024,128]{1,0:T(8,128)(2,1)}, bf16[64,1024]{1,0:T(8,128)(2,1)}, bf16[64,1024]{1,0:T(8,128)(2,1)}, f32[1024,128]{1,0:T(8,128)}) custom-call(s32[2]{0:T(128)S(1)} %add_convert_fusion.inside_ref, f32[256,1024]{1,0:T(8,128)} %get-tuple-element.32.first_in, f32[256,1024]{1,0:T(8,128)} %get-tuple-element.33.middle_in, ...), custom_call_target="tpu_custom_call" | custom-call | flops 2147483648 | bytes 5308424 | tf_op jit(solution)/shard_map/fake_branch/pallas_call | solution.py:565
  51.1 9.5 %all-to-all-start.1 = ((f32[128,8,128]{2,1,0:T(8,128)}), f32[128,8,128]{2,1,0:T(8,128)S(1)}, u32[]{:S(2)}, u32[]{:S(2)}) async-start(f32[128,8,128]{2,1,0:T(8,128)} %bitcast.17), calls=%async_computation.1 | async-start | bytes 1048576 | tf_op jit(solution)/shard_map/all_to_all | solution.py:731
  60.6 5.0 %collective-permute-start.3 = (bf16[64,1024]{1,0:T(8,128)(2,1)S(1)}, bf16[64,1024]{1,0:T(8,128)(2,1)S(1)}, u32[]{:S(2)}, u32[]{:S(2)}) collective-permute-start(bf16[64,1024]{1,0:T(8,128)(2,1)S(1)} %copy-done.6), channel_id=1, source_target_pairs={{0,2},{2,4},{4,6},{6,8},{8,10},{10,12},{12,14},{14,16},{16,18},{18... | collective-permute-start | bytes 393224 | tf_op jit(solution)/shard_map/ppermute | solution.py:580
  65.6 4.5 %pull_own.1 = (bf16[2,256,576]{2,1,0:T(8,128)(2,1)}, f32[128,1024]{1,0:T(8,128)}, f32[128,1024]{1,0:T(8,128)}, bf16[32,64,256]{2,1,0:T(8,128)(2,1)}) custom-call(bf16[64,1024]{1,0:T(8,128)(2,1)} %get-tuple-element.39.low_in, bf16[64,1024]{1,0:T(8,128)(2,1)} %get-tuple-element.40.high_in, bf16[2048,64]{1,0:T(8,128)(2,1)} %bitcast.42), custom_call_target="tpu_custom_call" | custom-call | flops 905969664 | bytes 3211264 | tf_op jit(solution)/shard_map/pull_own/pallas_call | solution.py:565
  70.1 0.0 collective-permute-done.3.prev_ref.edge_in
  70.1 4.1 %all-to-all-done.1 = f32[128,8,128]{2,1,0:T(8,128)S(1)} async-done(((f32[128,8,128]{2,1,0:T(8,128)}), f32[128,8,128]{2,1,0:T(8,128)S(1)}, u32[]{:S(2)}, u32[]{:S(2)}) %all-to-all-start.1) | async-done | bytes 524320 | tf_op jit(solution)/shard_map/all_to_all | solution.py:731
  74.2 0.9 sum_terms.1.after_ref
  75.1 6.6 %all-to-all-start.2 = ((bf16[128,8,128]{2,1,0:T(8,128)(2,1)}), bf16[128,8,128]{2,1,0:T(8,128)(2,1)S(1)}, u32[]{:S(2)}, u32[]{:S(2)}) async-start(bf16[128,8,128]{2,1,0:T(8,128)(2,1)} %bitcast.20), calls=%async_computation.2 | async-start | bytes 524288 | tf_op jit(solution)/shard_map/all_to_all | solution.py:770
  81.7 1.3 %collective-permute-start.2 = (bf16[64,1024]{1,0:T(8,128)(2,1)S(1)}, bf16[64,1024]{1,0:T(8,128)(2,1)S(1)}, u32[]{:S(2)}, u32[]{:S(2)}) collective-permute-start(bf16[64,1024]{1,0:T(8,128)(2,1)S(1)} %copy-done.5), channel_id=1, source_target_pairs={{2,0},{4,2},{6,4},{8,6},{10,8},{12,10},{14,12},{16,14},{18,16},{20... | collective-permute-start | bytes 393224 | tf_op jit(solution)/shard_map/ppermute | solution.py:585
  83.0 2.6 %pull_prev.1.image_in = bf16[32,64,256]{2,1,0:T(8,128)(2,1)} custom-call(bf16[64,1024]{1,0:T(8,128)(2,1)} %copy-done.4, bf16[2,256,576]{2,1,0:T(8,128)(2,1)} %get-tuple-element.41.wide_in, f32[128,1024]{1,0:T(8,128)} %get-tuple-element.44.first_ref.share_in, bf16[1024,128]{1,0:T(8,128)(2,1)} %sum_terms.1.after_ref, ...), custom_call_target="tpu_custom_call", output_to_operand_aliasing={{}: (4, {})} | custom-call | flops 150994944 | bytes 3604480 | tf_op jit(solution)/shard_map/pull_prev/pallas_call | solution.py:565
  85.6 5.9 %collective-permute-done.2.edge_in = bf16[64,1024]{1,0:T(8,128)(2,1)S(1)} collective-permute-done((bf16[64,1024]{1,0:T(8,128)(2,1)S(1)}, bf16[64,1024]{1,0:T(8,128)(2,1)S(1)}, u32[]{:S(2)}, u32[]{:S(2)}) %collective-permute-start.2) | collective-permute-done | bytes 131104 | tf_op jit(solution)/shard_map/ppermute | solution.py:585
  91.6 2.6 %pull_next.1 = bf16[32,64,256]{2,1,0:T(8,128)(2,1)} custom-call(bf16[64,1024]{1,0:T(8,128)(2,1)S(1)} %collective-permute-done.2.edge_in, bf16[2,256,576]{2,1,0:T(8,128)(2,1)} %get-tuple-element.41.wide_in, f32[128,1024]{1,0:T(8,128)} %get-tuple-element.42.share_in, bf16[1024,128]{1,0:T(8,128)(2,1)} %sum_terms.1.after_ref, ...), custom_call_target="tpu_custom_call", output_to_operand_aliasing={{}: (4, {})} | custom-call | flops 150994944 | bytes 3604480 | tf_op jit(solution)/shard_map/pull_next/pallas_call | solution.py:565
  94.2 1.1 %unpack.1 = f32[2,1024,64]{2,1,0:T(8,128)} custom-call(bf16[1024,128]{1,0:T(8,128)(2,1)S(1)} %bitcast.26), custom_call_target="tpu_custom_call" | custom-call | bytes 786432 | tf_op jit(solution)/shard_map/unpack/pallas_call | solution.py:565
  (15 shorter events, 0.0 us)
Async XLA Ops:
  1.7 14.2 %collective-permute-start.1 = (bf16[1536,128]{1,0:T(8,128)(2,1)S(1)}, bf16[1536,128]{1,0:T(8,128)(2,1)S(1)}, u32[]{:S(2)}, u32[]{:S(2)}) collective-permute-start(bf16[1536,128]{1,0:T(8,128)(2,1)S(1)} %edges.1), channel_id=1, source_target_pairs={{2,0},{4,2},{6,4},{8,6},{10,8},{12,10},{14,12},{16,14},{18,16},{20... | collective-permute-start | bytes 1179656 | tf_op jit(solution)/shard_map/ppermute | solution.py:585
  7.6 26.5 %collective-permute-start = (bf16[1536,128]{1,0:T(8,128)(2,1)S(1)}, bf16[1536,128]{1,0:T(8,128)(2,1)S(1)}, u32[]{:S(2)}, u32[]{:S(2)}) collective-permute-start(bf16[1536,128]{1,0:T(8,128)(2,1)S(1)} %get-tuple-element.25), channel_id=1, source_target_pairs={{0,2},{2,4},{4,6},{6,8},{8,10},{10,12},{12,14},{14,16},{16,18},{18... | collective-permute-start | bytes 1179656 | tf_op jit(solution)/shard_map/ppermute | solution.py:580
  15.9 18.2 %copy-start = (bf16[1,32,4,16,256]{4,3,2,1,0:T(8,128)(2,1)S(1)}, bf16[1,32,4,16,256]{4,3,2,1,0:T(8,128)(2,1)}, u32[]{:S(2)}) copy-start(bf16[1,32,4,16,256]{4,3,2,1,0:T(8,128)(2,1)} %param.12) | copy-start | bytes 3145732
  15.9 18.2 %copy-start.2 = (bf16[1,64,2,8,128]{4,3,2,1,0:T(8,128)(2,1)S(1)}, bf16[1,64,2,8,128]{4,3,2,1,0:T(8,128)(2,1)}, u32[]{:S(2)}) copy-start(bf16[1,64,2,8,128]{4,3,2,1,0:T(8,128)(2,1)} %param.15) | copy-start | bytes 786436
  19.4 24.2 %all-to-all-start = ((f32[128,1,128]{2,1,0:T(1,128)}), f32[128,1,128]{2,1,0:T(1,128)S(1)}, u32[]{:S(2)}, u32[]{:S(2)}) async-start(f32[128,1,128]{2,1,0:T(1,128)} %bitcast.37), calls=%async_computation | async-start | bytes 131072 | tf_op jit(solution)/shard_map/all_to_all | solution.py:660
  34.1 9.5 %copy-start.1 = (f32[256,1024]{1,0:T(8,128)S(1)}, f32[256,1024]{1,0:T(8,128)}, u32[]{:S(2)}) copy-start(f32[256,1024]{1,0:T(8,128)} %get-tuple-element.34.last_ref) | copy-start | bytes 3145732
  34.1 9.5 %copy-start.3 = (bf16[1,64,2,8,128]{4,3,2,1,0:T(8,128)(2,1)S(1)}, bf16[1,64,2,8,128]{4,3,2,1,0:T(8,128)(2,1)}, u32[]{:S(2)}) copy-start(bf16[1,64,2,8,128]{4,3,2,1,0:T(8,128)(2,1)} %param.14) | copy-start | bytes 786436
  51.0 9.5 %copy-start.6 = (bf16[64,1024]{1,0:T(8,128)(2,1)S(1)}, bf16[64,1024]{1,0:T(8,128)(2,1)}, u32[]{:S(2)}) copy-start(bf16[64,1024]{1,0:T(8,128)(2,1)} %get-tuple-element.40.high_in) | copy-start | bytes 393220
  51.1 23.2 %all-to-all-start.1 = ((f32[128,8,128]{2,1,0:T(8,128)}), f32[128,8,128]{2,1,0:T(8,128)S(1)}, u32[]{:S(2)}, u32[]{:S(2)}) async-start(f32[128,8,128]{2,1,0:T(8,128)} %bitcast.17), calls=%async_computation.1 | async-start | bytes 1048576 | tf_op jit(solution)/shard_map/all_to_all | solution.py:731
  60.6 9.5 %collective-permute-start.3 = (bf16[64,1024]{1,0:T(8,128)(2,1)S(1)}, bf16[64,1024]{1,0:T(8,128)(2,1)S(1)}, u32[]{:S(2)}, u32[]{:S(2)}) collective-permute-start(bf16[64,1024]{1,0:T(8,128)(2,1)S(1)} %copy-done.6), channel_id=1, source_target_pairs={{0,2},{2,4},{4,6},{6,8},{8,10},{10,12},{12,14},{14,16},{16,18},{18... | collective-permute-start | bytes 393224 | tf_op jit(solution)/shard_map/ppermute | solution.py:580
  70.1 4.1 %copy-start.4 = (bf16[64,1024]{1,0:T(8,128)(2,1)}, bf16[64,1024]{1,0:T(8,128)(2,1)S(1)}, u32[]{:S(2)}) copy-start(bf16[64,1024]{1,0:T(8,128)(2,1)S(1)} %collective-permute-done.3.prev_ref.edge_in) | copy-start | bytes 393220
  75.1 6.6 %copy-start.5 = (bf16[64,1024]{1,0:T(8,128)(2,1)S(1)}, bf16[64,1024]{1,0:T(8,128)(2,1)}, u32[]{:S(2)}) copy-start(bf16[64,1024]{1,0:T(8,128)(2,1)} %get-tuple-element.39.low_in) | copy-start | bytes 393220
  75.1 19.1 %all-to-all-start.2 = ((bf16[128,8,128]{2,1,0:T(8,128)(2,1)}), bf16[128,8,128]{2,1,0:T(8,128)(2,1)S(1)}, u32[]{:S(2)}, u32[]{:S(2)}) async-start(bf16[128,8,128]{2,1,0:T(8,128)(2,1)} %bitcast.20), calls=%async_computation.2 | async-start | bytes 524288 | tf_op jit(solution)/shard_map/all_to_all | solution.py:770
  81.7 9.8 %collective-permute-start.2 = (bf16[64,1024]{1,0:T(8,128)(2,1)S(1)}, bf16[64,1024]{1,0:T(8,128)(2,1)S(1)}, u32[]{:S(2)}, u32[]{:S(2)}) collective-permute-start(bf16[64,1024]{1,0:T(8,128)(2,1)S(1)} %copy-done.5), channel_id=1, source_target_pairs={{2,0},{4,2},{6,4},{8,6},{10,8},{12,10},{14,12},{16,14},{18,16},{20... | collective-permute-start | bytes 393224 | tf_op jit(solution)/shard_map/ppermute | solution.py:585

commit v8 on v7

--- a/solution.py
+++ b/solution.py
@@ -1,5 +1,3 @@
-import functools
-
 import jax
 import jax.numpy as jnp
 from jax import lax
@@ -253,7 +251,7 @@
     )
 
 
-def finish(pre, cot_ref, out_ref, wide_cot, wide_out, grad):
+def finish(pre, cot_ref, out, wide_cot, wide_out, grad):
     wide_cot[...] = cot_ref[...].astype(F32)
     nothing = jnp.zeros((C, CELLS), BF16)
     grad[0:C, :] = nothing
@@ -264,16 +262,14 @@
             wide_out[pl.ds(m * Y + y, C, stride=16), :] = output
             cot = wide_cot[pl.ds(m * Y + y, C, stride=16), :]
             grad[(2 - m) * C : (3 - m) * C, y * X : (y + 1) * X] = (cot * slope).astype(BF16)
-    out_ref[...] = wide_out[...].astype(BF16)
+    out[...] = wide_out[...].astype(BF16)
 
 
 def kernel_terms(planes, grad):
-    halves = []
     for half in range(2):
         terms = dot(planes[half], grad[128:256, :], (1, 1))
         terms += dot(planes[half + 2], grad[64:192, :], (1, 1))
-        halves.append(terms + dot(planes[half + 4], grad[0:128, :], (1, 1)))
-    return halves
+        yield terms + dot(planes[half + 4], grad[0:128, :], (1, 1))
 
 
 def split_depth(at, places, halves, rows, patch):
@@ -307,9 +303,10 @@
     cot_ref,
     wide_in,
     first_in,
-    out_ref,
+    out_out,
     terms_out,
     first_out,
+    out,
     edge,
     weight,
     wide,
@@ -351,12 +348,15 @@
         copy.wait()
     first[...] += dot(wide[...], lat_patch[...])
     first_copy = fetch(first, first_out, sems.at[4])
-    finish(convolve(weight, patch), cot_ref, out_ref, wide_cot, wide_out, grad)
+    finish(convolve(weight, patch), cot_ref, out, wide_cot, wide_out, grad)
+    stores = [first_copy, fetch(out, out_out, sems.at[5])]
     planes = [patch[depth * 512 : (depth + 1) * 512, :] for depth in range(6)]
     for half, terms in enumerate(kernel_terms(planes, grad)):
         terms_ref[half * 512 : (half + 1) * 512, :] = terms
-    fetch(terms_ref, terms_out, sems.at[5]).wait()
-    first_copy.wait()
+        piece = pl.ds(half * 512, 512)
+        stores.append(fetch(terms_ref.at[piece], terms_out.at[piece], sems.at[6 + half]))
+    for store in stores:
+        store.wait()
 
 
 def fake_kernel(
@@ -368,9 +368,11 @@
     weight_in,
     cot_ref,
     real_terms_in,
-    out_ref,
+    out_out,
     low_out,
     high_out,
+    terms_out,
+    out,
     terms_ref,
     first_ref,
     middle_ref,
@@ -429,8 +431,9 @@
                                 patch[at : at + G, to * X : (to + 1) * X] = piece
     weight_copy.wait()
     pre = convolve(weight_ref, patch)
-    finish(pre, cot_ref, out_ref, wide_cot, wide_out, grad)
-    edge_copies = [
+    finish(pre, cot_ref, out, wide_cot, wide_out, grad)
+    stores = [
+        fetch(out, out_out, sems.at[6]),
         fetch(grad.at[2 * C : 3 * C], low_out, sems.at[2]),
         fetch(grad.at[C : 2 * C], high_out, sems.at[3]),
     ]
@@ -439,8 +442,10 @@
     for half, terms in enumerate(kernel_terms(planes, grad)):
         rows = slice(half * 512, (half + 1) * 512)
         terms_ref[rows, :] = terms + real_terms[rows, :]
-    for copy in edge_copies:
-        copy.wait()
+        piece = pl.ds(half * 512, 512)
+        stores.append(fetch(terms_ref.at[piece], terms_out.at[piece], sems.at[7 + half]))
+    for store in stores:
+        store.wait()
 
 
 def sum_kernel(parts_ref, prev_ref, first_ref, sums_ref):
@@ -532,24 +537,55 @@
         copy.wait()
 
 
-def pull_outer_kernel(
-    side, edge_in, wide_in, share_in, after_ref, image_in, image_out, cells, wide, share, patch, wide_rows, image, sems
-):
-    del after_ref, image_in
-    edge_copy = fetch(edge_in, cells, sems.at[0])
-    copies = [
-        fetch(wide_in.at[side], wide, sems.at[1]),
-        fetch(share_in, share, sems.at[2]),
-    ]
-    edge_copy.wait()
+def add_edge(side, cells, wide, share, image_out, patch, wide_rows, image, sem):
     spread_edge(cells, 0, patch)
-    for copy in copies:
-        copy.wait()
     rows = slice(128 - side * 128, 256 - side * 128)
     weave_into((share[...] + dot(wide[rows, :], patch[...])).astype(BF16), 0, 16, wide_rows)
     for half in range(2):
         image[:, :, half * X : (half + 1) * X] = wide_rows[half].reshape(G, 16, X).astype(BF16)
-    fetch(image, image_out.at[:, pl.ds(side * 48, 16)], sems.at[3]).wait()
+    return fetch(image, image_out.at[:, pl.ds(side * 48, 16)], sem)
+
+
+def pull_prev_kernel(
+    edge_in,
+    wide_in,
+    first_in,
+    last_in,
+    sums_ref,
+    image_in,
+    image_out,
+    wide_next,
+    last_ref,
+    cells,
+    wide,
+    share,
+    patch,
+    wide_rows,
+    image,
+    sems,
+):
+    del sums_ref, image_in
+    copies = [
+        fetch(edge_in, cells, sems.at[0]),
+        fetch(wide_in.at[0], wide, sems.at[1]),
+        fetch(first_in, share, sems.at[2]),
+    ]
+    later = [
+        fetch(wide_in.at[1], wide_next, sems.at[3]),
+        fetch(last_in, last_ref, sems.at[4]),
+    ]
+    for copy in copies:
+        copy.wait()
+    later.append(add_edge(0, cells, wide, share, image_out, patch, wide_rows, image, sems.at[5]))
+    for copy in later:
+        copy.wait()
+
+
+def pull_next_kernel(
+    edge_ref, wide_ref, last_ref, image_in, image_out, patch, wide_rows, image, sem
+):
+    del image_in
+    add_edge(1, edge_ref, wide_ref, last_ref, image_out, patch, wide_rows, image, sem).wait()
 
 
 def call(body, name, args, outs, scratch, flops, mebibytes, smem=(), far=(), far_outs=(), aliases=()):
@@ -677,12 +713,13 @@
         ),
         [shape((C * 2 * Y, X), BF16), shape((1024, 2 * C), F32), shape((256, CELLS), F32)],
         [
+            pltpu.VMEM((C * 2 * Y, X), BF16),
             pltpu.VMEM((1024, X), BF16),
             pltpu.VMEM((C, 2048), BF16),
             pltpu.VMEM((256, 576), BF16),
             pltpu.VMEM((256, CELLS), F32),
             pltpu.VMEM((1024, 2 * C), F32),
-            pltpu.SemaphoreType.DMA((6,)),
+            pltpu.SemaphoreType.DMA((8,)),
             pltpu.VMEM((6 * 512, CELLS), BF16),
             pltpu.VMEM((576, CELLS), BF16),
             pltpu.VMEM((2, 3072, X), F32),
@@ -692,7 +729,7 @@
         16 * 2048 * C * CELLS,
         26,
         far=(2, 3, 5, 6),
-        far_outs=(1, 2),
+        far_outs=(0, 1, 2),
     )
     d_fake, low, high, terms = call(
         fake_kernel,
@@ -714,11 +751,13 @@
             shape((NDEV * 8, 128), F32),
         ],
         [
+            pltpu.VMEM((C * 2 * Y, X), BF16),
+            pltpu.VMEM((NDEV * 8, 128), F32),
             pltpu.VMEM((256, CELLS), F32),
             pltpu.VMEM((256, CELLS), F32),
             pltpu.VMEM((NDEV * 8, 128), F32),
             pltpu.VMEM((C, 2048), BF16),
-            pltpu.SemaphoreType.DMA((6,)),
+            pltpu.SemaphoreType.DMA((9,)),
             pltpu.VMEM((6 * 512, CELLS), BF16),
         ]
         + working,
@@ -726,7 +765,7 @@
         26,
         smem=(0,),
         far=(1, 2, 5, 7),
-        far_outs=(1, 2),
+        far_outs=(0, 1, 2, 3),
     )
     parts = lax.all_to_all(terms.reshape(NDEV, 8, 128), AXES, 0, 0, tiled=True)
     grad_prev = to_next(high)
@@ -768,27 +807,41 @@
         far=(1, 2),
     )
     whole = lax.all_to_all(sums.reshape(NDEV, 8, 128), AXES, 0, 0, tiled=True)
-    for side, edge, share in ((0, grad_prev, pull_first), (1, grad_next, pull_last)):
-        (image,) = call(
-            functools.partial(pull_outer_kernel, side),
-            "pull_prev" if side == 0 else "pull_next",
-            (edge, pull_wide, share, sums, image),
-            [shape((G, 64, 2 * X), BF16)],
-            [
-                pltpu.VMEM((C, CELLS), BF16),
-                pltpu.VMEM((256, 576), BF16),
-                pltpu.VMEM((128, CELLS), F32),
-                pltpu.VMEM((576, CELLS), BF16),
-                pltpu.VMEM((2, G * 16, X), F32),
-                pltpu.VMEM((G, 16, 2 * X), BF16),
-                pltpu.SemaphoreType.DMA((4,)),
-            ],
-            128 * 1152 * CELLS,
-            12,
-            far=(0, 1, 2, 3, 4) if side == 0 else (1, 2, 3, 4),
-            far_outs=(0,),
-            aliases=((4, 0),),
-        )
+    outer = [
+        pltpu.VMEM((576, CELLS), BF16),
+        pltpu.VMEM((2, G * 16, X), F32),
+        pltpu.VMEM((G, 16, 2 * X), BF16),
+    ]
+    image, wide_next, last_share = call(
+        pull_prev_kernel,
+        "pull_prev",
+        (grad_prev, pull_wide, pull_first, pull_last, sums, image),
+        [shape((G, 64, 2 * X), BF16), shape((256, 576), BF16), shape((128, CELLS), F32)],
+        [
+            pltpu.VMEM((C, CELLS), BF16),
+            pltpu.VMEM((256, 576), BF16),
+            pltpu.VMEM((128, CELLS), F32),
+        ]
+        + outer
+        + [pltpu.SemaphoreType.DMA((6,))],
+        128 * 1152 * CELLS,
+        12,
+        far=(0, 1, 2, 3, 4, 5),
+        far_outs=(0,),
+        aliases=((5, 0),),
+    )
+    (image,) = call(
+        pull_next_kernel,
+        "pull_next",
+        (grad_next, wide_next, last_share, image),
+        [shape((G, 64, 2 * X), BF16)],
+        outer + [pltpu.SemaphoreType.DMA],
+        128 * 1152 * CELLS,
+        12,
+        far=(3,),
+        far_outs=(0,),
+        aliases=((3, 0),),
+    )
     (weight_grad,) = call(
         unpack_kernel,
         "unpack",

time: 96.4 us -> 94.4 us (0.979)
  Pallas kernels: 37.4 us -> 35.6 us
    pallas_call x10, Pallas kernels: 37.4 us -> 35.6 us  [call(): pl.pallas_call(body, name=name, out_shape=outs, in_specs=[pl.BlockSpec(me...]
  transfers between devices with their start and end apart: 7 -> 7, of which waited for: 4 -> 4; matrix products, arithmetic and copies ran while one was open for 0% -> 0% of each run, Pallas kernels for 28% -> 27%
where the time goes in v8:
time: 94.4 us; the launch traced here: 93.6 us
  starting transfers between devices  44.2 us (47%)
  Pallas kernels  35.6 us (38%)
  waiting for transfers between devices  12.7 us (13%)
  between operations  1.02 us (1%)
    pallas_call x10, Pallas kernels, call(): pl.pallas_call(body, name=name, out_shape=outs, in_specs=[pl.BlockSpec(me...  35.6 us
    all_to_all x1, starting transfers between devices, local(): stats = lax.all_to_all(stats, AXES, 0, 0, tiled=True)  14.7 us
    ppermute x2, starting transfers between devices, to_next(): return lax.ppermute(edge, 'slab', [(i, i + 1) for i in range(ends)])  11.3 us
    all_to_all x1, starting transfers between devices, local(): parts = lax.all_to_all(terms.reshape(NDEV, 8, 128), AXES, 0, 0, tiled=True)  8.96 us
    ppermute x2, waiting for transfers between devices, to_prev(): return lax.ppermute(edge, 'slab', [(i + 1, i) for i in range(ends)])  7.73 us
    all_to_all x1, starting transfers between devices, local(): whole = lax.all_to_all(sums.reshape(NDEV, 8, 128), AXES, 0, 0, tiled=True)  6.63 us
    all_to_all x1, waiting for transfers between devices, local(): parts = lax.all_to_all(terms.reshape(NDEV, 8, 128), AXES, 0, 0, tiled=True)  4.12 us
    ppermute x2, starting transfers between devices, to_prev(): return lax.ppermute(edge, 'slab', [(i + 1, i) for i in range(ends)])  2.58 us
  transfers between devices with their start and end apart: 7, of which 4 were waited for; matrix products, arithmetic and copies ran while one was open for 0% of the time, Pallas kernels for 27%

profile of v8, /device:TPU:1, one launch (start us, length us, event | category | flops | bytes accessed | tf_op | source)
XLA Modules:
  0.0 93.6 jit_solution(10632724609814532262)
XLA Ops:
  0.6 1.1 %edges.1 = bf16[1536,128]{1,0:T(8,128)(2,1)S(1)} custom-call(bf16[64,2,8,128]{3,2,1,0:T(8,128)(2,1)} %bitcast.36, bf16[32,4,16,256]{3,2,1,0:T(8,128)(2,1)} %bitcast.27), custom_call_target="tpu_custom_call" | custom-call | bytes 1703936 | tf_op jit(solution)/shard_map/edges/pallas_call | solution.py:601
  1.7 1.3 %collective-permute-start.1 = (bf16[1536,128]{1,0:T(8,128)(2,1)S(1)}, bf16[1536,128]{1,0:T(8,128)(2,1)S(1)}, u32[]{:S(2)}, u32[]{:S(2)}) collective-permute-start(bf16[1536,128]{1,0:T(8,128)(2,1)S(1)} %edges.1), channel_id=1, source_target_pairs={{2,0},{4,2},{6,4},{8,6},{10,8},{12,10},{14,12},{16,14},{18,16},{20... | collective-permute-start | bytes 1179656 | tf_op jit(solution)/shard_map/ppermute | solution.py:621
  3.0 4.6 %own_cells.1 = (bf16[2,256,576]{2,1,0:T(8,128)(2,1)}, f32[256,1024]{1,0:T(8,128)}, f32[256,1024]{1,0:T(8,128)}, f32[256,1024]{1,0:T(8,128)}, f32[32,128]{1,0:T(8...) custom-call(bf16[64,2,8,128]{3,2,1,0:T(8,128)(2,1)} %bitcast.37, bf16[32,4,16,256]{3,2,1,0:T(8,128)(2,1)} %bitcast.28, ...), custom_call_target="tpu_custom_call" | custom-call | flops 1207959552 | bytes 6242304 | tf_op jit(solution)/shard_map/own_cells/pallas_call | solution.py:601
  7.6 6.3 %collective-permute-start = (bf16[1536,128]{1,0:T(8,128)(2,1)S(1)}, bf16[1536,128]{1,0:T(8,128)(2,1)S(1)}, u32[]{:S(2)}, u32[]{:S(2)}) collective-permute-start(bf16[1536,128]{1,0:T(8,128)(2,1)S(1)} %get-tuple-element.28), channel_id=1, source_target_pairs={{0,2},{2,4},{4,6},{6,8},{8,10},{10,12},{12,14},{14,16},{16,18},{18... | collective-permute-start | bytes 1179656 | tf_op jit(solution)/shard_map/ppermute | solution.py:616
  13.9 0.1 add_convert_fusion.inside_ref
  14.0 1.9 %collective-permute-done.1.next_ref = bf16[1536,128]{1,0:T(8,128)(2,1)S(1)} collective-permute-done((bf16[1536,128]{1,0:T(8,128)(2,1)S(1)}, bf16[1536,128]{1,0:T(8,128)(2,1)S(1)}, u32[]{:S(2)}, u32[]{:S(2)}) %collective-permute-start.1) | collective-permute-done | bytes 393248 | tf_op jit(solution)/shard_map/ppermute | solution.py:621
  15.9 3.5 %rim_cells.1 = (f32[256,1024]{1,0:T(8,128)}, f32[128,128]{1,0:T(8,128)}, bf16[1024,128]{1,0:T(8,128)(2,1)}) custom-call(s32[2]{0:T(128)S(1)} %add_convert_fusion.inside_ref, bf16[1536,128]{1,0:T(8,128)(2,1)S(1)} %collective-permute-done.1.next_ref, f32[32,128]{1,0:T(8,128)S(1)} %get-tuple-element.29.sums_ref, f32[1,32]{1,0:T(1,128)} %bitcast.39, ...), custom_call_target="tpu_custom_call" | custom-call | flops 301989888 | bytes 3424520 | tf_op jit(solution)/shard_map/rim_cells/pallas_call | solution.py:601
  19.4 14.7 %all-to-all-start = ((f32[128,1,128]{2,1,0:T(1,128)}), f32[128,1,128]{2,1,0:T(1,128)S(1)}, u32[]{:S(2)}, u32[]{:S(2)}) async-start(f32[128,1,128]{2,1,0:T(1,128)} %bitcast.38), calls=%async_computation | async-start | bytes 131072 | tf_op jit(solution)/shard_map/all_to_all | solution.py:696
  34.1 0.0 copy-start.3
  34.1 8.7 %real_branch.1 = (bf16[1024,128]{1,0:T(8,128)(2,1)}, f32[1024,128]{1,0:T(8,128)}, f32[256,1024]{1,0:T(8,128)}) custom-call(bf16[2048,256]{1,0:T(8,128)(2,1)S(1)} %bitcast.29, bf16[1536,128]{1,0:T(8,128)(2,1)S(1)} %collective-permute-done.prev_ref, bf16[1024,128]{1,0:T(8,128)(2,1)} %get-tuple-element.32.next_in, ...), custom_call_target="tpu_custom_call" | custom-call | flops 2147483648 | bytes 5701632 | tf_op jit(solution)/shard_map/real_branch/pallas_call | solution.py:601
  42.8 0.8 all-to-all-done
  43.6 7.2 %fake_branch.1 = (bf16[1024,128]{1,0:T(8,128)(2,1)}, bf16[64,1024]{1,0:T(8,128)(2,1)}, bf16[64,1024]{1,0:T(8,128)(2,1)}, f32[1024,128]{1,0:T(8,128)}) custom-call(s32[2]{0:T(128)S(1)} %add_convert_fusion.inside_ref, f32[256,1024]{1,0:T(8,128)} %get-tuple-element.35.first_in, f32[256,1024]{1,0:T(8,128)} %get-tuple-element.36.middle_in, ...), custom_call_target="tpu_custom_call" | custom-call | flops 2147483648 | bytes 5308424 | tf_op jit(solution)/shard_map/fake_branch/pallas_call | solution.py:601
  50.9 9.0 %all-to-all-start.1 = ((f32[128,8,128]{2,1,0:T(8,128)}), f32[128,8,128]{2,1,0:T(8,128)S(1)}, u32[]{:S(2)}, u32[]{:S(2)}) async-start(f32[128,8,128]{2,1,0:T(8,128)} %bitcast.35), calls=%async_computation.1 | async-start | bytes 1048576 | tf_op jit(solution)/shard_map/all_to_all | solution.py:770
  59.9 5.0 %collective-permute-start.3 = (bf16[64,1024]{1,0:T(8,128)(2,1)S(1)}, bf16[64,1024]{1,0:T(8,128)(2,1)S(1)}, u32[]{:S(2)}, u32[]{:S(2)}) collective-permute-start(bf16[64,1024]{1,0:T(8,128)(2,1)S(1)} %copy-done.6), channel_id=1, source_target_pairs={{0,2},{2,4},{4,6},{6,8},{8,10},{10,12},{12,14},{14,16},{16,18},{18... | collective-permute-start | bytes 393224 | tf_op jit(solution)/shard_map/ppermute | solution.py:616
  64.9 4.5 %pull_own.1 = (bf16[2,256,576]{2,1,0:T(8,128)(2,1)}, f32[128,1024]{1,0:T(8,128)}, f32[128,1024]{1,0:T(8,128)}, bf16[32,64,256]{2,1,0:T(8,128)(2,1)}) custom-call(bf16[64,1024]{1,0:T(8,128)(2,1)} %get-tuple-element.42.low_in, bf16[64,1024]{1,0:T(8,128)(2,1)} %get-tuple-element.43.high_in, bf16[2048,64]{1,0:T(8,128)(2,1)} %bitcast.43), custom_call_target="tpu_custom_call" | custom-call | flops 905969664 | bytes 3211264 | tf_op jit(solution)/shard_map/pull_own/pallas_call | solution.py:601
  69.4 0.0 collective-permute-done.3.prev_ref.edge_in
  69.4 4.1 %all-to-all-done.1 = f32[128,8,128]{2,1,0:T(8,128)S(1)} async-done(((f32[128,8,128]{2,1,0:T(8,128)}), f32[128,8,128]{2,1,0:T(8,128)S(1)}, u32[]{:S(2)}, u32[]{:S(2)}) %all-to-all-start.1) | async-done | bytes 524320 | tf_op jit(solution)/shard_map/all_to_all | solution.py:770
  73.5 0.8 sum_terms.1.sums_ref
  74.4 6.6 %all-to-all-start.2 = ((bf16[128,8,128]{2,1,0:T(8,128)(2,1)}), bf16[128,8,128]{2,1,0:T(8,128)(2,1)S(1)}, u32[]{:S(2)}, u32[]{:S(2)}) async-start(bf16[128,8,128]{2,1,0:T(8,128)(2,1)} %bitcast.20), calls=%async_computation.2 | async-start | bytes 524288 | tf_op jit(solution)/shard_map/all_to_all | solution.py:809
  81.0 1.3 %collective-permute-start.2 = (bf16[64,1024]{1,0:T(8,128)(2,1)S(1)}, bf16[64,1024]{1,0:T(8,128)(2,1)S(1)}, u32[]{:S(2)}, u32[]{:S(2)}) collective-permute-start(bf16[64,1024]{1,0:T(8,128)(2,1)S(1)} %copy-done.5), channel_id=1, source_target_pairs={{2,0},{4,2},{6,4},{8,6},{10,8},{12,10},{14,12},{16,14},{18,16},{20... | collective-permute-start | bytes 393224 | tf_op jit(solution)/shard_map/ppermute | solution.py:621
  82.3 2.7 %pull_prev.1 = (bf16[32,64,256]{2,1,0:T(8,128)(2,1)}, bf16[256,576]{1,0:T(8,128)(2,1)S(1)}, f32[128,1024]{1,0:T(8,128)S(1)}) custom-call(bf16[64,1024]{1,0:T(8,128)(2,1)} %copy-done.4, bf16[2,256,576]{2,1,0:T(8,128)(2,1)} %get-tuple-element.44.wide_in, f32[128,1024]{1,0:T(8,128)} %get-tuple-element.45.first_ref.first_in, ...), custom_call_target="tpu_custom_call", output_to_operand_aliasing={{0}: (5, {})} | custom-call | flops 150994944 | bytes 4947968 | tf_op jit(solution)/shard_map/pull_prev/pallas_call | solution.py:601
  85.0 5.8 %collective-permute-done.2.edge_ref = bf16[64,1024]{1,0:T(8,128)(2,1)S(1)} collective-permute-done((bf16[64,1024]{1,0:T(8,128)(2,1)S(1)}, bf16[64,1024]{1,0:T(8,128)(2,1)S(1)}, u32[]{:S(2)}, u32[]{:S(2)}) %collective-permute-start.2) | collective-permute-done | bytes 131104 | tf_op jit(solution)/shard_map/ppermute | solution.py:621
  90.8 1.4 %pull_next.1 = bf16[32,64,256]{2,1,0:T(8,128)(2,1)} custom-call(bf16[64,1024]{1,0:T(8,128)(2,1)S(1)} %collective-permute-done.2.edge_ref, bf16[256,576]{1,0:T(8,128)(2,1)S(1)} %get-tuple-element.49.wide_ref, f32[128,1024]{1,0:T(8,128)S(1)} %get-tuple-element.50.last_ref, bf16[32,64,256]{2,1,0:T(8,128)(2,1)} %get-tuple-element.51.image_in), custom_call_target="tpu_custom_call", output_to_operand_aliasing={{}: (3, {})} | custom-call | flops 150994944 | bytes 3047424 | tf_op jit(solution)/shard_map/pull_next/pallas_call | solution.py:601
  92.3 1.1 %unpack.1 = f32[2,1024,64]{2,1,0:T(8,128)} custom-call(bf16[1024,128]{1,0:T(8,128)(2,1)S(1)} %bitcast.26), custom_call_target="tpu_custom_call" | custom-call | bytes 786432 | tf_op jit(solution)/shard_map/unpack/pallas_call | solution.py:601
  (15 shorter events, 0.0 us)
Async XLA Ops:
  1.7 14.2 %collective-permute-start.1 = (bf16[1536,128]{1,0:T(8,128)(2,1)S(1)}, bf16[1536,128]{1,0:T(8,128)(2,1)S(1)}, u32[]{:S(2)}, u32[]{:S(2)}) collective-permute-start(bf16[1536,128]{1,0:T(8,128)(2,1)S(1)} %edges.1), channel_id=1, source_target_pairs={{2,0},{4,2},{6,4},{8,6},{10,8},{12,10},{14,12},{16,14},{18,16},{20... | collective-permute-start | bytes 1179656 | tf_op jit(solution)/shard_map/ppermute | solution.py:621
  7.6 26.5 %collective-permute-start = (bf16[1536,128]{1,0:T(8,128)(2,1)S(1)}, bf16[1536,128]{1,0:T(8,128)(2,1)S(1)}, u32[]{:S(2)}, u32[]{:S(2)}) collective-permute-start(bf16[1536,128]{1,0:T(8,128)(2,1)S(1)} %get-tuple-element.28), channel_id=1, source_target_pairs={{0,2},{2,4},{4,6},{6,8},{8,10},{10,12},{12,14},{14,16},{16,18},{18... | collective-permute-start | bytes 1179656 | tf_op jit(solution)/shard_map/ppermute | solution.py:616
  15.9 18.2 %copy-start = (bf16[1,32,4,16,256]{4,3,2,1,0:T(8,128)(2,1)S(1)}, bf16[1,32,4,16,256]{4,3,2,1,0:T(8,128)(2,1)}, u32[]{:S(2)}) copy-start(bf16[1,32,4,16,256]{4,3,2,1,0:T(8,128)(2,1)} %param.12) | copy-start | bytes 3145732
  15.9 18.2 %copy-start.2 = (bf16[1,64,2,8,128]{4,3,2,1,0:T(8,128)(2,1)S(1)}, bf16[1,64,2,8,128]{4,3,2,1,0:T(8,128)(2,1)}, u32[]{:S(2)}) copy-start(bf16[1,64,2,8,128]{4,3,2,1,0:T(8,128)(2,1)} %param.15) | copy-start | bytes 786436
  19.4 24.2 %all-to-all-start = ((f32[128,1,128]{2,1,0:T(1,128)}), f32[128,1,128]{2,1,0:T(1,128)S(1)}, u32[]{:S(2)}, u32[]{:S(2)}) async-start(f32[128,1,128]{2,1,0:T(1,128)} %bitcast.38), calls=%async_computation | async-start | bytes 131072 | tf_op jit(solution)/shard_map/all_to_all | solution.py:696
  34.1 9.5 %copy-start.1 = (f32[256,1024]{1,0:T(8,128)S(1)}, f32[256,1024]{1,0:T(8,128)}, u32[]{:S(2)}) copy-start(f32[256,1024]{1,0:T(8,128)} %get-tuple-element.37.last_ref) | copy-start | bytes 3145732
  34.1 9.5 %copy-start.3 = (bf16[1,64,2,8,128]{4,3,2,1,0:T(8,128)(2,1)S(1)}, bf16[1,64,2,8,128]{4,3,2,1,0:T(8,128)(2,1)}, u32[]{:S(2)}) copy-start(bf16[1,64,2,8,128]{4,3,2,1,0:T(8,128)(2,1)} %param.14) | copy-start | bytes 786436
  50.9 9.0 %copy-start.6 = (bf16[64,1024]{1,0:T(8,128)(2,1)S(1)}, bf16[64,1024]{1,0:T(8,128)(2,1)}, u32[]{:S(2)}) copy-start(bf16[64,1024]{1,0:T(8,128)(2,1)} %get-tuple-element.43.high_in) | copy-start | bytes 393220
  50.9 22.6 %all-to-all-start.1 = ((f32[128,8,128]{2,1,0:T(8,128)}), f32[128,8,128]{2,1,0:T(8,128)S(1)}, u32[]{:S(2)}, u32[]{:S(2)}) async-start(f32[128,8,128]{2,1,0:T(8,128)} %bitcast.35), calls=%async_computation.1 | async-start | bytes 1048576 | tf_op jit(solution)/shard_map/all_to_all | solution.py:770
  59.9 9.5 %collective-permute-start.3 = (bf16[64,1024]{1,0:T(8,128)(2,1)S(1)}, bf16[64,1024]{1,0:T(8,128)(2,1)S(1)}, u32[]{:S(2)}, u32[]{:S(2)}) collective-permute-start(bf16[64,1024]{1,0:T(8,128)(2,1)S(1)} %copy-done.6), channel_id=1, source_target_pairs={{0,2},{2,4},{4,6},{6,8},{8,10},{10,12},{12,14},{14,16},{16,18},{18... | collective-permute-start | bytes 393224 | tf_op jit(solution)/shard_map/ppermute | solution.py:616
  69.4 4.1 %copy-start.4 = (bf16[64,1024]{1,0:T(8,128)(2,1)}, bf16[64,1024]{1,0:T(8,128)(2,1)S(1)}, u32[]{:S(2)}) copy-start(bf16[64,1024]{1,0:T(8,128)(2,1)S(1)} %collective-permute-done.3.prev_ref.edge_in) | copy-start | bytes 393220
  74.4 6.6 %copy-start.5 = (bf16[64,1024]{1,0:T(8,128)(2,1)S(1)}, bf16[64,1024]{1,0:T(8,128)(2,1)}, u32[]{:S(2)}) copy-start(bf16[64,1024]{1,0:T(8,128)(2,1)} %get-tuple-element.42.low_in) | copy-start | bytes 393220
  74.4 17.9 %all-to-all-start.2 = ((bf16[128,8,128]{2,1,0:T(8,128)(2,1)}), bf16[128,8,128]{2,1,0:T(8,128)(2,1)S(1)}, u32[]{:S(2)}, u32[]{:S(2)}) async-start(bf16[128,8,128]{2,1,0:T(8,128)(2,1)} %bitcast.20), calls=%async_computation.2 | async-start | bytes 524288 | tf_op jit(solution)/shard_map/all_to_all | solution.py:809
  81.0 9.8 %collective-permute-start.2 = (bf16[64,1024]{1,0:T(8,128)(2,1)S(1)}, bf16[64,1024]{1,0:T(8,128)(2,1)S(1)}, u32[]{:S(2)}, u32[]{:S(2)}) collective-permute-start(bf16[64,1024]{1,0:T(8,128)(2,1)S(1)} %copy-done.5), channel_id=1, source_target_pairs={{2,0},{4,2},{6,4},{8,6},{10,8},{12,10},{14,12},{16,14},{18,16},{20... | collective-permute-start | bytes 393224 | tf_op jit(solution)/shard_map/ppermute | solution.py:621

commit v9 on v8

--- a/solution.py
+++ b/solution.py
@@ -241,14 +241,16 @@
     return (output, derivative)
 
 
-def convolve(weight_ref, patch):
+def convolve(weight_ref, patch, build):
     early = weight_ref[:, 0:1024]
     late = weight_ref[:, 1024:2048]
+    second = dot(late, patch[2048:3072, :])
+    build(2)
+    build(3)
     shared = dot(jnp.concatenate([late, early], axis=0), patch[1024:2048, :])
-    return (
-        dot(early, patch[0:1024, :]) + shared[0:C, :],
-        shared[C : 2 * C, :] + dot(late, patch[2048:3072, :]),
-    )
+    build(0)
+    build(1)
+    return dot(early, patch[0:1024, :]) + shared[0:C, :], second + shared[C : 2 * C, :]
 
 
 def finish(pre, cot_ref, out, wide_cot, wide_out, grad):
@@ -322,23 +324,27 @@
     grad,
 ):
     edge_copy = fetch(next_in, edge, sems.at[0])
+    weight_copy = fetch(weight_in, weight, sems.at[1])
+    copies = [
+        fetch(wide_in.at[0], wide, sems.at[2]),
+        fetch(first_in, first, sems.at[3]),
+    ]
     for half in range(2):
         part = slice(512 + half * 512, 1024 + half * 512)
         halves[half, 0:2048, :] = real_ref[:, half * X : (half + 1) * X].astype(F32)
         halves[half, 2048:2560, :] = prev_ref[part, :].astype(F32)
     places = ((2048, 16), (0, 64), (16, 64), (32, 64), (48, 64), (2560, 16))
-    for depth in range(2):
+
+    def build(depth):
         split_depth(depth * 512, places[depth], halves, rows, patch)
+
+    build(4)
     edge_copy.wait()
-    copies = [
-        fetch(weight_in, weight, sems.at[1]),
-        fetch(wide_in.at[0], wide, sems.at[2]),
-        fetch(first_in, first, sems.at[3]),
-    ]
     for half in range(2):
         halves[half, 2560:3072, :] = edge[half * 512 : (half + 1) * 512, :].astype(F32)
-    for depth in range(2, 6):
-        split_depth(depth * 512, places[depth], halves, rows, patch)
+    build(5)
+    weight_copy.wait()
+    pre = convolve(weight, patch, build)
     halves[0, 0:512, :] = prev_ref[0:512, :].astype(F32)
     lane = lanes((C, X))
     clear_rims(0, lat_patch)
@@ -348,7 +354,7 @@
         copy.wait()
     first[...] += dot(wide[...], lat_patch[...])
     first_copy = fetch(first, first_out, sems.at[4])
-    finish(convolve(weight, patch), cot_ref, out, wide_cot, wide_out, grad)
+    finish(pre, cot_ref, out, wide_cot, wide_out, grad)
     stores = [first_copy, fetch(out, out_out, sems.at[5])]
     planes = [patch[depth * 512 : (depth + 1) * 512, :] for depth in range(6)]
     for half, terms in enumerate(kernel_terms(planes, grad)):
@@ -384,9 +390,9 @@
     wide_out,
     grad,
 ):
+    weight_copy = fetch(weight_in, weight_ref, sems.at[5])
     middle_copy = fetch(middle_in, middle_ref, sems.at[4])
     first_copy = fetch(first_in, first_ref, sems.at[0])
-    weight_copy = fetch(weight_in, weight_ref, sems.at[5])
     real_copy = fetch(real_terms_in, real_terms, sems.at[1])
     stats = stats_ref[...]
     slab = lax.broadcasted_iota(jnp.int32, (NDEV, 128), 0) // 2 % 32
@@ -401,7 +407,8 @@
     shift = as_column(stats[0:1, :], 3 * G)
     lane = lanes((G, X))
     edge = jnp.zeros((128, X), BF16)
-    for depth in (4, 5, 2, 3, 0, 1):
+
+    def build(depth):
         if depth == 2:
             middle_copy.wait()
         elif depth == 0:
@@ -429,8 +436,11 @@
                             if 0 <= to < Y:
                                 at = depth * 512 + ky * 128 + kx * G
                                 patch[at : at + G, to * X : (to + 1) * X] = piece
+
+    build(4)
+    build(5)
     weight_copy.wait()
-    pre = convolve(weight_ref, patch)
+    pre = convolve(weight_ref, patch, build)
     finish(pre, cot_ref, out, wide_cot, wide_out, grad)
     stores = [
         fetch(out, out_out, sems.at[6]),

time: 94.4 us -> 94.1 us (level)
  no operation moved by 1% of the time
where the time goes in v9:
time: 94.1 us; the launch traced here: 93.2 us
  starting transfers between devices  43.8 us (47%)
  Pallas kernels  35.2 us (37%)
  waiting for transfers between devices  13.1 us (14%)
  between operations  1.02 us (1%)
    pallas_call x10, Pallas kernels, call(): pl.pallas_call(body, name=name, out_shape=outs, in_specs=[pl.BlockSpec(me...  35.2 us
    all_to_all x1, starting transfers between devices, local(): stats = lax.all_to_all(stats, AXES, 0, 0, tiled=True)  14.7 us
    ppermute x2, starting transfers between devices, to_next(): return lax.ppermute(edge, 'slab', [(i, i + 1) for i in range(ends)])  11.3 us
    all_to_all x1, starting transfers between devices, local(): parts = lax.all_to_all(terms.reshape(NDEV, 8, 128), AXES, 0, 0, tiled=True)  8.6 us
    ppermute x2, waiting for transfers between devices, to_prev(): return lax.ppermute(edge, 'slab', [(i + 1, i) for i in range(ends)])  7.73 us
    all_to_all x1, starting transfers between devices, local(): whole = lax.all_to_all(sums.reshape(NDEV, 8, 128), AXES, 0, 0, tiled=True)  6.63 us
    all_to_all x1, waiting for transfers between devices, local(): parts = lax.all_to_all(terms.reshape(NDEV, 8, 128), AXES, 0, 0, tiled=True)  4.12 us
    ppermute x2, starting transfers between devices, to_prev(): return lax.ppermute(edge, 'slab', [(i + 1, i) for i in range(ends)])  2.58 us
  transfers between devices with their start and end apart: 7, of which 4 were waited for; matrix products, arithmetic and copies ran while one was open for 0% of the time, Pallas kernels for 27%

profile of v9, /device:TPU:1, one launch (start us, length us, event | category | flops | bytes accessed | tf_op | source)
XLA Modules:
  0.0 93.2 jit_solution(890310538083363296)
XLA Ops:
  0.6 1.1 %edges.1 = bf16[1536,128]{1,0:T(8,128)(2,1)S(1)} custom-call(bf16[64,2,8,128]{3,2,1,0:T(8,128)(2,1)} %bitcast.36, bf16[32,4,16,256]{3,2,1,0:T(8,128)(2,1)} %bitcast.27), custom_call_target="tpu_custom_call" | custom-call | bytes 1703936 | tf_op jit(solution)/shard_map/edges/pallas_call | solution.py:611
  1.7 1.3 %collective-permute-start.1 = (bf16[1536,128]{1,0:T(8,128)(2,1)S(1)}, bf16[1536,128]{1,0:T(8,128)(2,1)S(1)}, u32[]{:S(2)}, u32[]{:S(2)}) collective-permute-start(bf16[1536,128]{1,0:T(8,128)(2,1)S(1)} %edges.1), channel_id=1, source_target_pairs={{2,0},{4,2},{6,4},{8,6},{10,8},{12,10},{14,12},{16,14},{18,16},{20... | collective-permute-start | bytes 1179656 | tf_op jit(solution)/shard_map/ppermute | solution.py:631
  3.0 4.6 %own_cells.1 = (bf16[2,256,576]{2,1,0:T(8,128)(2,1)}, f32[256,1024]{1,0:T(8,128)}, f32[256,1024]{1,0:T(8,128)}, f32[256,1024]{1,0:T(8,128)}, f32[32,128]{1,0:T(8...) custom-call(bf16[64,2,8,128]{3,2,1,0:T(8,128)(2,1)} %bitcast.37, bf16[32,4,16,256]{3,2,1,0:T(8,128)(2,1)} %bitcast.28, ...), custom_call_target="tpu_custom_call" | custom-call | flops 1207959552 | bytes 6242304 | tf_op jit(solution)/shard_map/own_cells/pallas_call | solution.py:611
  7.6 6.3 %collective-permute-start = (bf16[1536,128]{1,0:T(8,128)(2,1)S(1)}, bf16[1536,128]{1,0:T(8,128)(2,1)S(1)}, u32[]{:S(2)}, u32[]{:S(2)}) collective-permute-start(bf16[1536,128]{1,0:T(8,128)(2,1)S(1)} %get-tuple-element.28), channel_id=1, source_target_pairs={{0,2},{2,4},{4,6},{6,8},{8,10},{10,12},{12,14},{14,16},{16,18},{18... | collective-permute-start | bytes 1179656 | tf_op jit(solution)/shard_map/ppermute | solution.py:626
  13.9 0.1 add_convert_fusion.inside_ref
  14.0 1.9 %collective-permute-done.1.next_ref = bf16[1536,128]{1,0:T(8,128)(2,1)S(1)} collective-permute-done((bf16[1536,128]{1,0:T(8,128)(2,1)S(1)}, bf16[1536,128]{1,0:T(8,128)(2,1)S(1)}, u32[]{:S(2)}, u32[]{:S(2)}) %collective-permute-start.1) | collective-permute-done | bytes 393248 | tf_op jit(solution)/shard_map/ppermute | solution.py:631
  15.9 3.5 %rim_cells.1 = (f32[256,1024]{1,0:T(8,128)}, f32[128,128]{1,0:T(8,128)}, bf16[1024,128]{1,0:T(8,128)(2,1)}) custom-call(s32[2]{0:T(128)S(1)} %add_convert_fusion.inside_ref, bf16[1536,128]{1,0:T(8,128)(2,1)S(1)} %collective-permute-done.1.next_ref, f32[32,128]{1,0:T(8,128)S(1)} %get-tuple-element.29.sums_ref, f32[1,32]{1,0:T(1,128)} %bitcast.39, ...), custom_call_target="tpu_custom_call" | custom-call | flops 301989888 | bytes 3424520 | tf_op jit(solution)/shard_map/rim_cells/pallas_call | solution.py:611
  19.4 14.7 %all-to-all-start = ((f32[128,1,128]{2,1,0:T(1,128)}), f32[128,1,128]{2,1,0:T(1,128)S(1)}, u32[]{:S(2)}, u32[]{:S(2)}) async-start(f32[128,1,128]{2,1,0:T(1,128)} %bitcast.38), calls=%async_computation | async-start | bytes 131072 | tf_op jit(solution)/shard_map/all_to_all | solution.py:706
  34.1 0.0 copy-start.3
  34.1 8.3 %real_branch.1 = (bf16[1024,128]{1,0:T(8,128)(2,1)}, f32[1024,128]{1,0:T(8,128)}, f32[256,1024]{1,0:T(8,128)}) custom-call(bf16[2048,256]{1,0:T(8,128)(2,1)S(1)} %bitcast.29, bf16[1536,128]{1,0:T(8,128)(2,1)S(1)} %collective-permute-done.prev_ref, bf16[1024,128]{1,0:T(8,128)(2,1)} %get-tuple-element.32.next_in, ...), custom_call_target="tpu_custom_call" | custom-call | flops 2147483648 | bytes 5701632 | tf_op jit(solution)/shard_map/real_branch/pallas_call | solution.py:611
  42.4 1.2 %all-to-all-done = f32[128,1,128]{2,1,0:T(1,128)S(1)} async-done(((f32[128,1,128]{2,1,0:T(1,128)}), f32[128,1,128]{2,1,0:T(1,128)S(1)}, u32[]{:S(2)}, u32[]{:S(2)}) %all-to-all-start) | async-done | bytes 65568 | tf_op jit(solution)/shard_map/all_to_all | solution.py:706
  43.6 7.2 %fake_branch.1 = (bf16[1024,128]{1,0:T(8,128)(2,1)}, bf16[64,1024]{1,0:T(8,128)(2,1)}, bf16[64,1024]{1,0:T(8,128)(2,1)}, f32[1024,128]{1,0:T(8,128)}) custom-call(s32[2]{0:T(128)S(1)} %add_convert_fusion.inside_ref, f32[256,1024]{1,0:T(8,128)} %get-tuple-element.35.first_in, f32[256,1024]{1,0:T(8,128)} %get-tuple-element.36.middle_in, ...), custom_call_target="tpu_custom_call" | custom-call | flops 2147483648 | bytes 5308424 | tf_op jit(solution)/shard_map/fake_branch/pallas_call | solution.py:611
  50.9 8.6 %all-to-all-start.1 = ((f32[128,8,128]{2,1,0:T(8,128)}), f32[128,8,128]{2,1,0:T(8,128)S(1)}, u32[]{:S(2)}, u32[]{:S(2)}) async-start(f32[128,8,128]{2,1,0:T(8,128)} %bitcast.35), calls=%async_computation.1 | async-start | bytes 1048576 | tf_op jit(solution)/shard_map/all_to_all | solution.py:780
  59.5 5.0 %collective-permute-start.3 = (bf16[64,1024]{1,0:T(8,128)(2,1)S(1)}, bf16[64,1024]{1,0:T(8,128)(2,1)S(1)}, u32[]{:S(2)}, u32[]{:S(2)}) collective-permute-start(bf16[64,1024]{1,0:T(8,128)(2,1)S(1)} %copy-done.6), channel_id=1, source_target_pairs={{0,2},{2,4},{4,6},{6,8},{8,10},{10,12},{12,14},{14,16},{16,18},{18... | collective-permute-start | bytes 393224 | tf_op jit(solution)/shard_map/ppermute | solution.py:626
  64.5 4.5 %pull_own.1 = (bf16[2,256,576]{2,1,0:T(8,128)(2,1)}, f32[128,1024]{1,0:T(8,128)}, f32[128,1024]{1,0:T(8,128)}, bf16[32,64,256]{2,1,0:T(8,128)(2,1)}) custom-call(bf16[64,1024]{1,0:T(8,128)(2,1)} %get-tuple-element.42.low_in, bf16[64,1024]{1,0:T(8,128)(2,1)} %get-tuple-element.43.high_in, bf16[2048,64]{1,0:T(8,128)(2,1)} %bitcast.43), custom_call_target="tpu_custom_call" | custom-call | flops 905969664 | bytes 3211264 | tf_op jit(solution)/shard_map/pull_own/pallas_call | solution.py:611
  69.0 0.0 collective-permute-done.3.prev_ref.edge_in
  69.0 4.1 %all-to-all-done.1 = f32[128,8,128]{2,1,0:T(8,128)S(1)} async-done(((f32[128,8,128]{2,1,0:T(8,128)}), f32[128,8,128]{2,1,0:T(8,128)S(1)}, u32[]{:S(2)}, u32[]{:S(2)}) %all-to-all-start.1) | async-done | bytes 524320 | tf_op jit(solution)/shard_map/all_to_all | solution.py:780
  73.2 0.8 sum_terms.1.sums_ref
  74.0 6.6 %all-to-all-start.2 = ((bf16[128,8,128]{2,1,0:T(8,128)(2,1)}), bf16[128,8,128]{2,1,0:T(8,128)(2,1)S(1)}, u32[]{:S(2)}, u32[]{:S(2)}) async-start(bf16[128,8,128]{2,1,0:T(8,128)(2,1)} %bitcast.20), calls=%async_computation.2 | async-start | bytes 524288 | tf_op jit(solution)/shard_map/all_to_all | solution.py:819
  80.7 1.3 %collective-permute-start.2 = (bf16[64,1024]{1,0:T(8,128)(2,1)S(1)}, bf16[64,1024]{1,0:T(8,128)(2,1)S(1)}, u32[]{:S(2)}, u32[]{:S(2)}) collective-permute-start(bf16[64,1024]{1,0:T(8,128)(2,1)S(1)} %copy-done.5), channel_id=1, source_target_pairs={{2,0},{4,2},{6,4},{8,6},{10,8},{12,10},{14,12},{16,14},{18,16},{20... | collective-permute-start | bytes 393224 | tf_op jit(solution)/shard_map/ppermute | solution.py:631
  82.0 2.7 %pull_prev.1 = (bf16[32,64,256]{2,1,0:T(8,128)(2,1)}, bf16[256,576]{1,0:T(8,128)(2,1)S(1)}, f32[128,1024]{1,0:T(8,128)S(1)}) custom-call(bf16[64,1024]{1,0:T(8,128)(2,1)} %copy-done.4, bf16[2,256,576]{2,1,0:T(8,128)(2,1)} %get-tuple-element.44.wide_in, f32[128,1024]{1,0:T(8,128)} %get-tuple-element.45.first_ref.first_in, ...), custom_call_target="tpu_custom_call", output_to_operand_aliasing={{0}: (5, {})} | custom-call | flops 150994944 | bytes 4947968 | tf_op jit(solution)/shard_map/pull_prev/pallas_call | solution.py:611
  84.7 5.8 %collective-permute-done.2.edge_ref = bf16[64,1024]{1,0:T(8,128)(2,1)S(1)} collective-permute-done((bf16[64,1024]{1,0:T(8,128)(2,1)S(1)}, bf16[64,1024]{1,0:T(8,128)(2,1)S(1)}, u32[]{:S(2)}, u32[]{:S(2)}) %collective-permute-start.2) | collective-permute-done | bytes 131104 | tf_op jit(solution)/shard_map/ppermute | solution.py:631
  90.5 1.4 %pull_next.1 = bf16[32,64,256]{2,1,0:T(8,128)(2,1)} custom-call(bf16[64,1024]{1,0:T(8,128)(2,1)S(1)} %collective-permute-done.2.edge_ref, bf16[256,576]{1,0:T(8,128)(2,1)S(1)} %get-tuple-element.49.wide_ref, f32[128,1024]{1,0:T(8,128)S(1)} %get-tuple-element.50.last_ref, bf16[32,64,256]{2,1,0:T(8,128)(2,1)} %get-tuple-element.51.image_in), custom_call_target="tpu_custom_call", output_to_operand_aliasing={{}: (3, {})} | custom-call | flops 150994944 | bytes 3047424 | tf_op jit(solution)/shard_map/pull_next/pallas_call | solution.py:611
  91.9 1.1 %unpack.1 = f32[2,1024,64]{2,1,0:T(8,128)} custom-call(bf16[1024,128]{1,0:T(8,128)(2,1)S(1)} %bitcast.26), custom_call_target="tpu_custom_call" | custom-call | bytes 786432 | tf_op jit(solution)/shard_map/unpack/pallas_call | solution.py:611
  (15 shorter events, 0.0 us)
Async XLA Ops:
  1.7 14.2 %collective-permute-start.1 = (bf16[1536,128]{1,0:T(8,128)(2,1)S(1)}, bf16[1536,128]{1,0:T(8,128)(2,1)S(1)}, u32[]{:S(2)}, u32[]{:S(2)}) collective-permute-start(bf16[1536,128]{1,0:T(8,128)(2,1)S(1)} %edges.1), channel_id=1, source_target_pairs={{2,0},{4,2},{6,4},{8,6},{10,8},{12,10},{14,12},{16,14},{18,16},{20... | collective-permute-start | bytes 1179656 | tf_op jit(solution)/shard_map/ppermute | solution.py:631
  7.6 26.5 %collective-permute-start = (bf16[1536,128]{1,0:T(8,128)(2,1)S(1)}, bf16[1536,128]{1,0:T(8,128)(2,1)S(1)}, u32[]{:S(2)}, u32[]{:S(2)}) collective-permute-start(bf16[1536,128]{1,0:T(8,128)(2,1)S(1)} %get-tuple-element.28), channel_id=1, source_target_pairs={{0,2},{2,4},{4,6},{6,8},{8,10},{10,12},{12,14},{14,16},{16,18},{18... | collective-permute-start | bytes 1179656 | tf_op jit(solution)/shard_map/ppermute | solution.py:626
  15.9 18.2 %copy-start = (bf16[1,32,4,16,256]{4,3,2,1,0:T(8,128)(2,1)S(1)}, bf16[1,32,4,16,256]{4,3,2,1,0:T(8,128)(2,1)}, u32[]{:S(2)}) copy-start(bf16[1,32,4,16,256]{4,3,2,1,0:T(8,128)(2,1)} %param.12) | copy-start | bytes 3145732
  15.9 18.2 %copy-start.2 = (bf16[1,64,2,8,128]{4,3,2,1,0:T(8,128)(2,1)S(1)}, bf16[1,64,2,8,128]{4,3,2,1,0:T(8,128)(2,1)}, u32[]{:S(2)}) copy-start(bf16[1,64,2,8,128]{4,3,2,1,0:T(8,128)(2,1)} %param.15) | copy-start | bytes 786436
  19.4 24.2 %all-to-all-start = ((f32[128,1,128]{2,1,0:T(1,128)}), f32[128,1,128]{2,1,0:T(1,128)S(1)}, u32[]{:S(2)}, u32[]{:S(2)}) async-start(f32[128,1,128]{2,1,0:T(1,128)} %bitcast.38), calls=%async_computation | async-start | bytes 131072 | tf_op jit(solution)/shard_map/all_to_all | solution.py:706
  34.1 9.5 %copy-start.1 = (f32[256,1024]{1,0:T(8,128)S(1)}, f32[256,1024]{1,0:T(8,128)}, u32[]{:S(2)}) copy-start(f32[256,1024]{1,0:T(8,128)} %get-tuple-element.37.last_ref) | copy-start | bytes 3145732
  34.1 9.5 %copy-start.3 = (bf16[1,64,2,8,128]{4,3,2,1,0:T(8,128)(2,1)S(1)}, bf16[1,64,2,8,128]{4,3,2,1,0:T(8,128)(2,1)}, u32[]{:S(2)}) copy-start(bf16[1,64,2,8,128]{4,3,2,1,0:T(8,128)(2,1)} %param.14) | copy-start | bytes 786436
  50.9 8.6 %copy-start.6 = (bf16[64,1024]{1,0:T(8,128)(2,1)S(1)}, bf16[64,1024]{1,0:T(8,128)(2,1)}, u32[]{:S(2)}) copy-start(bf16[64,1024]{1,0:T(8,128)(2,1)} %get-tuple-element.43.high_in) | copy-start | bytes 393220
  50.9 22.3 %all-to-all-start.1 = ((f32[128,8,128]{2,1,0:T(8,128)}), f32[128,8,128]{2,1,0:T(8,128)S(1)}, u32[]{:S(2)}, u32[]{:S(2)}) async-start(f32[128,8,128]{2,1,0:T(8,128)} %bitcast.35), calls=%async_computation.1 | async-start | bytes 1048576 | tf_op jit(solution)/shard_map/all_to_all | solution.py:780
  59.5 9.5 %collective-permute-start.3 = (bf16[64,1024]{1,0:T(8,128)(2,1)S(1)}, bf16[64,1024]{1,0:T(8,128)(2,1)S(1)}, u32[]{:S(2)}, u32[]{:S(2)}) collective-permute-start(bf16[64,1024]{1,0:T(8,128)(2,1)S(1)} %copy-done.6), channel_id=1, source_target_pairs={{0,2},{2,4},{4,6},{6,8},{8,10},{10,12},{12,14},{14,16},{16,18},{18... | collective-permute-start | bytes 393224 | tf_op jit(solution)/shard_map/ppermute | solution.py:626
  69.0 4.1 %copy-start.4 = (bf16[64,1024]{1,0:T(8,128)(2,1)}, bf16[64,1024]{1,0:T(8,128)(2,1)S(1)}, u32[]{:S(2)}) copy-start(bf16[64,1024]{1,0:T(8,128)(2,1)S(1)} %collective-permute-done.3.prev_ref.edge_in) | copy-start | bytes 393220
  74.0 6.6 %copy-start.5 = (bf16[64,1024]{1,0:T(8,128)(2,1)S(1)}, bf16[64,1024]{1,0:T(8,128)(2,1)}, u32[]{:S(2)}) copy-start(bf16[64,1024]{1,0:T(8,128)(2,1)} %get-tuple-element.42.low_in) | copy-start | bytes 393220
  74.0 17.9 %all-to-all-start.2 = ((bf16[128,8,128]{2,1,0:T(8,128)(2,1)}), bf16[128,8,128]{2,1,0:T(8,128)(2,1)S(1)}, u32[]{:S(2)}, u32[]{:S(2)}) async-start(bf16[128,8,128]{2,1,0:T(8,128)(2,1)} %bitcast.20), calls=%async_computation.2 | async-start | bytes 524288 | tf_op jit(solution)/shard_map/all_to_all | solution.py:819
  80.7 9.8 %collective-permute-start.2 = (bf16[64,1024]{1,0:T(8,128)(2,1)S(1)}, bf16[64,1024]{1,0:T(8,128)(2,1)S(1)}, u32[]{:S(2)}, u32[]{:S(2)}) collective-permute-start(bf16[64,1024]{1,0:T(8,128)(2,1)S(1)} %copy-done.5), channel_id=1, source_target_pairs={{2,0},{4,2},{6,4},{8,6},{10,8},{12,10},{14,12},{16,14},{18,16},{20... | collective-permute-start | bytes 393224 | tf_op jit(solution)/shard_map/ppermute | solution.py:631

commit v10 on v9

--- a/solution.py
+++ b/solution.py
@@ -97,6 +97,10 @@
     edge = real_edge[...].reshape(512, 2 * X)
     edge_ref[512:1024, :] = edge[:, 0:X]
     edge_ref[1024:1536, :] = edge[:, X : 2 * X]
+
+
+def wide_column(row, shift):
+    return jnp.broadcast_to(as_column(row, shift), (G, X))
 
 
 def cell_stats(ref, first, count):
@@ -274,11 +278,14 @@
         yield terms + dot(planes[half + 4], grad[0:128, :], (1, 1))
 
 
-def split_depth(at, places, halves, rows, patch):
-    base, stride = places
+def column_picker():
     column = lanes((2 * X, 4 * X))
     source = lax.broadcasted_iota(jnp.int32, (2 * X, 4 * X), 0)
-    pick = jnp.where(source == 2 * (column % X) + column // X - 1, 1.0, 0.0).astype(BF16)
+    return jnp.where(source == 2 * (column % X) + column // X - 1, 1.0, 0.0).astype(BF16)
+
+
+def split_depth(at, places, halves, rows, patch, pick):
+    base, stride = places
     edge = jnp.zeros((128, X), BF16)
     patch[at : at + 128, 0:X] = edge
     patch[at + 384 : at + 512, CELLS - X : CELLS] = edge
@@ -286,7 +293,7 @@
         for half in range(2):
             cells = halves[half, pl.ds(base + row, G, stride=stride), :].astype(BF16)
             rows[at + row * G : at + (row + 1) * G, half * X : (half + 1) * X] = cells
-    split = dot(rows[at : at + 512, :], pick).astype(BF16)
+    split = dot(rows[at : at + 512, :], pick[...]).astype(BF16)
     for row in range(2 * Y):
         for kx in range(4):
             piece = split[row * G : (row + 1) * G, kx * X : (kx + 1) * X]
@@ -314,6 +321,7 @@
     wide,
     first,
     terms_ref,
+    pick,
     sems,
     patch,
     lat_patch,
@@ -336,8 +344,9 @@
     places = ((2048, 16), (0, 64), (16, 64), (32, 64), (48, 64), (2560, 16))
 
     def build(depth):
-        split_depth(depth * 512, places[depth], halves, rows, patch)
-
+        split_depth(depth * 512, places[depth], halves, rows, patch, pick)
+
+    pick[...] = column_picker()
     build(4)
     edge_copy.wait()
     for half in range(2):
@@ -399,12 +408,12 @@
     depths = jnp.where(slab == 0, 5.0, jnp.where(slab == 31, 3.0, 4.0))
     mean_row = jnp.sum(stats * depths, axis=0, keepdims=True) * (1.0 / (4.0 * NDEV))
     off = stats - mean_row
-    between = as_column(jnp.sum(off * off * depths, axis=0, keepdims=True), 0)
-    center = as_column(mean_row, 0)
-    within = as_column(jnp.sum(stats, axis=0, keepdims=True), G)
+    between = wide_column(jnp.sum(off * off * depths, axis=0, keepdims=True), 0)
+    center = wide_column(mean_row, 0)
+    within = wide_column(jnp.sum(stats, axis=0, keepdims=True), G)
     variance = (within + 4.0 * CELLS * between) * (1.0 / (16.0 * CELLS * NDEV))
-    factor = as_column(stats[0:1, :], 2 * G) * lax.rsqrt(variance + 1e-05)
-    shift = as_column(stats[0:1, :], 3 * G)
+    factor = wide_column(stats[0:1, :], 2 * G) * lax.rsqrt(variance + 1e-05)
+    shift = wide_column(stats[0:1, :], 3 * G)
     lane = lanes((G, X))
     edge = jnp.zeros((128, X), BF16)
 
@@ -729,6 +738,7 @@
             pltpu.VMEM((256, 576), BF16),
             pltpu.VMEM((256, CELLS), F32),
             pltpu.VMEM((1024, 2 * C), F32),
+            pltpu.VMEM((2 * X, 4 * X), BF16),
             pltpu.SemaphoreType.DMA((8,)),
             pltpu.VMEM((6 * 512, CELLS), BF16),
             pltpu.VMEM((576, CELLS), BF16),

time: 94.1 us -> 94.1 us (level)
  no operation moved by 1% of the time
where the time goes in v10:
time: 94.1 us; the launch traced here: 93.2 us
  starting transfers between devices  43.8 us (47%)
  Pallas kernels  35.2 us (37%)
  waiting for transfers between devices  13.1 us (14%)
  between operations  1.02 us (1%)
    pallas_call x10, Pallas kernels, call(): pl.pallas_call(body, name=name, out_shape=outs, in_specs=[pl.BlockSpec(me...  35.2 us
    all_to_all x1, starting transfers between devices, local(): stats = lax.all_to_all(stats, AXES, 0, 0, tiled=True)  14.7 us
    ppermute x2, starting transfers between devices, to_next(): return lax.ppermute(edge, 'slab', [(i, i + 1) for i in range(ends)])  11.3 us
    all_to_all x1, starting transfers between devices, local(): parts = lax.all_to_all(terms.reshape(NDEV, 8, 128), AXES, 0, 0, tiled=True)  8.6 us
    ppermute x2, waiting for transfers between devices, to_prev(): return lax.ppermute(edge, 'slab', [(i + 1, i) for i in range(ends)])  7.73 us
    all_to_all x1, starting transfers between devices, local(): whole = lax.all_to_all(sums.reshape(NDEV, 8, 128), AXES, 0, 0, tiled=True)  6.63 us
    all_to_all x1, waiting for transfers between devices, local(): parts = lax.all_to_all(terms.reshape(NDEV, 8, 128), AXES, 0, 0, tiled=True)  4.12 us
    ppermute x2, starting transfers between devices, to_prev(): return lax.ppermute(edge, 'slab', [(i + 1, i) for i in range(ends)])  2.58 us
  transfers between devices with their start and end apart: 7, of which 4 were waited for; matrix products, arithmetic and copies ran while one was open for 0% of the time, Pallas kernels for 27%

profile of v10, /device:TPU:1, one launch (start us, length us, event | category | flops | bytes accessed | tf_op | source)
XLA Modules:
  0.0 93.2 jit_solution(890310538083363296)
XLA Ops:
  0.6 1.1 %edges.1 = bf16[1536,128]{1,0:T(8,128)(2,1)S(1)} custom-call(bf16[64,2,8,128]{3,2,1,0:T(8,128)(2,1)} %bitcast.36, bf16[32,4,16,256]{3,2,1,0:T(8,128)(2,1)} %bitcast.27), custom_call_target="tpu_custom_call" | custom-call | bytes 1703936 | tf_op jit(solution)/shard_map/edges/pallas_call | solution.py:620
  1.7 1.3 %collective-permute-start.1 = (bf16[1536,128]{1,0:T(8,128)(2,1)S(1)}, bf16[1536,128]{1,0:T(8,128)(2,1)S(1)}, u32[]{:S(2)}, u32[]{:S(2)}) collective-permute-start(bf16[1536,128]{1,0:T(8,128)(2,1)S(1)} %edges.1), channel_id=1, source_target_pairs={{2,0},{4,2},{6,4},{8,6},{10,8},{12,10},{14,12},{16,14},{18,16},{20... | collective-permute-start | bytes 1179656 | tf_op jit(solution)/shard_map/ppermute | solution.py:640
  3.0 4.6 %own_cells.1 = (bf16[2,256,576]{2,1,0:T(8,128)(2,1)}, f32[256,1024]{1,0:T(8,128)}, f32[256,1024]{1,0:T(8,128)}, f32[256,1024]{1,0:T(8,128)}, f32[32,128]{1,0:T(8...) custom-call(bf16[64,2,8,128]{3,2,1,0:T(8,128)(2,1)} %bitcast.37, bf16[32,4,16,256]{3,2,1,0:T(8,128)(2,1)} %bitcast.28, ...), custom_call_target="tpu_custom_call" | custom-call | flops 1207959552 | bytes 6242304 | tf_op jit(solution)/shard_map/own_cells/pallas_call | solution.py:620
  7.6 6.3 %collective-permute-start = (bf16[1536,128]{1,0:T(8,128)(2,1)S(1)}, bf16[1536,128]{1,0:T(8,128)(2,1)S(1)}, u32[]{:S(2)}, u32[]{:S(2)}) collective-permute-start(bf16[1536,128]{1,0:T(8,128)(2,1)S(1)} %get-tuple-element.28), channel_id=1, source_target_pairs={{0,2},{2,4},{4,6},{6,8},{8,10},{10,12},{12,14},{14,16},{16,18},{18... | collective-permute-start | bytes 1179656 | tf_op jit(solution)/shard_map/ppermute | solution.py:635
  13.9 0.1 add_convert_fusion.inside_ref
  14.0 1.9 %collective-permute-done.1.next_ref = bf16[1536,128]{1,0:T(8,128)(2,1)S(1)} collective-permute-done((bf16[1536,128]{1,0:T(8,128)(2,1)S(1)}, bf16[1536,128]{1,0:T(8,128)(2,1)S(1)}, u32[]{:S(2)}, u32[]{:S(2)}) %collective-permute-start.1) | collective-permute-done | bytes 393248 | tf_op jit(solution)/shard_map/ppermute | solution.py:640
  15.9 3.5 %rim_cells.1 = (f32[256,1024]{1,0:T(8,128)}, f32[128,128]{1,0:T(8,128)}, bf16[1024,128]{1,0:T(8,128)(2,1)}) custom-call(s32[2]{0:T(128)S(1)} %add_convert_fusion.inside_ref, bf16[1536,128]{1,0:T(8,128)(2,1)S(1)} %collective-permute-done.1.next_ref, f32[32,128]{1,0:T(8,128)S(1)} %get-tuple-element.29.sums_ref, f32[1,32]{1,0:T(1,128)} %bitcast.39, ...), custom_call_target="tpu_custom_call" | custom-call | flops 301989888 | bytes 3424520 | tf_op jit(solution)/shard_map/rim_cells/pallas_call | solution.py:620
  19.4 14.7 %all-to-all-start = ((f32[128,1,128]{2,1,0:T(1,128)}), f32[128,1,128]{2,1,0:T(1,128)S(1)}, u32[]{:S(2)}, u32[]{:S(2)}) async-start(f32[128,1,128]{2,1,0:T(1,128)} %bitcast.38), calls=%async_computation | async-start | bytes 131072 | tf_op jit(solution)/shard_map/all_to_all | solution.py:715
  34.1 0.0 copy-start.3
  34.1 8.3 %real_branch.1 = (bf16[1024,128]{1,0:T(8,128)(2,1)}, f32[1024,128]{1,0:T(8,128)}, f32[256,1024]{1,0:T(8,128)}) custom-call(bf16[2048,256]{1,0:T(8,128)(2,1)S(1)} %bitcast.29, bf16[1536,128]{1,0:T(8,128)(2,1)S(1)} %collective-permute-done.prev_ref, bf16[1024,128]{1,0:T(8,128)(2,1)} %get-tuple-element.32.next_in, ...), custom_call_target="tpu_custom_call" | custom-call | flops 2147483648 | bytes 5701632 | tf_op jit(solution)/shard_map/real_branch/pallas_call | solution.py:620
  42.4 1.2 %all-to-all-done = f32[128,1,128]{2,1,0:T(1,128)S(1)} async-done(((f32[128,1,128]{2,1,0:T(1,128)}), f32[128,1,128]{2,1,0:T(1,128)S(1)}, u32[]{:S(2)}, u32[]{:S(2)}) %all-to-all-start) | async-done | bytes 65568 | tf_op jit(solution)/shard_map/all_to_all | solution.py:715
  43.6 7.2 %fake_branch.1 = (bf16[1024,128]{1,0:T(8,128)(2,1)}, bf16[64,1024]{1,0:T(8,128)(2,1)}, bf16[64,1024]{1,0:T(8,128)(2,1)}, f32[1024,128]{1,0:T(8,128)}) custom-call(s32[2]{0:T(128)S(1)} %add_convert_fusion.inside_ref, f32[256,1024]{1,0:T(8,128)} %get-tuple-element.35.first_in, f32[256,1024]{1,0:T(8,128)} %get-tuple-element.36.middle_in, ...), custom_call_target="tpu_custom_call" | custom-call | flops 2147483648 | bytes 5308424 | tf_op jit(solution)/shard_map/fake_branch/pallas_call | solution.py:620
  50.9 8.6 %all-to-all-start.1 = ((f32[128,8,128]{2,1,0:T(8,128)}), f32[128,8,128]{2,1,0:T(8,128)S(1)}, u32[]{:S(2)}, u32[]{:S(2)}) async-start(f32[128,8,128]{2,1,0:T(8,128)} %bitcast.35), calls=%async_computation.1 | async-start | bytes 1048576 | tf_op jit(solution)/shard_map/all_to_all | solution.py:790
  59.5 5.0 %collective-permute-start.3 = (bf16[64,1024]{1,0:T(8,128)(2,1)S(1)}, bf16[64,1024]{1,0:T(8,128)(2,1)S(1)}, u32[]{:S(2)}, u32[]{:S(2)}) collective-permute-start(bf16[64,1024]{1,0:T(8,128)(2,1)S(1)} %copy-done.6), channel_id=1, source_target_pairs={{0,2},{2,4},{4,6},{6,8},{8,10},{10,12},{12,14},{14,16},{16,18},{18... | collective-permute-start | bytes 393224 | tf_op jit(solution)/shard_map/ppermute | solution.py:635
  64.5 4.5 %pull_own.1 = (bf16[2,256,576]{2,1,0:T(8,128)(2,1)}, f32[128,1024]{1,0:T(8,128)}, f32[128,1024]{1,0:T(8,128)}, bf16[32,64,256]{2,1,0:T(8,128)(2,1)}) custom-call(bf16[64,1024]{1,0:T(8,128)(2,1)} %get-tuple-element.42.low_in, bf16[64,1024]{1,0:T(8,128)(2,1)} %get-tuple-element.43.high_in, bf16[2048,64]{1,0:T(8,128)(2,1)} %bitcast.43), custom_call_target="tpu_custom_call" | custom-call | flops 905969664 | bytes 3211264 | tf_op jit(solution)/shard_map/pull_own/pallas_call | solution.py:620
  69.0 0.0 collective-permute-done.3.prev_ref.edge_in
  69.0 4.1 %all-to-all-done.1 = f32[128,8,128]{2,1,0:T(8,128)S(1)} async-done(((f32[128,8,128]{2,1,0:T(8,128)}), f32[128,8,128]{2,1,0:T(8,128)S(1)}, u32[]{:S(2)}, u32[]{:S(2)}) %all-to-all-start.1) | async-done | bytes 524320 | tf_op jit(solution)/shard_map/all_to_all | solution.py:790
  73.2 0.8 sum_terms.1.sums_ref
  74.0 6.6 %all-to-all-start.2 = ((bf16[128,8,128]{2,1,0:T(8,128)(2,1)}), bf16[128,8,128]{2,1,0:T(8,128)(2,1)S(1)}, u32[]{:S(2)}, u32[]{:S(2)}) async-start(bf16[128,8,128]{2,1,0:T(8,128)(2,1)} %bitcast.20), calls=%async_computation.2 | async-start | bytes 524288 | tf_op jit(solution)/shard_map/all_to_all | solution.py:829
  80.7 1.3 %collective-permute-start.2 = (bf16[64,1024]{1,0:T(8,128)(2,1)S(1)}, bf16[64,1024]{1,0:T(8,128)(2,1)S(1)}, u32[]{:S(2)}, u32[]{:S(2)}) collective-permute-start(bf16[64,1024]{1,0:T(8,128)(2,1)S(1)} %copy-done.5), channel_id=1, source_target_pairs={{2,0},{4,2},{6,4},{8,6},{10,8},{12,10},{14,12},{16,14},{18,16},{20... | collective-permute-start | bytes 393224 | tf_op jit(solution)/shard_map/ppermute | solution.py:640
  82.0 2.7 %pull_prev.1 = (bf16[32,64,256]{2,1,0:T(8,128)(2,1)}, bf16[256,576]{1,0:T(8,128)(2,1)S(1)}, f32[128,1024]{1,0:T(8,128)S(1)}) custom-call(bf16[64,1024]{1,0:T(8,128)(2,1)} %copy-done.4, bf16[2,256,576]{2,1,0:T(8,128)(2,1)} %get-tuple-element.44.wide_in, f32[128,1024]{1,0:T(8,128)} %get-tuple-element.45.first_ref.first_in, ...), custom_call_target="tpu_custom_call", output_to_operand_aliasing={{0}: (5, {})} | custom-call | flops 150994944 | bytes 4947968 | tf_op jit(solution)/shard_map/pull_prev/pallas_call | solution.py:620
  84.7 5.8 %collective-permute-done.2.edge_ref = bf16[64,1024]{1,0:T(8,128)(2,1)S(1)} collective-permute-done((bf16[64,1024]{1,0:T(8,128)(2,1)S(1)}, bf16[64,1024]{1,0:T(8,128)(2,1)S(1)}, u32[]{:S(2)}, u32[]{:S(2)}) %collective-permute-start.2) | collective-permute-done | bytes 131104 | tf_op jit(solution)/shard_map/ppermute | solution.py:640
  90.5 1.4 %pull_next.1 = bf16[32,64,256]{2,1,0:T(8,128)(2,1)} custom-call(bf16[64,1024]{1,0:T(8,128)(2,1)S(1)} %collective-permute-done.2.edge_ref, bf16[256,576]{1,0:T(8,128)(2,1)S(1)} %get-tuple-element.49.wide_ref, f32[128,1024]{1,0:T(8,128)S(1)} %get-tuple-element.50.last_ref, bf16[32,64,256]{2,1,0:T(8,128)(2,1)} %get-tuple-element.51.image_in), custom_call_target="tpu_custom_call", output_to_operand_aliasing={{}: (3, {})} | custom-call | flops 150994944 | bytes 3047424 | tf_op jit(solution)/shard_map/pull_next/pallas_call | solution.py:620
  91.9 1.1 %unpack.1 = f32[2,1024,64]{2,1,0:T(8,128)} custom-call(bf16[1024,128]{1,0:T(8,128)(2,1)S(1)} %bitcast.26), custom_call_target="tpu_custom_call" | custom-call | bytes 786432 | tf_op jit(solution)/shard_map/unpack/pallas_call | solution.py:620
  (15 shorter events, 0.0 us)
Async XLA Ops:
  1.7 14.2 %collective-permute-start.1 = (bf16[1536,128]{1,0:T(8,128)(2,1)S(1)}, bf16[1536,128]{1,0:T(8,128)(2,1)S(1)}, u32[]{:S(2)}, u32[]{:S(2)}) collective-permute-start(bf16[1536,128]{1,0:T(8,128)(2,1)S(1)} %edges.1), channel_id=1, source_target_pairs={{2,0},{4,2},{6,4},{8,6},{10,8},{12,10},{14,12},{16,14},{18,16},{20... | collective-permute-start | bytes 1179656 | tf_op jit(solution)/shard_map/ppermute | solution.py:640
  7.6 26.5 %collective-permute-start = (bf16[1536,128]{1,0:T(8,128)(2,1)S(1)}, bf16[1536,128]{1,0:T(8,128)(2,1)S(1)}, u32[]{:S(2)}, u32[]{:S(2)}) collective-permute-start(bf16[1536,128]{1,0:T(8,128)(2,1)S(1)} %get-tuple-element.28), channel_id=1, source_target_pairs={{0,2},{2,4},{4,6},{6,8},{8,10},{10,12},{12,14},{14,16},{16,18},{18... | collective-permute-start | bytes 1179656 | tf_op jit(solution)/shard_map/ppermute | solution.py:635
  15.9 18.2 %copy-start = (bf16[1,32,4,16,256]{4,3,2,1,0:T(8,128)(2,1)S(1)}, bf16[1,32,4,16,256]{4,3,2,1,0:T(8,128)(2,1)}, u32[]{:S(2)}) copy-start(bf16[1,32,4,16,256]{4,3,2,1,0:T(8,128)(2,1)} %param.12) | copy-start | bytes 3145732
  15.9 18.2 %copy-start.2 = (bf16[1,64,2,8,128]{4,3,2,1,0:T(8,128)(2,1)S(1)}, bf16[1,64,2,8,128]{4,3,2,1,0:T(8,128)(2,1)}, u32[]{:S(2)}) copy-start(bf16[1,64,2,8,128]{4,3,2,1,0:T(8,128)(2,1)} %param.15) | copy-start | bytes 786436
  19.4 24.2 %all-to-all-start = ((f32[128,1,128]{2,1,0:T(1,128)}), f32[128,1,128]{2,1,0:T(1,128)S(1)}, u32[]{:S(2)}, u32[]{:S(2)}) async-start(f32[128,1,128]{2,1,0:T(1,128)} %bitcast.38), calls=%async_computation | async-start | bytes 131072 | tf_op jit(solution)/shard_map/all_to_all | solution.py:715
  34.1 9.5 %copy-start.1 = (f32[256,1024]{1,0:T(8,128)S(1)}, f32[256,1024]{1,0:T(8,128)}, u32[]{:S(2)}) copy-start(f32[256,1024]{1,0:T(8,128)} %get-tuple-element.37.last_ref) | copy-start | bytes 3145732
  34.1 9.5 %copy-start.3 = (bf16[1,64,2,8,128]{4,3,2,1,0:T(8,128)(2,1)S(1)}, bf16[1,64,2,8,128]{4,3,2,1,0:T(8,128)(2,1)}, u32[]{:S(2)}) copy-start(bf16[1,64,2,8,128]{4,3,2,1,0:T(8,128)(2,1)} %param.14) | copy-start | bytes 786436
  50.9 8.6 %copy-start.6 = (bf16[64,1024]{1,0:T(8,128)(2,1)S(1)}, bf16[64,1024]{1,0:T(8,128)(2,1)}, u32[]{:S(2)}) copy-start(bf16[64,1024]{1,0:T(8,128)(2,1)} %get-tuple-element.43.high_in) | copy-start | bytes 393220
  50.9 22.3 %all-to-all-start.1 = ((f32[128,8,128]{2,1,0:T(8,128)}), f32[128,8,128]{2,1,0:T(8,128)S(1)}, u32[]{:S(2)}, u32[]{:S(2)}) async-start(f32[128,8,128]{2,1,0:T(8,128)} %bitcast.35), calls=%async_computation.1 | async-start | bytes 1048576 | tf_op jit(solution)/shard_map/all_to_all | solution.py:790
  59.5 9.5 %collective-permute-start.3 = (bf16[64,1024]{1,0:T(8,128)(2,1)S(1)}, bf16[64,1024]{1,0:T(8,128)(2,1)S(1)}, u32[]{:S(2)}, u32[]{:S(2)}) collective-permute-start(bf16[64,1024]{1,0:T(8,128)(2,1)S(1)} %copy-done.6), channel_id=1, source_target_pairs={{0,2},{2,4},{4,6},{6,8},{8,10},{10,12},{12,14},{14,16},{16,18},{18... | collective-permute-start | bytes 393224 | tf_op jit(solution)/shard_map/ppermute | solution.py:635
  69.0 4.1 %copy-start.4 = (bf16[64,1024]{1,0:T(8,128)(2,1)}, bf16[64,1024]{1,0:T(8,128)(2,1)S(1)}, u32[]{:S(2)}) copy-start(bf16[64,1024]{1,0:T(8,128)(2,1)S(1)} %collective-permute-done.3.prev_ref.edge_in) | copy-start | bytes 393220
  74.0 6.6 %copy-start.5 = (bf16[64,1024]{1,0:T(8,128)(2,1)S(1)}, bf16[64,1024]{1,0:T(8,128)(2,1)}, u32[]{:S(2)}) copy-start(bf16[64,1024]{1,0:T(8,128)(2,1)} %get-tuple-element.42.low_in) | copy-start | bytes 393220
  74.0 17.9 %all-to-all-start.2 = ((bf16[128,8,128]{2,1,0:T(8,128)(2,1)}), bf16[128,8,128]{2,1,0:T(8,128)(2,1)S(1)}, u32[]{:S(2)}, u32[]{:S(2)}) async-start(bf16[128,8,128]{2,1,0:T(8,128)(2,1)} %bitcast.20), calls=%async_computation.2 | async-start | bytes 524288 | tf_op jit(solution)/shard_map/all_to_all | solution.py:829
  80.7 9.8 %collective-permute-start.2 = (bf16[64,1024]{1,0:T(8,128)(2,1)S(1)}, bf16[64,1024]{1,0:T(8,128)(2,1)S(1)}, u32[]{:S(2)}, u32[]{:S(2)}) collective-permute-start(bf16[64,1024]{1,0:T(8,128)(2,1)S(1)} %copy-done.5), channel_id=1, source_target_pairs={{2,0},{4,2},{6,4},{8,6},{10,8},{12,10},{14,12},{16,14},{18,16},{20... | collective-permute-start | bytes 393224 | tf_op jit(solution)/shard_map/ppermute | solution.py:640

commit v11 on v9

--- a/solution.py
+++ b/solution.py
@@ -241,30 +241,34 @@
     return (output, derivative)
 
 
-def convolve(weight_ref, patch, build):
+def convolve(weight_ref, patch, build, finish):
     early = weight_ref[:, 0:1024]
     late = weight_ref[:, 1024:2048]
     second = dot(late, patch[2048:3072, :])
     build(2)
     build(3)
     shared = dot(jnp.concatenate([late, early], axis=0), patch[1024:2048, :])
+    finish(1, second + shared[C : 2 * C, :])
     build(0)
     build(1)
-    return dot(early, patch[0:1024, :]) + shared[0:C, :], second + shared[C : 2 * C, :]
-
-
-def finish(pre, cot_ref, out, wide_cot, wide_out, grad):
-    wide_cot[...] = cot_ref[...].astype(F32)
+    finish(0, dot(early, patch[0:1024, :]) + shared[0:C, :])
+
+
+def finisher(cot_ref, wide_cot, wide_out, grad):
     nothing = jnp.zeros((C, CELLS), BF16)
     grad[0:C, :] = nothing
     grad[3 * C : 4 * C, :] = nothing
-    for m in range(2):
+
+    def finish(m, pre):
+        if m == 1:
+            wide_cot[...] = cot_ref[...].astype(F32)
         for y in range(Y):
-            output, slope = activate(pre[m][:, y * X : (y + 1) * X])
+            output, slope = activate(pre[:, y * X : (y + 1) * X])
             wide_out[pl.ds(m * Y + y, C, stride=16), :] = output
             cot = wide_cot[pl.ds(m * Y + y, C, stride=16), :]
             grad[(2 - m) * C : (3 - m) * C, y * X : (y + 1) * X] = (cot * slope).astype(BF16)
-    out[...] = wide_out[...].astype(BF16)
+
+    return finish
 
 
 def kernel_terms(planes, grad):
@@ -344,7 +348,7 @@
         halves[half, 2560:3072, :] = edge[half * 512 : (half + 1) * 512, :].astype(F32)
     build(5)
     weight_copy.wait()
-    pre = convolve(weight, patch, build)
+    convolve(weight, patch, build, finisher(cot_ref, wide_cot, wide_out, grad))
     halves[0, 0:512, :] = prev_ref[0:512, :].astype(F32)
     lane = lanes((C, X))
     clear_rims(0, lat_patch)
@@ -354,7 +358,7 @@
         copy.wait()
     first[...] += dot(wide[...], lat_patch[...])
     first_copy = fetch(first, first_out, sems.at[4])
-    finish(pre, cot_ref, out, wide_cot, wide_out, grad)
+    out[...] = wide_out[...].astype(BF16)
     stores = [first_copy, fetch(out, out_out, sems.at[5])]
     planes = [patch[depth * 512 : (depth + 1) * 512, :] for depth in range(6)]
     for half, terms in enumerate(kernel_terms(planes, grad)):
@@ -440,8 +444,8 @@
     build(4)
     build(5)
     weight_copy.wait()
-    pre = convolve(weight_ref, patch, build)
-    finish(pre, cot_ref, out, wide_cot, wide_out, grad)
+    convolve(weight_ref, patch, build, finisher(cot_ref, wide_cot, wide_out, grad))
+    out[...] = wide_out[...].astype(BF16)
     stores = [
         fetch(out, out_out, sems.at[6]),
         fetch(grad.at[2 * C : 3 * C], low_out, sems.at[2]),

time: 94.1 us -> 94.4 us (level)
  no operation moved by 1% of the time
where the time goes in v11:
time: 94.4 us; the launch traced here: 93.6 us
  starting transfers between devices  44.1 us (47%)
  Pallas kernels  35.6 us (38%)
  waiting for transfers between devices  12.8 us (14%)
  between operations  1.02 us (1%)
    pallas_call x10, Pallas kernels, call(): pl.pallas_call(body, name=name, out_shape=outs, in_specs=[pl.BlockSpec(me...  35.6 us
    all_to_all x1, starting transfers between devices, local(): stats = lax.all_to_all(stats, AXES, 0, 0, tiled=True)  14.7 us
    ppermute x2, starting transfers between devices, to_next(): return lax.ppermute(edge, 'slab', [(i, i + 1) for i in range(ends)])  11.3 us
    all_to_all x1, starting transfers between devices, local(): parts = lax.all_to_all(terms.reshape(NDEV, 8, 128), AXES, 0, 0, tiled=True)  8.87 us
    ppermute x2, waiting for transfers between devices, to_prev(): return lax.ppermute(edge, 'slab', [(i + 1, i) for i in range(ends)])  7.73 us
    all_to_all x1, starting transfers between devices, local(): whole = lax.all_to_all(sums.reshape(NDEV, 8, 128), AXES, 0, 0, tiled=True)  6.63 us
    all_to_all x1, waiting for transfers between devices, local(): parts = lax.all_to_all(terms.reshape(NDEV, 8, 128), AXES, 0, 0, tiled=True)  4.12 us
    ppermute x2, starting transfers between devices, to_prev(): return lax.ppermute(edge, 'slab', [(i + 1, i) for i in range(ends)])  2.58 us
  transfers between devices with their start and end apart: 7, of which 4 were waited for; matrix products, arithmetic and copies ran while one was open for 0% of the time, Pallas kernels for 27%

profile of v11, /device:TPU:1, one launch (start us, length us, event | category | flops | bytes accessed | tf_op | source)
XLA Modules:
  0.0 93.6 jit_solution(13667292595543277812)
XLA Ops:
  0.6 1.1 %edges.1 = bf16[1536,128]{1,0:T(8,128)(2,1)S(1)} custom-call(bf16[64,2,8,128]{3,2,1,0:T(8,128)(2,1)} %bitcast.36, bf16[32,4,16,256]{3,2,1,0:T(8,128)(2,1)} %bitcast.27), custom_call_target="tpu_custom_call" | custom-call | bytes 1703936 | tf_op jit(solution)/shard_map/edges/pallas_call | solution.py:615
  1.7 1.3 %collective-permute-start.1 = (bf16[1536,128]{1,0:T(8,128)(2,1)S(1)}, bf16[1536,128]{1,0:T(8,128)(2,1)S(1)}, u32[]{:S(2)}, u32[]{:S(2)}) collective-permute-start(bf16[1536,128]{1,0:T(8,128)(2,1)S(1)} %edges.1), channel_id=1, source_target_pairs={{2,0},{4,2},{6,4},{8,6},{10,8},{12,10},{14,12},{16,14},{18,16},{20... | collective-permute-start | bytes 1179656 | tf_op jit(solution)/shard_map/ppermute | solution.py:635
  3.0 4.6 %own_cells.1 = (bf16[2,256,576]{2,1,0:T(8,128)(2,1)}, f32[256,1024]{1,0:T(8,128)}, f32[256,1024]{1,0:T(8,128)}, f32[256,1024]{1,0:T(8,128)}, f32[32,128]{1,0:T(8...) custom-call(bf16[64,2,8,128]{3,2,1,0:T(8,128)(2,1)} %bitcast.37, bf16[32,4,16,256]{3,2,1,0:T(8,128)(2,1)} %bitcast.28, ...), custom_call_target="tpu_custom_call" | custom-call | flops 1207959552 | bytes 6242304 | tf_op jit(solution)/shard_map/own_cells/pallas_call | solution.py:615
  7.6 6.3 %collective-permute-start = (bf16[1536,128]{1,0:T(8,128)(2,1)S(1)}, bf16[1536,128]{1,0:T(8,128)(2,1)S(1)}, u32[]{:S(2)}, u32[]{:S(2)}) collective-permute-start(bf16[1536,128]{1,0:T(8,128)(2,1)S(1)} %get-tuple-element.28), channel_id=1, source_target_pairs={{0,2},{2,4},{4,6},{6,8},{8,10},{10,12},{12,14},{14,16},{16,18},{18... | collective-permute-start | bytes 1179656 | tf_op jit(solution)/shard_map/ppermute | solution.py:630
  13.9 0.1 add_convert_fusion.inside_ref
  14.0 1.9 %collective-permute-done.1.next_ref = bf16[1536,128]{1,0:T(8,128)(2,1)S(1)} collective-permute-done((bf16[1536,128]{1,0:T(8,128)(2,1)S(1)}, bf16[1536,128]{1,0:T(8,128)(2,1)S(1)}, u32[]{:S(2)}, u32[]{:S(2)}) %collective-permute-start.1) | collective-permute-done | bytes 393248 | tf_op jit(solution)/shard_map/ppermute | solution.py:635
  15.9 3.5 %rim_cells.1 = (f32[256,1024]{1,0:T(8,128)}, f32[128,128]{1,0:T(8,128)}, bf16[1024,128]{1,0:T(8,128)(2,1)}) custom-call(s32[2]{0:T(128)S(1)} %add_convert_fusion.inside_ref, bf16[1536,128]{1,0:T(8,128)(2,1)S(1)} %collective-permute-done.1.next_ref, f32[32,128]{1,0:T(8,128)S(1)} %get-tuple-element.29.sums_ref, f32[1,32]{1,0:T(1,128)} %bitcast.39, ...), custom_call_target="tpu_custom_call" | custom-call | flops 301989888 | bytes 3424520 | tf_op jit(solution)/shard_map/rim_cells/pallas_call | solution.py:615
  19.4 14.7 %all-to-all-start = ((f32[128,1,128]{2,1,0:T(1,128)}), f32[128,1,128]{2,1,0:T(1,128)S(1)}, u32[]{:S(2)}, u32[]{:S(2)}) async-start(f32[128,1,128]{2,1,0:T(1,128)} %bitcast.38), calls=%async_computation | async-start | bytes 131072 | tf_op jit(solution)/shard_map/all_to_all | solution.py:710
  34.1 0.0 copy-start.3
  34.1 8.6 %real_branch.1 = (bf16[1024,128]{1,0:T(8,128)(2,1)}, f32[1024,128]{1,0:T(8,128)}, f32[256,1024]{1,0:T(8,128)}) custom-call(bf16[2048,256]{1,0:T(8,128)(2,1)S(1)} %bitcast.29, bf16[1536,128]{1,0:T(8,128)(2,1)S(1)} %collective-permute-done.prev_ref, bf16[1024,128]{1,0:T(8,128)(2,1)} %get-tuple-element.32.next_in, ...), custom_call_target="tpu_custom_call" | custom-call | flops 2147483648 | bytes 5701632 | tf_op jit(solution)/shard_map/real_branch/pallas_call | solution.py:615
  42.7 0.9 all-to-all-done
  43.6 7.3 %fake_branch.1 = (bf16[1024,128]{1,0:T(8,128)(2,1)}, bf16[64,1024]{1,0:T(8,128)(2,1)}, bf16[64,1024]{1,0:T(8,128)(2,1)}, f32[1024,128]{1,0:T(8,128)}) custom-call(s32[2]{0:T(128)S(1)} %add_convert_fusion.inside_ref, f32[256,1024]{1,0:T(8,128)} %get-tuple-element.35.first_in, f32[256,1024]{1,0:T(8,128)} %get-tuple-element.36.middle_in, ...), custom_call_target="tpu_custom_call" | custom-call | flops 2147483648 | bytes 5308424 | tf_op jit(solution)/shard_map/fake_branch/pallas_call | solution.py:615
  51.0 8.9 %all-to-all-start.1 = ((f32[128,8,128]{2,1,0:T(8,128)}), f32[128,8,128]{2,1,0:T(8,128)S(1)}, u32[]{:S(2)}, u32[]{:S(2)}) async-start(f32[128,8,128]{2,1,0:T(8,128)} %bitcast.35), calls=%async_computation.1 | async-start | bytes 1048576 | tf_op jit(solution)/shard_map/all_to_all | solution.py:784
  59.8 5.0 %collective-permute-start.3 = (bf16[64,1024]{1,0:T(8,128)(2,1)S(1)}, bf16[64,1024]{1,0:T(8,128)(2,1)S(1)}, u32[]{:S(2)}, u32[]{:S(2)}) collective-permute-start(bf16[64,1024]{1,0:T(8,128)(2,1)S(1)} %copy-done.6), channel_id=1, source_target_pairs={{0,2},{2,4},{4,6},{6,8},{8,10},{10,12},{12,14},{14,16},{16,18},{18... | collective-permute-start | bytes 393224 | tf_op jit(solution)/shard_map/ppermute | solution.py:630
  64.9 4.5 %pull_own.1 = (bf16[2,256,576]{2,1,0:T(8,128)(2,1)}, f32[128,1024]{1,0:T(8,128)}, f32[128,1024]{1,0:T(8,128)}, bf16[32,64,256]{2,1,0:T(8,128)(2,1)}) custom-call(bf16[64,1024]{1,0:T(8,128)(2,1)} %get-tuple-element.42.low_in, bf16[64,1024]{1,0:T(8,128)(2,1)} %get-tuple-element.43.high_in, bf16[2048,64]{1,0:T(8,128)(2,1)} %bitcast.43), custom_call_target="tpu_custom_call" | custom-call | flops 905969664 | bytes 3211264 | tf_op jit(solution)/shard_map/pull_own/pallas_call | solution.py:615
  69.3 0.0 collective-permute-done.3.prev_ref.edge_in
  69.4 4.1 %all-to-all-done.1 = f32[128,8,128]{2,1,0:T(8,128)S(1)} async-done(((f32[128,8,128]{2,1,0:T(8,128)}), f32[128,8,128]{2,1,0:T(8,128)S(1)}, u32[]{:S(2)}, u32[]{:S(2)}) %all-to-all-start.1) | async-done | bytes 524320 | tf_op jit(solution)/shard_map/all_to_all | solution.py:784
  73.5 0.8 sum_terms.1.sums_ref
  74.3 6.6 %all-to-all-start.2 = ((bf16[128,8,128]{2,1,0:T(8,128)(2,1)}), bf16[128,8,128]{2,1,0:T(8,128)(2,1)S(1)}, u32[]{:S(2)}, u32[]{:S(2)}) async-start(bf16[128,8,128]{2,1,0:T(8,128)(2,1)} %bitcast.20), calls=%async_computation.2 | async-start | bytes 524288 | tf_op jit(solution)/shard_map/all_to_all | solution.py:823
  81.0 1.3 %collective-permute-start.2 = (bf16[64,1024]{1,0:T(8,128)(2,1)S(1)}, bf16[64,1024]{1,0:T(8,128)(2,1)S(1)}, u32[]{:S(2)}, u32[]{:S(2)}) collective-permute-start(bf16[64,1024]{1,0:T(8,128)(2,1)S(1)} %copy-done.5), channel_id=1, source_target_pairs={{2,0},{4,2},{6,4},{8,6},{10,8},{12,10},{14,12},{16,14},{18,16},{20... | collective-permute-start | bytes 393224 | tf_op jit(solution)/shard_map/ppermute | solution.py:635
  82.3 2.7 %pull_prev.1 = (bf16[32,64,256]{2,1,0:T(8,128)(2,1)}, bf16[256,576]{1,0:T(8,128)(2,1)S(1)}, f32[128,1024]{1,0:T(8,128)S(1)}) custom-call(bf16[64,1024]{1,0:T(8,128)(2,1)} %copy-done.4, bf16[2,256,576]{2,1,0:T(8,128)(2,1)} %get-tuple-element.44.wide_in, f32[128,1024]{1,0:T(8,128)} %get-tuple-element.45.first_ref.first_in, ...), custom_call_target="tpu_custom_call", output_to_operand_aliasing={{0}: (5, {})} | custom-call | flops 150994944 | bytes 4947968 | tf_op jit(solution)/shard_map/pull_prev/pallas_call | solution.py:615
  85.0 5.8 %collective-permute-done.2.edge_ref = bf16[64,1024]{1,0:T(8,128)(2,1)S(1)} collective-permute-done((bf16[64,1024]{1,0:T(8,128)(2,1)S(1)}, bf16[64,1024]{1,0:T(8,128)(2,1)S(1)}, u32[]{:S(2)}, u32[]{:S(2)}) %collective-permute-start.2) | collective-permute-done | bytes 131104 | tf_op jit(solution)/shard_map/ppermute | solution.py:635
  90.8 1.4 %pull_next.1 = bf16[32,64,256]{2,1,0:T(8,128)(2,1)} custom-call(bf16[64,1024]{1,0:T(8,128)(2,1)S(1)} %collective-permute-done.2.edge_ref, bf16[256,576]{1,0:T(8,128)(2,1)S(1)} %get-tuple-element.49.wide_ref, f32[128,1024]{1,0:T(8,128)S(1)} %get-tuple-element.50.last_ref, bf16[32,64,256]{2,1,0:T(8,128)(2,1)} %get-tuple-element.51.image_in), custom_call_target="tpu_custom_call", output_to_operand_aliasing={{}: (3, {})} | custom-call | flops 150994944 | bytes 3047424 | tf_op jit(solution)/shard_map/pull_next/pallas_call | solution.py:615
  92.3 1.1 %unpack.1 = f32[2,1024,64]{2,1,0:T(8,128)} custom-call(bf16[1024,128]{1,0:T(8,128)(2,1)S(1)} %bitcast.26), custom_call_target="tpu_custom_call" | custom-call | bytes 786432 | tf_op jit(solution)/shard_map/unpack/pallas_call | solution.py:615
  (15 shorter events, 0.0 us)
Async XLA Ops:
  1.7 14.2 %collective-permute-start.1 = (bf16[1536,128]{1,0:T(8,128)(2,1)S(1)}, bf16[1536,128]{1,0:T(8,128)(2,1)S(1)}, u32[]{:S(2)}, u32[]{:S(2)}) collective-permute-start(bf16[1536,128]{1,0:T(8,128)(2,1)S(1)} %edges.1), channel_id=1, source_target_pairs={{2,0},{4,2},{6,4},{8,6},{10,8},{12,10},{14,12},{16,14},{18,16},{20... | collective-permute-start | bytes 1179656 | tf_op jit(solution)/shard_map/ppermute | solution.py:635
  7.6 26.5 %collective-permute-start = (bf16[1536,128]{1,0:T(8,128)(2,1)S(1)}, bf16[1536,128]{1,0:T(8,128)(2,1)S(1)}, u32[]{:S(2)}, u32[]{:S(2)}) collective-permute-start(bf16[1536,128]{1,0:T(8,128)(2,1)S(1)} %get-tuple-element.28), channel_id=1, source_target_pairs={{0,2},{2,4},{4,6},{6,8},{8,10},{10,12},{12,14},{14,16},{16,18},{18... | collective-permute-start | bytes 1179656 | tf_op jit(solution)/shard_map/ppermute | solution.py:630
  15.9 18.2 %copy-start = (bf16[1,32,4,16,256]{4,3,2,1,0:T(8,128)(2,1)S(1)}, bf16[1,32,4,16,256]{4,3,2,1,0:T(8,128)(2,1)}, u32[]{:S(2)}) copy-start(bf16[1,32,4,16,256]{4,3,2,1,0:T(8,128)(2,1)} %param.12) | copy-start | bytes 3145732
  15.9 18.2 %copy-start.2 = (bf16[1,64,2,8,128]{4,3,2,1,0:T(8,128)(2,1)S(1)}, bf16[1,64,2,8,128]{4,3,2,1,0:T(8,128)(2,1)}, u32[]{:S(2)}) copy-start(bf16[1,64,2,8,128]{4,3,2,1,0:T(8,128)(2,1)} %param.15) | copy-start | bytes 786436
  19.4 24.2 %all-to-all-start = ((f32[128,1,128]{2,1,0:T(1,128)}), f32[128,1,128]{2,1,0:T(1,128)S(1)}, u32[]{:S(2)}, u32[]{:S(2)}) async-start(f32[128,1,128]{2,1,0:T(1,128)} %bitcast.38), calls=%async_computation | async-start | bytes 131072 | tf_op jit(solution)/shard_map/all_to_all | solution.py:710
  34.1 9.5 %copy-start.1 = (f32[256,1024]{1,0:T(8,128)S(1)}, f32[256,1024]{1,0:T(8,128)}, u32[]{:S(2)}) copy-start(f32[256,1024]{1,0:T(8,128)} %get-tuple-element.37.last_ref) | copy-start | bytes 3145732
  34.1 9.5 %copy-start.3 = (bf16[1,64,2,8,128]{4,3,2,1,0:T(8,128)(2,1)S(1)}, bf16[1,64,2,8,128]{4,3,2,1,0:T(8,128)(2,1)}, u32[]{:S(2)}) copy-start(bf16[1,64,2,8,128]{4,3,2,1,0:T(8,128)(2,1)} %param.14) | copy-start | bytes 786436
  50.9 8.9 %copy-start.6 = (bf16[64,1024]{1,0:T(8,128)(2,1)S(1)}, bf16[64,1024]{1,0:T(8,128)(2,1)}, u32[]{:S(2)}) copy-start(bf16[64,1024]{1,0:T(8,128)(2,1)} %get-tuple-element.43.high_in) | copy-start | bytes 393220
  51.0 22.5 %all-to-all-start.1 = ((f32[128,8,128]{2,1,0:T(8,128)}), f32[128,8,128]{2,1,0:T(8,128)S(1)}, u32[]{:S(2)}, u32[]{:S(2)}) async-start(f32[128,8,128]{2,1,0:T(8,128)} %bitcast.35), calls=%async_computation.1 | async-start | bytes 1048576 | tf_op jit(solution)/shard_map/all_to_all | solution.py:784
  59.8 9.5 %collective-permute-start.3 = (bf16[64,1024]{1,0:T(8,128)(2,1)S(1)}, bf16[64,1024]{1,0:T(8,128)(2,1)S(1)}, u32[]{:S(2)}, u32[]{:S(2)}) collective-permute-start(bf16[64,1024]{1,0:T(8,128)(2,1)S(1)} %copy-done.6), channel_id=1, source_target_pairs={{0,2},{2,4},{4,6},{6,8},{8,10},{10,12},{12,14},{14,16},{16,18},{18... | collective-permute-start | bytes 393224 | tf_op jit(solution)/shard_map/ppermute | solution.py:630
  69.4 4.1 %copy-start.4 = (bf16[64,1024]{1,0:T(8,128)(2,1)}, bf16[64,1024]{1,0:T(8,128)(2,1)S(1)}, u32[]{:S(2)}) copy-start(bf16[64,1024]{1,0:T(8,128)(2,1)S(1)} %collective-permute-done.3.prev_ref.edge_in) | copy-start | bytes 393220
  74.3 6.6 %copy-start.5 = (bf16[64,1024]{1,0:T(8,128)(2,1)S(1)}, bf16[64,1024]{1,0:T(8,128)(2,1)}, u32[]{:S(2)}) copy-start(bf16[64,1024]{1,0:T(8,128)(2,1)} %get-tuple-element.42.low_in) | copy-start | bytes 393220
  74.3 17.9 %all-to-all-start.2 = ((bf16[128,8,128]{2,1,0:T(8,128)(2,1)}), bf16[128,8,128]{2,1,0:T(8,128)(2,1)S(1)}, u32[]{:S(2)}, u32[]{:S(2)}) async-start(bf16[128,8,128]{2,1,0:T(8,128)(2,1)} %bitcast.20), calls=%async_computation.2 | async-start | bytes 524288 | tf_op jit(solution)/shard_map/all_to_all | solution.py:823
  81.0 9.8 %collective-permute-start.2 = (bf16[64,1024]{1,0:T(8,128)(2,1)S(1)}, bf16[64,1024]{1,0:T(8,128)(2,1)S(1)}, u32[]{:S(2)}, u32[]{:S(2)}) collective-permute-start(bf16[64,1024]{1,0:T(8,128)(2,1)S(1)} %copy-done.5), channel_id=1, source_target_pairs={{2,0},{4,2},{6,4},{8,6},{10,8},{12,10},{14,12},{16,14},{18,16},{20... | collective-permute-start | bytes 393224 | tf_op jit(solution)/shard_map/ppermute | solution.py:635
